TPU v7x, 32 devices: a whole 2x2x4 slice. The times are simulated.
32 devices in a mesh: orb: 8 (over y, x, core), pln: 4 (over z).
Axes of the slice: x: 2, y: 2, z: 4, core: 2. Of those that a mesh axis runs over, the one named last changes fastest.
Arguments:
- orbitals: bfloat16 [32, 32768], P('orb'), may hold values from -6 to 6
- occupations: float32 [32], P('orb'), may hold values from 0.5 to 2
- box_offsets: int32 [32, 3], P('orb'), may hold values from 0 to 96
- kernel_spectrum: float32 [256, 256, 256], P(None, 'pln', 'orb'), may hold values from 0.05 to 3.4, as said below
Outputs:
- hartree_terms: bfloat16 [32, 32768], P('orb', 'pln')
Inputs may be any that keep to these rules, and one draw needn't show every extreme that they name: `box_offsets`: each orbital's box of 32 cells a side lies inside the fine grid. `kernel_spectrum`: positive and even: unchanged when any index k is replaced by (256 - k) mod 256.
All inputs are finite; a program needn't handle non-finite values.
Results may differ from a plain program's by a relative error of at most 0.003.
Values may be sent and summed in bfloat16 or wider, within the bound.
No kernel may reach another device: no remote copies, remote signals or barrier semaphores. Data moves between devices by JAX's collectives and lax.ppermute only.
A program may use at most 128 MiB of HBM per device.

v0:
```python
import math

import jax
import jax.numpy as jnp
from jax import lax
from jax.sharding import PartitionSpec as P

G = 128
BOX = 32


MAGIC_TAPS = (
    8.433424733352934e-07,
    -1.290557201342061e-05,
    8.76298447621056e-05,
    -0.00030158038132690465,
    0.001747237136729939,
    -0.009420470302010804,
    0.023738214637249424,
    0.0612625895831208,
    0.9940415697834004,
    -0.06048952891969835,
    -0.021030251609303816,
    0.013372634148547948,
    -0.0034412814449349387,
    0.0004944322768868992,
    -5.185986881173433e-05,
    2.7273449291197967e-06,
)
PRECISE = lax.Precision.HIGHEST


def magic_matrix(positions, width):
    taps = jnp.array(MAGIC_TAPS, dtype=jnp.float32)
    shifted = jnp.arange(width, dtype=jnp.int32)[None, :] - positions[:, None]
    hits = (shifted[:, :, None] == jnp.arange(-8, 8, dtype=jnp.int32)[None, None, :]).astype(
        jnp.float32
    )
    inside = ((positions >= 0) & (positions < width)).astype(jnp.float32)
    return jnp.sum(hits * taps, axis=2) * inside[:, None]


def expand_all(coefs, depth_filters, filters):
    section = jnp.einsum("ojk,okyx->ojyx", depth_filters, coefs, precision=PRECISE)
    section = jnp.einsum("ak,ojkx->ojax", filters, section, precision=PRECISE)
    return jnp.einsum("bx,ojax->ojab", filters, section, precision=PRECISE)


def contract_all(weighted, depth_filters, filters):
    section = jnp.einsum("bx,ojab->ojax", filters, weighted, precision=PRECISE)
    section = jnp.einsum("ak,ojax->ojkx", filters, section, precision=PRECISE)
    return jnp.einsum("ojk,ojyx->okyx", depth_filters, section, precision=PRECISE)


def fourier_table(count_in, count_out, doubled, sign):
    inputs = jnp.arange(count_in, dtype=jnp.int32)[:, None]
    outputs = jnp.arange(count_out, dtype=jnp.int32)[None, :]
    phase = inputs * outputs % doubled
    angle = phase.astype(jnp.float32) * (2.0 * math.pi / doubled)
    return (jnp.cos(angle), sign * jnp.sin(angle))


def along(stack, which, tables):
    letters = "abcd"[: stack.ndim - 1]
    target = letters[:which] + "e" + letters[which + 1 :]
    pattern = letters + "," + letters[which] + "e->" + target
    cosine, sine = tables
    real_part = stack[0]
    imag_part = stack[1]

    def multiply(values, table):
        return jnp.einsum(pattern, values, table, precision=PRECISE)

    return jnp.stack(
        [
            multiply(real_part, cosine) - multiply(imag_part, sine),
            multiply(real_part, sine) + multiply(imag_part, cosine),
        ]
    )


def per_device(orbitals, occupations, box_offsets, kernel_spectrum):
    orbital_count = orbitals.shape[0]
    plane_groups = lax.axis_size("pln")
    slab_depth = G // plane_groups
    doubled = 2 * G
    plane_index = lax.axis_index("pln")
    filters = magic_matrix(jnp.arange(BOX, dtype=jnp.int32), BOX)
    coefs = orbitals.astype(jnp.float32).reshape(orbital_count, BOX, BOX, BOX)
    plane_rows = plane_index * slab_depth + jnp.arange(slab_depth, dtype=jnp.int32)
    local_rows = plane_rows[None, :] - box_offsets[:, 0:1]
    depth_filters = jax.vmap(lambda rows: magic_matrix(rows, BOX))(local_rows)
    psi_planes = expand_all(coefs, depth_filters, filters)
    density_terms = occupations[:, None, None, None] * psi_planes * psi_planes
    box_steps = jnp.arange(BOX, dtype=jnp.int32)
    grid_rows = (box_offsets[:, 1:2] + box_steps[None, :])[:, :, None]
    grid_cols = (box_offsets[:, 2:3] + box_steps[None, :])[:, None, :]
    placed_terms = jnp.moveaxis(density_terms, 1, 0)
    partial_density = (
        jnp.zeros((slab_depth, G, G), jnp.float32).at[:, grid_rows, grid_cols].add(placed_terms)
    )
    forward_cos, forward_sin = fourier_table(G, doubled, doubled, -1.0)
    slab = lax.psum_scatter(partial_density, "orb", scatter_dimension=1, tiled=True)
    spectrum = jnp.stack(
        [
            jnp.dot(slab, forward_cos, precision=PRECISE),
            jnp.dot(slab, forward_sin, precision=PRECISE),
        ]
    )
    spectrum = lax.all_to_all(
        spectrum.astype(jnp.bfloat16), "orb", split_axis=3, concat_axis=2, tiled=True
    ).astype(spectrum.dtype)
    spectrum = along(spectrum, 1, (forward_cos, forward_sin))
    spectrum = lax.all_to_all(spectrum, "pln", split_axis=2, concat_axis=1, tiled=True)
    spectrum = along(spectrum, 0, (forward_cos, forward_sin))
    spectrum = spectrum * kernel_spectrum[None]
    inverse_cos, inverse_sin = fourier_table(doubled, G, doubled, 1.0)
    spectrum = along(spectrum, 0, (inverse_cos, inverse_sin))
    spectrum = lax.all_to_all(spectrum, "pln", split_axis=1, concat_axis=2, tiled=True)
    spectrum = along(spectrum, 1, (inverse_cos, inverse_sin))
    spectrum = lax.all_to_all(spectrum, "orb", split_axis=2, concat_axis=3, tiled=True)
    scale = 1.0 / float(doubled) ** 3
    potential_rows = (
        jnp.dot(spectrum[0], inverse_cos, precision=PRECISE)
        - jnp.dot(spectrum[1], inverse_sin, precision=PRECISE)
    ) * scale
    potential_slab = lax.all_gather(potential_rows, "orb", axis=1, tiled=True)
    potential_whole = lax.all_gather(potential_slab, "pln", axis=0, tiled=True)
    own_count = orbital_count // plane_groups
    first = plane_index * own_count
    own_coefs = lax.dynamic_slice_in_dim(coefs, first, own_count, 0)
    own_offsets = lax.dynamic_slice_in_dim(box_offsets, first, own_count, 0)
    full_filters = jnp.broadcast_to(filters, (own_count, BOX, BOX))
    own_psi = expand_all(own_coefs, full_filters, filters)
    own_potential = jax.vmap(
        lambda corner: lax.dynamic_slice(
            potential_whole, (corner[0], corner[1], corner[2]), (BOX, BOX, BOX)
        )
    )(own_offsets)
    finished = (
        contract_all(own_potential * own_psi, full_filters, filters)
        .reshape(own_count, BOX * BOX * BOX)
        .astype(jnp.bfloat16)
    )
    return lax.all_to_all(finished, "pln", split_axis=1, concat_axis=0, tiled=True)


def solution(mesh):
    in_specs = (P("orb", None), P("orb"), P("orb", None), P(None, "pln", "orb"))
    out_specs = P("orb", "pln")
    return jax.shard_map(
        per_device, mesh=mesh, in_specs=in_specs, out_specs=out_specs, check_vma=False
    )
```

profile of v0, /device:TPU:0, one launch (start us, length us, event | category | flops | bytes accessed | tf_op | source)
XLA Modules:
  0.0 628.1 jit_solution(11408609934072445522)
XLA Ops:
  16.3 5.0 fusion.2
  24.7 26.4 %scatter_custom_fusion = f32[32,16384]{0,1:T(8,128)} fusion(s32[4096]{0:T(1024)S(1)} %reshape.294, f32[4096,32]{1,0:T(8,128)} %bitcast.257, f32[]{:T(128)} %constant.19.clone.1), kind=kCustom, calls=%fused_computation.2 | custom fusion | flops 131072 | bytes 2097664
  51.0 6.5 %copy.172 = f32[32,128,128]{2,1,0:T(8,128)} copy(f32[32,128,128]{0,2,1:T(8,128)} %bitcast.226) | data formatting | bytes 4194304 | tf_op jit(solution)/shard_map/scatter-add | solution.py:100
  57.5 44.1 %reduce-scatter.2.cloned.1.call-done = f32[32,16,128]{2,1,0:T(8,128)} async-done(((f32[32,128,128]{2,1,0:T(8,128)}), f32[32,16,128]{2,1,0:T(8,128)}) %reduce-scatter.2.cloned.1.call-update) | async-done | bytes 262160 | tf_op jit(solution)/shard_map/reduce_scatter | solution.py:103
  113.7 12.5 %all_to_all.73 = bf16[8,2,16384]{2,1,0:T(2,128)(2,1)S(1)} all-to-all(bf16[8,2,16384]{2,1,0:T(2,128)(2,1)S(1)} %reshape.330), channel_id=1, replica_groups=mesh['orb'=8,'pln'=4] {'orb'}, dimensions={0} | all-to-all | bytes 1048576 | tf_op jit(solution)/shard_map/all_to_all | solution.py:110
  128.2 5.7 copy.174
  145.1 8.4 %copy.179 = f32[2,32,256,32]{3,1,0,2:T(8,128)} copy(f32[2,32,256,32]{2,3,1,0:T(8,128)} %pad_maximum_fusion) | data formatting | bytes 4194304 | tf_op jit(solution)/shard_map/stack | solution.py:74
  153.5 7.1 %reshape.332 = f32[4,1,131072]{2,1,0:T(1,128)} reshape(f32[256,2,32,32]{3,2,1,0:T(8,128)} %bitcast.224) | data formatting | bytes 4194304
  160.6 4.6 all-to-all-start.1
  169.8 43.1 %all-to-all-done.1 = f32[4,1,131072]{2,1,0:T(1,128)} async-done(((f32[4,1,131072]{2,1,0:T(1,128)}), f32[4,1,131072]{2,1,0:T(1,128)}, u32[]{:S(2)}, u32[]{:S(2)}) %all-to-all-start.1) | async-done | bytes 2097184 | tf_op jit(solution)/shard_map/all_to_all | solution.py:114
  213.4 9.1 %reduce.10 = f32[4,131072]{1,0:T(4,128)} reduce(f32[4,1,131072]{2,1,0:T(1,128)} %all-to-all-done.1, f32[]{:T(128)} %broadcast.254), dimensions={1}, to_apply=%all_to_all.57.reduce_sub_computation | reduce | bytes 4194308 | tf_op jit(solution)/shard_map/all_to_all | solution.py:114
  222.5 7.7 %reshape.333 = f32[256,2,32,32]{3,2,1,0:T(8,128)} reshape(f32[4,131072]{1,0:T(4,128)} %reduce.10) | data formatting | bytes 4194304
  230.2 8.0 %copy.180 = f32[2,32,4,64,32]{3,4,1,2,0:T(8,128)} copy(f32[2,32,4,64,32]{4,1,0,3,2:T(8,128)} %bitcast.225) | data formatting | bytes 4194304 | tf_op jit(solution)/shard_map/all_to_all | solution.py:114
  238.2 4.6 fusion.209
  274.3 5.6 copy.186
  279.8 5.7 reshape.334
  285.5 52.1 %all_to_all.74 = f32[4,1,131072]{2,1,0:T(1,128)} all-to-all(f32[4,1,131072]{2,1,0:T(1,128)} %reshape.334), channel_id=1, replica_groups=mesh['orb'=8,'pln'=4] {'pln'}, dimensions={0} | all-to-all | bytes 4194304 | tf_op jit(solution)/shard_map/all_to_all | solution.py:119
  337.6 9.0 %reduce.11 = f32[4,131072]{1,0:T(4,128)} reduce(f32[4,1,131072]{2,1,0:T(1,128)} %all_to_all.74, f32[]{:T(128)} %broadcast.254), dimensions={1}, to_apply=%all_to_all.60.reduce_sub_computation | reduce | bytes 4194308 | tf_op jit(solution)/shard_map/all_to_all | solution.py:119
  346.7 5.5 reshape.335
  382.9 18.2 %all_to_all.75 = f32[8,1,32768]{2,1,0:T(1,128)S(1)} all-to-all(f32[8,1,32768]{2,1,0:T(1,128)S(1)} %reshape.336), channel_id=1, replica_groups=mesh['orb'=8,'pln'=4] {'orb'}, dimensions={0} | all-to-all | bytes 2097152 | tf_op jit(solution)/shard_map/all_to_all | solution.py:121
  407.5 4.6 copy.191
  427.2 25.5 %all-gather.3.cloned.1.call-done = f32[32,128,128]{2,1,0:T(8,128)} async-done(((f32[32,16,128]{2,1,0:T(8,128)}), f32[32,128,128]{2,1,0:T(8,128)}) %all-gather.3.cloned.1.call-update) | async-done | bytes 2097168 | tf_op jit(solution)/shard_map/all_gather | solution.py:127
  461.7 142.3 %all-gather.5.cloned.1.call-done = f32[128,128,128]{2,1,0:T(8,128)} async-done(((f32[32,128,128]{2,1,0:T(8,128)}), f32[128,128,128]{2,1,0:T(8,128)}) %all-gather.5.cloned.1.call-update) | async-done | bytes 8388624 | tf_op jit(solution)/shard_map/all_gather | solution.py:128
  612.5 8.1 %all_to_all.76 = bf16[4,2,4096]{2,1,0:T(2,128)(2,1)S(1)} all-to-all(bf16[4,2,4096]{2,1,0:T(2,128)(2,1)S(1)} %reshape.338), channel_id=1, replica_groups=mesh['orb'=8,'pln'=4] {'pln'}, dimensions={0} | all-to-all | bytes 131072 | tf_op jit(solution)/shard_map/all_to_all | solution.py:145
  (108 shorter events, 139.4 us)
Async XLA Ops:
  6.5 3.9 copy-start.3
  6.5 95.0 %reduce-scatter.2.cloned.1.call-start = ((), (), s32[]{:S(2)}) async-start(), calls=%async_computation.6 | async-start | bytes 2359296 | tf_op jit(solution)/shard_map/reduce_scatter | solution.py:103
  12.0 4.3 copy-start.4
  160.6 52.3 %all-to-all-start.1 = ((f32[4,1,131072]{2,1,0:T(1,128)}), f32[4,1,131072]{2,1,0:T(1,128)}, u32[]{:S(2)}, u32[]{:S(2)}) async-start(f32[4,1,131072]{2,1,0:T(1,128)} %reshape.332), calls=%async_computation.2 | async-start | bytes 4194304 | tf_op jit(solution)/shard_map/all_to_all | solution.py:114
  165.2 287.5 %all-gather.3.cloned.1.call-start = ((), (), s32[]{:S(2)}) async-start(), calls=%async_computation.7 | async-start | bytes 2359296 | tf_op jit(solution)/shard_map/all_gather | solution.py:127
  255.4 4.1 copy-start.1
  259.5 2.9 copy-start
  362.7 3.0 copy-start.2
  427.1 176.9 %all-gather.5.cloned.1.call-start = ((), (), s32[]{:S(2)}) async-start(), calls=%async_computation.8 | async-start | bytes 10485760 | tf_op jit(solution)/shard_map/all_gather | solution.py:128
Sparse Core Ops, SparseCore 0:
  57.6 43.8 reduce-scatter.1
  427.3 25.4 all-gather.2
  454.4 149.6 all-gather.4
where the time goes:
time: 638 us; the launch traced here: 628 us
  waiting for transfers between devices  255 us (40%)
  local copies, waits for them, and re-layouts  144 us (23%)
  blocking collectives  90.9 us (14%)
  matrix products  58.7 us (9%)
  other arithmetic  54.8 us (9%)
  between operations  19.4 us (3%)
    all_gather x1, waiting for transfers between devices, per_device(): potential_whole = lax.all_gather(potential_slab, 'pln', axis=0, tiled=True)  142 us
    all_to_all x1, blocking collectives, per_device(): lax.all_to_all(spectrum, 'pln', split_axis=1, concat_axis=2, tiled=True)  52.1 us
    unnamed x24, local copies, waits for them, and re-layouts  44.6 us
    reduce_scatter x1, waiting for transfers between devices, per_device(): lax.psum_scatter(partial_density, 'orb', scatter_dimension=1, tiled=True)  44.1 us
    all_to_all x1, waiting for transfers between devices, per_device(): lax.all_to_all(spectrum, 'pln', split_axis=2, concat_axis=1, tiled=True)  43.1 us
    unnamed x5, other arithmetic  28.2 us
    all_gather x1, waiting for transfers between devices, per_device(): potential_slab = lax.all_gather(potential_rows, 'orb', axis=1, tiled=True)  25.5 us
    dot_general x8, matrix products, multiply(): return jnp.einsum(pattern, values, table, precision=PRECISE)  23.6 us
  transfers between devices with their start and end apart: 4, of which 4 were waited for; matrix products, arithmetic and copies ran while one was open for 1% of the time, Pallas kernels for 0%

commit v1 on v0

v1 whole, which is shorter than its diff:
```python
import functools
import math

import jax
import jax.numpy as jnp
import numpy as np
from jax import lax
from jax.experimental import pallas as pl
from jax.experimental.pallas import tpu as pltpu
from jax.sharding import PartitionSpec as P

MAGIC_TAPS = (
    8.433424733352934e-07,
    -1.290557201342061e-05,
    8.76298447621056e-05,
    -0.00030158038132690465,
    0.001747237136729939,
    -0.009420470302010804,
    0.023738214637249424,
    0.0612625895831208,
    0.9940415697834004,
    -0.06048952891969835,
    -0.021030251609303816,
    0.013372634148547948,
    -0.0034412814449349387,
    0.0004944322768868992,
    -5.185986881173433e-05,
    2.7273449291197967e-06,
)
F32 = jnp.float32
BF16 = jnp.bfloat16
SUB = 8
VMEM_LIMIT = 48 * 1024 * 1024


def magic_filter(box):
    table = np.zeros((box, box))
    for row in range(box):
        for tap in range(-8, 8):
            if 0 <= row + tap < box:
                table[row, row + tap] = MAGIC_TAPS[tap + 8]
    return table.astype(np.float32).astype(np.float64)


def cas(product, doubled):
    angle = 2.0 * math.pi * (product % doubled) / doubled
    return np.cos(angle) + np.sin(angle)


def halves(table):
    high = np.asarray(table, np.float32).astype(jnp.bfloat16)
    low = (np.asarray(table, np.float64) - high.astype(np.float64)).astype(jnp.bfloat16)
    return high, low


def split(values):
    high = values.astype(BF16)
    low = (values - high.astype(F32)).astype(BF16)
    return high, low


def dot(left, right, dims=((1,), (0,))):
    return lax.dot_general(left, right, (dims, ((), ())), preferred_element_type=F32)


def table_dot(high, low, values):
    up, down = split(values)
    return dot(high, up) + dot(low, up) + dot(high, down)


def dot_table(values, high, low):
    up, down = split(values)
    return dot(up, high) + dot(up, low) + dot(down, high)


class Plan:
    def __init__(self, mesh, orbital_shape, kernel_shape):
        self.orb = mesh.shape["orb"]
        self.pln = mesh.shape["pln"]
        self.doubled = doubled = kernel_shape[0]
        self.grid = grid = doubled // 2
        self.box = box = round(orbital_shape[1] ** (1 / 3))
        self.per_group = grid // box
        self.groups = orbital_shape[0] // self.orb // self.per_group
        self.ky_block = kernel_shape[1] // self.pln
        self.kx_block = kernel_shape[2] // self.orb
        self.slots = SUB * -(-self.kx_block // (SUB * self.pln))
        self.half = self.pln // 2
        self.rows = self.orb * self.slots
        self.box_part = box // self.pln
        magic = magic_filter(box)
        eye = np.eye(SUB)
        depth = np.zeros((box, self.per_group, self.per_group, box))
        for n in range(self.per_group):
            depth[:, n, n, :] = magic.T
        depth = depth.reshape(grid, grid)
        self.depth = halves(depth)
        self.inner = halves(np.kron(eye, magic))
        self.outer = halves(np.kron(magic, eye))
        self.inner_back = halves(np.kron(eye, magic.T))
        self.outer_back = halves(np.kron(magic.T, eye))
        places = np.arange(grid)
        wave = np.zeros((self.pln, self.orb, self.slots, grid))
        for p in range(self.pln):
            for s in range(self.slots):
                within = p * self.slots + s
                if within < self.kx_block:
                    k = self.kx_block * np.arange(self.orb) + within
                    wave[p, :, s, :] = cas(k[:, None] * places[None, :], doubled)
        self.wave = wave.reshape(self.pln, self.rows, grid).astype(np.float32)
        along_z = cas(places[:, None] * np.arange(doubled)[None, :], doubled)
        self.forward_z = halves(along_z)
        self.inverse_z = halves(along_z.T / doubled)
        forward = np.zeros((self.pln, 2, grid, grid))
        weight = np.zeros((self.pln, 2, grid))
        for p in range(self.pln):
            group, index = divmod(p, self.half)
            base = grid * group
            for piece in range(self.half):
                block = (index - piece) % self.half
                for r in range(self.ky_block):
                    j = block * self.ky_block + r
                    row = piece * self.ky_block + r
                    angle = 2.0 * math.pi * ((base + j) * places % doubled) / doubled
                    forward[p, 0, row] = np.cos(angle)
                    forward[p, 1, row] = np.sin(angle)
                    weight[p, :, row] = 2.0
                    if j == 0:
                        edge = (base + grid) % doubled
                        forward[p, 1, row] = np.cos(2.0 * math.pi * (edge * places % doubled) / doubled)
                        weight[p, :, row] = 1.0
        inverse = forward * weight[..., None] / doubled**2
        self.forward_y = halves(forward.reshape(self.pln, doubled, grid))
        self.inverse_y = halves(inverse.reshape(self.pln, doubled, grid).transpose(0, 2, 1))


def lane_owner(shape, box):
    return lax.broadcasted_iota(jnp.int32, shape, len(shape) - 1) // box


def density_kernel(
    plan, where_ref, corner_ref, weight_ref, coef_ref, dh_ref, dl_ref, ih_ref, il_ref, oh_ref, ol_ref, wave_ref,
    send_ref, psi_ref, wave_out_ref, stage_ref,
):
    box, grid, count = plan.box, plan.grid, plan.per_group
    section = box * box
    group = pl.program_id(0)
    for p in range(box):
        stage_ref[count * p : count * (p + 1), :] = coef_ref[0, :, section * p : section * (p + 1)].astype(F32)
    coef = stage_ref[...].astype(BF16)
    doubled_coef = jnp.concatenate([coef, coef], axis=0)
    depth = jnp.concatenate([dh_ref[...], dl_ref[...]], axis=0)
    first = dot(doubled_coef, depth, ((0,), (0,)))
    span = SUB * box
    ih, il, oh, ol = ih_ref[...], il_ref[...], oh_ref[...], ol_ref[...]
    second = [table_dot(ih, il, first[span * t : span * (t + 1)]) for t in range(box // SUB)]
    second = jnp.concatenate(second, axis=0).reshape(box, box // SUB, SUB, grid)
    for t in range(box // SUB):
        third = table_dot(oh, ol, second[:, t].reshape(span, grid))
        psi_ref[0, :, SUB * t : SUB * (t + 1), :] = third.reshape(box, SUB, grid)
    owner = lane_owner((1, grid), box)
    whole_wave = wave_ref[where_ref[0]]
    wave = jnp.zeros_like(whole_wave)
    weight = jnp.zeros((1, grid), F32)
    for n in range(count):
        shift = lax.rem(box * n - corner_ref[group * count + n, 2] + grid, grid)
        wave = jnp.where(owner == n, pltpu.roll(whole_wave, shift, 1), wave)
        weight = jnp.where(owner == n, weight_ref[group * count + n], weight)
    wave_out_ref[0] = wave
    wave_both = jnp.concatenate(split(wave), axis=1)
    for pair in range(box // 2):
        columns = []
        for b in (2 * pair, 2 * pair + 1):
            psi = psi_ref[0, b]
            density = psi * psi * weight
            parts = [jnp.where(owner == n, density, 0.0) for n in range(count)]
            columns.append(jnp.concatenate(parts, axis=0).astype(BF16))
        both = jnp.concatenate(columns, axis=1)
        out = dot(wave_both, jnp.concatenate([both, both], axis=0))
        for o in range(plan.orb):
            rows = out[plan.slots * o : plan.slots * (o + 1)]
            tile = jnp.concatenate([rows[:, :grid], rows[:, grid:]], axis=0)
            send_ref[o, 0, 2 * plan.slots * pair : 2 * plan.slots * (pair + 1), :] = tile.astype(send_ref.dtype)


def solve_kernel(plan, where_ref, corner_ref, recv_ref, *refs):
    half, slots, grid, box, count = plan.half, plan.slots, plan.grid, plan.box, plan.per_group
    kernel_refs = refs[:half]
    edge_refs = refs[half : 2 * half]
    zh_ref, zl_ref, yh_ref, yl_ref, vh_ref, vl_ref, wh_ref, wl_ref, send_ref, field_ref = refs[2 * half :]
    index = where_ref[0]
    depth = box * slots
    owner = lane_owner((1, grid), box)
    field_ref[...] = jnp.zeros_like(field_ref)

    def start(number):
        return pl.multiple_of(corner_ref[number, 1] * slots, SUB)

    def place(group, carry):
        values = recv_ref[group].astype(F32)
        for n in range(count):
            number = group * count + n
            shift = lax.rem(corner_ref[number, 0] - box * n + grid, grid)
            moved = pltpu.roll(jnp.where(owner == n, values, 0.0), shift, 1)
            field_ref[pl.ds(start(number), depth), :] += moved
        return carry

    lax.fori_loop(0, plan.orb * plan.groups, place, 0)
    zh, zl, wh, wl = zh_ref[...], zl_ref[...], wh_ref[...], wl_ref[...]
    yh, yl, vh, vl = yh_ref[index], yl_ref[index], vh_ref[index], vl_ref[index]
    row = lax.broadcasted_iota(jnp.int32, (grid, 1), 0)
    edge_row = lax.rem(index, half) * plan.ky_block
    for s in range(slots):
        plane = field_ref[pl.ds(s, grid, stride=slots), :]
        modes = table_dot(yh, yl, dot_table(plane, zh, zl))
        kernel = jnp.concatenate([ref[:, s, :] for ref in kernel_refs], axis=0)
        edge = edge_refs[0][0, s : s + 1, :]
        for ref in edge_refs[1:]:
            edge = edge + ref[0, s : s + 1, :]
        other = jnp.where(row == edge_row, edge, kernel)
        modes = modes * jnp.concatenate([kernel, other], axis=0)
        plane = dot_table(table_dot(vh, vl, modes), wh, wl)
        field_ref[pl.ds(s, grid, stride=slots), :] = plane

    def cut(group, carry):
        values = jnp.zeros((depth, grid), F32)
        for n in range(count):
            number = group * count + n
            shift = lax.rem(box * n - corner_ref[number, 0] + grid, grid)
            rows = field_ref[pl.ds(start(number), depth), :]
            values = jnp.where(owner == n, pltpu.roll(rows, shift, 1), values)
        send_ref[group] = values.astype(send_ref.dtype)
        return carry

    lax.fori_loop(0, plan.orb * plan.groups, cut, 0)


def terms_kernel(
    plan, recv_ref, psi_ref, wave_ref, dh_ref, dl_ref, ih_ref, il_ref, oh_ref, ol_ref, send_ref, stage_ref,
):
    box, grid, count, slots = plan.box, plan.grid, plan.per_group, plan.slots
    owner = lane_owner((1, grid), box)
    high, low = split(wave_ref[0].T)
    wave = jnp.concatenate([high, low, high], axis=1)
    for pair in range(box // 2):
        columns = []
        for b in (2 * pair, 2 * pair + 1):
            columns.append(
                jnp.concatenate([recv_ref[o, 0, slots * b : slots * (b + 1), :].astype(F32) for o in range(plan.orb)], axis=0)
            )
        up, down = split(jnp.concatenate(columns, axis=1))
        out = dot(wave, jnp.concatenate([up, up, down], axis=0))
        for side, b in enumerate((2 * pair, 2 * pair + 1)):
            mine = out[:, grid * side : grid * (side + 1)]
            potential = jnp.zeros((box, grid), F32)
            for n in range(count):
                potential = jnp.where(owner == n, mine[box * n : box * (n + 1)], potential)
            stage_ref[b] = potential * psi_ref[0, b]
    span = SUB * box
    ih, il, oh, ol = ih_ref[...], il_ref[...], oh_ref[...], ol_ref[...]
    for t in range(box // SUB):
        values = stage_ref[SUB * t : SUB * (t + 1)].reshape(span, grid)
        stage_ref[SUB * t : SUB * (t + 1)] = table_dot(ih, il, values).reshape(SUB, box, grid)
    for t in range(box // SUB):
        values = stage_ref[:, SUB * t : SUB * (t + 1), :].reshape(span, grid)
        stage_ref[:, SUB * t : SUB * (t + 1), :] = table_dot(oh, ol, values).reshape(box, SUB, grid)
    up, down = split(stage_ref[...].reshape(box * box, grid))
    dh, dl = dh_ref[...], dl_ref[...]
    last = ((1,), (1,))
    out = dot(dh, up, last) + dot(dl, up, last) + dot(dh, down, last)
    part = plan.box_part * count
    for p in range(plan.pln):
        send_ref[p, 0] = out[part * p : part * (p + 1)].astype(send_ref.dtype)


def sum_kernel(plan, recv_ref, out_ref):
    total = recv_ref[0, 0].astype(F32)
    for p in range(1, plan.pln):
        total = total + recv_ref[p, 0].astype(F32)
    section = plan.box * plan.box
    count = plan.per_group
    for j in range(plan.box_part):
        out_ref[0, :, section * j : section * (j + 1)] = total[count * j : count * (j + 1)].astype(out_ref.dtype)


def whole_spec(array):
    rank = len(array.shape)
    return pl.BlockSpec(array.shape, lambda *_: (0,) * rank)


def per_device(plan, orbitals, occupations, box_offsets, kernel_spectrum):
    orb, pln, half, slots = plan.orb, plan.pln, plan.half, plan.slots
    groups, count, box, grid = plan.groups, plan.per_group, plan.box, plan.grid
    plane_index = lax.axis_index("pln")
    where = plane_index.astype(jnp.int32)[None]
    corners = lax.all_gather(box_offsets, "orb", axis=0, tiled=True)
    by_ky = jnp.transpose(kernel_spectrum, (1, 2, 0))

    def columns_for(target, rows):
        first = jnp.minimum(target * slots, max(plan.kx_block - slots, 0))
        return lax.dynamic_slice(by_ky, (0, first, 0), (rows, slots, plan.doubled))

    group_of, index = plane_index // half, plane_index % half
    pieces = [columns_for(plane_index, plan.ky_block)]
    for step in range(1, half):
        target = group_of * half + (index + step) % half
        pairs = [(g * half + i, g * half + (i + step) % half) for g in range(2) for i in range(half)]
        pieces.append(lax.ppermute(columns_for(target, plan.ky_block), "pln", pairs))
    edges = []
    for step in range(half):
        target = (1 - group_of) * half + step
        edges.append(lax.ppermute(columns_for(target, 1), "pln", [(0, half + step), (half, step)]))

    smem = pl.BlockSpec(memory_space=pltpu.SMEM)
    params = pltpu.CompilerParams(vmem_limit_bytes=VMEM_LIMIT)
    coefs = orbitals.reshape(groups, count, orbitals.shape[1])
    area = box * slots
    tables = [*plan.depth, *plan.inner, *plan.outer]
    send, psi, wave = pl.pallas_call(
        functools.partial(density_kernel, plan),
        grid=(groups,),
        in_specs=[smem, smem, smem, pl.BlockSpec((1, count, orbitals.shape[1]), lambda g: (g, 0, 0))]
        + [whole_spec(t) for t in tables]
        + [whole_spec(plan.wave)],
        out_specs=[
            pl.BlockSpec((orb, 1, area, grid), lambda g: (0, g, 0, 0)),
            pl.BlockSpec((1, box, box, grid), lambda g: (g, 0, 0, 0)),
            pl.BlockSpec((1, plan.rows, grid), lambda g: (g, 0, 0)),
        ],
        out_shape=[
            jax.ShapeDtypeStruct((orb, groups, area, grid), BF16),
            jax.ShapeDtypeStruct((groups, box, box, grid), F32),
            jax.ShapeDtypeStruct((groups, plan.rows, grid), F32),
        ],
        scratch_shapes=[pltpu.VMEM((grid, box * box), F32)],
        compiler_params=params,
        name="density",
    )(where, box_offsets, occupations, coefs, *tables, plan.wave)
    received = lax.all_to_all(send, "orb", split_axis=0, concat_axis=0, tiled=True)
    received = received.reshape(orb * groups, area, grid)
    tables = [*plan.forward_z, *plan.forward_y, *plan.inverse_y, *plan.inverse_z]
    blocks = [received, *pieces, *edges, *tables]
    send = pl.pallas_call(
        functools.partial(solve_kernel, plan),
        grid=(1,),
        in_specs=[smem, smem] + [whole_spec(t) for t in blocks],
        out_specs=pl.BlockSpec((orb * groups, area, grid), lambda g: (0, 0, 0)),
        out_shape=jax.ShapeDtypeStruct((orb * groups, area, grid), F32),
        scratch_shapes=[pltpu.VMEM((grid * slots, grid), F32)],
        compiler_params=params,
        name="solve",
    )(where, corners, *blocks)
    send = send.reshape(orb, groups, area, grid)
    received = lax.all_to_all(send, "orb", split_axis=0, concat_axis=0, tiled=True)
    tables = [*plan.depth, *plan.inner_back, *plan.outer_back]
    part = plan.box_part * count
    send = pl.pallas_call(
        functools.partial(terms_kernel, plan),
        grid=(groups,),
        in_specs=[
            pl.BlockSpec((orb, 1, area, grid), lambda g: (0, g, 0, 0)),
            pl.BlockSpec((1, box, box, grid), lambda g: (g, 0, 0, 0)),
            pl.BlockSpec((1, plan.rows, grid), lambda g: (g, 0, 0)),
        ]
        + [whole_spec(t) for t in tables],
        out_specs=pl.BlockSpec((pln, 1, part, box * box), lambda g: (0, g, 0, 0)),
        out_shape=jax.ShapeDtypeStruct((pln, groups, part, box * box), F32),
        scratch_shapes=[pltpu.VMEM((box, box, grid), F32)],
        compiler_params=params,
        name="terms",
    )(received, psi, wave, *tables)
    received = lax.all_to_all(send, "pln", split_axis=0, concat_axis=0, tiled=True)
    cells = plan.box_part * box * box
    result = pl.pallas_call(
        functools.partial(sum_kernel, plan),
        grid=(groups,),
        in_specs=[pl.BlockSpec((pln, 1, part, box * box), lambda g: (0, g, 0, 0))],
        out_specs=pl.BlockSpec((1, count, cells), lambda g: (g, 0, 0)),
        out_shape=jax.ShapeDtypeStruct((groups, count, cells), BF16),
        compiler_params=params,
        name="sum",
    )(received)
    return result.reshape(groups * count, cells)


def solution(mesh):
    in_specs = (P("orb", None), P("orb"), P("orb", None), P(None, "pln", "orb"))
    out_specs = P("orb", "pln")

    def whole(orbitals, occupations, box_offsets, kernel_spectrum):
        plan = Plan(mesh, orbitals.shape, kernel_spectrum.shape)
        return jax.shard_map(
            functools.partial(per_device, plan), mesh=mesh, in_specs=in_specs, out_specs=out_specs, check_vma=False
        )(orbitals, occupations, box_offsets, kernel_spectrum)

    return whole
```

time: 638 us -> 81.6 us (0.13); the launches traced: 628 us -> 81 us
  waiting for transfers between devices: 255 us -> 0.01 us
  local copies, waits for them, and re-layouts: 144 us -> 6.76 us
  matrix products: 58.7 us -> 0 us
  other arithmetic: 54.8 us -> 0 us
  blocking collectives: 90.9 us -> 45.1 us
  between operations: 19.4 us -> 0.31 us
  Pallas kernels: 0 us -> 15.9 us
  starting transfers between devices: 5.07 us -> 12.9 us
    all_gather x2 -> x0, waiting for transfers between devices: 168 us -> none  [the longest x1 142 us: per_device(): potential_whole = lax.all_gather(potential_slab, 'pln', axis=0, tiled=True)]
    all_to_all x4 -> x2, blocking collectives: 90.9 us -> 35.7 us  [the longest x1 17.9 us: per_device(): lax.all_to_all(send, 'orb', split_axis=0, concat_axis=0, tiled=True)]
    dot_general x21 -> x0, matrix products: 48.4 us -> none  [the longest x8 23.6 us: multiply(): return jnp.einsum(pattern, values, table, precision=PRECISE)]
    reduce_scatter x1 -> x0, waiting for transfers between devices: 44.1 us -> none  [per_device(): lax.psum_scatter(partial_density, 'orb', scatter_dimension=1, tiled=True)]
    all_to_all x1, waiting for transfers between devices: 43.1 us -> 0.01 us  [per_device(): lax.all_to_all(send, 'orb', split_axis=0, concat_axis=0, tiled=True)]
    unnamed x24 -> x48, local copies, waits for them, and re-layouts: 44.6 us -> 3.23 us
    unnamed x5 -> x0, other arithmetic: 28.2 us -> none
    slice x10 -> x0, local copies, waits for them, and re-layouts: 25.2 us -> none  [the longest x4 12.8 us: along(): imag_part = stack[1]]
  transfers between devices with their start and end apart: 4 -> 4, of which waited for: 4 -> 0; matrix products, arithmetic and copies ran while one was open for 1% -> 1% of each run, Pallas kernels for 0% -> 4%
where the time goes in v1:
time: 81.6 us; the launch traced here: 81 us
  blocking collectives  45.1 us (55%)
  Pallas kernels  15.9 us (19%)
  starting transfers between devices  12.9 us (16%)
  local copies, waits for them, and re-layouts  6.76 us (8%)
    all_to_all x1, blocking collectives, per_device(): lax.all_to_all(send, 'orb', split_axis=0, concat_axis=0, tiled=True)  17.9 us
    all_to_all x1, blocking collectives, per_device(): lax.all_to_all(send, 'pln', split_axis=0, concat_axis=0, tiled=True)  17.8 us
    pallas_call x1, Pallas kernels, per_device(): pl.pallas_call(functools.partial(solve_kernel, plan), grid=(1,), in_specs...  10.1 us
    all_gather x1, blocking collectives, per_device(): corners = lax.all_gather(box_offsets, 'orb', axis=0, tiled=True)  9.41 us
    ppermute x2, starting transfers between devices, per_device(): lax.ppermute(columns_for(target, 1), 'pln', [(0, half + step), (half, ste...  6.13 us
    all_to_all x1, starting transfers between devices, per_device(): lax.all_to_all(send, 'orb', split_axis=0, concat_axis=0, tiled=True)  3.72 us
    dynamic_slice x2, local copies, waits for them, and re-layouts, columns_for(): return lax.dynamic_slice(by_ky, (0, first, 0), (rows, slots, plan.doubled))  3.54 us
    pallas_call x1, Pallas kernels, per_device(): pl.pallas_call(functools.partial(density_kernel, plan), grid=(groups,), i...  3.34 us
  transfers between devices with their start and end apart: 4, of which 0 were waited for; matrix products, arithmetic and copies ran while one was open for 1% of the time, Pallas kernels for 4%

profile of v1, /device:TPU:0, one launch (start us, length us, event | category | flops | bytes accessed | tf_op | source)
XLA Modules:
  0.0 81.0 jit_solution(466500054623648299)
XLA Ops:
  0.0 0.0 copy-start.10
  0.1 0.0 copy-start.11
  0.1 0.0 copy-start.1
  0.1 0.0 copy-start.2
  0.1 0.0 copy-start.3
  0.1 0.0 copy-start.4
  0.2 2.7 %dynamic-slice_bitcast_fusion = (f32[64,8,256]{2,1,0:T(8,128)}, f32[64,8,256]{2,1,0:T(8,128)S(1)}) fusion(f32[256,64,32]{0,2,1:T(8,128)} %param.26, s32[]{:T(128)S(6)} %select_n.31, s32[]{:T(128)S(6)} %select_n.27), kind=kLoop, calls=%fused_computation | loop fusion | bytes 2097160 | tf_op jit(solution)/shard_map/dynamic_slice | solution.py:301
  2.9 3.0 %collective-permute-start = (f32[64,8,256]{2,1,0:T(8,128)}, f32[64,8,256]{2,1,0:T(8,128)S(1)}, u32[]{:S(2)}, u32[]{:S(2)}) collective-permute-start(f32[64,8,256]{2,1,0:T(8,128)} %get-tuple-element.13), channel_id=1, source_target_pairs={{0,1},{1,0},{2,3},{3,2},{4,5},{5,4},{6,7},{7,6},{8,9},{9,8},{10,11... | collective-permute-start | bytes 1572872 | tf_op jit(solution)/shard_map/ppermute | solution.py:308
  6.0 3.3 %density.1 = (bf16[8,1,256,128]{3,2,1,0:T(8,128)(2,1)}, f32[1,32,32,128]{3,2,1,0:T(8,128)S(1)}, f32[1,64,128]{2,1,0:T(8,128)S(1)}) custom-call(s32[1]{0:T(128)} %bitcast.where_ref, s32[4,3]{1,0:T(4,128)S(1)} %copy-done.22, f32[4]{0:T(128)S(1)} %copy-done.23, bf16[1,4,32768]{2,1,0:T(4,128)(2,1)S(1)} %bitcast.17, bf16[128,128]{1,0:T(8,128)(2,1)S(1)} %copy-done.6, ...), custom_call_target="tpu_custom_call" | custom-call | tf_op jit(solution)/shard_map/density/pallas_call | solution.py:319
  9.4 0.6 copy-done.20
  10.0 3.7 %all-to-all-start = ((bf16[8,1,256,128]{3,2,1,0:T(8,128)(2,1)}), bf16[8,1,256,128]{3,2,1,0:T(8,128)(2,1)S(1)}, u32[]{:S(2)}, u32[]{:S(2)}) async-start(bf16[8,1,256,128]{3,2,1,0:T(8,128)(2,1)} %get-tuple-element.8), calls=%async_computation | async-start | bytes 1048576 | tf_op jit(solution)/shard_map/all_to_all | solution.py:339
  13.7 0.8 dynamic-slice_bitcast_fusion.2
  14.5 4.2 %collective-permute-start.2 = (f32[1,8,256]{2,1,0:T(8,128)S(1)}, f32[1,8,256]{2,1,0:T(8,128)S(1)}, u32[]{:S(2)}, u32[]{:S(2)}) collective-permute-start(f32[1,8,256]{2,1,0:T(8,128)S(1)} %get-tuple-element.11), channel_id=1, source_target_pairs={{0,3},{2,1},{4,7},{6,5},{8,11},{10,9},{12,15},{14,13},{16,19},{18,... | collective-permute-start | bytes 24584 | tf_op jit(solution)/shard_map/ppermute | solution.py:312
  18.7 1.9 %collective-permute-start.1 = (f32[1,8,256]{2,1,0:T(8,128)S(1)}, f32[1,8,256]{2,1,0:T(8,128)S(1)}, u32[]{:S(2)}, u32[]{:S(2)}) collective-permute-start(f32[1,8,256]{2,1,0:T(8,128)S(1)} %get-tuple-element.12), channel_id=1, source_target_pairs={{0,2},{2,0},{4,6},{6,4},{8,10},{10,8},{12,14},{14,12},{16,18},{18,... | collective-permute-start | bytes 24584 | tf_op jit(solution)/shard_map/ppermute | solution.py:312
  20.6 9.4 %all-gather = s32[8,4,3]{2,1,0:T(4,128)S(1)} all-gather(s32[1,4,3]{2,1,0:T(4,128)S(1)} %bitcast.19), channel_id=1, replica_groups=mesh['orb'=8,'pln'=4] {'orb'}, dimensions={0}, use_global_device_ids=true | all-gather | bytes 432 | tf_op jit(solution)/shard_map/all_gather | solution.py:296
  30.1 0.0 copy-start.17
  30.1 0.8 %copy-done.17 = bf16[256,128]{1,0:T(8,128)(2,1)S(1)} copy-done((bf16[256,128]{1,0:T(8,128)(2,1)S(1)}, bf16[256,128]{1,0:T(8,128)(2,1)}, u32[]{:S(2)}) %copy-start.17) | copy-done | bytes 65560
  31.0 0.8 %copy-done.18 = bf16[128,256]{1,0:T(8,128)(2,1)S(1)} copy-done((bf16[128,256]{1,0:T(8,128)(2,1)S(1)}, bf16[128,256]{1,0:T(8,128)(2,1)}, u32[]{:S(2)}) %copy-start.18) | copy-done | bytes 65560
  31.8 0.8 %copy-done.19 = bf16[128,256]{1,0:T(8,128)(2,1)S(1)} copy-done((bf16[128,256]{1,0:T(8,128)(2,1)S(1)}, bf16[128,256]{1,0:T(8,128)(2,1)}, u32[]{:S(2)}) %copy-start.19) | copy-done | bytes 65560
  32.7 10.1 %solve.1 = f32[8,256,128]{2,1,0:T(8,128)S(1)} custom-call(s32[1]{0:T(128)} %bitcast.where_ref, s32[32,3]{1,0:T(8,128)S(1)} %bitcast.18, bf16[8,256,128]{2,1,0:T(8,128)(2,1)S(1)} %bitcast.16, f32[64,8,256]{2,1,0:T(8,128)S(1)} %get-tuple-element.14.refs_0_, f32[64,8,256]{2,1,0:T(8,128)S(1)} %collective-permute-done.refs_1_, ...), custom_call_target="tpu_custom_call" | custom-call | tf_op jit(solution)/shard_map/solve/pallas_call | solution.py:343
  42.8 17.9 %all_to_all.15.recv_ref = f32[8,1,256,128]{3,2,1,0:T(8,128)S(1)} all-to-all(f32[8,1,256,128]{3,2,1,0:T(8,128)S(1)} %bitcast.15), channel_id=1, replica_groups=mesh['orb'=8,'pln'=4] {'orb'}, dimensions={0} | all-to-all | bytes 2097152 | tf_op jit(solution)/shard_map/all_to_all | solution.py:354
  60.7 1.8 %terms.1 = f32[4,1,32,1024]{3,2,1,0:T(8,128)S(1)} custom-call(f32[8,1,256,128]{3,2,1,0:T(8,128)S(1)} %all_to_all.15.recv_ref, f32[1,32,32,128]{3,2,1,0:T(8,128)S(1)} %get-tuple-element.9.psi_ref, f32[1,64,128]{2,1,0:T(8,128)S(1)} %copy-done.21, bf16[128,128]{1,0:T(8,128)(2,1)S(1)} %copy-done.6, bf16[128,128]{1,0:T(8,128)(2,1)S(1)} %copy-done.5, ...), custom_call_target="tpu_custom_call" | custom-call | tf_op jit(solution)/shard_map/terms/pallas_call | solution.py:357
  62.6 17.8 %all_to_all.16.recv_ref = f32[4,1,32,1024]{3,2,1,0:T(8,128)S(1)} all-to-all(f32[4,1,32,1024]{3,2,1,0:T(8,128)S(1)} %terms.1), channel_id=1, replica_groups=mesh['orb'=8,'pln'=4] {'pln'}, dimensions={0} | all-to-all | bytes 1048576 | tf_op jit(solution)/shard_map/all_to_all | solution.py:372
  80.4 0.7 sum.1
  (41 shorter events, 0.1 us)
Async XLA Ops:
  0.0 6.0 %copy-start.5 = (bf16[128,128]{1,0:T(8,128)(2,1)S(1)}, bf16[128,128]{1,0:T(8,128)(2,1)}, u32[]{:S(2)}) copy-start(bf16[128,128]{1,0:T(8,128)(2,1)} %constant.81.clone.dl_ref) | copy-start | bytes 98308
  0.0 6.0 %copy-start.6 = (bf16[128,128]{1,0:T(8,128)(2,1)S(1)}, bf16[128,128]{1,0:T(8,128)(2,1)}, u32[]{:S(2)}) copy-start(bf16[128,128]{1,0:T(8,128)(2,1)} %constant.80.clone.dh_ref) | copy-start | bytes 98308
  0.0 6.0 %copy-start.7 = (f32[4,64,128]{2,1,0:T(8,128)S(1)}, f32[4,64,128]{2,1,0:T(8,128)}, u32[]{:S(2)}) copy-start(f32[4,64,128]{2,1,0:T(8,128)} %constant.86.clone.wave_ref) | copy-start | bytes 393220
  0.0 6.0 %copy-start.8 = (bf16[256,256]{1,0:T(8,128)(2,1)S(1)}, bf16[256,256]{1,0:T(8,128)(2,1)}, u32[]{:S(2)}) copy-start(bf16[256,256]{1,0:T(8,128)(2,1)} %constant.85.clone.ol_ref) | copy-start | bytes 393220
  0.0 6.0 %copy-start.9 = (bf16[256,256]{1,0:T(8,128)(2,1)S(1)}, bf16[256,256]{1,0:T(8,128)(2,1)}, u32[]{:S(2)}) copy-start(bf16[256,256]{1,0:T(8,128)(2,1)} %constant.84.clone.oh_ref) | copy-start | bytes 393220
  0.0 6.0 %copy-start.10 = (bf16[256,256]{1,0:T(8,128)(2,1)S(1)}, bf16[256,256]{1,0:T(8,128)(2,1)}, u32[]{:S(2)}) copy-start(bf16[256,256]{1,0:T(8,128)(2,1)} %constant.83.clone.il_ref) | copy-start | bytes 393220
  0.0 6.0 %copy-start.22 = (s32[4,3]{1,0:T(4,128)S(1)}, s32[4,3]{1,0:T(4,128)}, u32[]{:S(2)}) copy-start(s32[4,3]{1,0:T(4,128)} %corner_ref.1) | copy-start | bytes 148
  0.0 6.0 %copy-start.23 = (f32[4]{0:T(128)S(1)}, f32[4]{0:T(128)}, u32[]{:S(2)}) copy-start(f32[4]{0:T(128)} %weight_ref.1) | copy-start | bytes 52
  0.0 6.0 %copy-start = (bf16[4,32768]{1,0:T(4,128)(2,1)S(1)}, bf16[4,32768]{1,0:T(4,128)(2,1)}, u32[]{:S(2)}) copy-start(bf16[4,32768]{1,0:T(4,128)(2,1)} %param.23) | copy-start | bytes 786436
  0.1 5.9 %copy-start.11 = (bf16[256,256]{1,0:T(8,128)(2,1)S(1)}, bf16[256,256]{1,0:T(8,128)(2,1)}, u32[]{:S(2)}) copy-start(bf16[256,256]{1,0:T(8,128)(2,1)} %constant.82.clone.ih_ref) | copy-start | bytes 393220
  0.1 30.0 %copy-start.1 = (bf16[4,128,256]{2,1,0:T(8,128)(2,1)S(1)}, bf16[4,128,256]{2,1,0:T(8,128)(2,1)}, u32[]{:S(2)}) copy-start(bf16[4,128,256]{2,1,0:T(8,128)(2,1)} %constant.92.clone.refs_9_) | copy-start | bytes 786436
  0.1 30.0 %copy-start.2 = (bf16[4,128,256]{2,1,0:T(8,128)(2,1)S(1)}, bf16[4,128,256]{2,1,0:T(8,128)(2,1)}, u32[]{:S(2)}) copy-start(bf16[4,128,256]{2,1,0:T(8,128)(2,1)} %constant.91.clone.refs_8_) | copy-start | bytes 786436
  0.1 30.0 %copy-start.3 = (bf16[4,256,128]{2,1,0:T(8,128)(2,1)S(1)}, bf16[4,256,128]{2,1,0:T(8,128)(2,1)}, u32[]{:S(2)}) copy-start(bf16[4,256,128]{2,1,0:T(8,128)(2,1)} %constant.90.clone.refs_7_) | copy-start | bytes 786436
  0.1 30.0 %copy-start.4 = (bf16[4,256,128]{2,1,0:T(8,128)(2,1)S(1)}, bf16[4,256,128]{2,1,0:T(8,128)(2,1)}, u32[]{:S(2)}) copy-start(bf16[4,256,128]{2,1,0:T(8,128)(2,1)} %constant.89.clone.refs_6_) | copy-start | bytes 786436
  0.2 30.0 %copy-start.16 = (bf16[256,128]{1,0:T(8,128)(2,1)S(1)}, bf16[256,128]{1,0:T(8,128)(2,1)}, u32[]{:S(2)}) copy-start(bf16[256,128]{1,0:T(8,128)(2,1)} %constant.94.clone.refs_11_) | copy-start | bytes 196612
  2.9 27.2 %collective-permute-start = (f32[64,8,256]{2,1,0:T(8,128)}, f32[64,8,256]{2,1,0:T(8,128)S(1)}, u32[]{:S(2)}, u32[]{:S(2)}) collective-permute-start(f32[64,8,256]{2,1,0:T(8,128)} %get-tuple-element.13), channel_id=1, source_target_pairs={{0,1},{1,0},{2,3},{3,2},{4,5},{5,4},{6,7},{7,6},{8,9},{9,8},{10,11... | collective-permute-start | bytes 1572872 | tf_op jit(solution)/shard_map/ppermute | solution.py:308
  10.0 20.1 %all-to-all-start = ((bf16[8,1,256,128]{3,2,1,0:T(8,128)(2,1)}), bf16[8,1,256,128]{3,2,1,0:T(8,128)(2,1)S(1)}, u32[]{:S(2)}, u32[]{:S(2)}) async-start(bf16[8,1,256,128]{3,2,1,0:T(8,128)(2,1)} %get-tuple-element.8), calls=%async_computation | async-start | bytes 1048576 | tf_op jit(solution)/shard_map/all_to_all | solution.py:339
  14.5 15.6 %collective-permute-start.2 = (f32[1,8,256]{2,1,0:T(8,128)S(1)}, f32[1,8,256]{2,1,0:T(8,128)S(1)}, u32[]{:S(2)}, u32[]{:S(2)}) collective-permute-start(f32[1,8,256]{2,1,0:T(8,128)S(1)} %get-tuple-element.11), channel_id=1, source_target_pairs={{0,3},{2,1},{4,7},{6,5},{8,11},{10,9},{12,15},{14,13},{16,19},{18,... | collective-permute-start | bytes 24584 | tf_op jit(solution)/shard_map/ppermute | solution.py:312
  18.7 11.3 %collective-permute-start.1 = (f32[1,8,256]{2,1,0:T(8,128)S(1)}, f32[1,8,256]{2,1,0:T(8,128)S(1)}, u32[]{:S(2)}, u32[]{:S(2)}) collective-permute-start(f32[1,8,256]{2,1,0:T(8,128)S(1)} %get-tuple-element.12), channel_id=1, source_target_pairs={{0,2},{2,0},{4,6},{6,4},{8,10},{10,8},{12,14},{14,12},{16,18},{18,... | collective-permute-start | bytes 24584 | tf_op jit(solution)/shard_map/ppermute | solution.py:312
  32.7 28.0 %copy-start.12 = (bf16[256,256]{1,0:T(8,128)(2,1)S(1)}, bf16[256,256]{1,0:T(8,128)(2,1)}, u32[]{:S(2)}) copy-start(bf16[256,256]{1,0:T(8,128)(2,1)} %constant.98.clone.ol_ref) | copy-start | bytes 393220
  32.7 28.0 %copy-start.13 = (bf16[256,256]{1,0:T(8,128)(2,1)S(1)}, bf16[256,256]{1,0:T(8,128)(2,1)}, u32[]{:S(2)}) copy-start(bf16[256,256]{1,0:T(8,128)(2,1)} %constant.97.clone.oh_ref) | copy-start | bytes 393220
  32.7 28.0 %copy-start.14 = (bf16[256,256]{1,0:T(8,128)(2,1)S(1)}, bf16[256,256]{1,0:T(8,128)(2,1)}, u32[]{:S(2)}) copy-start(bf16[256,256]{1,0:T(8,128)(2,1)} %constant.96.clone.il_ref) | copy-start | bytes 393220
  32.7 28.0 %copy-start.15 = (bf16[256,256]{1,0:T(8,128)(2,1)S(1)}, bf16[256,256]{1,0:T(8,128)(2,1)}, u32[]{:S(2)}) copy-start(bf16[256,256]{1,0:T(8,128)(2,1)} %constant.95.clone.ih_ref) | copy-start | bytes 393220
  32.7 28.0 %copy-start.21 = (f32[1,64,128]{2,1,0:T(8,128)S(1)}, f32[1,64,128]{2,1,0:T(8,128)}, u32[]{:S(2)}) copy-start(f32[1,64,128]{2,1,0:T(8,128)} %copy-done.20) | copy-start | bytes 98308
  (4 other events, 3.1 us)

commit v2 on v1

--- a/solution.py
+++ b/solution.py
@@ -87,6 +87,7 @@
         self.slots = SUB * -(-self.kx_block // (SUB * self.pln))
         self.half = self.pln // 2
         self.rows = self.orb * self.slots
+        self.area = box * self.slots
         self.box_part = box // self.pln
         magic = magic_filter(box)
         eye = np.eye(SUB)
@@ -108,7 +109,9 @@
                     k = self.kx_block * np.arange(self.orb) + within
                     wave[p, :, s, :] = cas(k[:, None] * places[None, :], doubled)
         self.wave = wave.reshape(self.pln, self.rows, grid).astype(np.float32)
-        along_z = cas(places[:, None] * np.arange(doubled)[None, :], doubled)
+        kz = np.concatenate([places, doubled - places])
+        along_z = cas(places[:, None] * kz[None, :], doubled)
+        along_z[:, grid] = 0.0
         self.forward_z = halves(along_z)
         self.inverse_z = halves(along_z.T / doubled)
         forward = np.zeros((self.pln, 2, grid, grid))
@@ -167,45 +170,93 @@
         wave = jnp.where(owner == n, pltpu.roll(whole_wave, shift, 1), wave)
         weight = jnp.where(owner == n, weight_ref[group * count + n], weight)
     wave_out_ref[0] = wave
-    wave_both = jnp.concatenate(split(wave), axis=1)
+    high, low = split(wave)
+    wave_terms = jnp.concatenate([high, low, high], axis=1)
+    kind = lax.broadcasted_iota(jnp.int32, (2 * SUB, 1), 0)
+    corner = jnp.zeros((2 * SUB, grid), F32)
+    for n in range(count):
+        place = jnp.where(kind == 0, corner_ref[group * count + n, 0], corner_ref[group * count + n, 1])
+        corner = jnp.where(owner == n, place.astype(F32), corner)
+    for o in range(plan.orb):
+        send_ref[o, 0, plan.area :, :] = corner.astype(send_ref.dtype)
     for pair in range(box // 2):
         columns = []
         for b in (2 * pair, 2 * pair + 1):
             psi = psi_ref[0, b]
             density = psi * psi * weight
             parts = [jnp.where(owner == n, density, 0.0) for n in range(count)]
-            columns.append(jnp.concatenate(parts, axis=0).astype(BF16))
-        both = jnp.concatenate(columns, axis=1)
-        out = dot(wave_both, jnp.concatenate([both, both], axis=0))
+            columns.append(jnp.concatenate(parts, axis=0))
+        up, down = split(jnp.concatenate(columns, axis=1))
+        out = dot(wave_terms, jnp.concatenate([up, up, down], axis=0))
         for o in range(plan.orb):
             rows = out[plan.slots * o : plan.slots * (o + 1)]
             tile = jnp.concatenate([rows[:, :grid], rows[:, grid:]], axis=0)
             send_ref[o, 0, 2 * plan.slots * pair : 2 * plan.slots * (pair + 1), :] = tile.astype(send_ref.dtype)
 
 
-def solve_kernel(plan, where_ref, corner_ref, recv_ref, *refs):
+def spectrum_kernel(plan, where_ref, after_ref, spectrum_ref, *refs):
+    half, slots, grid, rows = plan.half, plan.slots, plan.grid, plan.ky_block
+    outs = refs[: 2 * half]
+    block_ref, edge_ref, sems = refs[2 * half :]
+    me = where_ref[0]
+    group, index = me // half, lax.rem(me, half)
+    copies = []
+
+    def fetch(target, source, buffer, number):
+        first = jnp.minimum(target * slots, max(plan.kx_block - slots, 0))
+        first = pl.multiple_of(first, SUB)
+        copy = pltpu.make_async_copy(source.at[:, pl.ds(first, slots), :], buffer, sems.at[number])
+        copy.start()
+        copies.append(copy)
+
+    for step in range(half):
+        fetch(group * half + lax.rem(index + step, half), spectrum_ref, block_ref.at[step], step)
+    for step in range(half):
+        fetch((1 - group) * half + step, spectrum_ref.at[pl.ds(0, 1)], edge_ref.at[pl.ds(step, 1)], half + step)
+    odd = lax.rem(lax.broadcasted_iota(jnp.int32, (1, 1, grid), 2), 2) == 1
+
+    def fold(values):
+        last = values[:, :, grid : grid + 1]
+        return values[:, :, :grid] + jnp.where(odd, last, -last)
+
+    for step in range(half):
+        copies[half + step].wait()
+        outs[half + step][...] = fold(edge_ref[pl.ds(step, 1)])
+    for step in list(range(1, half)) + [0]:
+        copies[step].wait()
+        outs[step][...] = fold(block_ref[step])
+
+
+def solve_kernel(plan, where_ref, recv_ref, *refs):
     half, slots, grid, box, count = plan.half, plan.slots, plan.grid, plan.box, plan.per_group
-    kernel_refs = refs[:half]
+    spectrum_refs = refs[:half]
     edge_refs = refs[half : 2 * half]
-    zh_ref, zl_ref, yh_ref, yl_ref, vh_ref, vl_ref, wh_ref, wl_ref, send_ref, field_ref = refs[2 * half :]
+    zh_ref, zl_ref, yh_ref, yl_ref, vh_ref, vl_ref, wh_ref, wl_ref, send_ref = refs[2 * half : 2 * half + 9]
+    field_ref, table_ref, corner_ref, sem = refs[2 * half + 9 :]
     index = where_ref[0]
-    depth = box * slots
+    depth = plan.area
+    all_groups = plan.orb * plan.groups
     owner = lane_owner((1, grid), box)
+    for group in range(all_groups):
+        tile = recv_ref[group, depth : depth + 2 * SUB, :].astype(F32).astype(jnp.int32)
+        table_ref[2 * group : 2 * group + 2, :] = tile[:2]
+    copy = pltpu.make_async_copy(table_ref, corner_ref, sem)
+    copy.start()
     field_ref[...] = jnp.zeros_like(field_ref)
-
-    def start(number):
-        return pl.multiple_of(corner_ref[number, 1] * slots, SUB)
+    copy.wait()
+
+    def start(group, n):
+        return pl.multiple_of(corner_ref[2 * group + 1, box * n] * slots, SUB)
 
     def place(group, carry):
-        values = recv_ref[group].astype(F32)
+        values = recv_ref[group, :depth, :].astype(F32)
         for n in range(count):
-            number = group * count + n
-            shift = lax.rem(corner_ref[number, 0] - box * n + grid, grid)
+            shift = lax.rem(corner_ref[2 * group, box * n] - box * n + grid, grid)
             moved = pltpu.roll(jnp.where(owner == n, values, 0.0), shift, 1)
-            field_ref[pl.ds(start(number), depth), :] += moved
+            field_ref[pl.ds(start(group, n), depth), :] += moved
         return carry
 
-    lax.fori_loop(0, plan.orb * plan.groups, place, 0)
+    lax.fori_loop(0, all_groups, place, 0)
     zh, zl, wh, wl = zh_ref[...], zl_ref[...], wh_ref[...], wl_ref[...]
     yh, yl, vh, vl = yh_ref[index], yl_ref[index], vh_ref[index], vl_ref[index]
     row = lax.broadcasted_iota(jnp.int32, (grid, 1), 0)
@@ -213,26 +264,25 @@
     for s in range(slots):
         plane = field_ref[pl.ds(s, grid, stride=slots), :]
         modes = table_dot(yh, yl, dot_table(plane, zh, zl))
-        kernel = jnp.concatenate([ref[:, s, :] for ref in kernel_refs], axis=0)
+        spectrum = jnp.concatenate([ref[:, s, :] for ref in spectrum_refs], axis=0)
         edge = edge_refs[0][0, s : s + 1, :]
         for ref in edge_refs[1:]:
             edge = edge + ref[0, s : s + 1, :]
-        other = jnp.where(row == edge_row, edge, kernel)
-        modes = modes * jnp.concatenate([kernel, other], axis=0)
-        plane = dot_table(table_dot(vh, vl, modes), wh, wl)
-        field_ref[pl.ds(s, grid, stride=slots), :] = plane
+        other = jnp.where(row == edge_row, edge, spectrum)
+        both = jnp.concatenate([spectrum, other], axis=0)
+        modes = modes * jnp.concatenate([both, both], axis=1)
+        field_ref[pl.ds(s, grid, stride=slots), :] = dot_table(table_dot(vh, vl, modes), wh, wl)
 
     def cut(group, carry):
         values = jnp.zeros((depth, grid), F32)
         for n in range(count):
-            number = group * count + n
-            shift = lax.rem(box * n - corner_ref[number, 0] + grid, grid)
-            rows = field_ref[pl.ds(start(number), depth), :]
+            shift = lax.rem(box * n - corner_ref[2 * group, box * n] + grid, grid)
+            rows = field_ref[pl.ds(start(group, n), depth), :]
             values = jnp.where(owner == n, pltpu.roll(rows, shift, 1), values)
         send_ref[group] = values.astype(send_ref.dtype)
         return carry
 
-    lax.fori_loop(0, plan.orb * plan.groups, cut, 0)
+    lax.fori_loop(0, all_groups, cut, 0)
 
 
 def terms_kernel(
@@ -240,16 +290,12 @@
 ):
     box, grid, count, slots = plan.box, plan.grid, plan.per_group, plan.slots
     owner = lane_owner((1, grid), box)
-    high, low = split(wave_ref[0].T)
-    wave = jnp.concatenate([high, low, high], axis=1)
+    wave = jnp.concatenate(split(wave_ref[0].T), axis=1)
     for pair in range(box // 2):
-        columns = []
-        for b in (2 * pair, 2 * pair + 1):
-            columns.append(
-                jnp.concatenate([recv_ref[o, 0, slots * b : slots * (b + 1), :].astype(F32) for o in range(plan.orb)], axis=0)
-            )
-        up, down = split(jnp.concatenate(columns, axis=1))
-        out = dot(wave, jnp.concatenate([up, up, down], axis=0))
+        tiles = [recv_ref[o, 0, 2 * slots * pair : 2 * slots * (pair + 1), :].astype(F32) for o in range(plan.orb)]
+        columns = [jnp.concatenate([t[slots * side : slots * (side + 1)] for t in tiles], axis=0) for side in range(2)]
+        both = jnp.concatenate(columns, axis=1).astype(BF16)
+        out = dot(wave, jnp.concatenate([both, both], axis=0))
         for side, b in enumerate((2 * pair, 2 * pair + 1)):
             mine = out[:, grid * side : grid * (side + 1)]
             potential = jnp.zeros((box, grid), F32)
@@ -293,28 +339,10 @@
     groups, count, box, grid = plan.groups, plan.per_group, plan.box, plan.grid
     plane_index = lax.axis_index("pln")
     where = plane_index.astype(jnp.int32)[None]
-    corners = lax.all_gather(box_offsets, "orb", axis=0, tiled=True)
-    by_ky = jnp.transpose(kernel_spectrum, (1, 2, 0))
-
-    def columns_for(target, rows):
-        first = jnp.minimum(target * slots, max(plan.kx_block - slots, 0))
-        return lax.dynamic_slice(by_ky, (0, first, 0), (rows, slots, plan.doubled))
-
-    group_of, index = plane_index // half, plane_index % half
-    pieces = [columns_for(plane_index, plan.ky_block)]
-    for step in range(1, half):
-        target = group_of * half + (index + step) % half
-        pairs = [(g * half + i, g * half + (i + step) % half) for g in range(2) for i in range(half)]
-        pieces.append(lax.ppermute(columns_for(target, plan.ky_block), "pln", pairs))
-    edges = []
-    for step in range(half):
-        target = (1 - group_of) * half + step
-        edges.append(lax.ppermute(columns_for(target, 1), "pln", [(0, half + step), (half, step)]))
-
     smem = pl.BlockSpec(memory_space=pltpu.SMEM)
     params = pltpu.CompilerParams(vmem_limit_bytes=VMEM_LIMIT)
     coefs = orbitals.reshape(groups, count, orbitals.shape[1])
-    area = box * slots
+    area = plan.area
     tables = [*plan.depth, *plan.inner, *plan.outer]
     send, psi, wave = pl.pallas_call(
         functools.partial(density_kernel, plan),
@@ -323,12 +351,12 @@
         + [whole_spec(t) for t in tables]
         + [whole_spec(plan.wave)],
         out_specs=[
-            pl.BlockSpec((orb, 1, area, grid), lambda g: (0, g, 0, 0)),
+            pl.BlockSpec((orb, 1, area + 2 * SUB, grid), lambda g: (0, g, 0, 0)),
             pl.BlockSpec((1, box, box, grid), lambda g: (g, 0, 0, 0)),
             pl.BlockSpec((1, plan.rows, grid), lambda g: (g, 0, 0)),
         ],
         out_shape=[
-            jax.ShapeDtypeStruct((orb, groups, area, grid), BF16),
+            jax.ShapeDtypeStruct((orb, groups, area + 2 * SUB, grid), BF16),
             jax.ShapeDtypeStruct((groups, box, box, grid), F32),
             jax.ShapeDtypeStruct((groups, plan.rows, grid), F32),
         ],
@@ -337,19 +365,50 @@
         name="density",
     )(where, box_offsets, occupations, coefs, *tables, plan.wave)
     received = lax.all_to_all(send, "orb", split_axis=0, concat_axis=0, tiled=True)
-    received = received.reshape(orb * groups, area, grid)
+    received = received.reshape(orb * groups, area + 2 * SUB, grid)
+
+    anywhere = pl.BlockSpec(memory_space=pl.ANY)
+    by_ky = jnp.transpose(kernel_spectrum, (1, 2, 0))
+    shapes = [jax.ShapeDtypeStruct((plan.ky_block, slots, grid), F32)] * half
+    shapes += [jax.ShapeDtypeStruct((1, slots, grid), F32)] * half
+    pieces = pl.pallas_call(
+        functools.partial(spectrum_kernel, plan),
+        grid=(1,),
+        in_specs=[smem, anywhere, anywhere],
+        out_specs=[whole_spec(shape) for shape in shapes],
+        out_shape=shapes,
+        scratch_shapes=[
+            pltpu.VMEM((half, plan.ky_block, slots, plan.doubled), F32),
+            pltpu.VMEM((half, slots, plan.doubled), F32),
+            pltpu.SemaphoreType.DMA((2 * half,)),
+        ],
+        compiler_params=params,
+        name="spectrum",
+    )(where, wave, by_ky)
+    pieces = list(pieces)
+    for step in range(1, half):
+        pairs = [(g * half + i, g * half + (i + step) % half) for g in range(2) for i in range(half)]
+        pieces[step] = lax.ppermute(pieces[step], "pln", pairs)
+    for step in range(half):
+        pieces[half + step] = lax.ppermute(pieces[half + step], "pln", [(0, half + step), (half, step)])
+
     tables = [*plan.forward_z, *plan.forward_y, *plan.inverse_y, *plan.inverse_z]
-    blocks = [received, *pieces, *edges, *tables]
+    blocks = [received, *pieces, *tables]
     send = pl.pallas_call(
         functools.partial(solve_kernel, plan),
         grid=(1,),
-        in_specs=[smem, smem] + [whole_spec(t) for t in blocks],
+        in_specs=[smem] + [whole_spec(t) for t in blocks],
         out_specs=pl.BlockSpec((orb * groups, area, grid), lambda g: (0, 0, 0)),
-        out_shape=jax.ShapeDtypeStruct((orb * groups, area, grid), F32),
-        scratch_shapes=[pltpu.VMEM((grid * slots, grid), F32)],
+        out_shape=jax.ShapeDtypeStruct((orb * groups, area, grid), BF16),
+        scratch_shapes=[
+            pltpu.VMEM((grid * slots, grid), F32),
+            pltpu.VMEM((2 * orb * groups, grid), jnp.int32),
+            pltpu.SMEM((2 * orb * groups, grid), jnp.int32),
+            pltpu.SemaphoreType.DMA,
+        ],
         compiler_params=params,
         name="solve",
-    )(where, corners, *blocks)
+    )(where, *blocks)
     send = send.reshape(orb, groups, area, grid)
     received = lax.all_to_all(send, "orb", split_axis=0, concat_axis=0, tiled=True)
     tables = [*plan.depth, *plan.inner_back, *plan.outer_back]
@@ -364,7 +423,7 @@
         ]
         + [whole_spec(t) for t in tables],
         out_specs=pl.BlockSpec((pln, 1, part, box * box), lambda g: (0, g, 0, 0)),
-        out_shape=jax.ShapeDtypeStruct((pln, groups, part, box * box), F32),
+        out_shape=jax.ShapeDtypeStruct((pln, groups, part, box * box), BF16),
         scratch_shapes=[pltpu.VMEM((box, box, grid), F32)],
         compiler_params=params,
         name="terms",

time: 81.6 us -> 78.1 us (0.957)
  blocking collectives: 45.1 us -> 27 us
  local copies, waits for them, and re-layouts: 6.76 us -> 20 us
  waiting for transfers between devices: 0.01 us -> 1.42 us
    unnamed x48 -> x54, local copies, waits for them, and re-layouts: 3.23 us -> 20 us
    all_gather x1 -> x0, blocking collectives: 9.41 us -> none  [per_device(): corners = lax.all_gather(box_offsets, 'orb', axis=0, tiled=True)]
    all_to_all x1, blocking collectives: 17.8 us -> 13.4 us  [per_device(): lax.all_to_all(send, 'pln', split_axis=0, concat_axis=0, tiled=True)]
    all_to_all x1, blocking collectives: 17.9 us -> 13.6 us  [per_device(): lax.all_to_all(send, 'orb', split_axis=0, concat_axis=0, tiled=True)]
    dynamic_slice x2 -> x0, local copies, waits for them, and re-layouts: 3.54 us -> none  [columns_for(): return lax.dynamic_slice(by_ky, (0, first, 0), (rows, slots, plan.doubled))]
    ppermute x3, starting transfers between devices: 9.18 us -> 7.35 us  [the longest x2 5.77 us: per_device(): lax.ppermute(pieces[half + step], 'pln', [(0, half + step), (half, step)])]
    all_to_all x1, starting transfers between devices: 3.72 us -> 5.18 us  [per_device(): lax.all_to_all(send, 'orb', split_axis=0, concat_axis=0, tiled=True)]
    ppermute x3, waiting for transfers between devices: 0.01 us -> 1.42 us  [the longest x2 1.31 us: per_device(): lax.ppermute(pieces[half + step], 'pln', [(0, half + step), (half, step)])]
  transfers between devices with their start and end apart: 4 -> 4, of which waited for: 0 -> 3; matrix products, arithmetic and copies ran while one was open for 1% -> 0% of each run, Pallas kernels for 4% -> 1%
where the time goes in v2:
time: 78.1 us; the launch traced here: 77.2 us
  blocking collectives  27 us (35%)
  local copies, waits for them, and re-layouts  20 us (26%)
  Pallas kernels  16.2 us (21%)
  starting transfers between devices  12.5 us (16%)
  waiting for transfers between devices  1.42 us (2%)
    unnamed x54, local copies, waits for them, and re-layouts  20 us
    all_to_all x1, blocking collectives, per_device(): lax.all_to_all(send, 'orb', split_axis=0, concat_axis=0, tiled=True)  13.6 us
    all_to_all x1, blocking collectives, per_device(): lax.all_to_all(send, 'pln', split_axis=0, concat_axis=0, tiled=True)  13.4 us
    pallas_call x1, Pallas kernels, per_device(): pl.pallas_call(functools.partial(solve_kernel, plan), grid=(1,), in_specs...  9.45 us
    ppermute x2, starting transfers between devices, per_device(): lax.ppermute(pieces[half + step], 'pln', [(0, half + step), (half, step)])  5.77 us
    all_to_all x1, starting transfers between devices, per_device(): lax.all_to_all(send, 'orb', split_axis=0, concat_axis=0, tiled=True)  5.18 us
    pallas_call x1, Pallas kernels, per_device(): pl.pallas_call(functools.partial(density_kernel, plan), grid=(groups,), i...  3.51 us
    pallas_call x1, Pallas kernels, per_device(): pl.pallas_call(functools.partial(terms_kernel, plan), grid=(groups,), in_...  1.82 us
  transfers between devices with their start and end apart: 4, of which 3 were waited for; matrix products, arithmetic and copies ran while one was open for 0% of the time, Pallas kernels for 1%

profile of v2, /device:TPU:0, one launch (start us, length us, event | category | flops | bytes accessed | tf_op | source)
XLA Modules:
  0.0 77.2 jit_solution(7677985964555174203)
XLA Ops:
  0.0 1.1 %copy-done.1 = bf16[4,32768]{1,0:T(4,128)(2,1)S(1)} copy-done((bf16[4,32768]{1,0:T(4,128)(2,1)S(1)}, bf16[4,32768]{1,0:T(4,128)(2,1)}, u32[]{:S(2)}) %copy-start.1) | copy-done | bytes 262168
  2.6 0.9 %copy-done.12 = f32[4,64,128]{2,1,0:T(8,128)S(1)} copy-done((f32[4,64,128]{2,1,0:T(8,128)S(1)}, f32[4,64,128]{2,1,0:T(8,128)}, u32[]{:S(2)}) %copy-start.12) | copy-done | bytes 131096
  3.5 0.9 %copy-done.13 = bf16[256,256]{1,0:T(8,128)(2,1)S(1)} copy-done((bf16[256,256]{1,0:T(8,128)(2,1)S(1)}, bf16[256,256]{1,0:T(8,128)(2,1)}, u32[]{:S(2)}) %copy-start.13) | copy-done | bytes 131096
  4.4 0.9 %copy-done.14 = bf16[256,256]{1,0:T(8,128)(2,1)S(1)} copy-done((bf16[256,256]{1,0:T(8,128)(2,1)S(1)}, bf16[256,256]{1,0:T(8,128)(2,1)}, u32[]{:S(2)}) %copy-start.14) | copy-done | bytes 131096
  5.3 0.9 %copy-done.15 = bf16[256,256]{1,0:T(8,128)(2,1)S(1)} copy-done((bf16[256,256]{1,0:T(8,128)(2,1)S(1)}, bf16[256,256]{1,0:T(8,128)(2,1)}, u32[]{:S(2)}) %copy-start.15) | copy-done | bytes 131096
  6.2 0.9 %copy-done.16 = bf16[256,256]{1,0:T(8,128)(2,1)S(1)} copy-done((bf16[256,256]{1,0:T(8,128)(2,1)S(1)}, bf16[256,256]{1,0:T(8,128)(2,1)}, u32[]{:S(2)}) %copy-start.16) | copy-done | bytes 131096
  8.5 3.5 %density.1 = (bf16[8,1,272,128]{3,2,1,0:T(8,128)(2,1)}, f32[1,32,32,128]{3,2,1,0:T(8,128)S(1)}, f32[1,64,128]{2,1,0:T(8,128)S(1)}) custom-call(s32[1]{0:T(128)} %bitcast.where_ref, s32[4,3]{1,0:T(4,128)S(1)} %copy-done.25, f32[4]{0:T(128)S(1)} %copy-done.26, bf16[1,4,32768]{2,1,0:T(4,128)(2,1)S(1)} %bitcast.9, bf16[128,128]{1,0:T(8,128)(2,1)S(1)} %copy-done.10, ...), custom_call_target="tpu_custom_call" | custom-call | tf_op jit(solution)/shard_map/density/pallas_call | solution.py:347
  12.0 5.2 %all-to-all-start = ((bf16[8,1,272,128]{3,2,1,0:T(8,128)(2,1)}), bf16[8,1,272,128]{3,2,1,0:T(8,128)(2,1)S(1)}, u32[]{:S(2)}, u32[]{:S(2)}) async-start(bf16[8,1,272,128]{3,2,1,0:T(8,128)(2,1)} %get-tuple-element.12), calls=%async_computation | async-start | bytes 1114112 | tf_op jit(solution)/shard_map/all_to_all | solution.py:367
  18.7 1.6 %collective-permute-start = (f32[64,8,128]{2,1,0:T(8,128)S(1)}, f32[64,8,128]{2,1,0:T(8,128)S(1)}, u32[]{:S(2)}, u32[]{:S(2)}) collective-permute-start(f32[64,8,128]{2,1,0:T(8,128)S(1)} %get-tuple-element.15), channel_id=1, source_target_pairs={{0,1},{1,0},{2,3},{3,2},{4,5},{5,4},{6,7},{7,6},{8,9},{9,8},{10,11... | collective-permute-start | bytes 786440 | tf_op jit(solution)/shard_map/ppermute | solution.py:391
  20.3 4.5 %collective-permute-start.1 = (f32[1,8,128]{2,1,0:T(8,128)S(1)}, f32[1,8,128]{2,1,0:T(8,128)S(1)}, u32[]{:S(2)}, u32[]{:S(2)}) collective-permute-start(f32[1,8,128]{2,1,0:T(8,128)S(1)} %get-tuple-element.16), channel_id=1, source_target_pairs={{0,2},{2,0},{4,6},{6,4},{8,10},{10,8},{12,14},{14,12},{16,18},{18,... | collective-permute-start | bytes 12296 | tf_op jit(solution)/shard_map/ppermute | solution.py:393
  24.8 1.3 %collective-permute-start.2 = (f32[1,8,128]{2,1,0:T(8,128)S(1)}, f32[1,8,128]{2,1,0:T(8,128)S(1)}, u32[]{:S(2)}, u32[]{:S(2)}) collective-permute-start(f32[1,8,128]{2,1,0:T(8,128)S(1)} %get-tuple-element.17), channel_id=1, source_target_pairs={{0,3},{2,1},{4,7},{6,5},{8,11},{10,9},{12,15},{14,13},{16,19},{18,... | collective-permute-start | bytes 12296 | tf_op jit(solution)/shard_map/ppermute | solution.py:393
  27.5 0.9 %copy-done.3 = bf16[4,128,256]{2,1,0:T(8,128)(2,1)S(1)} copy-done((bf16[4,128,256]{2,1,0:T(8,128)(2,1)S(1)}, bf16[4,128,256]{2,1,0:T(8,128)(2,1)}, u32[]{:S(2)}) %copy-start.3) | copy-done | bytes 262168
  28.4 0.9 %copy-done.4 = bf16[4,256,128]{2,1,0:T(8,128)(2,1)S(1)} copy-done((bf16[4,256,128]{2,1,0:T(8,128)(2,1)S(1)}, bf16[4,256,128]{2,1,0:T(8,128)(2,1)}, u32[]{:S(2)}) %copy-start.4) | copy-done | bytes 262168
  29.4 0.9 %copy-done.5 = bf16[4,256,128]{2,1,0:T(8,128)(2,1)S(1)} copy-done((bf16[4,256,128]{2,1,0:T(8,128)(2,1)S(1)}, bf16[4,256,128]{2,1,0:T(8,128)(2,1)}, u32[]{:S(2)}) %copy-start.5) | copy-done | bytes 262168
  30.3 0.9 %copy-done.7 = f32[64,8,128]{2,1,0:T(8,128)S(1)} copy-done((f32[64,8,128]{2,1,0:T(8,128)S(1)}, f32[64,8,128]{2,1,0:T(8,128)}, u32[]{:S(2)}) %copy-start.7) | copy-done | bytes 262168
  31.3 0.8 %copy-done.21 = bf16[256,128]{1,0:T(8,128)(2,1)S(1)} copy-done((bf16[256,128]{1,0:T(8,128)(2,1)S(1)}, bf16[256,128]{1,0:T(8,128)(2,1)}, u32[]{:S(2)}) %copy-start.21) | copy-done | bytes 65560
  34.7 9.4 %solve.1 = bf16[8,256,128]{2,1,0:T(8,128)(2,1)S(1)} custom-call(s32[1]{0:T(128)} %bitcast.where_ref, bf16[8,272,128]{2,1,0:T(8,128)(2,1)S(1)} %bitcast.6, f32[64,8,128]{2,1,0:T(8,128)S(1)} %copy-done.7, f32[64,8,128]{2,1,0:T(8,128)S(1)} %collective-permute-done.refs_1_, f32[1,8,128]{2,1,0:T(8,128)S(1)} %collective-permute-done.1.refs_2_, ...), custom_call_target="tpu_custom_call" | custom-call | tf_op jit(solution)/shard_map/solve/pallas_call | solution.py:397
  44.1 13.6 %all_to_all.15.recv_ref = bf16[8,1,256,128]{3,2,1,0:T(8,128)(2,1)S(1)} all-to-all(bf16[8,1,256,128]{3,2,1,0:T(8,128)(2,1)S(1)} %bitcast.7), channel_id=1, replica_groups=mesh['orb'=8,'pln'=4] {'orb'}, dimensions={0} | all-to-all | bytes 1048576 | tf_op jit(solution)/shard_map/all_to_all | solution.py:413
  57.7 0.9 %copy-done.17 = bf16[256,256]{1,0:T(8,128)(2,1)S(1)} copy-done((bf16[256,256]{1,0:T(8,128)(2,1)S(1)}, bf16[256,256]{1,0:T(8,128)(2,1)}, u32[]{:S(2)}) %copy-start.17) | copy-done | bytes 131096
  58.6 0.9 %copy-done.18 = bf16[256,256]{1,0:T(8,128)(2,1)S(1)} copy-done((bf16[256,256]{1,0:T(8,128)(2,1)S(1)}, bf16[256,256]{1,0:T(8,128)(2,1)}, u32[]{:S(2)}) %copy-start.18) | copy-done | bytes 131096
  59.5 0.9 %copy-done.19 = bf16[256,256]{1,0:T(8,128)(2,1)S(1)} copy-done((bf16[256,256]{1,0:T(8,128)(2,1)S(1)}, bf16[256,256]{1,0:T(8,128)(2,1)}, u32[]{:S(2)}) %copy-start.19) | copy-done | bytes 131096
  60.5 0.9 %copy-done.20 = bf16[256,256]{1,0:T(8,128)(2,1)S(1)} copy-done((bf16[256,256]{1,0:T(8,128)(2,1)S(1)}, bf16[256,256]{1,0:T(8,128)(2,1)}, u32[]{:S(2)}) %copy-start.20) | copy-done | bytes 131096
  61.4 1.8 %terms.1 = bf16[4,1,32,1024]{3,2,1,0:T(8,128)(2,1)S(1)} custom-call(bf16[8,1,256,128]{3,2,1,0:T(8,128)(2,1)S(1)} %all_to_all.15.recv_ref, f32[1,32,32,128]{3,2,1,0:T(8,128)S(1)} %get-tuple-element.18.psi_ref, f32[1,64,128]{2,1,0:T(8,128)S(1)} %get-tuple-element.13.after_ref.wave_ref, bf16[128,128]{1,0:T(8,128)(2,1)S(1)} %copy-done.11, ...), custom_call_target="tpu_custom_call" | custom-call | tf_op jit(solution)/shard_map/terms/pallas_call | solution.py:416
  63.2 13.4 %all_to_all.16.recv_ref = bf16[4,1,32,1024]{3,2,1,0:T(8,128)(2,1)S(1)} all-to-all(bf16[4,1,32,1024]{3,2,1,0:T(8,128)(2,1)S(1)} %terms.1), channel_id=1, replica_groups=mesh['orb'=8,'pln'=4] {'pln'}, dimensions={0} | all-to-all | bytes 524288 | tf_op jit(solution)/shard_map/all_to_all | solution.py:431
  (45 shorter events, 9.0 us)
Async XLA Ops:
  0.0 17.2 %copy-start = (f32[256,64,32]{0,2,1:T(8,128)S(1)}, f32[256,64,32]{0,2,1:T(8,128)}, u32[]{:S(2)}) copy-start(f32[256,64,32]{0,2,1:T(8,128)} %param.26) | copy-start | bytes 6291460
  0.0 1.1 %copy-start.1 = (bf16[4,32768]{1,0:T(4,128)(2,1)S(1)}, bf16[4,32768]{1,0:T(4,128)(2,1)}, u32[]{:S(2)}) copy-start(bf16[4,32768]{1,0:T(4,128)(2,1)} %param.23) | copy-start | bytes 786436
  2.6 0.9 %copy-start.12 = (f32[4,64,128]{2,1,0:T(8,128)S(1)}, f32[4,64,128]{2,1,0:T(8,128)}, u32[]{:S(2)}) copy-start(f32[4,64,128]{2,1,0:T(8,128)} %constant.48.clone.wave_ref) | copy-start | bytes 393220
  3.5 0.9 %copy-start.13 = (bf16[256,256]{1,0:T(8,128)(2,1)S(1)}, bf16[256,256]{1,0:T(8,128)(2,1)}, u32[]{:S(2)}) copy-start(bf16[256,256]{1,0:T(8,128)(2,1)} %constant.47.clone.ol_ref) | copy-start | bytes 393220
  4.4 0.9 %copy-start.14 = (bf16[256,256]{1,0:T(8,128)(2,1)S(1)}, bf16[256,256]{1,0:T(8,128)(2,1)}, u32[]{:S(2)}) copy-start(bf16[256,256]{1,0:T(8,128)(2,1)} %constant.46.clone.oh_ref) | copy-start | bytes 393220
  5.3 0.9 %copy-start.15 = (bf16[256,256]{1,0:T(8,128)(2,1)S(1)}, bf16[256,256]{1,0:T(8,128)(2,1)}, u32[]{:S(2)}) copy-start(bf16[256,256]{1,0:T(8,128)(2,1)} %constant.45.clone.il_ref) | copy-start | bytes 393220
  6.2 0.9 %copy-start.16 = (bf16[256,256]{1,0:T(8,128)(2,1)S(1)}, bf16[256,256]{1,0:T(8,128)(2,1)}, u32[]{:S(2)}) copy-start(bf16[256,256]{1,0:T(8,128)(2,1)} %constant.44.clone.ih_ref) | copy-start | bytes 393220
  8.5 19.0 %copy-start.2 = (bf16[4,128,256]{2,1,0:T(8,128)(2,1)S(1)}, bf16[4,128,256]{2,1,0:T(8,128)(2,1)}, u32[]{:S(2)}) copy-start(bf16[4,128,256]{2,1,0:T(8,128)(2,1)} %constant.54.clone.refs_9_) | copy-start | bytes 786436
  12.0 15.5 %all-to-all-start = ((bf16[8,1,272,128]{3,2,1,0:T(8,128)(2,1)}), bf16[8,1,272,128]{3,2,1,0:T(8,128)(2,1)S(1)}, u32[]{:S(2)}, u32[]{:S(2)}) async-start(bf16[8,1,272,128]{3,2,1,0:T(8,128)(2,1)} %get-tuple-element.12), calls=%async_computation | async-start | bytes 1114112 | tf_op jit(solution)/shard_map/all_to_all | solution.py:367
  17.2 40.6 %copy-start.9 = (bf16[128,128]{1,0:T(8,128)(2,1)S(1)}, bf16[128,128]{1,0:T(8,128)(2,1)}, u32[]{:S(2)}) copy-start(bf16[128,128]{1,0:T(8,128)(2,1)} %constant.43.clone.dl_ref) | copy-start | bytes 98308
  17.2 40.5 %copy-start.11 = (bf16[128,128]{1,0:T(8,128)(2,1)S(1)}, bf16[128,128]{1,0:T(8,128)(2,1)}, u32[]{:S(2)}) copy-start(bf16[128,128]{1,0:T(8,128)(2,1)} %constant.42.clone.dh_ref) | copy-start | bytes 98308
  18.7 8.8 %collective-permute-start = (f32[64,8,128]{2,1,0:T(8,128)S(1)}, f32[64,8,128]{2,1,0:T(8,128)S(1)}, u32[]{:S(2)}, u32[]{:S(2)}) collective-permute-start(f32[64,8,128]{2,1,0:T(8,128)S(1)} %get-tuple-element.15), channel_id=1, source_target_pairs={{0,1},{1,0},{2,3},{3,2},{4,5},{5,4},{6,7},{7,6},{8,9},{9,8},{10,11... | collective-permute-start | bytes 786440 | tf_op jit(solution)/shard_map/ppermute | solution.py:391
  20.3 6.5 %collective-permute-start.1 = (f32[1,8,128]{2,1,0:T(8,128)S(1)}, f32[1,8,128]{2,1,0:T(8,128)S(1)}, u32[]{:S(2)}, u32[]{:S(2)}) collective-permute-start(f32[1,8,128]{2,1,0:T(8,128)S(1)} %get-tuple-element.16), channel_id=1, source_target_pairs={{0,2},{2,0},{4,6},{6,4},{8,10},{10,8},{12,14},{14,12},{16,18},{18,... | collective-permute-start | bytes 12296 | tf_op jit(solution)/shard_map/ppermute | solution.py:393
  24.8 2.6 %collective-permute-start.2 = (f32[1,8,128]{2,1,0:T(8,128)S(1)}, f32[1,8,128]{2,1,0:T(8,128)S(1)}, u32[]{:S(2)}, u32[]{:S(2)}) collective-permute-start(f32[1,8,128]{2,1,0:T(8,128)S(1)} %get-tuple-element.17), channel_id=1, source_target_pairs={{0,3},{2,1},{4,7},{6,5},{8,11},{10,9},{12,15},{14,13},{16,19},{18,... | collective-permute-start | bytes 12296 | tf_op jit(solution)/shard_map/ppermute | solution.py:393
  27.5 1.0 %copy-start.3 = (bf16[4,128,256]{2,1,0:T(8,128)(2,1)S(1)}, bf16[4,128,256]{2,1,0:T(8,128)(2,1)}, u32[]{:S(2)}) copy-start(bf16[4,128,256]{2,1,0:T(8,128)(2,1)} %constant.53.clone.refs_8_) | copy-start | bytes 786436
  28.4 0.9 %copy-start.4 = (bf16[4,256,128]{2,1,0:T(8,128)(2,1)S(1)}, bf16[4,256,128]{2,1,0:T(8,128)(2,1)}, u32[]{:S(2)}) copy-start(bf16[4,256,128]{2,1,0:T(8,128)(2,1)} %constant.52.clone.refs_7_) | copy-start | bytes 786436
  29.4 0.9 %copy-start.5 = (bf16[4,256,128]{2,1,0:T(8,128)(2,1)S(1)}, bf16[4,256,128]{2,1,0:T(8,128)(2,1)}, u32[]{:S(2)}) copy-start(bf16[4,256,128]{2,1,0:T(8,128)(2,1)} %constant.51.clone.refs_6_) | copy-start | bytes 786436
  30.3 0.9 %copy-start.7 = (f32[64,8,128]{2,1,0:T(8,128)S(1)}, f32[64,8,128]{2,1,0:T(8,128)}, u32[]{:S(2)}) copy-start(f32[64,8,128]{2,1,0:T(8,128)} %copy-done.6) | copy-start | bytes 786436
  31.3 0.8 %copy-start.21 = (bf16[256,128]{1,0:T(8,128)(2,1)S(1)}, bf16[256,128]{1,0:T(8,128)(2,1)}, u32[]{:S(2)}) copy-start(bf16[256,128]{1,0:T(8,128)(2,1)} %constant.56.clone.refs_11_) | copy-start | bytes 196612
  32.1 0.8 %copy-start.22 = (bf16[256,128]{1,0:T(8,128)(2,1)S(1)}, bf16[256,128]{1,0:T(8,128)(2,1)}, u32[]{:S(2)}) copy-start(bf16[256,128]{1,0:T(8,128)(2,1)} %constant.55.clone.refs_10_) | copy-start | bytes 196612
  57.7 0.9 %copy-start.17 = (bf16[256,256]{1,0:T(8,128)(2,1)S(1)}, bf16[256,256]{1,0:T(8,128)(2,1)}, u32[]{:S(2)}) copy-start(bf16[256,256]{1,0:T(8,128)(2,1)} %constant.60.clone.ol_ref) | copy-start | bytes 393220
  58.6 0.9 %copy-start.18 = (bf16[256,256]{1,0:T(8,128)(2,1)S(1)}, bf16[256,256]{1,0:T(8,128)(2,1)}, u32[]{:S(2)}) copy-start(bf16[256,256]{1,0:T(8,128)(2,1)} %constant.59.clone.oh_ref) | copy-start | bytes 393220
  59.5 0.9 %copy-start.19 = (bf16[256,256]{1,0:T(8,128)(2,1)S(1)}, bf16[256,256]{1,0:T(8,128)(2,1)}, u32[]{:S(2)}) copy-start(bf16[256,256]{1,0:T(8,128)(2,1)} %constant.58.clone.il_ref) | copy-start | bytes 393220
  60.5 0.9 %copy-start.20 = (bf16[256,256]{1,0:T(8,128)(2,1)S(1)}, bf16[256,256]{1,0:T(8,128)(2,1)}, u32[]{:S(2)}) copy-start(bf16[256,256]{1,0:T(8,128)(2,1)} %constant.57.clone.ih_ref) | copy-start | bytes 393220
  (7 other events, 5.2 us)

commit v3 on v2

v3 whole, which is shorter than its diff:
```python
import functools
import math

import jax
import jax.numpy as jnp
import numpy as np
from jax import lax
from jax.experimental import pallas as pl
from jax.experimental.pallas import tpu as pltpu
from jax.sharding import PartitionSpec as P

MAGIC_TAPS = (
    8.433424733352934e-07,
    -1.290557201342061e-05,
    8.76298447621056e-05,
    -0.00030158038132690465,
    0.001747237136729939,
    -0.009420470302010804,
    0.023738214637249424,
    0.0612625895831208,
    0.9940415697834004,
    -0.06048952891969835,
    -0.021030251609303816,
    0.013372634148547948,
    -0.0034412814449349387,
    0.0004944322768868992,
    -5.185986881173433e-05,
    2.7273449291197967e-06,
)
F32 = jnp.float32
BF16 = jnp.bfloat16
SUB = 8
VMEM_LIMIT = 60 * 1024 * 1024


def magic_filter(box):
    table = np.zeros((box, box))
    for row in range(box):
        for tap in range(-8, 8):
            if 0 <= row + tap < box:
                table[row, row + tap] = MAGIC_TAPS[tap + 8]
    return table.astype(np.float32).astype(np.float64)


def cas(product, doubled):
    angle = 2.0 * math.pi * (product % doubled) / doubled
    return np.cos(angle) + np.sin(angle)


def halves(table):
    high = np.asarray(table, np.float32).astype(jnp.bfloat16)
    low = (np.asarray(table, np.float64) - high.astype(np.float64)).astype(jnp.bfloat16)
    return high, low


def split(values):
    high = values.astype(BF16)
    low = (values - high.astype(F32)).astype(BF16)
    return high, low


def dot(left, right, dims=((1,), (0,))):
    return lax.dot_general(left, right, (dims, ((), ())), preferred_element_type=F32)


def terms_of(values, axis):
    high, low = split(values)
    return jnp.concatenate([high, high, low], axis=axis)


def stacked(table, axis):
    high, low = halves(table)
    return np.concatenate([high, low, high], axis=axis)


class Plan:
    def __init__(self, mesh, orbital_shape, kernel_shape):
        self.orb = mesh.shape["orb"]
        self.pln = mesh.shape["pln"]
        self.doubled = doubled = kernel_shape[0]
        self.grid = grid = doubled // 2
        self.box = box = round(orbital_shape[1] ** (1 / 3))
        self.per_group = grid // box
        self.groups = orbital_shape[0] // self.orb // self.per_group
        self.ky_block = kernel_shape[1] // self.pln
        self.kx_block = kernel_shape[2] // self.orb
        self.slots = SUB * -(-self.kx_block // (SUB * self.pln))
        self.half = self.pln // 2
        self.rows = self.orb * self.slots
        self.area = box * self.slots
        self.box_part = box // self.pln
        magic = magic_filter(box)
        eye = np.eye(SUB)
        depth = np.zeros((box, self.per_group, self.per_group, box))
        for n in range(self.per_group):
            depth[:, n, n, :] = magic.T
        depth = depth.reshape(grid, grid)
        self.depth = np.concatenate(halves(depth), axis=0)
        self.depth_back = stacked(depth, 1)
        self.inner = stacked(np.kron(eye, magic), 1)
        self.outer = stacked(np.kron(magic, eye), 1)
        self.inner_back = stacked(np.kron(eye, magic.T), 1)
        self.outer_back = stacked(np.kron(magic.T, eye), 1)
        places = np.arange(grid)
        wave = np.zeros((self.pln, self.orb, self.slots, grid))
        for p in range(self.pln):
            for s in range(self.slots):
                within = p * self.slots + s
                if within < self.kx_block:
                    k = self.kx_block * np.arange(self.orb) + within
                    wave[p, :, s, :] = cas(k[:, None] * places[None, :], doubled)
        self.wave = wave.reshape(self.pln, self.rows, grid).astype(np.float32)
        kz = np.concatenate([places, doubled - places])
        along_z = cas(places[:, None] * kz[None, :], doubled)
        along_z[:, grid] = 0.0
        self.forward_z = stacked(along_z, 0)
        self.inverse_z = stacked(along_z.T / doubled, 0)
        forward = np.zeros((self.pln, 2, grid, grid))
        weight = np.zeros((self.pln, 2, grid))
        for p in range(self.pln):
            group, index = divmod(p, self.half)
            base = grid * group
            for piece in range(self.half):
                block = (index - piece) % self.half
                for r in range(self.ky_block):
                    j = block * self.ky_block + r
                    row = piece * self.ky_block + r
                    angle = 2.0 * math.pi * ((base + j) * places % doubled) / doubled
                    forward[p, 0, row] = np.cos(angle)
                    forward[p, 1, row] = np.sin(angle)
                    weight[p, :, row] = 2.0
                    if j == 0:
                        edge = (base + grid) % doubled
                        forward[p, 1, row] = np.cos(2.0 * math.pi * (edge * places % doubled) / doubled)
                        weight[p, :, row] = 1.0
        inverse = forward * weight[..., None] / doubled**2
        self.forward_y = stacked(forward.reshape(self.pln, doubled, grid), 2)
        self.inverse_y = stacked(inverse.reshape(self.pln, doubled, grid).transpose(0, 2, 1), 2)
        self.quarter = box // 4


def lane_owner(shape, box):
    return lax.broadcasted_iota(jnp.int32, shape, len(shape) - 1) // box


def start_copies(sems, first, *pairs):
    copies = []
    for number, (source, target) in enumerate(pairs):
        copy = pltpu.make_async_copy(source, target, sems.at[first + number])
        copy.start()
        copies.append(copy)
    return copies


def wait_copies(copies):
    for copy in copies:
        copy.wait()


def density_kernel(
    plan, where_ref, corner_ref, weight_ref, coef_any, depth_any, inner_any, outer_any, wave_any,
    send_any, psi_any, wave_out_any,
    coef_ref, depth_ref, inner_ref, outer_ref, wave_ref, stage_ref, psi_ref, send_ref, sems,
):
    box, grid, count, slots = plan.box, plan.grid, plan.per_group, plan.slots
    section = box * box
    group = pl.program_id(0)
    fetched = start_copies(
        sems, 0, (coef_any.at[group], coef_ref), (depth_any, depth_ref), (inner_any, inner_ref),
        (outer_any, outer_ref), (wave_any.at[where_ref[0]], wave_ref),
    )
    wait_copies(fetched[:2])
    for p in range(box):
        stage_ref[count * p : count * (p + 1), :] = coef_ref[:, section * p : section * (p + 1)].astype(F32)
    coef = stage_ref[...].astype(BF16)
    first = dot(jnp.concatenate([coef, coef], axis=0), depth_ref[...], ((0,), (0,)))
    span = SUB * box
    wait_copies(fetched[2:])
    inner, outer = inner_ref[...], outer_ref[...]
    second = [dot(inner, terms_of(first[span * t : span * (t + 1)], 0)) for t in range(box // SUB)]
    second = jnp.concatenate(second, axis=0).reshape(box, box // SUB, SUB, grid)
    for t in range(box // SUB):
        third = dot(outer, terms_of(second[:, t].reshape(span, grid), 0))
        psi_ref[:, SUB * t : SUB * (t + 1), :] = third.reshape(box, SUB, grid)
    owner = lane_owner((1, grid), box)
    whole_wave = wave_ref[...]
    wave = jnp.zeros_like(whole_wave)
    weight = jnp.zeros((1, grid), F32)
    kind = lax.broadcasted_iota(jnp.int32, (2 * SUB, 1), 0)
    corner = jnp.zeros((2 * SUB, grid), F32)
    for n in range(count):
        number = group * count + n
        shift = lax.rem(box * n - corner_ref[number, 2] + grid, grid)
        wave = jnp.where(owner == n, pltpu.roll(whole_wave, shift, 1), wave)
        weight = jnp.where(owner == n, weight_ref[number], weight)
        place = jnp.where(kind == 0, corner_ref[number, 0], corner_ref[number, 1])
        corner = jnp.where(owner == n, place.astype(F32), corner)
    wave_ref[...] = wave
    for o in range(plan.orb):
        send_ref[o, plan.area :, :] = corner.astype(send_ref.dtype)
    high, low = split(wave)
    wave_terms = jnp.concatenate([high, low, high], axis=1)
    rows = pl.ds(plan.area, 2 * SUB)
    sent = start_copies(
        sems, 5, (psi_ref, psi_any.at[group]), (wave_ref, wave_out_any.at[group]),
        (send_ref.at[:, rows, :], send_any.at[:, group, rows, :]),
    )
    per_part = plan.quarter // 2
    for pair in range(box // 2):
        columns = []
        for b in (2 * pair, 2 * pair + 1):
            psi = psi_ref[b]
            density = psi * psi * weight
            columns.append(jnp.concatenate([jnp.where(owner == n, density, 0.0) for n in range(count)], axis=0))
        out = dot(wave_terms, terms_of(jnp.concatenate(columns, axis=1), 0))
        for o in range(plan.orb):
            mine = out[slots * o : slots * (o + 1)]
            tile = jnp.concatenate([mine[:, :grid], mine[:, grid:]], axis=0)
            send_ref[o, 2 * slots * pair : 2 * slots * (pair + 1), :] = tile.astype(send_ref.dtype)
        if pair % per_part == per_part - 1:
            part = pair // per_part
            rows = pl.ds(plan.quarter * slots * part, plan.quarter * slots)
            sent += start_copies(sems, 8 + part, (send_ref.at[:, rows, :], send_any.at[:, group, rows, :]))
    wait_copies(sent)


def spectrum_kernel(plan, where_ref, after_ref, spectrum_ref, *refs):
    half, slots, grid, rows = plan.half, plan.slots, plan.grid, plan.ky_block
    outs = refs[: 2 * half]
    block_ref, edge_ref, sems = refs[2 * half :]
    me = where_ref[0]
    group, index = me // half, lax.rem(me, half)
    copies = []

    def fetch(target, source, buffer, number):
        first = jnp.minimum(target * slots, max(plan.kx_block - slots, 0))
        first = pl.multiple_of(first, SUB)
        copy = pltpu.make_async_copy(source.at[:, pl.ds(first, slots), :], buffer, sems.at[number])
        copy.start()
        copies.append(copy)

    for step in range(half):
        fetch(group * half + lax.rem(index + step, half), spectrum_ref, block_ref.at[step], step)
    for step in range(half):
        fetch((1 - group) * half + step, spectrum_ref.at[pl.ds(0, 1)], edge_ref.at[pl.ds(step, 1)], half + step)
    odd = lax.rem(lax.broadcasted_iota(jnp.int32, (1, 1, grid), 2), 2) == 1

    def fold(values):
        last = values[:, :, grid : grid + 1]
        return values[:, :, :grid] + jnp.where(odd, last, -last)

    for step in range(half):
        copies[half + step].wait()
        outs[half + step][...] = fold(edge_ref[pl.ds(step, 1)])
    for step in list(range(1, half)) + [0]:
        copies[step].wait()
        outs[step][...] = fold(block_ref[step])


def solve_kernel(plan, where_ref, recv_any, *refs):
    half, slots, grid, box, count = plan.half, plan.slots, plan.grid, plan.box, plan.per_group
    piece_anys = refs[: 2 * half]
    forward_z_any, forward_y_any, inverse_y_any, inverse_z_any, send_any = refs[2 * half : 2 * half + 5]
    (
        recv_ref, spectrum_ref, edge_ref, forward_z_ref, forward_y_ref, inverse_y_ref, inverse_z_ref,
        field_ref, result_ref, send_ref, table_ref, corner_ref, corner_sem, recv_sems, sems, send_sems,
    ) = refs[2 * half + 5 :]
    index = where_ref[0]
    depth = plan.area
    all_groups = plan.orb * plan.groups
    owner = lane_owner((1, grid), box)
    rows = pl.ds(depth, 2 * SUB)
    first = start_copies(sems, 0, (recv_any.at[:, rows, :], recv_ref.at[:, rows, :]))

    def data_copy(group):
        rows = pl.ds(0, depth)
        return pltpu.make_async_copy(recv_any.at[group, rows, :], recv_ref.at[group, rows, :], recv_sems.at[group])

    def fetch(group, carry):
        data_copy(group).start()
        return carry

    lax.fori_loop(0, all_groups, fetch, 0)
    pairs = [(forward_z_any, forward_z_ref), (forward_y_any.at[index], forward_y_ref)]
    pairs += [(inverse_y_any.at[index], inverse_y_ref), (inverse_z_any, inverse_z_ref)]
    pairs += [(piece_anys[step], spectrum_ref.at[step]) for step in range(half)]
    pairs += [(piece_anys[half + step], edge_ref.at[pl.ds(step, 1)]) for step in range(half)]
    later = start_copies(sems, 1, *pairs)
    field_ref[...] = jnp.zeros_like(field_ref)
    wait_copies(first)
    for group in range(all_groups):
        tile = recv_ref[group, depth : depth + 2 * SUB, :].astype(F32).astype(jnp.int32)
        table_ref[2 * group : 2 * group + 2, :] = tile[:2]
    copy = pltpu.make_async_copy(table_ref, corner_ref, corner_sem)
    copy.start()
    copy.wait()

    def start(group, n):
        return pl.multiple_of(corner_ref[2 * group + 1, box * n] * slots, SUB)

    def place(group, carry):
        data_copy(group).wait()
        values = recv_ref[group, :depth, :].astype(F32)
        for n in range(count):
            shift = lax.rem(corner_ref[2 * group, box * n] - box * n + grid, grid)
            moved = pltpu.roll(jnp.where(owner == n, values, 0.0), shift, 1)
            field_ref[pl.ds(start(group, n), depth), :] += moved
        return carry

    lax.fori_loop(0, all_groups, place, 0)
    wait_copies(later)
    forward_z, forward_y = forward_z_ref[...], forward_y_ref[...]
    inverse_y, inverse_z = inverse_y_ref[...], inverse_z_ref[...]
    row = lax.broadcasted_iota(jnp.int32, (grid, 1), 0)
    edge_row = lax.rem(index, half) * plan.ky_block
    edges = edge_ref[0]
    for step in range(1, half):
        edges = edges + edge_ref[step]
    for s in range(slots):
        plane = field_ref[pl.ds(s, grid, stride=slots), :]
        modes = dot(forward_y, terms_of(dot(terms_of(plane, 1), forward_z), 0))
        spectrum = jnp.concatenate([spectrum_ref[step, :, s, :] for step in range(half)], axis=0)
        other = jnp.where(row == edge_row, edges[s : s + 1], spectrum)
        both = jnp.concatenate([spectrum, other], axis=0)
        modes = modes * jnp.concatenate([both, both], axis=1)
        plane = dot(terms_of(dot(inverse_y, terms_of(modes, 0)), 1), inverse_z)
        result_ref[pl.ds(s, grid, stride=slots), :] = plane

    def send_copy(group):
        return pltpu.make_async_copy(send_ref.at[group], send_any.at[group], send_sems.at[group])

    def cut(group, carry):
        values = jnp.zeros((depth, grid), F32)
        for n in range(count):
            shift = lax.rem(box * n - corner_ref[2 * group, box * n] + grid, grid)
            rows = result_ref[pl.ds(start(group, n), depth), :]
            values = jnp.where(owner == n, pltpu.roll(rows, shift, 1), values)
        send_ref[group] = values.astype(send_ref.dtype)
        send_copy(group).start()
        return carry

    lax.fori_loop(0, all_groups, cut, 0)

    def finish(group, carry):
        send_copy(group).wait()
        return carry

    lax.fori_loop(0, all_groups, finish, 0)


def terms_kernel(plan, where_ref, recv_any, psi_any, wave_any, depth_any, inner_any, outer_any, *refs):
    box, grid, count, slots, pln = plan.box, plan.grid, plan.per_group, plan.slots, plan.pln
    out_anys = refs[:pln]
    recv_ref, psi_ref, wave_ref, depth_ref, inner_ref, outer_ref, stage_ref, own_ref, send_ref, sems = refs[pln:]
    group = pl.program_id(0)
    fetched = start_copies(sems, 0, (wave_any.at[group], wave_ref))
    quarter = plan.quarter
    for part in range(4):
        rows = pl.ds(quarter * slots * part, quarter * slots)
        boxes = pl.ds(quarter * part, quarter)
        fetched += start_copies(
            sems, 1 + 2 * part, (recv_any.at[:, group, rows, :], recv_ref.at[:, rows, :]),
            (psi_any.at[group, boxes], psi_ref.at[boxes]),
        )
    tables = start_copies(sems, 9, (inner_any, inner_ref), (outer_any, outer_ref), (depth_any, depth_ref))
    owner = lane_owner((1, grid), box)
    wait_copies(fetched[:1])
    wave = jnp.concatenate(split(wave_ref[...].T), axis=1)
    for pair in range(box // 2):
        if pair % (quarter // 2) == 0:
            part = pair // (quarter // 2)
            wait_copies(fetched[1 + 2 * part : 3 + 2 * part])
        tiles = [recv_ref[o, 2 * slots * pair : 2 * slots * (pair + 1), :].astype(F32) for o in range(plan.orb)]
        columns = [jnp.concatenate([t[slots * side : slots * (side + 1)] for t in tiles], axis=0) for side in range(2)]
        both = jnp.concatenate(columns, axis=1).astype(BF16)
        out = dot(wave, jnp.concatenate([both, both], axis=0))
        for side, b in enumerate((2 * pair, 2 * pair + 1)):
            mine = out[:, grid * side : grid * (side + 1)]
            potential = jnp.zeros((box, grid), F32)
            for n in range(count):
                potential = jnp.where(owner == n, mine[box * n : box * (n + 1)], potential)
            stage_ref[b] = potential * psi_ref[b]
    span = SUB * box
    wait_copies(tables)
    inner, outer = inner_ref[...], outer_ref[...]
    second = []
    for t in range(box // SUB):
        values = stage_ref[SUB * t : SUB * (t + 1)].reshape(span, grid)
        second.append(dot(inner, terms_of(values, 0)))
    second = jnp.concatenate(second, axis=0).reshape(box, box // SUB, SUB, grid)
    for t in range(box // SUB):
        values = dot(outer, terms_of(second[:, t].reshape(span, grid), 0))
        stage_ref[:, SUB * t : SUB * (t + 1), :] = values.reshape(box, SUB, grid)
    values = terms_of(stage_ref[...].reshape(box * box, grid), 1)
    out = dot(depth_ref[...], values, ((1,), (1,)))
    part = plan.box_part * count
    for p in range(pln):
        own_ref[p] = out[part * p : part * (p + 1)]
        send_ref[p] = own_ref[p].astype(send_ref.dtype)
    me = where_ref[0]
    pairs = [(own_ref.at[me], out_anys[0].at[group])]
    pairs += [(send_ref.at[lax.rem(me + step, pln)], out_anys[step].at[group]) for step in range(1, pln)]
    wait_copies(start_copies(sems, 12, *pairs))


def sum_kernel(plan, *refs):
    out_ref = refs[plan.pln]
    total = refs[0][0]
    for ref in refs[1 : plan.pln]:
        total = total + ref[0].astype(F32)
    section = plan.box * plan.box
    count = plan.per_group
    for j in range(plan.box_part):
        out_ref[0, :, section * j : section * (j + 1)] = total[count * j : count * (j + 1)].astype(out_ref.dtype)


def whole_spec(array):
    rank = len(array.shape)
    return pl.BlockSpec(array.shape, lambda *_: (0,) * rank)


def per_device(plan, orbitals, occupations, box_offsets, kernel_spectrum):
    orb, pln, half, slots = plan.orb, plan.pln, plan.half, plan.slots
    groups, count, box, grid = plan.groups, plan.per_group, plan.box, plan.grid
    plane_index = lax.axis_index("pln")
    where = plane_index.astype(jnp.int32)[None]
    smem = pl.BlockSpec(memory_space=pltpu.SMEM)
    params = pltpu.CompilerParams(vmem_limit_bytes=VMEM_LIMIT)
    coefs = orbitals.reshape(groups, count, orbitals.shape[1])
    area = plan.area
    anywhere = pl.BlockSpec(memory_space=pl.ANY)
    dma = pltpu.SemaphoreType.DMA

    def buffer(array, dtype=None):
        return pltpu.VMEM(array.shape, dtype or array.dtype)

    tables = [plan.depth, plan.inner, plan.outer]
    send, psi, wave = pl.pallas_call(
        functools.partial(density_kernel, plan),
        grid=(groups,),
        in_specs=[smem, smem, smem] + [anywhere] * 5,
        out_specs=[anywhere] * 3,
        out_shape=[
            jax.ShapeDtypeStruct((orb, groups, area + 2 * SUB, grid), BF16),
            jax.ShapeDtypeStruct((groups, box, box, grid), F32),
            jax.ShapeDtypeStruct((groups, plan.rows, grid), F32),
        ],
        scratch_shapes=[
            pltpu.VMEM((count, orbitals.shape[1]), BF16),
            *[buffer(t) for t in tables],
            pltpu.VMEM((plan.rows, grid), F32),
            pltpu.VMEM((grid, box * box), F32),
            pltpu.VMEM((box, box, grid), F32),
            pltpu.VMEM((orb, area + 2 * SUB, grid), BF16),
            dma((12,)),
        ],
        compiler_params=params,
        name="density",
    )(where, box_offsets, occupations, coefs, *tables, plan.wave)
    received = lax.all_to_all(send, "orb", split_axis=0, concat_axis=0, tiled=True)
    received = received.reshape(orb * groups, area + 2 * SUB, grid)

    by_ky = jnp.transpose(kernel_spectrum, (1, 2, 0))
    shapes = [jax.ShapeDtypeStruct((plan.ky_block, slots, grid), F32)] * half
    shapes += [jax.ShapeDtypeStruct((1, slots, grid), F32)] * half
    pieces = pl.pallas_call(
        functools.partial(spectrum_kernel, plan),
        grid=(1,),
        in_specs=[smem, anywhere, anywhere],
        out_specs=[whole_spec(shape) for shape in shapes],
        out_shape=shapes,
        scratch_shapes=[
            pltpu.VMEM((half, plan.ky_block, slots, plan.doubled), F32),
            pltpu.VMEM((half, slots, plan.doubled), F32),
            pltpu.SemaphoreType.DMA((2 * half,)),
        ],
        compiler_params=params,
        name="spectrum",
    )(where, wave, by_ky)
    pieces = list(pieces)
    for step in range(1, half):
        pairs = [(g * half + i, g * half + (i + step) % half) for g in range(2) for i in range(half)]
        pieces[step] = lax.ppermute(pieces[step], "pln", pairs)
    for step in range(half):
        pieces[half + step] = lax.ppermute(pieces[half + step], "pln", [(0, half + step), (half, step)])

    tables = [plan.forward_z, plan.forward_y, plan.inverse_y, plan.inverse_z]
    blocks = [received, *pieces, *tables]
    send = pl.pallas_call(
        functools.partial(solve_kernel, plan),
        in_specs=[smem] + [anywhere] * len(blocks),
        out_specs=anywhere,
        out_shape=jax.ShapeDtypeStruct((orb * groups, area, grid), BF16),
        scratch_shapes=[
            buffer(received),
            pltpu.VMEM((half, plan.ky_block, slots, grid), F32),
            pltpu.VMEM((half, slots, grid), F32),
            buffer(plan.forward_z),
            buffer(plan.forward_y[0]),
            buffer(plan.inverse_y[0]),
            buffer(plan.inverse_z),
            pltpu.VMEM((grid * slots, grid), F32),
            pltpu.VMEM((grid * slots, grid), F32),
            pltpu.VMEM((orb * groups, area, grid), BF16),
            pltpu.VMEM((2 * orb * groups, grid), jnp.int32),
            pltpu.SMEM((2 * orb * groups, grid), jnp.int32),
            dma,
            dma((orb * groups,)),
            dma((5 + 2 * half,)),
            dma((orb * groups,)),
        ],
        compiler_params=params,
        name="solve",
    )(where, *blocks)
    send = send.reshape(orb, groups, area, grid)
    received = lax.all_to_all(send, "orb", split_axis=0, concat_axis=0, tiled=True)
    tables = [plan.depth_back, plan.inner_back, plan.outer_back]
    part = plan.box_part * count
    finished = pl.pallas_call(
        functools.partial(terms_kernel, plan),
        grid=(groups,),
        in_specs=[smem] + [anywhere] * 6,
        out_specs=[anywhere] * pln,
        out_shape=[jax.ShapeDtypeStruct((groups, part, box * box), BF16 if step else F32) for step in range(pln)],
        scratch_shapes=[
            pltpu.VMEM((orb, area, grid), BF16),
            pltpu.VMEM((box, box, grid), F32),
            pltpu.VMEM((plan.rows, grid), F32),
            *[buffer(t) for t in tables],
            pltpu.VMEM((box, box, grid), F32),
            pltpu.VMEM((pln, part, box * box), F32),
            pltpu.VMEM((pln, part, box * box), BF16),
            dma((12 + pln,)),
        ],
        compiler_params=params,
        name="terms",
    )(where, received, psi, wave, *tables)
    finished = list(finished)
    for step in range(1, pln):
        finished[step] = lax.ppermute(finished[step], "pln", [(p, (p + step) % pln) for p in range(pln)])
    cells = plan.box_part * box * box
    result = pl.pallas_call(
        functools.partial(sum_kernel, plan),
        grid=(groups,),
        in_specs=[pl.BlockSpec((1, part, box * box), lambda g: (g, 0, 0))] * pln,
        out_specs=pl.BlockSpec((1, count, cells), lambda g: (g, 0, 0)),
        out_shape=jax.ShapeDtypeStruct((groups, count, cells), BF16),
        compiler_params=params,
        name="sum",
    )(*finished)
    return result.reshape(groups * count, cells)


def solution(mesh):
    in_specs = (P("orb", None), P("orb"), P("orb", None), P(None, "pln", "orb"))
    out_specs = P("orb", "pln")

    def whole(orbitals, occupations, box_offsets, kernel_spectrum):
        plan = Plan(mesh, orbitals.shape, kernel_spectrum.shape)
        return jax.shard_map(
            functools.partial(per_device, plan), mesh=mesh, in_specs=in_specs, out_specs=out_specs, check_vma=False
        )(orbitals, occupations, box_offsets, kernel_spectrum)

    return whole
```

time: 78.1 us -> 62.9 us (0.81)
  local copies, waits for them, and re-layouts: 20 us -> 1.51 us
  blocking collectives: 27 us -> 13.9 us
  Pallas kernels: 16.2 us -> 23.2 us
  starting transfers between devices: 12.5 us -> 18.1 us
  waiting for transfers between devices: 1.42 us -> 5.61 us
    unnamed x54 -> x14, local copies, waits for them, and re-layouts: 20 us -> 1.51 us
    all_to_all x1 -> x0, blocking collectives: 13.4 us -> none  [per_device(): lax.all_to_all(send, 'pln', split_axis=0, concat_axis=0, tiled=True)]
    ppermute x0 -> x3, starting transfers between devices: none -> 5.46 us  [per_device(): lax.ppermute(finished[step], 'pln', [(p, (p + step) % pln) for p in range...]
    ppermute x0 -> x3, waiting for transfers between devices: none -> 3.98 us  [per_device(): lax.ppermute(finished[step], 'pln', [(p, (p + step) % pln) for p in range...]
    pallas_call x1, Pallas kernels: 1.82 us -> 4.13 us  [per_device(): pl.pallas_call(functools.partial(terms_kernel, plan), grid=(groups,), in_...]
    pallas_call x1, Pallas kernels: 0.79 us -> 2.36 us  [per_device(): pl.pallas_call(functools.partial(spectrum_kernel, plan), grid=(1,), in_sp...]
    pallas_call x1, Pallas kernels: 3.51 us -> 4.77 us  [per_device(): pl.pallas_call(functools.partial(density_kernel, plan), grid=(groups,), i...]
    pallas_call x1, Pallas kernels: 0.67 us -> 1.63 us  [per_device(): pl.pallas_call(functools.partial(sum_kernel, plan), grid=(groups,), in_sp...]
  transfers between devices with their start and end apart: 4 -> 7, of which waited for: 3 -> 6; matrix products, arithmetic and copies ran while one was open for 0% -> 0% of each run, Pallas kernels for 1% -> 4%
where the time goes in v3:
time: 62.9 us; the launch traced here: 62.4 us
  Pallas kernels  23.2 us (37%)
  starting transfers between devices  18.1 us (29%)
  blocking collectives  13.9 us (22%)
  waiting for transfers between devices  5.61 us (9%)
  local copies, waits for them, and re-layouts  1.51 us (2%)
    all_to_all x1, blocking collectives, per_device(): lax.all_to_all(send, 'orb', split_axis=0, concat_axis=0, tiled=True)  13.9 us
    pallas_call x1, Pallas kernels, per_device(): pl.pallas_call(functools.partial(solve_kernel, plan), in_specs=[smem] + [...  10.4 us
    ppermute x2, starting transfers between devices, per_device(): lax.ppermute(pieces[half + step], 'pln', [(0, half + step), (half, step)])  5.79 us
    ppermute x3, starting transfers between devices, per_device(): lax.ppermute(finished[step], 'pln', [(p, (p + step) % pln) for p in range...  5.46 us
    all_to_all x1, starting transfers between devices, per_device(): lax.all_to_all(send, 'orb', split_axis=0, concat_axis=0, tiled=True)  5.18 us
    pallas_call x1, Pallas kernels, per_device(): pl.pallas_call(functools.partial(density_kernel, plan), grid=(groups,), i...  4.77 us
    pallas_call x1, Pallas kernels, per_device(): pl.pallas_call(functools.partial(terms_kernel, plan), grid=(groups,), in_...  4.13 us
    ppermute x3, waiting for transfers between devices, per_device(): lax.ppermute(finished[step], 'pln', [(p, (p + step) % pln) for p in range...  3.98 us
  transfers between devices with their start and end apart: 7, of which 6 were waited for; matrix products, arithmetic and copies ran while one was open for 0% of the time, Pallas kernels for 4%

profile of v3, /device:TPU:0, one launch (start us, length us, event | category | flops | bytes accessed | tf_op | source)
XLA Modules:
  0.0 62.4 jit_solution(308120089345642154)
XLA Ops:
  0.0 4.8 %density.1 = (bf16[8,1,272,128]{3,2,1,0:T(8,128)(2,1)}, f32[1,32,32,128]{3,2,1,0:T(8,128)}, f32[1,64,128]{2,1,0:T(8,128)}) custom-call(s32[1]{0:T(128)} %bitcast.where_ref, s32[4,3]{1,0:T(4,128)} %corner_ref.1, f32[4]{0:T(128)} %weight_ref.1, bf16[1,4,32768]{2,1,0:T(4,128)(2,1)} %bitcast.9, bf16[256,128]{1,0:T(8,128)(2,1)} %constant.26.clone.depth_any, ...), custom_call_target="tpu_custom_call" | custom-call | tf_op jit(solution)/shard_map/density/pallas_call | solution.py:438
  4.8 5.2 %all-to-all-start = ((bf16[8,1,272,128]{3,2,1,0:T(8,128)(2,1)}), bf16[8,1,272,128]{3,2,1,0:T(8,128)(2,1)S(1)}, u32[]{:S(2)}, u32[]{:S(2)}) async-start(bf16[8,1,272,128]{3,2,1,0:T(8,128)(2,1)} %get-tuple-element.16), calls=%async_computation | async-start | bytes 1114112 | tf_op jit(solution)/shard_map/all_to_all | solution.py:460
  10.0 2.4 %spectrum.1 = (f32[64,8,128]{2,1,0:T(8,128)}, f32[64,8,128]{2,1,0:T(8,128)}, f32[1,8,128]{2,1,0:T(8,128)}, f32[1,8,128]{2,1,0:T(8,128)}) custom-call(s32[1]{0:T(128)} %bitcast.where_ref, f32[1,64,128]{2,1,0:T(8,128)} %get-tuple-element.17.after_ref.wave_any, f32[64,32,256]{2,1,0:T(8,128)} %bitcast.7), custom_call_target="tpu_custom_call" | custom-call | tf_op jit(solution)/shard_map/spectrum/pallas_call | solution.py:466
  12.3 1.6 %collective-permute-start = (f32[64,8,128]{2,1,0:T(8,128)}, f32[64,8,128]{2,1,0:T(8,128)S(1)}, u32[]{:S(2)}, u32[]{:S(2)}) collective-permute-start(f32[64,8,128]{2,1,0:T(8,128)} %get-tuple-element.19), channel_id=1, source_target_pairs={{0,1},{1,0},{2,3},{3,2},{4,5},{5,4},{6,7},{7,6},{8,9},{9,8},{10,11... | collective-permute-start | bytes 786440 | tf_op jit(solution)/shard_map/ppermute | solution.py:483
  14.0 4.5 %collective-permute-start.1 = (f32[1,8,128]{2,1,0:T(8,128)}, f32[1,8,128]{2,1,0:T(8,128)S(1)}, u32[]{:S(2)}, u32[]{:S(2)}) collective-permute-start(f32[1,8,128]{2,1,0:T(8,128)} %get-tuple-element.20), channel_id=1, source_target_pairs={{0,2},{2,0},{4,6},{6,4},{8,10},{10,8},{12,14},{14,12},{16,18},{18,... | collective-permute-start | bytes 12296 | tf_op jit(solution)/shard_map/ppermute | solution.py:485
  18.5 1.3 %collective-permute-start.2 = (f32[1,8,128]{2,1,0:T(8,128)}, f32[1,8,128]{2,1,0:T(8,128)S(1)}, u32[]{:S(2)}, u32[]{:S(2)}) collective-permute-start(f32[1,8,128]{2,1,0:T(8,128)} %get-tuple-element.21), channel_id=1, source_target_pairs={{0,3},{2,1},{4,7},{6,5},{8,11},{10,9},{12,15},{14,13},{16,19},{18,... | collective-permute-start | bytes 12296 | tf_op jit(solution)/shard_map/ppermute | solution.py:485
  19.8 0.9 %collective-permute-done.1.refs_2_ = f32[1,8,128]{2,1,0:T(8,128)S(1)} collective-permute-done((f32[1,8,128]{2,1,0:T(8,128)}, f32[1,8,128]{2,1,0:T(8,128)S(1)}, u32[]{:S(2)}, u32[]{:S(2)}) %collective-permute-start.1) | collective-permute-done | bytes 4128 | tf_op jit(solution)/shard_map/ppermute | solution.py:485
  20.7 0.6 collective-permute-done.2.refs_3_
  21.3 0.1 collective-permute-done.refs_1_
  21.4 0.5 copy-done.6
  21.9 0.2 copy-done.1
  22.1 0.2 copy-done
  22.3 10.4 %solve.1 = bf16[8,256,128]{2,1,0:T(8,128)(2,1)} custom-call(s32[1]{0:T(128)} %bitcast.where_ref, bf16[8,272,128]{2,1,0:T(8,128)(2,1)} %bitcast.6, f32[64,8,128]{2,1,0:T(8,128)} %get-tuple-element.18.refs_0_, f32[64,8,128]{2,1,0:T(8,128)} %copy-done.1, f32[1,8,128]{2,1,0:T(8,128)} %copy-done.5, f32[1,8,128]{2,1,0:T(8,128)} %copy-done.6, ...), custom_call_target="tpu_custom_call" | custom-call | tf_op jit(solution)/shard_map/solve/pallas_call | solution.py:489
  32.7 13.9 %all_to_all.10.recv_any = bf16[8,1,256,128]{3,2,1,0:T(8,128)(2,1)} all-to-all(bf16[8,1,256,128]{3,2,1,0:T(8,128)(2,1)} %bitcast.8), channel_id=1, replica_groups=mesh['orb'=8,'pln'=4] {'orb'}, dimensions={0} | all-to-all | bytes 1048576 | tf_op jit(solution)/shard_map/all_to_all | solution.py:516
  46.6 4.1 %terms.1 = (f32[1,32,1024]{2,1,0:T(8,128)}, bf16[1,32,1024]{2,1,0:T(8,128)(2,1)}, bf16[1,32,1024]{2,1,0:T(8,128)(2,1)}, bf16[1,32,1024]{2,1,0:T(8,128)(2,1)}) custom-call(s32[1]{0:T(128)} %bitcast.where_ref, bf16[8,1,256,128]{3,2,1,0:T(8,128)(2,1)} %all_to_all.10.recv_any, f32[1,32,32,128]{3,2,1,0:T(8,128)} %get-tuple-element.22.psi_any, ...), custom_call_target="tpu_custom_call" | custom-call | tf_op jit(solution)/shard_map/terms/pallas_call | solution.py:519
  50.7 1.6 %collective-permute-start.3 = (bf16[1,32,1024]{2,1,0:T(8,128)(2,1)}, bf16[1,32,1024]{2,1,0:T(8,128)(2,1)S(1)}, u32[]{:S(2)}, u32[]{:S(2)}) collective-permute-start(bf16[1,32,1024]{2,1,0:T(8,128)(2,1)} %get-tuple-element.24), channel_id=1, source_target_pairs={{0,1},{1,2},{2,3},{3,0},{4,5},{5,6},{6,7},{7,4},{8,9},{9,10},{10,1... | collective-permute-start | bytes 196616 | tf_op jit(solution)/shard_map/ppermute | solution.py:540
  52.3 3.1 %collective-permute-start.4 = (bf16[1,32,1024]{2,1,0:T(8,128)(2,1)}, bf16[1,32,1024]{2,1,0:T(8,128)(2,1)S(1)}, u32[]{:S(2)}, u32[]{:S(2)}) collective-permute-start(bf16[1,32,1024]{2,1,0:T(8,128)(2,1)} %get-tuple-element.25), channel_id=1, source_target_pairs={{0,2},{1,3},{2,0},{3,1},{4,6},{5,7},{6,4},{7,5},{8,10},{9,11},{10,... | collective-permute-start | bytes 196616 | tf_op jit(solution)/shard_map/ppermute | solution.py:540
  55.4 0.8 %collective-permute-start.5 = (bf16[1,32,1024]{2,1,0:T(8,128)(2,1)}, bf16[1,32,1024]{2,1,0:T(8,128)(2,1)S(1)}, u32[]{:S(2)}, u32[]{:S(2)}) collective-permute-start(bf16[1,32,1024]{2,1,0:T(8,128)(2,1)} %get-tuple-element.26), channel_id=1, source_target_pairs={{0,3},{1,0},{2,1},{3,2},{4,7},{5,4},{6,5},{7,6},{8,11},{9,8},{10,9... | collective-permute-start | bytes 196616 | tf_op jit(solution)/shard_map/ppermute | solution.py:540
  56.2 1.9 %collective-permute-done.3.refs_1_ = bf16[1,32,1024]{2,1,0:T(8,128)(2,1)S(1)} collective-permute-done((bf16[1,32,1024]{2,1,0:T(8,128)(2,1)}, bf16[1,32,1024]{2,1,0:T(8,128)(2,1)S(1)}, u32[]{:S(2)}, u32[]{:S(2)}) %collective-permute-start.3) | collective-permute-done | bytes 65568 | tf_op jit(solution)/shard_map/ppermute | solution.py:540
  58.1 1.7 %collective-permute-done.4.refs_2_ = bf16[1,32,1024]{2,1,0:T(8,128)(2,1)S(1)} collective-permute-done((bf16[1,32,1024]{2,1,0:T(8,128)(2,1)}, bf16[1,32,1024]{2,1,0:T(8,128)(2,1)S(1)}, u32[]{:S(2)}, u32[]{:S(2)}) %collective-permute-start.4) | collective-permute-done | bytes 65568 | tf_op jit(solution)/shard_map/ppermute | solution.py:540
  59.8 0.4 collective-permute-done.5.refs_3_
  60.2 0.2 copy-done.3
  60.4 0.4 copy-done.4
  60.8 1.6 %sum.1 = bf16[1,4,8192]{2,1,0:T(4,128)(2,1)} custom-call(f32[1,32,1024]{2,1,0:T(8,128)} %get-tuple-element.23.refs_0_, bf16[1,32,1024]{2,1,0:T(8,128)(2,1)} %copy-done.2, bf16[1,32,1024]{2,1,0:T(8,128)(2,1)} %copy-done.3, bf16[1,32,1024]{2,1,0:T(8,128)(2,1)} %copy-done.4), custom_call_target="tpu_custom_call" | custom-call | tf_op jit(solution)/shard_map/sum/pallas_call | solution.py:542
  (10 shorter events, 0.0 us)
Async XLA Ops:
  4.8 16.6 %all-to-all-start = ((bf16[8,1,272,128]{3,2,1,0:T(8,128)(2,1)}), bf16[8,1,272,128]{3,2,1,0:T(8,128)(2,1)S(1)}, u32[]{:S(2)}, u32[]{:S(2)}) async-start(bf16[8,1,272,128]{3,2,1,0:T(8,128)(2,1)} %get-tuple-element.16), calls=%async_computation | async-start | bytes 1114112 | tf_op jit(solution)/shard_map/all_to_all | solution.py:460
  12.3 9.1 %collective-permute-start = (f32[64,8,128]{2,1,0:T(8,128)}, f32[64,8,128]{2,1,0:T(8,128)S(1)}, u32[]{:S(2)}, u32[]{:S(2)}) collective-permute-start(f32[64,8,128]{2,1,0:T(8,128)} %get-tuple-element.19), channel_id=1, source_target_pairs={{0,1},{1,0},{2,3},{3,2},{4,5},{5,4},{6,7},{7,6},{8,9},{9,8},{10,11... | collective-permute-start | bytes 786440 | tf_op jit(solution)/shard_map/ppermute | solution.py:483
  14.0 6.7 %collective-permute-start.1 = (f32[1,8,128]{2,1,0:T(8,128)}, f32[1,8,128]{2,1,0:T(8,128)S(1)}, u32[]{:S(2)}, u32[]{:S(2)}) collective-permute-start(f32[1,8,128]{2,1,0:T(8,128)} %get-tuple-element.20), channel_id=1, source_target_pairs={{0,2},{2,0},{4,6},{6,4},{8,10},{10,8},{12,14},{14,12},{16,18},{18,... | collective-permute-start | bytes 12296 | tf_op jit(solution)/shard_map/ppermute | solution.py:485
  18.5 2.8 %collective-permute-start.2 = (f32[1,8,128]{2,1,0:T(8,128)}, f32[1,8,128]{2,1,0:T(8,128)S(1)}, u32[]{:S(2)}, u32[]{:S(2)}) collective-permute-start(f32[1,8,128]{2,1,0:T(8,128)} %get-tuple-element.21), channel_id=1, source_target_pairs={{0,3},{2,1},{4,7},{6,5},{8,11},{10,9},{12,15},{14,13},{16,19},{18,... | collective-permute-start | bytes 12296 | tf_op jit(solution)/shard_map/ppermute | solution.py:485
  20.7 0.7 %copy-start.5 = (f32[1,8,128]{2,1,0:T(8,128)}, f32[1,8,128]{2,1,0:T(8,128)S(1)}, u32[]{:S(2)}) copy-start(f32[1,8,128]{2,1,0:T(8,128)S(1)} %collective-permute-done.1.refs_2_) | copy-start | bytes 12292
  21.3 0.6 copy-start.6
  21.4 0.7 %copy-start.1 = (f32[64,8,128]{2,1,0:T(8,128)}, f32[64,8,128]{2,1,0:T(8,128)S(1)}, u32[]{:S(2)}) copy-start(f32[64,8,128]{2,1,0:T(8,128)S(1)} %collective-permute-done.refs_1_) | copy-start | bytes 786436
  21.4 0.9 %copy-start = (bf16[8,1,272,128]{3,2,1,0:T(8,128)(2,1)}, bf16[8,1,272,128]{3,2,1,0:T(8,128)(2,1)S(1)}, u32[]{:S(2)}) copy-start(bf16[8,1,272,128]{3,2,1,0:T(8,128)(2,1)S(1)} %all-to-all-done) | copy-start | bytes 1671172
  50.7 7.4 %collective-permute-start.3 = (bf16[1,32,1024]{2,1,0:T(8,128)(2,1)}, bf16[1,32,1024]{2,1,0:T(8,128)(2,1)S(1)}, u32[]{:S(2)}, u32[]{:S(2)}) collective-permute-start(bf16[1,32,1024]{2,1,0:T(8,128)(2,1)} %get-tuple-element.24), channel_id=1, source_target_pairs={{0,1},{1,2},{2,3},{3,0},{4,5},{5,6},{6,7},{7,4},{8,9},{9,10},{10,1... | collective-permute-start | bytes 196616 | tf_op jit(solution)/shard_map/ppermute | solution.py:540
  52.3 7.4 %collective-permute-start.4 = (bf16[1,32,1024]{2,1,0:T(8,128)(2,1)}, bf16[1,32,1024]{2,1,0:T(8,128)(2,1)S(1)}, u32[]{:S(2)}, u32[]{:S(2)}) collective-permute-start(bf16[1,32,1024]{2,1,0:T(8,128)(2,1)} %get-tuple-element.25), channel_id=1, source_target_pairs={{0,2},{1,3},{2,0},{3,1},{4,6},{5,7},{6,4},{7,5},{8,10},{9,11},{10,... | collective-permute-start | bytes 196616 | tf_op jit(solution)/shard_map/ppermute | solution.py:540
  55.4 4.8 %collective-permute-start.5 = (bf16[1,32,1024]{2,1,0:T(8,128)(2,1)}, bf16[1,32,1024]{2,1,0:T(8,128)(2,1)S(1)}, u32[]{:S(2)}, u32[]{:S(2)}) collective-permute-start(bf16[1,32,1024]{2,1,0:T(8,128)(2,1)} %get-tuple-element.26), channel_id=1, source_target_pairs={{0,3},{1,0},{2,1},{3,2},{4,7},{5,4},{6,5},{7,6},{8,11},{9,8},{10,9... | collective-permute-start | bytes 196616 | tf_op jit(solution)/shard_map/ppermute | solution.py:540
  58.1 2.1 %copy-start.2 = (bf16[1,32,1024]{2,1,0:T(8,128)(2,1)}, bf16[1,32,1024]{2,1,0:T(8,128)(2,1)S(1)}, u32[]{:S(2)}) copy-start(bf16[1,32,1024]{2,1,0:T(8,128)(2,1)S(1)} %collective-permute-done.3.refs_1_) | copy-start | bytes 196612
  59.8 0.6 copy-start.3
  60.2 0.6 copy-start.4

commit v4 on v3

v4 whole, which is shorter than its diff:
```python
import functools
import math

import jax
import jax.numpy as jnp
import numpy as np
from jax import lax
from jax.experimental import pallas as pl
from jax.experimental.pallas import tpu as pltpu
from jax.sharding import PartitionSpec as P

MAGIC_TAPS = (
    8.433424733352934e-07,
    -1.290557201342061e-05,
    8.76298447621056e-05,
    -0.00030158038132690465,
    0.001747237136729939,
    -0.009420470302010804,
    0.023738214637249424,
    0.0612625895831208,
    0.9940415697834004,
    -0.06048952891969835,
    -0.021030251609303816,
    0.013372634148547948,
    -0.0034412814449349387,
    0.0004944322768868992,
    -5.185986881173433e-05,
    2.7273449291197967e-06,
)
F32 = jnp.float32
BF16 = jnp.bfloat16
SUB = 8
LARGE = 60 * 1024 * 1024
SMALL = 32 * 1024 * 1024


def magic_filter(box):
    table = np.zeros((box, box))
    for row in range(box):
        for tap in range(-8, 8):
            if 0 <= row + tap < box:
                table[row, row + tap] = MAGIC_TAPS[tap + 8]
    return table.astype(np.float32).astype(np.float64)


def cas(product, doubled):
    angle = 2.0 * math.pi * (product % doubled) / doubled
    return np.cos(angle) + np.sin(angle)


def halves(table):
    high = np.asarray(table, np.float32).astype(jnp.bfloat16)
    low = (np.asarray(table, np.float64) - high.astype(np.float64)).astype(jnp.bfloat16)
    return high, low


def split(values):
    high = values.astype(BF16)
    low = (values - high.astype(F32)).astype(BF16)
    return high, low


def dot(left, right, dims=((1,), (0,))):
    return lax.dot_general(left, right, (dims, ((), ())), preferred_element_type=F32)


def terms_of(values, axis):
    high, low = split(values)
    return jnp.concatenate([high, high, low], axis=axis)


def stacked(table, axis):
    high, low = halves(table)
    return np.concatenate([high, low, high], axis=axis)


SINE = (1.0, -1.0 / 6, 1.0 / 120, -1.0 / 5040, 1.0 / 362880)
COSINE = (1.0, -1.0 / 2, 1.0 / 24, -1.0 / 720, 1.0 / 40320)


def turn(steps, doubled):
    quarter = doubled // 4
    place = (steps + quarter // 2) & (doubled - 1)
    quadrant = place // quarter
    angle = (place - quadrant * quarter - quarter // 2).astype(F32) * (2.0 * math.pi / doubled)
    square = angle * angle
    cosine, sine = COSINE[-1], SINE[-1]
    for even, odd in zip(COSINE[-2::-1], SINE[-2::-1]):
        cosine, sine = cosine * square + even, sine * square + odd
    return quadrant, cosine, sine * angle


def cosine_table(steps, doubled):
    quadrant, cosine, sine = turn(steps, doubled)
    value = jnp.where((quadrant & 1) == 0, cosine, -sine)
    return jnp.where(quadrant < 2, value, -value)


def cas_table(steps, doubled):
    quadrant, cosine, sine = turn(steps, doubled)
    value = jnp.where((quadrant & 1) == 0, cosine + sine, cosine - sine)
    return jnp.where(quadrant < 2, value, -value)


def iota(shape, axis):
    return lax.broadcasted_iota(jnp.int32, shape, axis)


def stack_terms(table, axis):
    high, low = split(table)
    return jnp.concatenate([high, low, high], axis=axis)


def tap_table(step):
    value = jnp.zeros(step.shape, F32)
    for tap in range(-8, 8):
        value = jnp.where(step == tap, np.float32(MAGIC_TAPS[tap + 8]), value)
    return value


def inner_back_table(box):
    span = SUB * box
    one = tap_table(iota((box, span), 0) - (iota((box, span), 1) & (box - 1)))
    whole = jnp.concatenate([one] * SUB, axis=0)
    return jnp.where(iota((span, span), 0) // box == iota((span, span), 1) // box, whole, 0.0)


def outer_back_table(box):
    span = SUB * box
    row, column = iota((span, span), 0), iota((span, span), 1)
    value = tap_table(row // SUB - column // SUB)
    return jnp.where((row & (SUB - 1)) == (column & (SUB - 1)), value, 0.0)


def depth_back_table(plan):
    grid, box, count = plan.grid, plan.box, plan.per_group
    row, column = iota((grid, grid), 0), iota((grid, grid), 1)
    value = tap_table(row // count - (column & (box - 1)))
    return jnp.where((row & (count - 1)) == column // box, value, 0.0)


def mode_table(plan, me, shape, axis):
    grid, doubled, half = plan.grid, plan.doubled, plan.half
    line = tuple(doubled if dim == axis else 1 for dim in range(2))
    group, index = me // half, lax.rem(me, half)
    mode = iota(line, axis)
    within = mode & (grid - 1)
    block = (index - within // plan.ky_block + half) & (half - 1)
    step = block * plan.ky_block + (within & (plan.ky_block - 1))
    edge = (mode >= grid) & (step == 0)
    frequency = jnp.where(edge, ((1 - group) * grid), group * grid + step)
    quarter = jnp.where((mode >= grid) & (step != 0), doubled // 4, 0)
    weight = jnp.where(step == 0, 1.0, 2.0)
    return cosine_table(frequency * iota(shape, 1 - axis) - quarter, doubled), weight


def depth_mode_table(plan, shape, axis):
    grid, doubled = plan.grid, plan.doubled
    place = iota(shape, axis)
    frequency = jnp.where(place < grid, place, grid - place)
    return jnp.where(place == grid, 0.0, cas_table(frequency * iota(shape, 1 - axis), doubled))


class Plan:
    def __init__(self, mesh, orbital_shape, kernel_shape):
        self.orb = mesh.shape["orb"]
        self.pln = mesh.shape["pln"]
        self.doubled = doubled = kernel_shape[0]
        self.grid = grid = doubled // 2
        self.box = box = round(orbital_shape[1] ** (1 / 3))
        self.per_group = grid // box
        self.groups = orbital_shape[0] // self.orb // self.per_group
        self.ky_block = kernel_shape[1] // self.pln
        self.kx_block = kernel_shape[2] // self.orb
        self.slots = SUB * -(-self.kx_block // (SUB * self.pln))
        self.half = self.pln // 2
        self.rows = self.orb * self.slots
        self.area = box * self.slots
        self.box_part = box // self.pln
        magic = magic_filter(box)
        eye = np.eye(SUB)
        depth = np.zeros((box, self.per_group, self.per_group, box))
        for n in range(self.per_group):
            depth[:, n, n, :] = magic.T
        depth = depth.reshape(grid, grid)
        self.depth = np.concatenate(halves(depth), axis=0)
        self.inner = stacked(np.kron(eye, magic), 1)
        self.outer = stacked(np.kron(magic, eye), 1)
        places = np.arange(grid)
        wave = np.zeros((self.pln, self.orb, self.slots, grid))
        for p in range(self.pln):
            for s in range(self.slots):
                within = p * self.slots + s
                if within < self.kx_block:
                    k = self.kx_block * np.arange(self.orb) + within
                    wave[p, :, s, :] = cas(k[:, None] * places[None, :], doubled)
        self.wave = wave.reshape(self.pln, self.rows, grid).astype(np.float32)
        self.quarter = box // 4


def lane_owner(shape, box):
    return lax.broadcasted_iota(jnp.int32, shape, len(shape) - 1) // box


def start_copies(sems, first, *pairs):
    copies = []
    for number, (source, target) in enumerate(pairs):
        copy = pltpu.make_async_copy(source, target, sems.at[first + number])
        copy.start()
        copies.append(copy)
    return copies


def wait_copies(copies):
    for copy in copies:
        copy.wait()


def density_kernel(
    plan, where_ref, corner_ref, weight_ref, coef_any, depth_any, inner_any, outer_any, wave_any, spectrum_any,
    send_any, psi_any, wave_out_any, *refs,
):
    piece_anys = refs[: 2 * plan.half]
    coef_ref, depth_ref, inner_ref, outer_ref, wave_ref, stage_ref, psi_ref, send_ref, *spectrum_refs, sems = refs[2 * plan.half :]
    box, grid, count, slots = plan.box, plan.grid, plan.per_group, plan.slots
    section = box * box
    group = pl.program_id(0)
    fetched = start_copies(
        sems, 0, (coef_any.at[group], coef_ref), (depth_any, depth_ref), (inner_any, inner_ref),
        (outer_any, outer_ref), (wave_any.at[where_ref[0]], wave_ref),
    )

    @pl.when(group == 0)
    def _():
        start_spectrum(plan, where_ref[0], spectrum_any, *spectrum_refs)

    wait_copies(fetched[:2])
    for p in range(box):
        stage_ref[count * p : count * (p + 1), :] = coef_ref[:, section * p : section * (p + 1)].astype(F32)
    coef = stage_ref[...].astype(BF16)
    first = dot(jnp.concatenate([coef, coef], axis=0), depth_ref[...], ((0,), (0,)))
    span = SUB * box
    wait_copies(fetched[2:])
    inner, outer = inner_ref[...], outer_ref[...]
    second = [dot(inner, terms_of(first[span * t : span * (t + 1)], 0)) for t in range(box // SUB)]
    second = jnp.concatenate(second, axis=0).reshape(box, box // SUB, SUB, grid)
    for t in range(box // SUB):
        third = dot(outer, terms_of(second[:, t].reshape(span, grid), 0))
        psi_ref[:, SUB * t : SUB * (t + 1), :] = third.reshape(box, SUB, grid)
    owner = lane_owner((1, grid), box)
    whole_wave = wave_ref[...]
    wave = jnp.zeros_like(whole_wave)
    weight = jnp.zeros((1, grid), F32)
    kind = lax.broadcasted_iota(jnp.int32, (2 * SUB, 1), 0)
    corner = jnp.zeros((2 * SUB, grid), F32)
    for n in range(count):
        number = group * count + n
        shift = lax.rem(box * n - corner_ref[number, 2] + grid, grid)
        wave = jnp.where(owner == n, pltpu.roll(whole_wave, shift, 1), wave)
        weight = jnp.where(owner == n, weight_ref[number], weight)
        place = jnp.where(kind == 0, corner_ref[number, 0], corner_ref[number, 1])
        corner = jnp.where(owner == n, place.astype(F32), corner)
    wave_ref[...] = wave
    for o in range(plan.orb):
        send_ref[o, plan.area :, :] = corner.astype(send_ref.dtype)
    high, low = split(wave)
    wave_terms = jnp.concatenate([high, low, high], axis=1)
    rows = pl.ds(plan.area, 2 * SUB)
    sent = start_copies(
        sems, 5, (psi_ref, psi_any.at[group]), (wave_ref, wave_out_any.at[group]),
        (send_ref.at[:, rows, :], send_any.at[:, group, rows, :]),
    )
    per_part = plan.quarter // 2
    for pair in range(box // 2):
        columns = []
        for b in (2 * pair, 2 * pair + 1):
            psi = psi_ref[b]
            density = psi * psi * weight
            columns.append(jnp.concatenate([jnp.where(owner == n, density, 0.0) for n in range(count)], axis=0))
        out = dot(wave_terms, terms_of(jnp.concatenate(columns, axis=1), 0))
        for o in range(plan.orb):
            mine = out[slots * o : slots * (o + 1)]
            tile = jnp.concatenate([mine[:, :grid], mine[:, grid:]], axis=0)
            send_ref[o, 2 * slots * pair : 2 * slots * (pair + 1), :] = tile.astype(send_ref.dtype)
        if pair % per_part == per_part - 1:
            part = pair // per_part
            rows = pl.ds(plan.quarter * slots * part, plan.quarter * slots)
            sent += start_copies(sems, 8 + part, (send_ref.at[:, rows, :], send_any.at[:, group, rows, :]))

    @pl.when(group == 0)
    def _():
        finish_spectrum(plan, where_ref[0], spectrum_any, piece_anys, *spectrum_refs)

    wait_copies(sent)


def spectrum_copies(plan, me, spectrum_any, block_ref, edge_ref, sems):
    half, slots = plan.half, plan.slots
    group, index = me // half, lax.rem(me, half)

    def fetch(target, source, buffer, number):
        first = jnp.minimum(target * slots, max(plan.kx_block - slots, 0))
        first = pl.multiple_of(first, SUB)
        return pltpu.make_async_copy(source.at[:, pl.ds(first, slots), :], buffer, sems.at[number])

    copies = []
    for step in range(half):
        copies.append(fetch(group * half + lax.rem(index + step, half), spectrum_any, block_ref.at[step], step))
    for step in range(half):
        target = (1 - group) * half + step
        copies.append(fetch(target, spectrum_any.at[pl.ds(0, 1)], edge_ref.at[pl.ds(step, 1)], half + step))
    return copies


def start_spectrum(plan, me, spectrum_any, block_ref, edge_ref, block_out_ref, edge_out_ref, sems, out_sems):
    for copy in spectrum_copies(plan, me, spectrum_any, block_ref, edge_ref, sems):
        copy.start()


def finish_spectrum(plan, me, spectrum_any, piece_anys, block_ref, edge_ref, block_out_ref, edge_out_ref, sems, out_sems):
    half, grid = plan.half, plan.grid
    wait_copies(spectrum_copies(plan, me, spectrum_any, block_ref, edge_ref, sems))
    odd = (iota((1, 1, grid), 2) & 1) == 1

    def fold(values):
        last = values[..., grid : grid + 1]
        return values[..., :grid] + jnp.where(odd, last, -last)

    edge_out_ref[...] = fold(edge_ref[...])
    pairs = []
    for step in range(half):
        block_out_ref[step] = fold(block_ref[step])
        pairs.append((block_out_ref.at[step], piece_anys[step]))
    pairs += [(edge_out_ref.at[pl.ds(step, 1)], piece_anys[half + step]) for step in range(half)]
    wait_copies(start_copies(out_sems, 0, *pairs))


def solve_kernel(plan, where_ref, recv_ref, *refs):
    half, slots, grid, box, count = plan.half, plan.slots, plan.grid, plan.box, plan.per_group
    doubled = plan.doubled
    piece_refs, edge_refs = refs[:half], refs[half : 2 * half]
    send_ref, field_ref, result_ref, table_ref, corner_ref, sem = refs[2 * half :]
    me = where_ref[0]
    depth = plan.area
    all_groups = plan.orb * plan.groups
    owner = lane_owner((1, grid), box)
    for group in range(all_groups):
        tile = recv_ref[group, depth : depth + 2 * SUB, :].astype(F32).astype(jnp.int32)
        table_ref[2 * group : 2 * group + 2, :] = tile[:2]
    copy = pltpu.make_async_copy(table_ref, corner_ref, sem)
    copy.start()
    field_ref[...] = jnp.zeros_like(field_ref)
    forward, _ = mode_table(plan, me, (doubled, grid), 0)
    forward_y = stack_terms(forward, 1)
    inverse, weight = mode_table(plan, me, (grid, doubled), 1)
    inverse_y = stack_terms(inverse * (weight * (1.0 / doubled**3)), 1)
    forward_z = stack_terms(depth_mode_table(plan, (grid, doubled), 1), 0)
    inverse_z = stack_terms(depth_mode_table(plan, (doubled, grid), 0), 0)
    copy.wait()

    def start(group, n):
        return pl.multiple_of(corner_ref[2 * group + 1, box * n] * slots, SUB)

    def place(group, carry):
        values = recv_ref[group, :depth, :].astype(F32)
        for n in range(count):
            shift = lax.rem(corner_ref[2 * group, box * n] - box * n + grid, grid)
            moved = pltpu.roll(jnp.where(owner == n, values, 0.0), shift, 1)
            field_ref[pl.ds(start(group, n), depth), :] += moved
        return carry

    lax.fori_loop(0, all_groups, place, 0)
    row = iota((grid, 1), 0)
    edge_row = lax.rem(me, half) * plan.ky_block
    edges = edge_refs[0][0]
    for ref in edge_refs[1:]:
        edges = edges + ref[0]
    for pair in range(slots // 2):
        both = (2 * pair, 2 * pair + 1)
        planes = jnp.concatenate([field_ref[pl.ds(s, grid, stride=slots), :] for s in both], axis=1)
        modes = dot(forward_y, terms_of(planes, 0))
        back = []
        for side, s in enumerate(both):
            spectrum = jnp.concatenate([ref[pl.ds(s, plan.ky_block, stride=slots), :] for ref in piece_refs], axis=0)
            other = jnp.where(row == edge_row, edges[s : s + 1], spectrum)
            spectrum = jnp.concatenate([spectrum, other], axis=0)
            mine = dot(terms_of(modes[:, grid * side : grid * (side + 1)], 1), forward_z)
            mine = mine * jnp.concatenate([spectrum, spectrum], axis=1)
            back.append(dot(terms_of(mine, 1), inverse_z))
        planes = dot(inverse_y, terms_of(jnp.concatenate(back, axis=1), 0))
        for side, s in enumerate(both):
            result_ref[pl.ds(s, grid, stride=slots), :] = planes[:, grid * side : grid * (side + 1)]

    def cut(group, carry):
        values = jnp.zeros((depth, grid), F32)
        for n in range(count):
            shift = lax.rem(box * n - corner_ref[2 * group, box * n] + grid, grid)
            rows = result_ref[pl.ds(start(group, n), depth), :]
            values = jnp.where(owner == n, pltpu.roll(rows, shift, 1), values)
        send_ref[group] = values.astype(send_ref.dtype)
        return carry

    lax.fori_loop(0, all_groups, cut, 0)


def terms_kernel(plan, where_ref, recv_ref, psi_any, wave_ref, *refs):
    box, grid, count, slots, pln = plan.box, plan.grid, plan.per_group, plan.slots, plan.pln
    out_refs = refs[:pln]
    psi_ref, stage_ref, own_ref, sem = refs[pln:]
    group = pl.program_id(0)
    copy = pltpu.make_async_copy(psi_any.at[group], psi_ref, sem)
    copy.start()
    owner = lane_owner((1, grid), box)
    wave = jnp.concatenate(split(wave_ref[0].T), axis=1)
    inner = stack_terms(inner_back_table(box), 1)
    outer = stack_terms(outer_back_table(box), 1)
    back = stack_terms(depth_back_table(plan), 1)
    copy.wait()
    for pair in range(box // 2):
        tiles = [recv_ref[o, 0, 2 * slots * pair : 2 * slots * (pair + 1), :].astype(F32) for o in range(plan.orb)]
        columns = [jnp.concatenate([t[slots * side : slots * (side + 1)] for t in tiles], axis=0) for side in range(2)]
        both = jnp.concatenate(columns, axis=1).astype(BF16)
        out = dot(wave, jnp.concatenate([both, both], axis=0))
        for side, b in enumerate((2 * pair, 2 * pair + 1)):
            mine = out[:, grid * side : grid * (side + 1)]
            potential = jnp.zeros((box, grid), F32)
            for n in range(count):
                potential = jnp.where(owner == n, mine[box * n : box * (n + 1)], potential)
            stage_ref[b] = potential * psi_ref[b]
    span = SUB * box
    second = []
    for t in range(box // SUB):
        values = stage_ref[SUB * t : SUB * (t + 1)].reshape(span, grid)
        second.append(dot(inner, terms_of(values, 0)))
    second = jnp.concatenate(second, axis=0).reshape(box, box // SUB, SUB, grid)
    for t in range(box // SUB):
        values = dot(outer, terms_of(second[:, t].reshape(span, grid), 0))
        stage_ref[:, SUB * t : SUB * (t + 1), :] = values.reshape(box, SUB, grid)
    values = terms_of(stage_ref[...].reshape(box * box, grid), 1)
    out = dot(back, values, ((1,), (1,)))
    part = plan.box_part * count
    for p in range(pln):
        own_ref[p] = out[part * p : part * (p + 1)]
    me = where_ref[0]
    out_refs[0][0] = own_ref[me]
    for step in range(1, pln):
        out_refs[step][0] = own_ref[lax.rem(me + step, pln)].astype(BF16)


def sum_kernel(plan, *refs):
    out_ref = refs[plan.pln]
    total = refs[0][0]
    for ref in refs[1 : plan.pln]:
        total = total + ref[0].astype(F32)
    section = plan.box * plan.box
    count = plan.per_group
    for j in range(plan.box_part):
        out_ref[0, :, section * j : section * (j + 1)] = total[count * j : count * (j + 1)].astype(out_ref.dtype)


def per_device(plan, orbitals, occupations, box_offsets, kernel_spectrum):
    orb, pln, half, slots = plan.orb, plan.pln, plan.half, plan.slots
    groups, count, box, grid = plan.groups, plan.per_group, plan.box, plan.grid
    plane_index = lax.axis_index("pln")
    where = plane_index.astype(jnp.int32)[None]
    smem = pl.BlockSpec(memory_space=pltpu.SMEM)
    anywhere = pl.BlockSpec(memory_space=pl.ANY)
    vmem = pl.BlockSpec(memory_space=pltpu.VMEM)
    dma = pltpu.SemaphoreType.DMA
    coefs = orbitals.reshape(groups, count, orbitals.shape[1])
    by_ky = jnp.transpose(kernel_spectrum, (1, 2, 0))
    area = plan.area
    padded = area + 2 * SUB
    tables = [plan.depth, plan.inner, plan.outer]
    piece = jax.ShapeDtypeStruct((plan.ky_block, slots, grid), F32)
    edge = jax.ShapeDtypeStruct((1, slots, grid), F32)
    send, psi, wave, *pieces = pl.pallas_call(
        functools.partial(density_kernel, plan),
        grid=(groups,),
        in_specs=[smem, smem, smem] + [anywhere] * 6,
        out_specs=[anywhere] * (3 + 2 * half),
        out_shape=[
            jax.ShapeDtypeStruct((orb, groups, padded, grid), BF16),
            jax.ShapeDtypeStruct((groups, box, box, grid), F32),
            jax.ShapeDtypeStruct((groups, plan.rows, grid), F32),
            *[piece] * half,
            *[edge] * half,
        ],
        scratch_shapes=[
            pltpu.VMEM((count, orbitals.shape[1]), BF16),
            *[pltpu.VMEM(t.shape, t.dtype) for t in tables],
            pltpu.VMEM((plan.rows, grid), F32),
            pltpu.VMEM((grid, box * box), F32),
            pltpu.VMEM((box, box, grid), F32),
            pltpu.VMEM((orb, padded, grid), BF16),
            pltpu.VMEM((half, plan.ky_block, slots, plan.doubled), F32),
            pltpu.VMEM((half, slots, plan.doubled), F32),
            pltpu.VMEM((half, plan.ky_block, slots, grid), F32),
            pltpu.VMEM((half, slots, grid), F32),
            dma((2 * half,)),
            dma((2 * half,)),
            dma((12,)),
        ],
        compiler_params=pltpu.CompilerParams(vmem_limit_bytes=LARGE),
        name="density",
    )(where, box_offsets, occupations, coefs, *tables, plan.wave, by_ky)
    received = lax.all_to_all(send, "orb", split_axis=0, concat_axis=0, tiled=True)
    received = received.reshape(orb * groups, padded, grid)
    for step in range(1, half):
        pairs = [(g * half + i, g * half + (i + step) % half) for g in range(2) for i in range(half)]
        pieces[step] = lax.ppermute(pieces[step], "pln", pairs)
    for step in range(half):
        pieces[half + step] = lax.ppermute(pieces[half + step], "pln", [(0, half + step), (half, step)])
    pieces[:half] = [p.reshape(plan.ky_block * slots, grid) for p in pieces[:half]]

    small = pltpu.CompilerParams(vmem_limit_bytes=SMALL)
    send = pl.pallas_call(
        functools.partial(solve_kernel, plan),
        in_specs=[smem] + [vmem] * (1 + 2 * half),
        out_specs=vmem,
        out_shape=jax.ShapeDtypeStruct((orb * groups, area, grid), BF16),
        scratch_shapes=[
            pltpu.VMEM((grid * slots, grid), F32),
            pltpu.VMEM((grid * slots, grid), F32),
            pltpu.VMEM((2 * orb * groups, grid), jnp.int32),
            pltpu.SMEM((2 * orb * groups, grid), jnp.int32),
            dma,
        ],
        compiler_params=small,
        name="solve",
    )(where, received, *pieces)
    send = send.reshape(orb, groups, area, grid)
    received = lax.all_to_all(send, "orb", split_axis=0, concat_axis=0, tiled=True)
    part = plan.box_part * count
    finished = pl.pallas_call(
        functools.partial(terms_kernel, plan),
        grid=(groups,),
        in_specs=[
            smem,
            pl.BlockSpec((orb, 1, area, grid), lambda g: (0, g, 0, 0)),
            anywhere,
            pl.BlockSpec((1, plan.rows, grid), lambda g: (g, 0, 0)),
        ],
        out_specs=[pl.BlockSpec((1, part, box * box), lambda g: (g, 0, 0))] * pln,
        out_shape=[jax.ShapeDtypeStruct((groups, part, box * box), BF16 if step else F32) for step in range(pln)],
        scratch_shapes=[
            pltpu.VMEM((box, box, grid), F32),
            pltpu.VMEM((box, box, grid), F32),
            pltpu.VMEM((pln, part, box * box), F32),
            dma,
        ],
        compiler_params=small,
        name="terms",
    )(where, received, psi, wave)
    finished = list(finished)
    for step in range(1, pln):
        finished[step] = lax.ppermute(finished[step], "pln", [(p, (p + step) % pln) for p in range(pln)])
    cells = plan.box_part * box * box
    result = pl.pallas_call(
        functools.partial(sum_kernel, plan),
        grid=(groups,),
        in_specs=[pl.BlockSpec((1, part, box * box), lambda g: (g, 0, 0))] * pln,
        out_specs=pl.BlockSpec((1, count, cells), lambda g: (g, 0, 0)),
        out_shape=jax.ShapeDtypeStruct((groups, count, cells), BF16),
        compiler_params=small,
        name="sum",
    )(*finished)
    return result.reshape(groups * count, cells)


def solution(mesh):
    in_specs = (P("orb", None), P("orb"), P("orb", None), P(None, "pln", "orb"))
    out_specs = P("orb", "pln")

    def whole(orbitals, occupations, box_offsets, kernel_spectrum):
        plan = Plan(mesh, orbitals.shape, kernel_spectrum.shape)
        return jax.shard_map(
            functools.partial(per_device, plan), mesh=mesh, in_specs=in_specs, out_specs=out_specs, check_vma=False
        )(orbitals, occupations, box_offsets, kernel_spectrum)

    return whole
```

time: 62.9 us -> 54.4 us (0.86)
  Pallas kernels: 23.2 us -> 15.9 us
  blocking collectives: 13.9 us -> 12.5 us
  waiting for transfers between devices: 5.61 us -> 6.69 us
    pallas_call x1, Pallas kernels: 10.4 us -> 7.32 us  [per_device(): pl.pallas_call(functools.partial(solve_kernel, plan), in_specs=[smem] + [...]
    pallas_call x1 -> x0, Pallas kernels: 2.36 us -> none  [per_device(): pl.pallas_call(functools.partial(spectrum_kernel, plan), grid=(1,), in_sp...]
    pallas_call x1, Pallas kernels: 4.13 us -> 2.44 us  [per_device(): pl.pallas_call(functools.partial(terms_kernel, plan), grid=(groups,), in_...]
    all_to_all x1, blocking collectives: 13.9 us -> 12.5 us  [per_device(): lax.all_to_all(send, 'orb', split_axis=0, concat_axis=0, tiled=True)]
    all_to_all x1, waiting for transfers between devices: 0.01 us -> 1.08 us  [per_device(): lax.all_to_all(send, 'orb', split_axis=0, concat_axis=0, tiled=True)]
    pallas_call x1, Pallas kernels: 1.63 us -> 0.67 us  [per_device(): pl.pallas_call(functools.partial(sum_kernel, plan), grid=(groups,), in_sp...]
    pallas_call x1, Pallas kernels: 4.77 us -> 5.44 us  [per_device(): pl.pallas_call(functools.partial(density_kernel, plan), grid=(groups,), i...]
    unnamed x14 -> x6, local copies, waits for them, and re-layouts: 1.51 us -> 0.96 us
  transfers between devices with their start and end apart: 7 -> 7, of which waited for: 6 -> 7; matrix products, arithmetic and copies ran while one was open for 0% -> 0% of each run, Pallas kernels for 4% -> 0%
where the time goes in v4:
time: 54.4 us; the launch traced here: 54 us
  starting transfers between devices  17.9 us (33%)
  Pallas kernels  15.9 us (29%)
  blocking collectives  12.5 us (23%)
  waiting for transfers between devices  6.69 us (12%)
  local copies, waits for them, and re-layouts  0.96 us (2%)
    all_to_all x1, blocking collectives, per_device(): lax.all_to_all(send, 'orb', split_axis=0, concat_axis=0, tiled=True)  12.5 us
    pallas_call x1, Pallas kernels, per_device(): pl.pallas_call(functools.partial(solve_kernel, plan), in_specs=[smem] + [...  7.32 us
    ppermute x2, starting transfers between devices, per_device(): lax.ppermute(pieces[half + step], 'pln', [(0, half + step), (half, step)])  5.77 us
    pallas_call x1, Pallas kernels, per_device(): pl.pallas_call(functools.partial(density_kernel, plan), grid=(groups,), i...  5.44 us
    all_to_all x1, starting transfers between devices, per_device(): lax.all_to_all(send, 'orb', split_axis=0, concat_axis=0, tiled=True)  5.32 us
    ppermute x3, starting transfers between devices, per_device(): lax.ppermute(finished[step], 'pln', [(p, (p + step) % pln) for p in range...  5.27 us
    ppermute x3, waiting for transfers between devices, per_device(): lax.ppermute(finished[step], 'pln', [(p, (p + step) % pln) for p in range...  3.96 us
    pallas_call x1, Pallas kernels, per_device(): pl.pallas_call(functools.partial(terms_kernel, plan), grid=(groups,), in_...  2.44 us
  transfers between devices with their start and end apart: 7, of which 7 were waited for; matrix products, arithmetic and copies ran while one was open for 0% of the time, Pallas kernels for 0%

profile of v4, /device:TPU:0, one launch (start us, length us, event | category | flops | bytes accessed | tf_op | source)
XLA Modules:
  0.0 54.0 jit_solution(15920043310315866100)
XLA Ops:
  0.0 5.4 %density.1 = (bf16[8,1,272,128]{3,2,1,0:T(8,128)(2,1)}, f32[1,32,32,128]{3,2,1,0:T(8,128)}, f32[1,64,128]{2,1,0:T(8,128)}, f32[64,8,128]{2,1,0:T(8,128)}, f32[64...) custom-call(s32[1]{0:T(128)} %bitcast.where_ref, s32[4,3]{1,0:T(4,128)} %corner_ref.1, f32[4]{0:T(128)} %weight_ref.1, ...), custom_call_target="tpu_custom_call" | custom-call | tf_op jit(solution)/shard_map/density/pallas_call | solution.py:477
  5.4 0.0 copy-start
  5.5 0.0 copy-start.2
  5.5 5.3 %all-to-all-start = ((bf16[8,1,272,128]{3,2,1,0:T(8,128)(2,1)}), bf16[8,1,272,128]{3,2,1,0:T(8,128)(2,1)S(1)}, u32[]{:S(2)}, u32[]{:S(2)}) async-start(bf16[8,1,272,128]{3,2,1,0:T(8,128)(2,1)} %get-tuple-element.16), calls=%async_computation | async-start | bytes 1114112 | tf_op jit(solution)/shard_map/all_to_all | solution.py:507
  10.8 1.6 %collective-permute-start = (f32[64,8,128]{2,1,0:T(8,128)}, f32[64,8,128]{2,1,0:T(8,128)S(1)}, u32[]{:S(2)}, u32[]{:S(2)}) collective-permute-start(f32[64,8,128]{2,1,0:T(8,128)} %get-tuple-element.18), channel_id=1, source_target_pairs={{0,1},{1,0},{2,3},{3,2},{4,5},{5,4},{6,7},{7,6},{8,9},{9,8},{10,11... | collective-permute-start | bytes 786440 | tf_op jit(solution)/shard_map/ppermute | solution.py:511
  12.4 4.5 %collective-permute-start.1 = (f32[1,8,128]{2,1,0:T(8,128)}, f32[1,8,128]{2,1,0:T(8,128)S(1)}, u32[]{:S(2)}, u32[]{:S(2)}) collective-permute-start(f32[1,8,128]{2,1,0:T(8,128)} %get-tuple-element.19), channel_id=1, source_target_pairs={{0,2},{2,0},{4,6},{6,4},{8,10},{10,8},{12,14},{14,12},{16,18},{18,... | collective-permute-start | bytes 12296 | tf_op jit(solution)/shard_map/ppermute | solution.py:513
  16.9 1.3 %collective-permute-start.2 = (f32[1,8,128]{2,1,0:T(8,128)}, f32[1,8,128]{2,1,0:T(8,128)S(1)}, u32[]{:S(2)}, u32[]{:S(2)}) collective-permute-start(f32[1,8,128]{2,1,0:T(8,128)} %get-tuple-element.20), channel_id=1, source_target_pairs={{0,3},{2,1},{4,7},{6,5},{8,11},{10,9},{12,15},{14,13},{16,19},{18,... | collective-permute-start | bytes 12296 | tf_op jit(solution)/shard_map/ppermute | solution.py:513
  18.1 0.9 %collective-permute-done.1.refs_2_ = f32[1,8,128]{2,1,0:T(8,128)S(1)} collective-permute-done((f32[1,8,128]{2,1,0:T(8,128)}, f32[1,8,128]{2,1,0:T(8,128)S(1)}, u32[]{:S(2)}, u32[]{:S(2)}) %collective-permute-start.1) | collective-permute-done | bytes 4128 | tf_op jit(solution)/shard_map/ppermute | solution.py:513
  19.1 0.6 %collective-permute-done.2.refs_3_ = f32[1,8,128]{2,1,0:T(8,128)S(1)} collective-permute-done((f32[1,8,128]{2,1,0:T(8,128)}, f32[1,8,128]{2,1,0:T(8,128)S(1)}, u32[]{:S(2)}, u32[]{:S(2)}) %collective-permute-start.2) | collective-permute-done | bytes 4128 | tf_op jit(solution)/shard_map/ppermute | solution.py:513
  19.7 0.1 collective-permute-done
  19.8 1.1 %all-to-all-done = bf16[8,1,272,128]{3,2,1,0:T(8,128)(2,1)S(1)} async-done(((bf16[8,1,272,128]{3,2,1,0:T(8,128)(2,1)}), bf16[8,1,272,128]{3,2,1,0:T(8,128)(2,1)S(1)}, u32[]{:S(2)}, u32[]{:S(2)}) %all-to-all-start) | async-done | bytes 557088 | tf_op jit(solution)/shard_map/all_to_all | solution.py:507
  20.9 0.9 %copy-done.1 = f32[64,8,128]{2,1,0:T(8,128)S(1)} copy-done((f32[64,8,128]{2,1,0:T(8,128)S(1)}, f32[64,8,128]{2,1,0:T(8,128)}, u32[]{:S(2)}) %copy-start.1) | copy-done | bytes 262168
  21.8 7.3 %solve.1 = bf16[8,256,128]{2,1,0:T(8,128)(2,1)S(1)} custom-call(s32[1]{0:T(128)} %bitcast.where_ref, bf16[8,272,128]{2,1,0:T(8,128)(2,1)S(1)} %bitcast.8, f32[512,128]{1,0:T(8,128)S(1)} %bitcast.10, f32[512,128]{1,0:T(8,128)S(1)} %bitcast.11, f32[1,8,128]{2,1,0:T(8,128)S(1)} %collective-permute-done.1.refs_2_, f32[1,8,128]{2,1,0:T(8,128)S(1)} %collective-permute-done.2.refs_3_), custom_call_target="tpu_custom_call" | custom-call | tf_op jit(solution)/shard_map/solve/pallas_call | solution.py:517
  29.2 12.5 %all_to_all.10.recv_ref = bf16[8,1,256,128]{3,2,1,0:T(8,128)(2,1)S(1)} all-to-all(bf16[8,1,256,128]{3,2,1,0:T(8,128)(2,1)S(1)} %bitcast.9), channel_id=1, replica_groups=mesh['orb'=8,'pln'=4] {'orb'}, dimensions={0} | all-to-all | bytes 1048576 | tf_op jit(solution)/shard_map/all_to_all | solution.py:533
  41.7 0.0 copy-done
  41.7 0.0 copy-done.2
  41.7 2.4 %terms.1 = (f32[1,32,1024]{2,1,0:T(8,128)S(1)}, bf16[1,32,1024]{2,1,0:T(8,128)(2,1)S(1)}, bf16[1,32,1024]{2,1,0:T(8,128)(2,1)S(1)}, bf16[1,32,1024]{2,1,0:T(8,128)(2,1)S(1)}) custom-call(s32[1]{0:T(128)} %bitcast.where_ref, bf16[8,1,256,128]{3,2,1,0:T(8,128)(2,1)S(1)} %all_to_all.10.recv_ref, f32[1,32,32,128]{3,2,1,0:T(8,128)S(1)} %copy-done, ...), custom_call_target="tpu_custom_call" | custom-call | tf_op jit(solution)/shard_map/terms/pallas_call | solution.py:535
  44.2 1.4 %collective-permute-start.3 = (bf16[1,32,1024]{2,1,0:T(8,128)(2,1)S(1)}, bf16[1,32,1024]{2,1,0:T(8,128)(2,1)S(1)}, u32[]{:S(2)}, u32[]{:S(2)}) collective-permute-start(bf16[1,32,1024]{2,1,0:T(8,128)(2,1)S(1)} %get-tuple-element.24), channel_id=1, source_target_pairs={{0,1},{1,2},{2,3},{3,0},{4,5},{5,6},{6,7},{7,4},{8,9},{9,10},{10,1... | collective-permute-start | bytes 196616 | tf_op jit(solution)/shard_map/ppermute | solution.py:557
  45.5 3.3 %collective-permute-start.4 = (bf16[1,32,1024]{2,1,0:T(8,128)(2,1)S(1)}, bf16[1,32,1024]{2,1,0:T(8,128)(2,1)S(1)}, u32[]{:S(2)}, u32[]{:S(2)}) collective-permute-start(bf16[1,32,1024]{2,1,0:T(8,128)(2,1)S(1)} %get-tuple-element.25), channel_id=1, source_target_pairs={{0,2},{1,3},{2,0},{3,1},{4,6},{5,7},{6,4},{7,5},{8,10},{9,11},{10,... | collective-permute-start | bytes 196616 | tf_op jit(solution)/shard_map/ppermute | solution.py:557
  48.8 0.6 %collective-permute-start.5 = (bf16[1,32,1024]{2,1,0:T(8,128)(2,1)S(1)}, bf16[1,32,1024]{2,1,0:T(8,128)(2,1)S(1)}, u32[]{:S(2)}, u32[]{:S(2)}) collective-permute-start(bf16[1,32,1024]{2,1,0:T(8,128)(2,1)S(1)} %get-tuple-element.26), channel_id=1, source_target_pairs={{0,3},{1,0},{2,1},{3,2},{4,7},{5,4},{6,5},{7,6},{8,11},{9,8},{10,9... | collective-permute-start | bytes 196616 | tf_op jit(solution)/shard_map/ppermute | solution.py:557
  49.4 1.9 %collective-permute-done.3.refs_1_ = bf16[1,32,1024]{2,1,0:T(8,128)(2,1)S(1)} collective-permute-done((bf16[1,32,1024]{2,1,0:T(8,128)(2,1)S(1)}, bf16[1,32,1024]{2,1,0:T(8,128)(2,1)S(1)}, u32[]{:S(2)}, u32[]{:S(2)}) %collective-permute-start.3) | collective-permute-done | bytes 65568 | tf_op jit(solution)/shard_map/ppermute | solution.py:557
  51.3 1.7 %collective-permute-done.4.refs_2_ = bf16[1,32,1024]{2,1,0:T(8,128)(2,1)S(1)} collective-permute-done((bf16[1,32,1024]{2,1,0:T(8,128)(2,1)S(1)}, bf16[1,32,1024]{2,1,0:T(8,128)(2,1)S(1)}, u32[]{:S(2)}, u32[]{:S(2)}) %collective-permute-start.4) | collective-permute-done | bytes 65568 | tf_op jit(solution)/shard_map/ppermute | solution.py:557
  53.0 0.4 collective-permute-done.5.refs_3_
  53.4 0.7 %sum.1 = bf16[1,4,8192]{2,1,0:T(4,128)(2,1)} custom-call(f32[1,32,1024]{2,1,0:T(8,128)S(1)} %get-tuple-element.23.refs_0_, bf16[1,32,1024]{2,1,0:T(8,128)(2,1)S(1)} %collective-permute-done.3.refs_1_, bf16[1,32,1024]{2,1,0:T(8,128)(2,1)S(1)} %collective-permute-done.4.refs_2_, bf16[1,32,1024]{2,1,0:T(8,128)(2,1)S(1)} %collective-permute-done.5.refs_3_), custom_call_target="tpu_custom_call" | custom-call | tf_op jit(solution)/shard_map/sum/pallas_call | solution.py:559
  (1 shorter events, 0.0 us)
Async XLA Ops:
  5.4 36.3 %copy-start = (f32[1,32,32,128]{3,2,1,0:T(8,128)S(1)}, f32[1,32,32,128]{3,2,1,0:T(8,128)}, u32[]{:S(2)}) copy-start(f32[1,32,32,128]{3,2,1,0:T(8,128)} %get-tuple-element.21.psi_any) | copy-start | bytes 1572868
  5.5 36.3 %copy-start.2 = (f32[1,64,128]{2,1,0:T(8,128)S(1)}, f32[1,64,128]{2,1,0:T(8,128)}, u32[]{:S(2)}) copy-start(f32[1,64,128]{2,1,0:T(8,128)} %get-tuple-element.22.wave_ref) | copy-start | bytes 98308
  5.5 15.4 %all-to-all-start = ((bf16[8,1,272,128]{3,2,1,0:T(8,128)(2,1)}), bf16[8,1,272,128]{3,2,1,0:T(8,128)(2,1)S(1)}, u32[]{:S(2)}, u32[]{:S(2)}) async-start(bf16[8,1,272,128]{3,2,1,0:T(8,128)(2,1)} %get-tuple-element.16), calls=%async_computation | async-start | bytes 1114112 | tf_op jit(solution)/shard_map/all_to_all | solution.py:507
  10.8 9.0 %collective-permute-start = (f32[64,8,128]{2,1,0:T(8,128)}, f32[64,8,128]{2,1,0:T(8,128)S(1)}, u32[]{:S(2)}, u32[]{:S(2)}) collective-permute-start(f32[64,8,128]{2,1,0:T(8,128)} %get-tuple-element.18), channel_id=1, source_target_pairs={{0,1},{1,0},{2,3},{3,2},{4,5},{5,4},{6,7},{7,6},{8,9},{9,8},{10,11... | collective-permute-start | bytes 786440 | tf_op jit(solution)/shard_map/ppermute | solution.py:511
  12.4 6.7 %collective-permute-start.1 = (f32[1,8,128]{2,1,0:T(8,128)}, f32[1,8,128]{2,1,0:T(8,128)S(1)}, u32[]{:S(2)}, u32[]{:S(2)}) collective-permute-start(f32[1,8,128]{2,1,0:T(8,128)} %get-tuple-element.19), channel_id=1, source_target_pairs={{0,2},{2,0},{4,6},{6,4},{8,10},{10,8},{12,14},{14,12},{16,18},{18,... | collective-permute-start | bytes 12296 | tf_op jit(solution)/shard_map/ppermute | solution.py:513
  16.9 2.8 %collective-permute-start.2 = (f32[1,8,128]{2,1,0:T(8,128)}, f32[1,8,128]{2,1,0:T(8,128)S(1)}, u32[]{:S(2)}, u32[]{:S(2)}) collective-permute-start(f32[1,8,128]{2,1,0:T(8,128)} %get-tuple-element.20), channel_id=1, source_target_pairs={{0,3},{2,1},{4,7},{6,5},{8,11},{10,9},{12,15},{14,13},{16,19},{18,... | collective-permute-start | bytes 12296 | tf_op jit(solution)/shard_map/ppermute | solution.py:513
  20.9 1.0 %copy-start.1 = (f32[64,8,128]{2,1,0:T(8,128)S(1)}, f32[64,8,128]{2,1,0:T(8,128)}, u32[]{:S(2)}) copy-start(f32[64,8,128]{2,1,0:T(8,128)} %get-tuple-element.17) | copy-start | bytes 786436
  44.2 7.1 %collective-permute-start.3 = (bf16[1,32,1024]{2,1,0:T(8,128)(2,1)S(1)}, bf16[1,32,1024]{2,1,0:T(8,128)(2,1)S(1)}, u32[]{:S(2)}, u32[]{:S(2)}) collective-permute-start(bf16[1,32,1024]{2,1,0:T(8,128)(2,1)S(1)} %get-tuple-element.24), channel_id=1, source_target_pairs={{0,1},{1,2},{2,3},{3,0},{4,5},{5,6},{6,7},{7,4},{8,9},{9,10},{10,1... | collective-permute-start | bytes 196616 | tf_op jit(solution)/shard_map/ppermute | solution.py:557
  45.5 7.4 %collective-permute-start.4 = (bf16[1,32,1024]{2,1,0:T(8,128)(2,1)S(1)}, bf16[1,32,1024]{2,1,0:T(8,128)(2,1)S(1)}, u32[]{:S(2)}, u32[]{:S(2)}) collective-permute-start(bf16[1,32,1024]{2,1,0:T(8,128)(2,1)S(1)} %get-tuple-element.25), channel_id=1, source_target_pairs={{0,2},{1,3},{2,0},{3,1},{4,6},{5,7},{6,4},{7,5},{8,10},{9,11},{10,... | collective-permute-start | bytes 196616 | tf_op jit(solution)/shard_map/ppermute | solution.py:557
  48.8 4.6 %collective-permute-start.5 = (bf16[1,32,1024]{2,1,0:T(8,128)(2,1)S(1)}, bf16[1,32,1024]{2,1,0:T(8,128)(2,1)S(1)}, u32[]{:S(2)}, u32[]{:S(2)}) collective-permute-start(bf16[1,32,1024]{2,1,0:T(8,128)(2,1)S(1)} %get-tuple-element.26), channel_id=1, source_target_pairs={{0,3},{1,0},{2,1},{3,2},{4,7},{5,4},{6,5},{7,6},{8,11},{9,8},{10,9... | collective-permute-start | bytes 196616 | tf_op jit(solution)/shard_map/ppermute | solution.py:557

commit v5 on v4

--- a/solution.py
+++ b/solution.py
@@ -218,80 +218,71 @@
 
 def density_kernel(
     plan, where_ref, corner_ref, weight_ref, coef_any, depth_any, inner_any, outer_any, wave_any, spectrum_any,
-    send_any, psi_any, wave_out_any, *refs,
+    send_ref, psi_any, wave_out_any, *refs,
 ):
-    piece_anys = refs[: 2 * plan.half]
-    coef_ref, depth_ref, inner_ref, outer_ref, wave_ref, stage_ref, psi_ref, send_ref, *spectrum_refs, sems = refs[2 * plan.half :]
+    piece_refs = refs[: 2 * plan.half]
+    coef_ref, depth_ref, inner_ref, outer_ref, wave_ref, own_wave_ref, stage_ref, psi_ref = refs[2 * plan.half : -4]
+    block_ref, edge_ref, spectrum_sems, sems = refs[-4:]
     box, grid, count, slots = plan.box, plan.grid, plan.per_group, plan.slots
     section = box * box
-    group = pl.program_id(0)
+    span = SUB * box
+    me = where_ref[0]
+    coef_copy = pltpu.make_async_copy(coef_any, coef_ref, sems.at[0])
+    coef_copy.start()
     fetched = start_copies(
-        sems, 0, (coef_any.at[group], coef_ref), (depth_any, depth_ref), (inner_any, inner_ref),
-        (outer_any, outer_ref), (wave_any.at[where_ref[0]], wave_ref),
+        sems, 1, (depth_any, depth_ref), (inner_any, inner_ref), (outer_any, outer_ref), (wave_any.at[me], wave_ref)
     )
-
-    @pl.when(group == 0)
-    def _():
-        start_spectrum(plan, where_ref[0], spectrum_any, *spectrum_refs)
-
-    wait_copies(fetched[:2])
-    for p in range(box):
-        stage_ref[count * p : count * (p + 1), :] = coef_ref[:, section * p : section * (p + 1)].astype(F32)
-    coef = stage_ref[...].astype(BF16)
-    first = dot(jnp.concatenate([coef, coef], axis=0), depth_ref[...], ((0,), (0,)))
-    span = SUB * box
-    wait_copies(fetched[2:])
-    inner, outer = inner_ref[...], outer_ref[...]
-    second = [dot(inner, terms_of(first[span * t : span * (t + 1)], 0)) for t in range(box // SUB)]
-    second = jnp.concatenate(second, axis=0).reshape(box, box // SUB, SUB, grid)
-    for t in range(box // SUB):
-        third = dot(outer, terms_of(second[:, t].reshape(span, grid), 0))
-        psi_ref[:, SUB * t : SUB * (t + 1), :] = third.reshape(box, SUB, grid)
+    spectrum = spectrum_copies(plan, me, spectrum_any, block_ref, edge_ref, spectrum_sems)
+    for copy in spectrum:
+        copy.start()
     owner = lane_owner((1, grid), box)
-    whole_wave = wave_ref[...]
-    wave = jnp.zeros_like(whole_wave)
-    weight = jnp.zeros((1, grid), F32)
-    kind = lax.broadcasted_iota(jnp.int32, (2 * SUB, 1), 0)
-    corner = jnp.zeros((2 * SUB, grid), F32)
-    for n in range(count):
-        number = group * count + n
-        shift = lax.rem(box * n - corner_ref[number, 2] + grid, grid)
-        wave = jnp.where(owner == n, pltpu.roll(whole_wave, shift, 1), wave)
-        weight = jnp.where(owner == n, weight_ref[number], weight)
-        place = jnp.where(kind == 0, corner_ref[number, 0], corner_ref[number, 1])
-        corner = jnp.where(owner == n, place.astype(F32), corner)
-    wave_ref[...] = wave
-    for o in range(plan.orb):
-        send_ref[o, plan.area :, :] = corner.astype(send_ref.dtype)
-    high, low = split(wave)
-    wave_terms = jnp.concatenate([high, low, high], axis=1)
-    rows = pl.ds(plan.area, 2 * SUB)
-    sent = start_copies(
-        sems, 5, (psi_ref, psi_any.at[group]), (wave_ref, wave_out_any.at[group]),
-        (send_ref.at[:, rows, :], send_any.at[:, group, rows, :]),
-    )
-    per_part = plan.quarter // 2
-    for pair in range(box // 2):
-        columns = []
-        for b in (2 * pair, 2 * pair + 1):
-            psi = psi_ref[b]
-            density = psi * psi * weight
-            columns.append(jnp.concatenate([jnp.where(owner == n, density, 0.0) for n in range(count)], axis=0))
-        out = dot(wave_terms, terms_of(jnp.concatenate(columns, axis=1), 0))
+    coef_copy.wait()
+    wait_copies(fetched)
+    for group in range(plan.groups):
+        for p in range(box):
+            stage_ref[count * p : count * (p + 1), :] = coef_ref[group, :, section * p : section * (p + 1)].astype(F32)
+        coef = stage_ref[...].astype(BF16)
+        first = dot(jnp.concatenate([coef, coef], axis=0), depth_ref[...], ((0,), (0,)))
+        inner, outer = inner_ref[...], outer_ref[...]
+        second = [dot(inner, terms_of(first[span * t : span * (t + 1)], 0)) for t in range(box // SUB)]
+        second = jnp.concatenate(second, axis=0).reshape(box, box // SUB, SUB, grid)
+        for t in range(box // SUB):
+            third = dot(outer, terms_of(second[:, t].reshape(span, grid), 0))
+            psi_ref[:, SUB * t : SUB * (t + 1), :] = third.reshape(box, SUB, grid)
+        sent = start_copies(sems, 5, (psi_ref, psi_any.at[group]))
+        whole_wave = wave_ref[...]
+        wave = jnp.zeros_like(whole_wave)
+        weight = jnp.zeros((1, grid), F32)
+        kind = iota((2 * SUB, 1), 0)
+        corner = jnp.zeros((2 * SUB, grid), F32)
+        for n in range(count):
+            number = group * count + n
+            shift = lax.rem(box * n - corner_ref[number, 2] + grid, grid)
+            wave = jnp.where(owner == n, pltpu.roll(whole_wave, shift, 1), wave)
+            weight = jnp.where(owner == n, weight_ref[number], weight)
+            place = jnp.where(kind == 0, corner_ref[number, 0], corner_ref[number, 1])
+            corner = jnp.where(owner == n, place.astype(F32), corner)
+        own_wave_ref[...] = wave
+        sent += start_copies(sems, 6, (own_wave_ref, wave_out_any.at[group]))
         for o in range(plan.orb):
-            mine = out[slots * o : slots * (o + 1)]
-            tile = jnp.concatenate([mine[:, :grid], mine[:, grid:]], axis=0)
-            send_ref[o, 2 * slots * pair : 2 * slots * (pair + 1), :] = tile.astype(send_ref.dtype)
-        if pair % per_part == per_part - 1:
-            part = pair // per_part
-            rows = pl.ds(plan.quarter * slots * part, plan.quarter * slots)
-            sent += start_copies(sems, 8 + part, (send_ref.at[:, rows, :], send_any.at[:, group, rows, :]))
-
-    @pl.when(group == 0)
-    def _():
-        finish_spectrum(plan, where_ref[0], spectrum_any, piece_anys, *spectrum_refs)
-
-    wait_copies(sent)
+            send_ref[o, group, plan.area :, :] = corner.astype(send_ref.dtype)
+        high, low = split(wave)
+        wave_terms = jnp.concatenate([high, low, high], axis=1)
+        if group == 0:
+            wait_copies(spectrum)
+            fold_spectrum(plan, piece_refs, block_ref, edge_ref)
+        for pair in range(box // 2):
+            columns = []
+            for b in (2 * pair, 2 * pair + 1):
+                psi = psi_ref[b]
+                density = psi * psi * weight
+                columns.append(jnp.concatenate([jnp.where(owner == n, density, 0.0) for n in range(count)], axis=0))
+            out = dot(wave_terms, terms_of(jnp.concatenate(columns, axis=1), 0))
+            for o in range(plan.orb):
+                mine = out[slots * o : slots * (o + 1)]
+                tile = jnp.concatenate([mine[:, :grid], mine[:, grid:]], axis=0)
+                send_ref[o, group, 2 * slots * pair : 2 * slots * (pair + 1), :] = tile.astype(send_ref.dtype)
+        wait_copies(sent)
 
 
 def spectrum_copies(plan, me, spectrum_any, block_ref, edge_ref, sems):
@@ -312,34 +303,43 @@
     return copies
 
 
-def start_spectrum(plan, me, spectrum_any, block_ref, edge_ref, block_out_ref, edge_out_ref, sems, out_sems):
-    for copy in spectrum_copies(plan, me, spectrum_any, block_ref, edge_ref, sems):
-        copy.start()
-
-
-def finish_spectrum(plan, me, spectrum_any, piece_anys, block_ref, edge_ref, block_out_ref, edge_out_ref, sems, out_sems):
+def fold_spectrum(plan, piece_refs, block_ref, edge_ref):
     half, grid = plan.half, plan.grid
-    wait_copies(spectrum_copies(plan, me, spectrum_any, block_ref, edge_ref, sems))
     odd = (iota((1, 1, grid), 2) & 1) == 1
 
     def fold(values):
         last = values[..., grid : grid + 1]
         return values[..., :grid] + jnp.where(odd, last, -last)
 
-    edge_out_ref[...] = fold(edge_ref[...])
-    pairs = []
     for step in range(half):
-        block_out_ref[step] = fold(block_ref[step])
-        pairs.append((block_out_ref.at[step], piece_anys[step]))
-    pairs += [(edge_out_ref.at[pl.ds(step, 1)], piece_anys[half + step]) for step in range(half)]
-    wait_copies(start_copies(out_sems, 0, *pairs))
+        piece_refs[step][...] = fold(block_ref[step])
+        piece_refs[half + step][...] = fold(edge_ref[pl.ds(step, 1)])
+
+
+def tables_kernel(plan, where_ref, wave_any, piece_any, *refs):
+    forward_y_ref, forward_z_ref, inverse_y_ref, inverse_z_ref, inner_ref, outer_ref, back_ref = refs[:7]
+    wave_out_ref, piece_ref, wave_ref, sems = refs[7:]
+    grid, doubled, me = plan.grid, plan.doubled, where_ref[0]
+    copies = start_copies(sems, 0, (wave_any, wave_ref), (piece_any, piece_ref))
+    forward, _ = mode_table(plan, me, (doubled, grid), 0)
+    forward_y_ref[...] = jnp.concatenate(split(forward), axis=1)
+    forward_z_ref[...] = jnp.concatenate(split(depth_mode_table(plan, (grid, doubled), 1)), axis=0)
+    inverse, weight = mode_table(plan, me, (grid, doubled), 1)
+    inverse_y_ref[...] = stack_terms(inverse * (weight * (1.0 / doubled**3)), 1)
+    inverse_z_ref[...] = stack_terms(depth_mode_table(plan, (doubled, grid), 0), 0)
+    inner_ref[...] = stack_terms(inner_back_table(plan.box), 1)
+    outer_ref[...] = stack_terms(outer_back_table(plan.box), 1)
+    back_ref[...] = stack_terms(depth_back_table(plan), 1)
+    wait_copies(copies)
+    for group in range(plan.groups):
+        wave_out_ref[group] = jnp.concatenate(split(wave_ref[group].T), axis=1)
 
 
 def solve_kernel(plan, where_ref, recv_ref, *refs):
     half, slots, grid, box, count = plan.half, plan.slots, plan.grid, plan.box, plan.per_group
-    doubled = plan.doubled
     piece_refs, edge_refs = refs[:half], refs[half : 2 * half]
-    send_ref, field_ref, result_ref, table_ref, corner_ref, sem = refs[2 * half :]
+    forward_y_ref, forward_z_ref, inverse_y_ref, inverse_z_ref = refs[2 * half : 2 * half + 4]
+    send_ref, field_ref, result_ref, table_ref, corner_ref, sem = refs[2 * half + 4 :]
     me = where_ref[0]
     depth = plan.area
     all_groups = plan.orb * plan.groups
@@ -350,12 +350,8 @@
     copy = pltpu.make_async_copy(table_ref, corner_ref, sem)
     copy.start()
     field_ref[...] = jnp.zeros_like(field_ref)
-    forward, _ = mode_table(plan, me, (doubled, grid), 0)
-    forward_y = stack_terms(forward, 1)
-    inverse, weight = mode_table(plan, me, (grid, doubled), 1)
-    inverse_y = stack_terms(inverse * (weight * (1.0 / doubled**3)), 1)
-    forward_z = stack_terms(depth_mode_table(plan, (grid, doubled), 1), 0)
-    inverse_z = stack_terms(depth_mode_table(plan, (doubled, grid), 0), 0)
+    forward_y, forward_z = forward_y_ref[...], forward_z_ref[...]
+    inverse_y, inverse_z = inverse_y_ref[...], inverse_z_ref[...]
     copy.wait()
 
     def start(group, n):
@@ -378,13 +374,15 @@
     for pair in range(slots // 2):
         both = (2 * pair, 2 * pair + 1)
         planes = jnp.concatenate([field_ref[pl.ds(s, grid, stride=slots), :] for s in both], axis=1)
-        modes = dot(forward_y, terms_of(planes, 0))
+        planes = planes.astype(BF16)
+        modes = dot(forward_y, jnp.concatenate([planes, planes], axis=0)).astype(BF16)
         back = []
         for side, s in enumerate(both):
             spectrum = jnp.concatenate([ref[pl.ds(s, plan.ky_block, stride=slots), :] for ref in piece_refs], axis=0)
             other = jnp.where(row == edge_row, edges[s : s + 1], spectrum)
             spectrum = jnp.concatenate([spectrum, other], axis=0)
-            mine = dot(terms_of(modes[:, grid * side : grid * (side + 1)], 1), forward_z)
+            mine = modes[:, grid * side : grid * (side + 1)]
+            mine = dot(jnp.concatenate([mine, mine], axis=1), forward_z)
             mine = mine * jnp.concatenate([spectrum, spectrum], axis=1)
             back.append(dot(terms_of(mine, 1), inverse_z))
         planes = dot(inverse_y, terms_of(jnp.concatenate(back, axis=1), 0))
@@ -403,7 +401,7 @@
     lax.fori_loop(0, all_groups, cut, 0)
 
 
-def terms_kernel(plan, where_ref, recv_ref, psi_any, wave_ref, *refs):
+def terms_kernel(plan, where_ref, recv_ref, psi_any, wave_ref, inner_ref, outer_ref, back_ref, *refs):
     box, grid, count, slots, pln = plan.box, plan.grid, plan.per_group, plan.slots, plan.pln
     out_refs = refs[:pln]
     psi_ref, stage_ref, own_ref, sem = refs[pln:]
@@ -411,10 +409,7 @@
     copy = pltpu.make_async_copy(psi_any.at[group], psi_ref, sem)
     copy.start()
     owner = lane_owner((1, grid), box)
-    wave = jnp.concatenate(split(wave_ref[0].T), axis=1)
-    inner = stack_terms(inner_back_table(box), 1)
-    outer = stack_terms(outer_back_table(box), 1)
-    back = stack_terms(depth_back_table(plan), 1)
+    wave, inner, outer, back = wave_ref[0], inner_ref[...], outer_ref[...], back_ref[...]
     copy.wait()
     for pair in range(box // 2):
         tiles = [recv_ref[o, 0, 2 * slots * pair : 2 * slots * (pair + 1), :].astype(F32) for o in range(plan.orb)]
@@ -476,9 +471,8 @@
     edge = jax.ShapeDtypeStruct((1, slots, grid), F32)
     send, psi, wave, *pieces = pl.pallas_call(
         functools.partial(density_kernel, plan),
-        grid=(groups,),
         in_specs=[smem, smem, smem] + [anywhere] * 6,
-        out_specs=[anywhere] * (3 + 2 * half),
+        out_specs=[vmem, anywhere, anywhere] + [vmem] * (2 * half),
         out_shape=[
             jax.ShapeDtypeStruct((orb, groups, padded, grid), BF16),
             jax.ShapeDtypeStruct((groups, box, box, grid), F32),
@@ -487,19 +481,16 @@
             *[edge] * half,
         ],
         scratch_shapes=[
-            pltpu.VMEM((count, orbitals.shape[1]), BF16),
+            pltpu.VMEM(coefs.shape, BF16),
             *[pltpu.VMEM(t.shape, t.dtype) for t in tables],
+            pltpu.VMEM((plan.rows, grid), F32),
             pltpu.VMEM((plan.rows, grid), F32),
             pltpu.VMEM((grid, box * box), F32),
             pltpu.VMEM((box, box, grid), F32),
-            pltpu.VMEM((orb, padded, grid), BF16),
             pltpu.VMEM((half, plan.ky_block, slots, plan.doubled), F32),
             pltpu.VMEM((half, slots, plan.doubled), F32),
-            pltpu.VMEM((half, plan.ky_block, slots, grid), F32),
-            pltpu.VMEM((half, slots, grid), F32),
             dma((2 * half,)),
-            dma((2 * half,)),
-            dma((12,)),
+            dma((7,)),
         ],
         compiler_params=pltpu.CompilerParams(vmem_limit_bytes=LARGE),
         name="density",
@@ -514,9 +505,22 @@
     pieces[:half] = [p.reshape(plan.ky_block * slots, grid) for p in pieces[:half]]
 
     small = pltpu.CompilerParams(vmem_limit_bytes=SMALL)
+    span = SUB * box
+    shapes = [(plan.doubled, 2 * grid), (2 * grid, plan.doubled), (grid, 3 * plan.doubled), (3 * plan.doubled, grid)]
+    shapes += [(span, 3 * span), (span, 3 * span), (grid, 3 * grid), (groups, grid, 2 * plan.rows)]
+    tables = pl.pallas_call(
+        functools.partial(tables_kernel, plan),
+        in_specs=[smem, anywhere, anywhere],
+        out_specs=[vmem] * (len(shapes) + 1),
+        out_shape=[*[jax.ShapeDtypeStruct(shape, BF16) for shape in shapes], jax.ShapeDtypeStruct(pieces[0].shape, F32)],
+        scratch_shapes=[pltpu.VMEM(wave.shape, F32), dma((2,))],
+        compiler_params=small,
+        name="tables",
+    )(where, wave, pieces[0])
+    pieces[0] = tables[8]
     send = pl.pallas_call(
         functools.partial(solve_kernel, plan),
-        in_specs=[smem] + [vmem] * (1 + 2 * half),
+        in_specs=[smem] + [vmem] * (5 + 2 * half),
         out_specs=vmem,
         out_shape=jax.ShapeDtypeStruct((orb * groups, area, grid), BF16),
         scratch_shapes=[
@@ -528,7 +532,7 @@
         ],
         compiler_params=small,
         name="solve",
-    )(where, received, *pieces)
+    )(where, received, *pieces, *tables[:4])
     send = send.reshape(orb, groups, area, grid)
     received = lax.all_to_all(send, "orb", split_axis=0, concat_axis=0, tiled=True)
     part = plan.box_part * count
@@ -539,7 +543,10 @@
             smem,
             pl.BlockSpec((orb, 1, area, grid), lambda g: (0, g, 0, 0)),
             anywhere,
-            pl.BlockSpec((1, plan.rows, grid), lambda g: (g, 0, 0)),
+            pl.BlockSpec((1, grid, 2 * plan.rows), lambda g: (g, 0, 0)),
+            vmem,
+            vmem,
+            vmem,
         ],
         out_specs=[pl.BlockSpec((1, part, box * box), lambda g: (g, 0, 0))] * pln,
         out_shape=[jax.ShapeDtypeStruct((groups, part, box * box), BF16 if step else F32) for step in range(pln)],
@@ -551,7 +558,7 @@
         ],
         compiler_params=small,
         name="terms",
-    )(where, received, psi, wave)
+    )(where, received, psi, tables[7], *tables[4:7])
     finished = list(finished)
     for step in range(1, pln):
         finished[step] = lax.ppermute(finished[step], "pln", [(p, (p + step) % pln) for p in range(pln)])

time: 54.4 us -> 52 us (0.956)
  waiting for transfers between devices: 6.69 us -> 3.89 us
  starting transfers between devices: 17.9 us -> 16.5 us
  blocking collectives: 12.5 us -> 13.7 us
  local copies, waits for them, and re-layouts: 0.96 us -> 1.7 us
    pallas_call x1 -> x2, Pallas kernels: 5.44 us -> 7.24 us  [the longest x1 5.66 us: per_device(): pl.pallas_call(functools.partial(density_kernel, plan), in_specs=[smem, s...]
    ppermute x2, waiting for transfers between devices: 1.52 us -> 0.01 us  [per_device(): lax.ppermute(pieces[half + step], 'pln', [(0, half + step), (half, step)])]
    ppermute x3, starting transfers between devices: 5.27 us -> 3.87 us  [per_device(): lax.ppermute(finished[step], 'pln', [(p, (p + step) % pln) for p in range...]
    pallas_call x1, Pallas kernels: 7.32 us -> 6.02 us  [per_device(): pl.pallas_call(functools.partial(solve_kernel, plan), in_specs=[smem] + [...]
    all_to_all x1, blocking collectives: 12.5 us -> 13.7 us  [per_device(): lax.all_to_all(send, 'orb', split_axis=0, concat_axis=0, tiled=True)]
    all_to_all x1, waiting for transfers between devices: 1.08 us -> 0.01 us  [per_device(): lax.all_to_all(send, 'orb', split_axis=0, concat_axis=0, tiled=True)]
    unnamed x6, local copies, waits for them, and re-layouts: 0.96 us -> 1.7 us
    pallas_call x1, Pallas kernels: 2.44 us -> 1.85 us  [per_device(): pl.pallas_call(functools.partial(terms_kernel, plan), grid=(groups,), in_...]
  transfers between devices with their start and end apart: 7 -> 7, of which waited for: 7 -> 2; matrix products, arithmetic and copies ran while one was open for 0% -> 0% of each run, Pallas kernels for 0% -> 3%
where the time goes in v5:
time: 52 us; the launch traced here: 51.6 us
  starting transfers between devices  16.5 us (32%)
  Pallas kernels  15.8 us (30%)
  blocking collectives  13.7 us (26%)
  waiting for transfers between devices  3.89 us (7%)
  local copies, waits for them, and re-layouts  1.7 us (3%)
    all_to_all x1, blocking collectives, per_device(): lax.all_to_all(send, 'orb', split_axis=0, concat_axis=0, tiled=True)  13.7 us
    pallas_call x1, Pallas kernels, per_device(): pl.pallas_call(functools.partial(solve_kernel, plan), in_specs=[smem] + [...  6.02 us
    ppermute x2, starting transfers between devices, per_device(): lax.ppermute(pieces[half + step], 'pln', [(0, half + step), (half, step)])  5.77 us
    pallas_call x1, Pallas kernels, per_device(): pl.pallas_call(functools.partial(density_kernel, plan), in_specs=[smem, s...  5.66 us
    all_to_all x1, starting transfers between devices, per_device(): lax.all_to_all(send, 'orb', split_axis=0, concat_axis=0, tiled=True)  5.18 us
    ppermute x3, waiting for transfers between devices, per_device(): lax.ppermute(finished[step], 'pln', [(p, (p + step) % pln) for p in range...  3.88 us
    ppermute x3, starting transfers between devices, per_device(): lax.ppermute(finished[step], 'pln', [(p, (p + step) % pln) for p in range...  3.87 us
    pallas_call x1, Pallas kernels, per_device(): pl.pallas_call(functools.partial(terms_kernel, plan), grid=(groups,), in_...  1.85 us
  transfers between devices with their start and end apart: 7, of which 2 were waited for; matrix products, arithmetic and copies ran while one was open for 0% of the time, Pallas kernels for 3%

profile of v5, /device:TPU:0, one launch (start us, length us, event | category | flops | bytes accessed | tf_op | source)
XLA Modules:
  0.0 51.6 jit_solution(12162372190426713079)
XLA Ops:
  0.0 5.7 %density.1 = (bf16[8,1,272,128]{3,2,1,0:T(8,128)(2,1)}, f32[1,32,32,128]{3,2,1,0:T(8,128)}, f32[1,64,128]{2,1,0:T(8,128)}, f32[64,8,128]{2,1,0:T(8,128)}, f32[64...) custom-call(s32[1]{0:T(128)} %bitcast.where_ref, s32[4,3]{1,0:T(4,128)} %corner_ref.1, f32[4]{0:T(128)} %weight_ref.1, ...), custom_call_target="tpu_custom_call" | custom-call | tf_op jit(solution)/shard_map/density/pallas_call | solution.py:472
  5.7 5.2 %all-to-all-start = ((bf16[8,1,272,128]{3,2,1,0:T(8,128)(2,1)}), bf16[8,1,272,128]{3,2,1,0:T(8,128)(2,1)S(1)}, u32[]{:S(2)}, u32[]{:S(2)}) async-start(bf16[8,1,272,128]{3,2,1,0:T(8,128)(2,1)} %get-tuple-element.25), calls=%async_computation | async-start | bytes 1114112 | tf_op jit(solution)/shard_map/all_to_all | solution.py:498
  10.9 1.6 %collective-permute-start = (f32[64,8,128]{2,1,0:T(8,128)}, f32[64,8,128]{2,1,0:T(8,128)S(1)}, u32[]{:S(2)}, u32[]{:S(2)}) collective-permute-start(f32[64,8,128]{2,1,0:T(8,128)} %get-tuple-element.29), channel_id=1, source_target_pairs={{0,1},{1,0},{2,3},{3,2},{4,5},{5,4},{6,7},{7,6},{8,9},{9,8},{10,11... | collective-permute-start | bytes 786440 | tf_op jit(solution)/shard_map/ppermute | solution.py:502
  12.5 4.5 %collective-permute-start.1 = (f32[1,8,128]{2,1,0:T(8,128)}, f32[1,8,128]{2,1,0:T(8,128)S(1)}, u32[]{:S(2)}, u32[]{:S(2)}) collective-permute-start(f32[1,8,128]{2,1,0:T(8,128)} %get-tuple-element.30), channel_id=1, source_target_pairs={{0,2},{2,0},{4,6},{6,4},{8,10},{10,8},{12,14},{14,12},{16,18},{18,... | collective-permute-start | bytes 12296 | tf_op jit(solution)/shard_map/ppermute | solution.py:504
  17.0 1.3 %collective-permute-start.2 = (f32[1,8,128]{2,1,0:T(8,128)}, f32[1,8,128]{2,1,0:T(8,128)S(1)}, u32[]{:S(2)}, u32[]{:S(2)}) collective-permute-start(f32[1,8,128]{2,1,0:T(8,128)} %get-tuple-element.31), channel_id=1, source_target_pairs={{0,3},{2,1},{4,7},{6,5},{8,11},{10,9},{12,15},{14,13},{16,19},{18,... | collective-permute-start | bytes 12296 | tf_op jit(solution)/shard_map/ppermute | solution.py:504
  18.3 0.0 copy-start.1
  18.3 0.9 %copy-done.1 = f32[64,8,128]{2,1,0:T(8,128)S(1)} copy-done((f32[64,8,128]{2,1,0:T(8,128)S(1)}, f32[64,8,128]{2,1,0:T(8,128)}, u32[]{:S(2)}) %copy-start.1) | copy-done | bytes 262168
  19.2 0.8 %copy-done.2 = f32[1,64,128]{2,1,0:T(8,128)S(1)} copy-done((f32[1,64,128]{2,1,0:T(8,128)S(1)}, f32[1,64,128]{2,1,0:T(8,128)}, u32[]{:S(2)}) %copy-start.2) | copy-done | bytes 32792
  20.0 1.6 %tables.1 = (bf16[256,256]{1,0:T(8,128)(2,1)S(1)}, bf16[256,256]{1,0:T(8,128)(2,1)S(1)}, bf16[128,768]{1,0:T(8,128)(2,1)S(1)}, bf16[768,128]{1,0:T(8,128)(2,1)S(...) custom-call(s32[1]{0:T(128)} %bitcast.where_ref, ...), custom_call_target="tpu_custom_call" | custom-call | tf_op jit(solution)/shard_map/tables/pallas_call | solution.py:511
  21.6 0.0 collective-permute-done.1.refs_2_
  21.6 0.0 collective-permute-done.2.refs_3_
  21.6 0.0 collective-permute-done
  21.6 0.0 all-to-all-done
  21.6 6.0 %solve.1 = bf16[8,256,128]{2,1,0:T(8,128)(2,1)S(1)} custom-call(s32[1]{0:T(128)} %bitcast.where_ref, bf16[8,272,128]{2,1,0:T(8,128)(2,1)S(1)} %bitcast.8, f32[512,128]{1,0:T(8,128)S(1)} %get-tuple-element.28.refs_0_, f32[512,128]{1,0:T(8,128)S(1)} %bitcast.10, f32[1,8,128]{2,1,0:T(8,128)S(1)} %collective-permute-done.1.refs_2_, ...), custom_call_target="tpu_custom_call" | custom-call | tf_op jit(solution)/shard_map/solve/pallas_call | solution.py:521
  27.7 13.7 %all_to_all.10.recv_ref = bf16[8,1,256,128]{3,2,1,0:T(8,128)(2,1)S(1)} all-to-all(bf16[8,1,256,128]{3,2,1,0:T(8,128)(2,1)S(1)} %bitcast.9), channel_id=1, replica_groups=mesh['orb'=8,'pln'=4] {'orb'}, dimensions={0} | all-to-all | bytes 1048576 | tf_op jit(solution)/shard_map/all_to_all | solution.py:537
  41.3 0.0 copy-done
  41.3 1.8 %terms.1 = (f32[1,32,1024]{2,1,0:T(8,128)S(1)}, bf16[1,32,1024]{2,1,0:T(8,128)(2,1)S(1)}, bf16[1,32,1024]{2,1,0:T(8,128)(2,1)S(1)}, bf16[1,32,1024]{2,1,0:T(8,128)(2,1)S(1)}) custom-call(s32[1]{0:T(128)} %bitcast.where_ref, bf16[8,1,256,128]{3,2,1,0:T(8,128)(2,1)S(1)} %all_to_all.10.recv_ref, f32[1,32,32,128]{3,2,1,0:T(8,128)S(1)} %copy-done, ...), custom_call_target="tpu_custom_call" | custom-call | tf_op jit(solution)/shard_map/terms/pallas_call | solution.py:539
  43.2 0.1 collective-permute-start.3
  43.2 2.8 %collective-permute-start.4 = (bf16[1,32,1024]{2,1,0:T(8,128)(2,1)S(1)}, bf16[1,32,1024]{2,1,0:T(8,128)(2,1)S(1)}, u32[]{:S(2)}, u32[]{:S(2)}) collective-permute-start(bf16[1,32,1024]{2,1,0:T(8,128)(2,1)S(1)} %get-tuple-element.43), channel_id=1, source_target_pairs={{0,2},{1,3},{2,0},{3,1},{4,6},{5,7},{6,4},{7,5},{8,10},{9,11},{10,... | collective-permute-start | bytes 196616 | tf_op jit(solution)/shard_map/ppermute | solution.py:564
  46.0 1.0 %collective-permute-start.5 = (bf16[1,32,1024]{2,1,0:T(8,128)(2,1)S(1)}, bf16[1,32,1024]{2,1,0:T(8,128)(2,1)S(1)}, u32[]{:S(2)}, u32[]{:S(2)}) collective-permute-start(bf16[1,32,1024]{2,1,0:T(8,128)(2,1)S(1)} %get-tuple-element.44), channel_id=1, source_target_pairs={{0,3},{1,0},{2,1},{3,2},{4,7},{5,4},{6,5},{7,6},{8,11},{9,8},{10,9... | collective-permute-start | bytes 196616 | tf_op jit(solution)/shard_map/ppermute | solution.py:564
  47.0 2.5 %collective-permute-done.3.refs_1_ = bf16[1,32,1024]{2,1,0:T(8,128)(2,1)S(1)} collective-permute-done((bf16[1,32,1024]{2,1,0:T(8,128)(2,1)S(1)}, bf16[1,32,1024]{2,1,0:T(8,128)(2,1)S(1)}, u32[]{:S(2)}, u32[]{:S(2)}) %collective-permute-start.3) | collective-permute-done | bytes 65568 | tf_op jit(solution)/shard_map/ppermute | solution.py:564
  49.6 1.3 %collective-permute-done.4.refs_2_ = bf16[1,32,1024]{2,1,0:T(8,128)(2,1)S(1)} collective-permute-done((bf16[1,32,1024]{2,1,0:T(8,128)(2,1)S(1)}, bf16[1,32,1024]{2,1,0:T(8,128)(2,1)S(1)}, u32[]{:S(2)}, u32[]{:S(2)}) %collective-permute-start.4) | collective-permute-done | bytes 65568 | tf_op jit(solution)/shard_map/ppermute | solution.py:564
  50.9 0.0 collective-permute-done.5.refs_3_
  50.9 0.7 %sum.1 = bf16[1,4,8192]{2,1,0:T(4,128)(2,1)} custom-call(f32[1,32,1024]{2,1,0:T(8,128)S(1)} %get-tuple-element.41.refs_0_, bf16[1,32,1024]{2,1,0:T(8,128)(2,1)S(1)} %collective-permute-done.3.refs_1_, bf16[1,32,1024]{2,1,0:T(8,128)(2,1)S(1)} %collective-permute-done.4.refs_2_, bf16[1,32,1024]{2,1,0:T(8,128)(2,1)S(1)} %collective-permute-done.5.refs_3_), custom_call_target="tpu_custom_call" | custom-call | tf_op jit(solution)/shard_map/sum/pallas_call | solution.py:566
  (2 shorter events, 0.0 us)
Async XLA Ops:
  5.7 15.9 %all-to-all-start = ((bf16[8,1,272,128]{3,2,1,0:T(8,128)(2,1)}), bf16[8,1,272,128]{3,2,1,0:T(8,128)(2,1)S(1)}, u32[]{:S(2)}, u32[]{:S(2)}) async-start(bf16[8,1,272,128]{3,2,1,0:T(8,128)(2,1)} %get-tuple-element.25), calls=%async_computation | async-start | bytes 1114112 | tf_op jit(solution)/shard_map/all_to_all | solution.py:498
  10.8 30.5 %copy-start = (f32[1,32,32,128]{3,2,1,0:T(8,128)S(1)}, f32[1,32,32,128]{3,2,1,0:T(8,128)}, u32[]{:S(2)}) copy-start(f32[1,32,32,128]{3,2,1,0:T(8,128)} %get-tuple-element.36.psi_any) | copy-start | bytes 1572868
  10.9 10.8 %collective-permute-start = (f32[64,8,128]{2,1,0:T(8,128)}, f32[64,8,128]{2,1,0:T(8,128)S(1)}, u32[]{:S(2)}, u32[]{:S(2)}) collective-permute-start(f32[64,8,128]{2,1,0:T(8,128)} %get-tuple-element.29), channel_id=1, source_target_pairs={{0,1},{1,0},{2,3},{3,2},{4,5},{5,4},{6,7},{7,6},{8,9},{9,8},{10,11... | collective-permute-start | bytes 786440 | tf_op jit(solution)/shard_map/ppermute | solution.py:502
  12.5 9.1 %collective-permute-start.1 = (f32[1,8,128]{2,1,0:T(8,128)}, f32[1,8,128]{2,1,0:T(8,128)S(1)}, u32[]{:S(2)}, u32[]{:S(2)}) collective-permute-start(f32[1,8,128]{2,1,0:T(8,128)} %get-tuple-element.30), channel_id=1, source_target_pairs={{0,2},{2,0},{4,6},{6,4},{8,10},{10,8},{12,14},{14,12},{16,18},{18,... | collective-permute-start | bytes 12296 | tf_op jit(solution)/shard_map/ppermute | solution.py:504
  17.0 4.6 %collective-permute-start.2 = (f32[1,8,128]{2,1,0:T(8,128)}, f32[1,8,128]{2,1,0:T(8,128)S(1)}, u32[]{:S(2)}, u32[]{:S(2)}) collective-permute-start(f32[1,8,128]{2,1,0:T(8,128)} %get-tuple-element.31), channel_id=1, source_target_pairs={{0,3},{2,1},{4,7},{6,5},{8,11},{10,9},{12,15},{14,13},{16,19},{18,... | collective-permute-start | bytes 12296 | tf_op jit(solution)/shard_map/ppermute | solution.py:504
  18.3 1.0 %copy-start.1 = (f32[64,8,128]{2,1,0:T(8,128)S(1)}, f32[64,8,128]{2,1,0:T(8,128)}, u32[]{:S(2)}) copy-start(f32[64,8,128]{2,1,0:T(8,128)} %get-tuple-element.27) | copy-start | bytes 786436
  19.2 0.8 %copy-start.2 = (f32[1,64,128]{2,1,0:T(8,128)S(1)}, f32[1,64,128]{2,1,0:T(8,128)}, u32[]{:S(2)}) copy-start(f32[1,64,128]{2,1,0:T(8,128)} %get-tuple-element.26.wave_any) | copy-start | bytes 98308
  43.2 6.4 %collective-permute-start.3 = (bf16[1,32,1024]{2,1,0:T(8,128)(2,1)S(1)}, bf16[1,32,1024]{2,1,0:T(8,128)(2,1)S(1)}, u32[]{:S(2)}, u32[]{:S(2)}) collective-permute-start(bf16[1,32,1024]{2,1,0:T(8,128)(2,1)S(1)} %get-tuple-element.42), channel_id=1, source_target_pairs={{0,1},{1,2},{2,3},{3,0},{4,5},{5,6},{6,7},{7,4},{8,9},{9,10},{10,1... | collective-permute-start | bytes 196616 | tf_op jit(solution)/shard_map/ppermute | solution.py:564
  43.2 7.7 %collective-permute-start.4 = (bf16[1,32,1024]{2,1,0:T(8,128)(2,1)S(1)}, bf16[1,32,1024]{2,1,0:T(8,128)(2,1)S(1)}, u32[]{:S(2)}, u32[]{:S(2)}) collective-permute-start(bf16[1,32,1024]{2,1,0:T(8,128)(2,1)S(1)} %get-tuple-element.43), channel_id=1, source_target_pairs={{0,2},{1,3},{2,0},{3,1},{4,6},{5,7},{6,4},{7,5},{8,10},{9,11},{10,... | collective-permute-start | bytes 196616 | tf_op jit(solution)/shard_map/ppermute | solution.py:564
  46.0 4.9 %collective-permute-start.5 = (bf16[1,32,1024]{2,1,0:T(8,128)(2,1)S(1)}, bf16[1,32,1024]{2,1,0:T(8,128)(2,1)S(1)}, u32[]{:S(2)}, u32[]{:S(2)}) collective-permute-start(bf16[1,32,1024]{2,1,0:T(8,128)(2,1)S(1)} %get-tuple-element.44), channel_id=1, source_target_pairs={{0,3},{1,0},{2,1},{3,2},{4,7},{5,4},{6,5},{7,6},{8,11},{9,8},{10,9... | collective-permute-start | bytes 196616 | tf_op jit(solution)/shard_map/ppermute | solution.py:564

commit v6 on v5

--- a/solution.py
+++ b/solution.py
@@ -218,15 +218,16 @@
 
 def density_kernel(
     plan, where_ref, corner_ref, weight_ref, coef_any, depth_any, inner_any, outer_any, wave_any, spectrum_any,
-    send_ref, psi_any, wave_out_any, *refs,
+    send_any, psi_any, wave_out_any, *refs,
 ):
-    piece_refs = refs[: 2 * plan.half]
-    coef_ref, depth_ref, inner_ref, outer_ref, wave_ref, own_wave_ref, stage_ref, psi_ref = refs[2 * plan.half : -4]
-    block_ref, edge_ref, spectrum_sems, sems = refs[-4:]
+    half = plan.half
+    piece_anys = refs[: 2 * half]
+    coef_ref, depth_ref, inner_ref, outer_ref, wave_ref, own_wave_ref, stage_ref, psi_ref, send_ref = refs[2 * half : -7]
+    block_ref, edge_ref, block_out_ref, edge_out_ref, spectrum_sems, out_sems, sems = refs[-7:]
     box, grid, count, slots = plan.box, plan.grid, plan.per_group, plan.slots
     section = box * box
     span = SUB * box
-    me = where_ref[0]
+    me = lax.rem(where_ref[0], plan.pln)
     coef_copy = pltpu.make_async_copy(coef_any, coef_ref, sems.at[0])
     coef_copy.start()
     fetched = start_copies(
@@ -265,12 +266,15 @@
         own_wave_ref[...] = wave
         sent += start_copies(sems, 6, (own_wave_ref, wave_out_any.at[group]))
         for o in range(plan.orb):
-            send_ref[o, group, plan.area :, :] = corner.astype(send_ref.dtype)
+            send_ref[o, plan.area :, :] = corner.astype(send_ref.dtype)
         high, low = split(wave)
         wave_terms = jnp.concatenate([high, low, high], axis=1)
         if group == 0:
             wait_copies(spectrum)
-            fold_spectrum(plan, piece_refs, block_ref, edge_ref)
+            folded = fold_spectrum(plan, piece_anys, block_ref, edge_ref, block_out_ref, edge_out_ref, out_sems)
+        rows = pl.ds(plan.area, 2 * SUB)
+        sent += start_copies(sems, 7, (send_ref.at[:, rows, :], send_any.at[:, group, rows, :]))
+        per_part = plan.quarter // 2
         for pair in range(box // 2):
             columns = []
             for b in (2 * pair, 2 * pair + 1):
@@ -281,8 +285,13 @@
             for o in range(plan.orb):
                 mine = out[slots * o : slots * (o + 1)]
                 tile = jnp.concatenate([mine[:, :grid], mine[:, grid:]], axis=0)
-                send_ref[o, group, 2 * slots * pair : 2 * slots * (pair + 1), :] = tile.astype(send_ref.dtype)
+                send_ref[o, 2 * slots * pair : 2 * slots * (pair + 1), :] = tile.astype(send_ref.dtype)
+            if pair % per_part == per_part - 1:
+                part = pair // per_part
+                rows = pl.ds(plan.quarter * slots * part, plan.quarter * slots)
+                sent += start_copies(sems, 8 + part, (send_ref.at[:, rows, :], send_any.at[:, group, rows, :]))
         wait_copies(sent)
+    wait_copies(folded)
 
 
 def spectrum_copies(plan, me, spectrum_any, block_ref, edge_ref, sems):
@@ -303,7 +312,7 @@
     return copies
 
 
-def fold_spectrum(plan, piece_refs, block_ref, edge_ref):
+def fold_spectrum(plan, piece_anys, block_ref, edge_ref, block_out_ref, edge_out_ref, sems):
     half, grid = plan.half, plan.grid
     odd = (iota((1, 1, grid), 2) & 1) == 1
 
@@ -312,15 +321,18 @@
         return values[..., :grid] + jnp.where(odd, last, -last)
 
     for step in range(half):
-        piece_refs[step][...] = fold(block_ref[step])
-        piece_refs[half + step][...] = fold(edge_ref[pl.ds(step, 1)])
-
-
-def tables_kernel(plan, where_ref, wave_any, piece_any, *refs):
+        block_out_ref[step] = fold(block_ref[step])
+    edge_out_ref[...] = fold(edge_ref[...])
+    pairs = [(block_out_ref.at[step], piece_anys[step]) for step in range(half)]
+    pairs += [(edge_out_ref.at[pl.ds(step, 1)], piece_anys[half + step]) for step in range(half)]
+    return start_copies(sems, 0, *pairs)
+
+
+def tables_kernel(plan, where_ref, piece_any, *refs):
     forward_y_ref, forward_z_ref, inverse_y_ref, inverse_z_ref, inner_ref, outer_ref, back_ref = refs[:7]
-    wave_out_ref, piece_ref, wave_ref, sems = refs[7:]
-    grid, doubled, me = plan.grid, plan.doubled, where_ref[0]
-    copies = start_copies(sems, 0, (wave_any, wave_ref), (piece_any, piece_ref))
+    piece_ref, sems = refs[7:]
+    grid, doubled, me = plan.grid, plan.doubled, lax.rem(where_ref[0], plan.pln)
+    copies = start_copies(sems, 0, (piece_any, piece_ref))
     forward, _ = mode_table(plan, me, (doubled, grid), 0)
     forward_y_ref[...] = jnp.concatenate(split(forward), axis=1)
     forward_z_ref[...] = jnp.concatenate(split(depth_mode_table(plan, (grid, doubled), 1)), axis=0)
@@ -331,16 +343,15 @@
     outer_ref[...] = stack_terms(outer_back_table(plan.box), 1)
     back_ref[...] = stack_terms(depth_back_table(plan), 1)
     wait_copies(copies)
-    for group in range(plan.groups):
-        wave_out_ref[group] = jnp.concatenate(split(wave_ref[group].T), axis=1)
 
 
 def solve_kernel(plan, where_ref, recv_ref, *refs):
     half, slots, grid, box, count = plan.half, plan.slots, plan.grid, plan.box, plan.per_group
     piece_refs, edge_refs = refs[:half], refs[half : 2 * half]
     forward_y_ref, forward_z_ref, inverse_y_ref, inverse_z_ref = refs[2 * half : 2 * half + 4]
-    send_ref, field_ref, result_ref, table_ref, corner_ref, sem = refs[2 * half + 4 :]
-    me = where_ref[0]
+    send_refs = refs[2 * half + 4 : 2 * half + 4 + plan.orb]
+    field_ref, result_ref, table_ref, corner_ref, sem = refs[2 * half + 4 + plan.orb :]
+    me, own = lax.rem(where_ref[0], plan.pln), where_ref[0] // plan.pln
     depth = plan.area
     all_groups = plan.orb * plan.groups
     owner = lane_owner((1, grid), box)
@@ -389,30 +400,40 @@
         for side, s in enumerate(both):
             result_ref[pl.ds(s, grid, stride=slots), :] = planes[:, grid * side : grid * (side + 1)]
 
-    def cut(group, carry):
+    def cut(d, group, carry):
+        number = (own ^ d) * plan.groups + group
         values = jnp.zeros((depth, grid), F32)
         for n in range(count):
-            shift = lax.rem(box * n - corner_ref[2 * group, box * n] + grid, grid)
-            rows = result_ref[pl.ds(start(group, n), depth), :]
+            shift = lax.rem(box * n - corner_ref[2 * number, box * n] + grid, grid)
+            rows = result_ref[pl.ds(start(number, n), depth), :]
             values = jnp.where(owner == n, pltpu.roll(rows, shift, 1), values)
-        send_ref[group] = values.astype(send_ref.dtype)
+        send_refs[d][group] = values.astype(BF16)
         return carry
 
-    lax.fori_loop(0, all_groups, cut, 0)
-
-
-def terms_kernel(plan, where_ref, recv_ref, psi_any, wave_ref, inner_ref, outer_ref, back_ref, *refs):
+    for d in range(plan.orb):
+        if plan.groups == 1:
+            cut(d, 0, 0)
+        else:
+            lax.fori_loop(0, plan.groups, functools.partial(cut, d), 0)
+
+
+def terms_kernel(plan, where_ref, *refs):
     box, grid, count, slots, pln = plan.box, plan.grid, plan.per_group, plan.slots, plan.pln
+    recv_refs = refs[: plan.orb]
+    psi_any, wave_ref, inner_ref, outer_ref, back_ref, *refs = refs[plan.orb :]
     out_refs = refs[:pln]
     psi_ref, stage_ref, own_ref, sem = refs[pln:]
     group = pl.program_id(0)
     copy = pltpu.make_async_copy(psi_any.at[group], psi_ref, sem)
     copy.start()
     owner = lane_owner((1, grid), box)
-    wave, inner, outer, back = wave_ref[0], inner_ref[...], outer_ref[...], back_ref[...]
+    own = where_ref[0] // pln
+    rows = [wave_ref[0, pl.ds(pl.multiple_of((own ^ d) * slots, SUB), slots), :] for d in range(plan.orb)]
+    wave = jnp.concatenate(split(jnp.concatenate(rows, axis=0).T), axis=1)
+    inner, outer, back = inner_ref[...], outer_ref[...], back_ref[...]
     copy.wait()
     for pair in range(box // 2):
-        tiles = [recv_ref[o, 0, 2 * slots * pair : 2 * slots * (pair + 1), :].astype(F32) for o in range(plan.orb)]
+        tiles = [ref[0, 2 * slots * pair : 2 * slots * (pair + 1), :].astype(F32) for ref in recv_refs]
         columns = [jnp.concatenate([t[slots * side : slots * (side + 1)] for t in tiles], axis=0) for side in range(2)]
         both = jnp.concatenate(columns, axis=1).astype(BF16)
         out = dot(wave, jnp.concatenate([both, both], axis=0))
@@ -436,7 +457,7 @@
     part = plan.box_part * count
     for p in range(pln):
         own_ref[p] = out[part * p : part * (p + 1)]
-    me = where_ref[0]
+    me = lax.rem(where_ref[0], pln)
     out_refs[0][0] = own_ref[me]
     for step in range(1, pln):
         out_refs[step][0] = own_ref[lax.rem(me + step, pln)].astype(BF16)
@@ -457,7 +478,7 @@
     orb, pln, half, slots = plan.orb, plan.pln, plan.half, plan.slots
     groups, count, box, grid = plan.groups, plan.per_group, plan.box, plan.grid
     plane_index = lax.axis_index("pln")
-    where = plane_index.astype(jnp.int32)[None]
+    where = (lax.axis_index("orb") * pln + plane_index).astype(jnp.int32)[None]
     smem = pl.BlockSpec(memory_space=pltpu.SMEM)
     anywhere = pl.BlockSpec(memory_space=pl.ANY)
     vmem = pl.BlockSpec(memory_space=pltpu.VMEM)
@@ -472,7 +493,7 @@
     send, psi, wave, *pieces = pl.pallas_call(
         functools.partial(density_kernel, plan),
         in_specs=[smem, smem, smem] + [anywhere] * 6,
-        out_specs=[vmem, anywhere, anywhere] + [vmem] * (2 * half),
+        out_specs=[anywhere] * (3 + 2 * half),
         out_shape=[
             jax.ShapeDtypeStruct((orb, groups, padded, grid), BF16),
             jax.ShapeDtypeStruct((groups, box, box, grid), F32),
@@ -487,10 +508,14 @@
             pltpu.VMEM((plan.rows, grid), F32),
             pltpu.VMEM((grid, box * box), F32),
             pltpu.VMEM((box, box, grid), F32),
+            pltpu.VMEM((orb, padded, grid), BF16),
             pltpu.VMEM((half, plan.ky_block, slots, plan.doubled), F32),
             pltpu.VMEM((half, slots, plan.doubled), F32),
+            pltpu.VMEM((half, plan.ky_block, slots, grid), F32),
+            pltpu.VMEM((half, slots, grid), F32),
             dma((2 * half,)),
-            dma((7,)),
+            dma((2 * half,)),
+            dma((12,)),
         ],
         compiler_params=pltpu.CompilerParams(vmem_limit_bytes=LARGE),
         name="density",
@@ -507,22 +532,22 @@
     small = pltpu.CompilerParams(vmem_limit_bytes=SMALL)
     span = SUB * box
     shapes = [(plan.doubled, 2 * grid), (2 * grid, plan.doubled), (grid, 3 * plan.doubled), (3 * plan.doubled, grid)]
-    shapes += [(span, 3 * span), (span, 3 * span), (grid, 3 * grid), (groups, grid, 2 * plan.rows)]
+    shapes += [(span, 3 * span), (span, 3 * span), (grid, 3 * grid)]
     tables = pl.pallas_call(
         functools.partial(tables_kernel, plan),
-        in_specs=[smem, anywhere, anywhere],
+        in_specs=[smem, anywhere],
         out_specs=[vmem] * (len(shapes) + 1),
         out_shape=[*[jax.ShapeDtypeStruct(shape, BF16) for shape in shapes], jax.ShapeDtypeStruct(pieces[0].shape, F32)],
-        scratch_shapes=[pltpu.VMEM(wave.shape, F32), dma((2,))],
+        scratch_shapes=[dma((1,))],
         compiler_params=small,
         name="tables",
-    )(where, wave, pieces[0])
-    pieces[0] = tables[8]
+    )(where, pieces[0])
+    pieces[0] = tables[7]
     send = pl.pallas_call(
         functools.partial(solve_kernel, plan),
         in_specs=[smem] + [vmem] * (5 + 2 * half),
-        out_specs=vmem,
-        out_shape=jax.ShapeDtypeStruct((orb * groups, area, grid), BF16),
+        out_specs=[vmem] * orb,
+        out_shape=[jax.ShapeDtypeStruct((groups, area, grid), BF16)] * orb,
         scratch_shapes=[
             pltpu.VMEM((grid * slots, grid), F32),
             pltpu.VMEM((grid * slots, grid), F32),
@@ -533,17 +558,18 @@
         compiler_params=small,
         name="solve",
     )(where, received, *pieces, *tables[:4])
-    send = send.reshape(orb, groups, area, grid)
-    received = lax.all_to_all(send, "orb", split_axis=0, concat_axis=0, tiled=True)
+    received = [send[0]] + [None] * (orb - 1)
+    for d in reversed(range(1, orb)):
+        received[d] = lax.ppermute(send[d], "orb", [(o, o ^ d) for o in range(orb)])
     part = plan.box_part * count
     finished = pl.pallas_call(
         functools.partial(terms_kernel, plan),
         grid=(groups,),
         in_specs=[
             smem,
-            pl.BlockSpec((orb, 1, area, grid), lambda g: (0, g, 0, 0)),
+            *[pl.BlockSpec((1, area, grid), lambda g: (g, 0, 0))] * orb,
             anywhere,
-            pl.BlockSpec((1, grid, 2 * plan.rows), lambda g: (g, 0, 0)),
+            pl.BlockSpec((1, plan.rows, grid), lambda g: (g, 0, 0)),
             vmem,
             vmem,
             vmem,
@@ -558,7 +584,7 @@
         ],
         compiler_params=small,
         name="terms",
-    )(where, received, psi, tables[7], *tables[4:7])
+    )(where, *received, psi, wave, *tables[4:7])
     finished = list(finished)
     for step in range(1, pln):
         finished[step] = lax.ppermute(finished[step], "pln", [(p, (p + step) % pln) for p in range(pln)])

time: 52 us -> 49.6 us (0.954)
  blocking collectives: 13.7 us -> 0 us
  starting transfers between devices: 16.5 us -> 23.7 us
  waiting for transfers between devices: 3.89 us -> 9.61 us
  Pallas kernels: 15.8 us -> 14.9 us
  local copies, waits for them, and re-layouts: 1.7 us -> 0.95 us
    all_to_all x1 -> x0, blocking collectives: 13.7 us -> none  [per_device(): lax.all_to_all(send, 'orb', split_axis=0, concat_axis=0, tiled=True)]
    ppermute x0 -> x7, starting transfers between devices: none -> 6.43 us  [per_device(): received[d] = lax.ppermute(send[d], 'orb', [(o, o ^ d) for o in range(orb)])]
    ppermute x0 -> x7, waiting for transfers between devices: none -> 4.74 us  [per_device(): received[d] = lax.ppermute(send[d], 'orb', [(o, o ^ d) for o in range(orb)])]
    unnamed x6, local copies, waits for them, and re-layouts: 1.7 us -> 0.95 us
    ppermute x3, starting transfers between devices: 3.87 us -> 4.58 us  [per_device(): lax.ppermute(finished[step], 'pln', [(p, (p + step) % pln) for p in range...]
    ppermute x3, waiting for transfers between devices: 3.88 us -> 4.52 us  [per_device(): lax.ppermute(finished[step], 'pln', [(p, (p + step) % pln) for p in range...]
  transfers between devices with their start and end apart: 7 -> 14, of which waited for: 2 -> 6; matrix products, arithmetic and copies ran while one was open for 0% -> 0% of each run, Pallas kernels for 3% -> 3%
where the time goes in v6:
time: 49.6 us; the launch traced here: 49.3 us
  starting transfers between devices  23.7 us (48%)
  Pallas kernels  14.9 us (30%)
  waiting for transfers between devices  9.61 us (19%)
  local copies, waits for them, and re-layouts  0.95 us (2%)
    ppermute x7, starting transfers between devices, per_device(): received[d] = lax.ppermute(send[d], 'orb', [(o, o ^ d) for o in range(orb)])  6.43 us
    ppermute x2, starting transfers between devices, per_device(): lax.ppermute(pieces[half + step], 'pln', [(0, half + step), (half, step)])  5.78 us
    pallas_call x1, Pallas kernels, per_device(): pl.pallas_call(functools.partial(solve_kernel, plan), in_specs=[smem] + [...  5.52 us
    pallas_call x1, Pallas kernels, per_device(): pl.pallas_call(functools.partial(density_kernel, plan), in_specs=[smem, s...  5.36 us
    all_to_all x1, starting transfers between devices, per_device(): lax.all_to_all(send, 'orb', split_axis=0, concat_axis=0, tiled=True)  5.31 us
    ppermute x7, waiting for transfers between devices, per_device(): received[d] = lax.ppermute(send[d], 'orb', [(o, o ^ d) for o in range(orb)])  4.74 us
    ppermute x3, starting transfers between devices, per_device(): lax.ppermute(finished[step], 'pln', [(p, (p + step) % pln) for p in range...  4.58 us
    ppermute x3, waiting for transfers between devices, per_device(): lax.ppermute(finished[step], 'pln', [(p, (p + step) % pln) for p in range...  4.52 us
  transfers between devices with their start and end apart: 14, of which 6 were waited for; matrix products, arithmetic and copies ran while one was open for 0% of the time, Pallas kernels for 3%

profile of v6, /device:TPU:0, one launch (start us, length us, event | category | flops | bytes accessed | tf_op | source)
XLA Modules:
  0.0 49.3 jit_solution(14885367954671270751)
XLA Ops:
  0.0 5.4 %density.1 = (bf16[8,1,272,128]{3,2,1,0:T(8,128)(2,1)}, f32[1,32,32,128]{3,2,1,0:T(8,128)}, f32[1,64,128]{2,1,0:T(8,128)}, f32[64,8,128]{2,1,0:T(8,128)}, f32[64...) custom-call(s32[1]{0:T(128)} %bitcast.where_ref, s32[4,3]{1,0:T(4,128)} %corner_ref.1, f32[4]{0:T(128)} %weight_ref.1, ...), custom_call_target="tpu_custom_call" | custom-call | tf_op jit(solution)/shard_map/density/pallas_call | solution.py:493
  5.4 5.3 %all-to-all-start = ((bf16[8,1,272,128]{3,2,1,0:T(8,128)(2,1)}), bf16[8,1,272,128]{3,2,1,0:T(8,128)(2,1)S(1)}, u32[]{:S(2)}, u32[]{:S(2)}) async-start(bf16[8,1,272,128]{3,2,1,0:T(8,128)(2,1)} %get-tuple-element.32), calls=%async_computation | async-start | bytes 1114112 | tf_op jit(solution)/shard_map/all_to_all | solution.py:523
  10.7 1.6 %collective-permute-start = (f32[64,8,128]{2,1,0:T(8,128)}, f32[64,8,128]{2,1,0:T(8,128)S(1)}, u32[]{:S(2)}, u32[]{:S(2)}) collective-permute-start(f32[64,8,128]{2,1,0:T(8,128)} %get-tuple-element.35), channel_id=1, source_target_pairs={{0,1},{1,0},{2,3},{3,2},{4,5},{5,4},{6,7},{7,6},{8,9},{9,8},{10,11... | collective-permute-start | bytes 786440 | tf_op jit(solution)/shard_map/ppermute | solution.py:527
  12.3 4.5 %collective-permute-start.1 = (f32[1,8,128]{2,1,0:T(8,128)}, f32[1,8,128]{2,1,0:T(8,128)S(1)}, u32[]{:S(2)}, u32[]{:S(2)}) collective-permute-start(f32[1,8,128]{2,1,0:T(8,128)} %get-tuple-element.36), channel_id=1, source_target_pairs={{0,2},{2,0},{4,6},{6,4},{8,10},{10,8},{12,14},{14,12},{16,18},{18,... | collective-permute-start | bytes 12296 | tf_op jit(solution)/shard_map/ppermute | solution.py:529
  16.8 1.3 %collective-permute-start.2 = (f32[1,8,128]{2,1,0:T(8,128)}, f32[1,8,128]{2,1,0:T(8,128)S(1)}, u32[]{:S(2)}, u32[]{:S(2)}) collective-permute-start(f32[1,8,128]{2,1,0:T(8,128)} %get-tuple-element.37), channel_id=1, source_target_pairs={{0,3},{2,1},{4,7},{6,5},{8,11},{10,9},{12,15},{14,13},{16,19},{18,... | collective-permute-start | bytes 12296 | tf_op jit(solution)/shard_map/ppermute | solution.py:529
  18.1 0.9 %copy-done.1 = f32[64,8,128]{2,1,0:T(8,128)S(1)} copy-done((f32[64,8,128]{2,1,0:T(8,128)S(1)}, f32[64,8,128]{2,1,0:T(8,128)}, u32[]{:S(2)}) %copy-start.1) | copy-done | bytes 262168
  19.0 1.4 %tables.1 = (bf16[256,256]{1,0:T(8,128)(2,1)S(1)}, bf16[256,256]{1,0:T(8,128)(2,1)S(1)}, bf16[128,768]{1,0:T(8,128)(2,1)S(1)}, bf16[768,128]{1,0:T(8,128)(2,1)S(...) custom-call(s32[1]{0:T(128)} %bitcast.where_ref, ...), custom_call_target="tpu_custom_call" | custom-call | tf_op jit(solution)/shard_map/tables/pallas_call | solution.py:536
  20.5 0.3 all-to-all-done
  20.8 5.5 %solve.1 = (bf16[1,256,128]{2,1,0:T(8,128)(2,1)S(1)}, bf16[1,256,128]{2,1,0:T(8,128)(2,1)S(1)}, bf16[1,256,128]{2,1,0:T(8,128)(2,1)S(1)}, bf16[1,256,128]{2,1,0:...) custom-call(s32[1]{0:T(128)} %bitcast.where_ref, ...), custom_call_target="tpu_custom_call" | custom-call | tf_op jit(solution)/shard_map/solve/pallas_call | solution.py:546
  26.4 1.8 %collective-permute-start.4 = (bf16[1,256,128]{2,1,0:T(8,128)(2,1)S(1)}, bf16[1,256,128]{2,1,0:T(8,128)(2,1)S(1)}, u32[]{:S(2)}, u32[]{:S(2)}) collective-permute-start(bf16[1,256,128]{2,1,0:T(8,128)(2,1)S(1)} %get-tuple-element.44), channel_id=1, source_target_pairs={{0,8},{4,12},{8,0},{12,4},{16,24},{20,28},{24,16},{28,20},{1,9},{5... | collective-permute-start | bytes 196616 | tf_op jit(solution)/shard_map/ppermute | solution.py:563
  28.2 0.1 collective-permute-start.5
  28.3 1.7 %collective-permute-start.6 = (bf16[1,256,128]{2,1,0:T(8,128)(2,1)S(1)}, bf16[1,256,128]{2,1,0:T(8,128)(2,1)S(1)}, u32[]{:S(2)}, u32[]{:S(2)}) collective-permute-start(bf16[1,256,128]{2,1,0:T(8,128)(2,1)S(1)} %get-tuple-element.46), channel_id=1, source_target_pairs={{0,16},{4,20},{8,24},{12,28},{16,0},{20,4},{24,8},{28,12},{1,17},{... | collective-permute-start | bytes 196616 | tf_op jit(solution)/shard_map/ppermute | solution.py:563
  30.0 2.6 %collective-permute-start.8 = (bf16[1,256,128]{2,1,0:T(8,128)(2,1)S(1)}, bf16[1,256,128]{2,1,0:T(8,128)(2,1)S(1)}, u32[]{:S(2)}, u32[]{:S(2)}) collective-permute-start(bf16[1,256,128]{2,1,0:T(8,128)(2,1)S(1)} %get-tuple-element.48), channel_id=1, source_target_pairs={{0,24},{4,28},{8,16},{12,20},{16,8},{20,12},{24,0},{28,4},{1,25},{... | collective-permute-start | bytes 196616 | tf_op jit(solution)/shard_map/ppermute | solution.py:563
  32.6 0.2 collective-permute-start.9
  32.8 2.7 %collective-permute-done.7.refs_5_ = bf16[1,256,128]{2,1,0:T(8,128)(2,1)S(1)} collective-permute-done((bf16[1,256,128]{2,1,0:T(8,128)(2,1)S(1)}, bf16[1,256,128]{2,1,0:T(8,128)(2,1)S(1)}, u32[]{:S(2)}, u32[]{:S(2)}) %collective-permute-start.7) | collective-permute-done | bytes 65568 | tf_op jit(solution)/shard_map/ppermute | solution.py:563
  35.5 2.0 %collective-permute-done.9.refs_7_ = bf16[1,256,128]{2,1,0:T(8,128)(2,1)S(1)} collective-permute-done((bf16[1,256,128]{2,1,0:T(8,128)(2,1)S(1)}, bf16[1,256,128]{2,1,0:T(8,128)(2,1)S(1)}, u32[]{:S(2)}, u32[]{:S(2)}) %collective-permute-start.9) | collective-permute-done | bytes 65568 | tf_op jit(solution)/shard_map/ppermute | solution.py:563
  37.5 2.0 %terms.1 = (f32[1,32,1024]{2,1,0:T(8,128)S(1)}, bf16[1,32,1024]{2,1,0:T(8,128)(2,1)S(1)}, bf16[1,32,1024]{2,1,0:T(8,128)(2,1)S(1)}, bf16[1,32,1024]{2,1,0:T(8,128)(2,1)S(1)}) custom-call(s32[1]{0:T(128)} %bitcast.where_ref, bf16[1,256,128]{2,1,0:T(8,128)(2,1)S(1)} %get-tuple-element.42.refs_0_, bf16[1,256,128]{2,1,0:T(8,128)(2,1)S(1)} %collective-permute-done.3.refs_1_, ...), custom_call_target="tpu_custom_call" | custom-call | tf_op jit(solution)/shard_map/terms/pallas_call | solution.py:565
  39.5 0.6 %collective-permute-start.10 = (bf16[1,32,1024]{2,1,0:T(8,128)(2,1)S(1)}, bf16[1,32,1024]{2,1,0:T(8,128)(2,1)S(1)}, u32[]{:S(2)}, u32[]{:S(2)}) collective-permute-start(bf16[1,32,1024]{2,1,0:T(8,128)(2,1)S(1)} %get-tuple-element.56), channel_id=1, source_target_pairs={{0,1},{1,2},{2,3},{3,0},{4,5},{5,6},{6,7},{7,4},{8,9},{9,10},{10,1... | collective-permute-start | bytes 196616 | tf_op jit(solution)/shard_map/ppermute | solution.py:590
  40.1 3.2 %collective-permute-start.11 = (bf16[1,32,1024]{2,1,0:T(8,128)(2,1)S(1)}, bf16[1,32,1024]{2,1,0:T(8,128)(2,1)S(1)}, u32[]{:S(2)}, u32[]{:S(2)}) collective-permute-start(bf16[1,32,1024]{2,1,0:T(8,128)(2,1)S(1)} %get-tuple-element.57), channel_id=1, source_target_pairs={{0,2},{1,3},{2,0},{3,1},{4,6},{5,7},{6,4},{7,5},{8,10},{9,11},{10,... | collective-permute-start | bytes 196616 | tf_op jit(solution)/shard_map/ppermute | solution.py:590
  43.3 0.7 %collective-permute-start.12 = (bf16[1,32,1024]{2,1,0:T(8,128)(2,1)S(1)}, bf16[1,32,1024]{2,1,0:T(8,128)(2,1)S(1)}, u32[]{:S(2)}, u32[]{:S(2)}) collective-permute-start(bf16[1,32,1024]{2,1,0:T(8,128)(2,1)S(1)} %get-tuple-element.58), channel_id=1, source_target_pairs={{0,3},{1,0},{2,1},{3,2},{4,7},{5,4},{6,5},{7,6},{8,11},{9,8},{10,9... | collective-permute-start | bytes 196616 | tf_op jit(solution)/shard_map/ppermute | solution.py:590
  44.1 2.4 %collective-permute-done.10.refs_1_ = bf16[1,32,1024]{2,1,0:T(8,128)(2,1)S(1)} collective-permute-done((bf16[1,32,1024]{2,1,0:T(8,128)(2,1)S(1)}, bf16[1,32,1024]{2,1,0:T(8,128)(2,1)S(1)}, u32[]{:S(2)}, u32[]{:S(2)}) %collective-permute-start.10) | collective-permute-done | bytes 65568 | tf_op jit(solution)/shard_map/ppermute | solution.py:590
  46.4 2.0 %collective-permute-done.11.refs_2_ = bf16[1,32,1024]{2,1,0:T(8,128)(2,1)S(1)} collective-permute-done((bf16[1,32,1024]{2,1,0:T(8,128)(2,1)S(1)}, bf16[1,32,1024]{2,1,0:T(8,128)(2,1)S(1)}, u32[]{:S(2)}, u32[]{:S(2)}) %collective-permute-start.11) | collective-permute-done | bytes 65568 | tf_op jit(solution)/shard_map/ppermute | solution.py:590
  48.4 0.2 collective-permute-done.12.refs_3_
  48.6 0.7 %sum.1 = bf16[1,4,8192]{2,1,0:T(4,128)(2,1)} custom-call(f32[1,32,1024]{2,1,0:T(8,128)S(1)} %get-tuple-element.55.refs_0_, bf16[1,32,1024]{2,1,0:T(8,128)(2,1)S(1)} %collective-permute-done.10.refs_1_, bf16[1,32,1024]{2,1,0:T(8,128)(2,1)S(1)} %collective-permute-done.11.refs_2_, bf16[1,32,1024]{2,1,0:T(8,128)(2,1)S(1)} %collective-permute-done.12.refs_3_), custom_call_target="tpu_custom_call" | custom-call | tf_op jit(solution)/shard_map/sum/pallas_call | solution.py:592
  (15 shorter events, 0.1 us)
Async XLA Ops:
  5.4 32.2 %copy-start = (f32[1,32,32,128]{3,2,1,0:T(8,128)S(1)}, f32[1,32,32,128]{3,2,1,0:T(8,128)}, u32[]{:S(2)}) copy-start(f32[1,32,32,128]{3,2,1,0:T(8,128)} %get-tuple-element.50.refs_8_) | copy-start | bytes 1572868
  5.4 32.1 %copy-start.2 = (f32[1,64,128]{2,1,0:T(8,128)S(1)}, f32[1,64,128]{2,1,0:T(8,128)}, u32[]{:S(2)}) copy-start(f32[1,64,128]{2,1,0:T(8,128)} %get-tuple-element.51.refs_9_) | copy-start | bytes 98308
  5.4 15.4 %all-to-all-start = ((bf16[8,1,272,128]{3,2,1,0:T(8,128)(2,1)}), bf16[8,1,272,128]{3,2,1,0:T(8,128)(2,1)S(1)}, u32[]{:S(2)}, u32[]{:S(2)}) async-start(bf16[8,1,272,128]{3,2,1,0:T(8,128)(2,1)} %get-tuple-element.32), calls=%async_computation | async-start | bytes 1114112 | tf_op jit(solution)/shard_map/all_to_all | solution.py:523
  10.7 9.7 %collective-permute-start = (f32[64,8,128]{2,1,0:T(8,128)}, f32[64,8,128]{2,1,0:T(8,128)S(1)}, u32[]{:S(2)}, u32[]{:S(2)}) collective-permute-start(f32[64,8,128]{2,1,0:T(8,128)} %get-tuple-element.35), channel_id=1, source_target_pairs={{0,1},{1,0},{2,3},{3,2},{4,5},{5,4},{6,7},{7,6},{8,9},{9,8},{10,11... | collective-permute-start | bytes 786440 | tf_op jit(solution)/shard_map/ppermute | solution.py:527
  12.3 8.1 %collective-permute-start.1 = (f32[1,8,128]{2,1,0:T(8,128)}, f32[1,8,128]{2,1,0:T(8,128)S(1)}, u32[]{:S(2)}, u32[]{:S(2)}) collective-permute-start(f32[1,8,128]{2,1,0:T(8,128)} %get-tuple-element.36), channel_id=1, source_target_pairs={{0,2},{2,0},{4,6},{6,4},{8,10},{10,8},{12,14},{14,12},{16,18},{18,... | collective-permute-start | bytes 12296 | tf_op jit(solution)/shard_map/ppermute | solution.py:529
  16.8 3.7 %collective-permute-start.2 = (f32[1,8,128]{2,1,0:T(8,128)}, f32[1,8,128]{2,1,0:T(8,128)S(1)}, u32[]{:S(2)}, u32[]{:S(2)}) collective-permute-start(f32[1,8,128]{2,1,0:T(8,128)} %get-tuple-element.37), channel_id=1, source_target_pairs={{0,3},{2,1},{4,7},{6,5},{8,11},{10,9},{12,15},{14,13},{16,19},{18,... | collective-permute-start | bytes 12296 | tf_op jit(solution)/shard_map/ppermute | solution.py:529
  18.1 1.0 %copy-start.1 = (f32[64,8,128]{2,1,0:T(8,128)S(1)}, f32[64,8,128]{2,1,0:T(8,128)}, u32[]{:S(2)}) copy-start(f32[64,8,128]{2,1,0:T(8,128)} %get-tuple-element.33) | copy-start | bytes 786436
  26.3 3.7 %collective-permute-start.3 = (bf16[1,256,128]{2,1,0:T(8,128)(2,1)S(1)}, bf16[1,256,128]{2,1,0:T(8,128)(2,1)S(1)}, u32[]{:S(2)}, u32[]{:S(2)}) collective-permute-start(bf16[1,256,128]{2,1,0:T(8,128)(2,1)S(1)} %get-tuple-element.43), channel_id=1, source_target_pairs={{0,4},{4,0},{8,12},{12,8},{16,20},{20,16},{24,28},{28,24},{1,5},{5... | collective-permute-start | bytes 196616 | tf_op jit(solution)/shard_map/ppermute | solution.py:563
  26.4 6.2 %collective-permute-start.4 = (bf16[1,256,128]{2,1,0:T(8,128)(2,1)S(1)}, bf16[1,256,128]{2,1,0:T(8,128)(2,1)S(1)}, u32[]{:S(2)}, u32[]{:S(2)}) collective-permute-start(bf16[1,256,128]{2,1,0:T(8,128)(2,1)S(1)} %get-tuple-element.44), channel_id=1, source_target_pairs={{0,8},{4,12},{8,0},{12,4},{16,24},{20,28},{24,16},{28,20},{1,9},{5... | collective-permute-start | bytes 196616 | tf_op jit(solution)/shard_map/ppermute | solution.py:563
  28.2 4.6 %collective-permute-start.5 = (bf16[1,256,128]{2,1,0:T(8,128)(2,1)S(1)}, bf16[1,256,128]{2,1,0:T(8,128)(2,1)S(1)}, u32[]{:S(2)}, u32[]{:S(2)}) collective-permute-start(bf16[1,256,128]{2,1,0:T(8,128)(2,1)S(1)} %get-tuple-element.45), channel_id=1, source_target_pairs={{0,12},{4,8},{8,4},{12,0},{16,28},{20,24},{24,20},{28,16},{1,13},{... | collective-permute-start | bytes 196616 | tf_op jit(solution)/shard_map/ppermute | solution.py:563
  28.3 4.5 %collective-permute-start.6 = (bf16[1,256,128]{2,1,0:T(8,128)(2,1)S(1)}, bf16[1,256,128]{2,1,0:T(8,128)(2,1)S(1)}, u32[]{:S(2)}, u32[]{:S(2)}) collective-permute-start(bf16[1,256,128]{2,1,0:T(8,128)(2,1)S(1)} %get-tuple-element.46), channel_id=1, source_target_pairs={{0,16},{4,20},{8,24},{12,28},{16,0},{20,4},{24,8},{28,12},{1,17},{... | collective-permute-start | bytes 196616 | tf_op jit(solution)/shard_map/ppermute | solution.py:563
  30.0 5.6 %collective-permute-start.7 = (bf16[1,256,128]{2,1,0:T(8,128)(2,1)S(1)}, bf16[1,256,128]{2,1,0:T(8,128)(2,1)S(1)}, u32[]{:S(2)}, u32[]{:S(2)}) collective-permute-start(bf16[1,256,128]{2,1,0:T(8,128)(2,1)S(1)} %get-tuple-element.47), channel_id=1, source_target_pairs={{0,20},{4,16},{8,28},{12,24},{16,4},{20,0},{24,12},{28,8},{1,21},{... | collective-permute-start | bytes 196616 | tf_op jit(solution)/shard_map/ppermute | solution.py:563
  30.0 5.5 %collective-permute-start.8 = (bf16[1,256,128]{2,1,0:T(8,128)(2,1)S(1)}, bf16[1,256,128]{2,1,0:T(8,128)(2,1)S(1)}, u32[]{:S(2)}, u32[]{:S(2)}) collective-permute-start(bf16[1,256,128]{2,1,0:T(8,128)(2,1)S(1)} %get-tuple-element.48), channel_id=1, source_target_pairs={{0,24},{4,28},{8,16},{12,20},{16,8},{20,12},{24,0},{28,4},{1,25},{... | collective-permute-start | bytes 196616 | tf_op jit(solution)/shard_map/ppermute | solution.py:563
  32.6 4.9 %collective-permute-start.9 = (bf16[1,256,128]{2,1,0:T(8,128)(2,1)S(1)}, bf16[1,256,128]{2,1,0:T(8,128)(2,1)S(1)}, u32[]{:S(2)}, u32[]{:S(2)}) collective-permute-start(bf16[1,256,128]{2,1,0:T(8,128)(2,1)S(1)} %get-tuple-element.49), channel_id=1, source_target_pairs={{0,28},{4,24},{8,20},{12,16},{16,12},{20,8},{24,4},{28,0},{1,29},{... | collective-permute-start | bytes 196616 | tf_op jit(solution)/shard_map/ppermute | solution.py:563
  39.5 6.9 %collective-permute-start.10 = (bf16[1,32,1024]{2,1,0:T(8,128)(2,1)S(1)}, bf16[1,32,1024]{2,1,0:T(8,128)(2,1)S(1)}, u32[]{:S(2)}, u32[]{:S(2)}) collective-permute-start(bf16[1,32,1024]{2,1,0:T(8,128)(2,1)S(1)} %get-tuple-element.56), channel_id=1, source_target_pairs={{0,1},{1,2},{2,3},{3,0},{4,5},{5,6},{6,7},{7,4},{8,9},{9,10},{10,1... | collective-permute-start | bytes 196616 | tf_op jit(solution)/shard_map/ppermute | solution.py:590
  40.1 8.3 %collective-permute-start.11 = (bf16[1,32,1024]{2,1,0:T(8,128)(2,1)S(1)}, bf16[1,32,1024]{2,1,0:T(8,128)(2,1)S(1)}, u32[]{:S(2)}, u32[]{:S(2)}) collective-permute-start(bf16[1,32,1024]{2,1,0:T(8,128)(2,1)S(1)} %get-tuple-element.57), channel_id=1, source_target_pairs={{0,2},{1,3},{2,0},{3,1},{4,6},{5,7},{6,4},{7,5},{8,10},{9,11},{10,... | collective-permute-start | bytes 196616 | tf_op jit(solution)/shard_map/ppermute | solution.py:590
  43.3 5.3 %collective-permute-start.12 = (bf16[1,32,1024]{2,1,0:T(8,128)(2,1)S(1)}, bf16[1,32,1024]{2,1,0:T(8,128)(2,1)S(1)}, u32[]{:S(2)}, u32[]{:S(2)}) collective-permute-start(bf16[1,32,1024]{2,1,0:T(8,128)(2,1)S(1)} %get-tuple-element.58), channel_id=1, source_target_pairs={{0,3},{1,0},{2,1},{3,2},{4,7},{5,4},{6,5},{7,6},{8,11},{9,8},{10,9... | collective-permute-start | bytes 196616 | tf_op jit(solution)/shard_map/ppermute | solution.py:590

commit v7 on v6

--- a/solution.py
+++ b/solution.py
@@ -159,6 +159,15 @@
     place = iota(shape, axis)
     frequency = jnp.where(place < grid, place, grid - place)
     return jnp.where(place == grid, 0.0, cas_table(frequency * iota(shape, 1 - axis), doubled))
+
+
+def side_by_side(table, parts):
+    results = []
+    for first, second in zip(parts[::2], parts[1::2]):
+        width = first.shape[1]
+        out = dot(table, terms_of(jnp.concatenate([first, second], axis=1), 0))
+        results += [out[:, :width], out[:, width:]]
+    return results
 
 
 class Plan:
@@ -245,11 +254,11 @@
         coef = stage_ref[...].astype(BF16)
         first = dot(jnp.concatenate([coef, coef], axis=0), depth_ref[...], ((0,), (0,)))
         inner, outer = inner_ref[...], outer_ref[...]
-        second = [dot(inner, terms_of(first[span * t : span * (t + 1)], 0)) for t in range(box // SUB)]
+        second = side_by_side(inner, [first[span * t : span * (t + 1)] for t in range(box // SUB)])
         second = jnp.concatenate(second, axis=0).reshape(box, box // SUB, SUB, grid)
+        third = side_by_side(outer, [second[:, t].reshape(span, grid) for t in range(box // SUB)])
         for t in range(box // SUB):
-            third = dot(outer, terms_of(second[:, t].reshape(span, grid), 0))
-            psi_ref[:, SUB * t : SUB * (t + 1), :] = third.reshape(box, SUB, grid)
+            psi_ref[:, SUB * t : SUB * (t + 1), :] = third[t].reshape(box, SUB, grid)
         sent = start_copies(sems, 5, (psi_ref, psi_any.at[group]))
         whole_wave = wave_ref[...]
         wave = jnp.zeros_like(whole_wave)
@@ -349,8 +358,9 @@
     half, slots, grid, box, count = plan.half, plan.slots, plan.grid, plan.box, plan.per_group
     piece_refs, edge_refs = refs[:half], refs[half : 2 * half]
     forward_y_ref, forward_z_ref, inverse_y_ref, inverse_z_ref = refs[2 * half : 2 * half + 4]
-    send_refs = refs[2 * half + 4 : 2 * half + 4 + plan.orb]
-    field_ref, result_ref, table_ref, corner_ref, sem = refs[2 * half + 4 + plan.orb :]
+    chips = plan.orb // 2
+    own_ref, swap_ref, *send_refs = refs[2 * half + 4 : 2 * half + 5 + chips]
+    field_ref, result_ref, table_ref, corner_ref, sem = refs[2 * half + 5 + chips :]
     me, own = lax.rem(where_ref[0], plan.pln), where_ref[0] // plan.pln
     depth = plan.area
     all_groups = plan.orb * plan.groups
@@ -407,7 +417,10 @@
             shift = lax.rem(box * n - corner_ref[2 * number, box * n] + grid, grid)
             rows = result_ref[pl.ds(start(number, n), depth), :]
             values = jnp.where(owner == n, pltpu.roll(rows, shift, 1), values)
-        send_refs[d][group] = values.astype(BF16)
+        if d < 2:
+            (own_ref, swap_ref)[d][group] = values.astype(BF16)
+        else:
+            send_refs[d // 2 - 1][d % 2, group] = values.astype(BF16)
         return carry
 
     for d in range(plan.orb):
@@ -417,12 +430,26 @@
             lax.fori_loop(0, plan.groups, functools.partial(cut, d), 0)
 
 
+def gather_kernel(swap_ref, *refs):
+    out_ref = refs[-1]
+    out_ref[0] = swap_ref[...]
+    for number, ref in enumerate(refs[:-1]):
+        out_ref[number + 1] = ref[1]
+
+
 def terms_kernel(plan, where_ref, *refs):
     box, grid, count, slots, pln = plan.box, plan.grid, plan.per_group, plan.slots, plan.pln
-    recv_refs = refs[: plan.orb]
-    psi_any, wave_ref, inner_ref, outer_ref, back_ref, *refs = refs[plan.orb :]
+    chips = plan.orb // 2
+    own_ref, other_ref, *chip_refs = refs[: chips + 1]
+    psi_any, wave_ref, inner_ref, outer_ref, back_ref, *refs = refs[chips + 1 :]
+
+    def tile(d, rows):
+        if d % 2:
+            return other_ref[d // 2, 0, rows]
+        return chip_refs[d // 2 - 1][0, 0, rows] if d else own_ref[0, rows]
+
     out_refs = refs[:pln]
-    psi_ref, stage_ref, own_ref, sem = refs[pln:]
+    psi_ref, stage_ref, result_ref, sem = refs[pln:]
     group = pl.program_id(0)
     copy = pltpu.make_async_copy(psi_any.at[group], psi_ref, sem)
     copy.start()
@@ -433,7 +460,7 @@
     inner, outer, back = inner_ref[...], outer_ref[...], back_ref[...]
     copy.wait()
     for pair in range(box // 2):
-        tiles = [ref[0, 2 * slots * pair : 2 * slots * (pair + 1), :].astype(F32) for ref in recv_refs]
+        tiles = [tile(d, pl.ds(2 * slots * pair, 2 * slots)).astype(F32) for d in range(plan.orb)]
         columns = [jnp.concatenate([t[slots * side : slots * (side + 1)] for t in tiles], axis=0) for side in range(2)]
         both = jnp.concatenate(columns, axis=1).astype(BF16)
         out = dot(wave, jnp.concatenate([both, both], axis=0))
@@ -444,23 +471,20 @@
                 potential = jnp.where(owner == n, mine[box * n : box * (n + 1)], potential)
             stage_ref[b] = potential * psi_ref[b]
     span = SUB * box
-    second = []
+    second = side_by_side(inner, [stage_ref[SUB * t : SUB * (t + 1)].reshape(span, grid) for t in range(box // SUB)])
+    second = jnp.concatenate(second, axis=0).reshape(box, box // SUB, SUB, grid)
+    third = side_by_side(outer, [second[:, t].reshape(span, grid) for t in range(box // SUB)])
     for t in range(box // SUB):
-        values = stage_ref[SUB * t : SUB * (t + 1)].reshape(span, grid)
-        second.append(dot(inner, terms_of(values, 0)))
-    second = jnp.concatenate(second, axis=0).reshape(box, box // SUB, SUB, grid)
-    for t in range(box // SUB):
-        values = dot(outer, terms_of(second[:, t].reshape(span, grid), 0))
-        stage_ref[:, SUB * t : SUB * (t + 1), :] = values.reshape(box, SUB, grid)
+        stage_ref[:, SUB * t : SUB * (t + 1), :] = third[t].reshape(box, SUB, grid)
     values = terms_of(stage_ref[...].reshape(box * box, grid), 1)
     out = dot(back, values, ((1,), (1,)))
     part = plan.box_part * count
     for p in range(pln):
-        own_ref[p] = out[part * p : part * (p + 1)]
+        result_ref[p] = out[part * p : part * (p + 1)]
     me = lax.rem(where_ref[0], pln)
-    out_refs[0][0] = own_ref[me]
+    out_refs[0][0] = result_ref[me]
     for step in range(1, pln):
-        out_refs[step][0] = own_ref[lax.rem(me + step, pln)].astype(BF16)
+        out_refs[step][0] = result_ref[lax.rem(me + step, pln)].astype(BF16)
 
 
 def sum_kernel(plan, *refs):
@@ -543,11 +567,13 @@
         name="tables",
     )(where, pieces[0])
     pieces[0] = tables[7]
+    chips = orb // 2
+    single = jax.ShapeDtypeStruct((groups, area, grid), BF16)
     send = pl.pallas_call(
         functools.partial(solve_kernel, plan),
         in_specs=[smem] + [vmem] * (5 + 2 * half),
-        out_specs=[vmem] * orb,
-        out_shape=[jax.ShapeDtypeStruct((groups, area, grid), BF16)] * orb,
+        out_specs=[vmem] * (1 + chips),
+        out_shape=[single] * 2 + [jax.ShapeDtypeStruct((2, groups, area, grid), BF16)] * (chips - 1),
         scratch_shapes=[
             pltpu.VMEM((grid * slots, grid), F32),
             pltpu.VMEM((grid * slots, grid), F32),
@@ -558,16 +584,29 @@
         compiler_params=small,
         name="solve",
     )(where, received, *pieces, *tables[:4])
-    received = [send[0]] + [None] * (orb - 1)
-    for d in reversed(range(1, orb)):
-        received[d] = lax.ppermute(send[d], "orb", [(o, o ^ d) for o in range(orb)])
+    own, swap, *send = send
+    core_pairs = [(o, o ^ 1) for o in range(orb)]
+    arrived = [None] * (chips - 1)
+    for e in reversed(range(1, chips)):
+        arrived[e - 1] = lax.ppermute(send[e - 1], "orb", [(o, o ^ (2 * e)) for o in range(orb)])
+    gathered = pl.pallas_call(
+        gather_kernel,
+        in_specs=[vmem] * chips,
+        out_specs=vmem,
+        out_shape=jax.ShapeDtypeStruct((chips, groups, area, grid), BF16),
+        compiler_params=small,
+        name="gather",
+    )(swap, *arrived)
+    other = lax.ppermute(gathered, "orb", core_pairs)
     part = plan.box_part * count
     finished = pl.pallas_call(
         functools.partial(terms_kernel, plan),
         grid=(groups,),
         in_specs=[
             smem,
-            *[pl.BlockSpec((1, area, grid), lambda g: (g, 0, 0))] * orb,
+            pl.BlockSpec((1, area, grid), lambda g: (g, 0, 0)),
+            pl.BlockSpec((chips, 1, area, grid), lambda g: (0, g, 0, 0)),
+            *[pl.BlockSpec((1, 1, area, grid), lambda g: (0, g, 0, 0))] * (chips - 1),
             anywhere,
             pl.BlockSpec((1, plan.rows, grid), lambda g: (g, 0, 0)),
             vmem,
@@ -584,7 +623,7 @@
         ],
         compiler_params=small,
         name="terms",
-    )(where, *received, psi, wave, *tables[4:7])
+    )(where, own, other, *arrived, psi, wave, *tables[4:7])
     finished = list(finished)
     for step in range(1, pln):
         finished[step] = lax.ppermute(finished[step], "pln", [(p, (p + step) % pln) for p in range(pln)])

time: 49.6 us -> 48.7 us (0.982)
  starting transfers between devices: 23.7 us -> 21 us
  waiting for transfers between devices: 9.61 us -> 12.1 us
  Pallas kernels: 14.9 us -> 14.3 us
    ppermute x7 -> x4, starting transfers between devices: 6.43 us -> 3.62 us  [the longest x3 3.55 us: per_device(): lax.ppermute(send[e - 1], 'orb', [(o, o ^ 2 * e) for o in range(orb)])]
    ppermute x7 -> x4, waiting for transfers between devices: 4.74 us -> 7.49 us  [the longest x3 5.97 us: per_device(): lax.ppermute(send[e - 1], 'orb', [(o, o ^ 2 * e) for o in range(orb)])]
  transfers between devices with their start and end apart: 14 -> 11, of which waited for: 6 -> 6; matrix products, arithmetic and copies ran while one was open for 0% -> 0% of each run, Pallas kernels for 3% -> 3%
where the time goes in v7:
time: 48.7 us; the launch traced here: 48.4 us
  starting transfers between devices  21 us (43%)
  Pallas kernels  14.3 us (29%)
  waiting for transfers between devices  12.1 us (25%)
  local copies, waits for them, and re-layouts  0.95 us (2%)
    ppermute x3, waiting for transfers between devices, per_device(): lax.ppermute(send[e - 1], 'orb', [(o, o ^ 2 * e) for o in range(orb)])  5.97 us
    ppermute x2, starting transfers between devices, per_device(): lax.ppermute(pieces[half + step], 'pln', [(0, half + step), (half, step)])  5.78 us
    pallas_call x1, Pallas kernels, per_device(): pl.pallas_call(functools.partial(solve_kernel, plan), in_specs=[smem] + [...  5.55 us
    all_to_all x1, starting transfers between devices, per_device(): lax.all_to_all(send, 'orb', split_axis=0, concat_axis=0, tiled=True)  5.32 us
    pallas_call x1, Pallas kernels, per_device(): pl.pallas_call(functools.partial(density_kernel, plan), in_specs=[smem, s...  4.99 us
    ppermute x3, starting transfers between devices, per_device(): lax.ppermute(finished[step], 'pln', [(p, (p + step) % pln) for p in range...  4.67 us
    ppermute x3, waiting for transfers between devices, per_device(): lax.ppermute(finished[step], 'pln', [(p, (p + step) % pln) for p in range...  4.21 us
    ppermute x3, starting transfers between devices, per_device(): lax.ppermute(send[e - 1], 'orb', [(o, o ^ 2 * e) for o in range(orb)])  3.55 us
  transfers between devices with their start and end apart: 11, of which 6 were waited for; matrix products, arithmetic and copies ran while one was open for 0% of the time, Pallas kernels for 3%

profile of v7, /device:TPU:0, one launch (start us, length us, event | category | flops | bytes accessed | tf_op | source)
XLA Modules:
  0.0 48.4 jit_solution(8223023102787556606)
XLA Ops:
  0.0 5.0 %density.1 = (bf16[8,1,272,128]{3,2,1,0:T(8,128)(2,1)}, f32[1,32,32,128]{3,2,1,0:T(8,128)}, f32[1,64,128]{2,1,0:T(8,128)}, f32[64,8,128]{2,1,0:T(8,128)}, f32[64...) custom-call(s32[1]{0:T(128)} %bitcast.where_ref, s32[4,3]{1,0:T(4,128)} %corner_ref.1, f32[4]{0:T(128)} %weight_ref.1, ...), custom_call_target="tpu_custom_call" | custom-call | tf_op jit(solution)/shard_map/density/pallas_call | solution.py:517
  5.0 0.0 copy-start.2
  5.0 5.3 %all-to-all-start = ((bf16[8,1,272,128]{3,2,1,0:T(8,128)(2,1)}), bf16[8,1,272,128]{3,2,1,0:T(8,128)(2,1)S(1)}, u32[]{:S(2)}, u32[]{:S(2)}) async-start(bf16[8,1,272,128]{3,2,1,0:T(8,128)(2,1)} %get-tuple-element.29), calls=%async_computation | async-start | bytes 1114112 | tf_op jit(solution)/shard_map/all_to_all | solution.py:547
  10.3 1.6 %collective-permute-start = (f32[64,8,128]{2,1,0:T(8,128)}, f32[64,8,128]{2,1,0:T(8,128)S(1)}, u32[]{:S(2)}, u32[]{:S(2)}) collective-permute-start(f32[64,8,128]{2,1,0:T(8,128)} %get-tuple-element.32), channel_id=1, source_target_pairs={{0,1},{1,0},{2,3},{3,2},{4,5},{5,4},{6,7},{7,6},{8,9},{9,8},{10,11... | collective-permute-start | bytes 786440 | tf_op jit(solution)/shard_map/ppermute | solution.py:551
  11.9 4.5 %collective-permute-start.1 = (f32[1,8,128]{2,1,0:T(8,128)}, f32[1,8,128]{2,1,0:T(8,128)S(1)}, u32[]{:S(2)}, u32[]{:S(2)}) collective-permute-start(f32[1,8,128]{2,1,0:T(8,128)} %get-tuple-element.33), channel_id=1, source_target_pairs={{0,2},{2,0},{4,6},{6,4},{8,10},{10,8},{12,14},{14,12},{16,18},{18,... | collective-permute-start | bytes 12296 | tf_op jit(solution)/shard_map/ppermute | solution.py:553
  16.4 1.3 %collective-permute-start.2 = (f32[1,8,128]{2,1,0:T(8,128)}, f32[1,8,128]{2,1,0:T(8,128)S(1)}, u32[]{:S(2)}, u32[]{:S(2)}) collective-permute-start(f32[1,8,128]{2,1,0:T(8,128)} %get-tuple-element.34), channel_id=1, source_target_pairs={{0,3},{2,1},{4,7},{6,5},{8,11},{10,9},{12,15},{14,13},{16,19},{18,... | collective-permute-start | bytes 12296 | tf_op jit(solution)/shard_map/ppermute | solution.py:553
  17.7 0.9 %copy-done.1 = f32[64,8,128]{2,1,0:T(8,128)S(1)} copy-done((f32[64,8,128]{2,1,0:T(8,128)S(1)}, f32[64,8,128]{2,1,0:T(8,128)}, u32[]{:S(2)}) %copy-start.1) | copy-done | bytes 262168
  18.6 1.4 %tables.1 = (bf16[256,256]{1,0:T(8,128)(2,1)S(1)}, bf16[256,256]{1,0:T(8,128)(2,1)S(1)}, bf16[128,768]{1,0:T(8,128)(2,1)S(1)}, bf16[768,128]{1,0:T(8,128)(2,1)S(...) custom-call(s32[1]{0:T(128)} %bitcast.where_ref, ...), custom_call_target="tpu_custom_call" | custom-call | tf_op jit(solution)/shard_map/tables/pallas_call | solution.py:560
  20.1 0.4 all-to-all-done
  20.4 5.5 %solve.1 = (bf16[1,256,128]{2,1,0:T(8,128)(2,1)S(1)}, bf16[1,256,128]{2,1,0:T(8,128)(2,1)S(1)}, bf16[2,1,256,128]{3,2,1,0:T(8,128)(2,1)S(1)}, bf16[2,1,256,128]{...) custom-call(s32[1]{0:T(128)} %bitcast.where_ref, bf16[8,272,128]{2,1,0:T(8,128)(2,1)S(1)} %bitcast.7, ...), custom_call_target="tpu_custom_call" | custom-call | tf_op jit(solution)/shard_map/solve/pallas_call | solution.py:572
  26.0 1.7 %collective-permute-start.3 = (bf16[2,1,256,128]{3,2,1,0:T(8,128)(2,1)S(1)}, bf16[2,1,256,128]{3,2,1,0:T(8,128)(2,1)S(1)}, u32[]{:S(2)}, u32[]{:S(2)}) collective-permute-start(bf16[2,1,256,128]{3,2,1,0:T(8,128)(2,1)S(1)} %get-tuple-element.41), channel_id=1, source_target_pairs={{0,8},{4,12},{8,0},{12,4},{16,24},{20,28},{24,16},{28,20},{1,9},{5... | collective-permute-start | bytes 393224 | tf_op jit(solution)/shard_map/ppermute | solution.py:591
  27.7 1.5 %collective-permute-start.4 = (bf16[2,1,256,128]{3,2,1,0:T(8,128)(2,1)S(1)}, bf16[2,1,256,128]{3,2,1,0:T(8,128)(2,1)S(1)}, u32[]{:S(2)}, u32[]{:S(2)}) collective-permute-start(bf16[2,1,256,128]{3,2,1,0:T(8,128)(2,1)S(1)} %get-tuple-element.42), channel_id=1, source_target_pairs={{0,16},{4,20},{8,24},{12,28},{16,0},{20,4},{24,8},{28,12},{1,17},{... | collective-permute-start | bytes 393224 | tf_op jit(solution)/shard_map/ppermute | solution.py:591
  29.2 0.3 collective-permute-start.5
  29.5 2.1 %collective-permute-done.3.refs_0_.refs_2_ = bf16[2,1,256,128]{3,2,1,0:T(8,128)(2,1)S(1)} collective-permute-done((bf16[2,1,256,128]{3,2,1,0:T(8,128)(2,1)S(1)}, bf16[2,1,256,128]{3,2,1,0:T(8,128)(2,1)S(1)}, u32[]{:S(2)}, u32[]{:S(2)}) %collective-permute-start.3) | collective-permute-done | bytes 131104 | tf_op jit(solution)/shard_map/ppermute | solution.py:591
  31.7 3.8 %collective-permute-done.4.refs_1_.refs_3_ = bf16[2,1,256,128]{3,2,1,0:T(8,128)(2,1)S(1)} collective-permute-done((bf16[2,1,256,128]{3,2,1,0:T(8,128)(2,1)S(1)}, bf16[2,1,256,128]{3,2,1,0:T(8,128)(2,1)S(1)}, u32[]{:S(2)}, u32[]{:S(2)}) %collective-permute-start.4) | collective-permute-done | bytes 131104 | tf_op jit(solution)/shard_map/ppermute | solution.py:591
  35.5 0.1 collective-permute-start.6
  35.6 1.5 %collective-permute-done.6.refs_1_ = bf16[4,1,256,128]{3,2,1,0:T(8,128)(2,1)S(1)} collective-permute-done((bf16[4,1,256,128]{3,2,1,0:T(8,128)(2,1)S(1)}, bf16[4,1,256,128]{3,2,1,0:T(8,128)(2,1)S(1)}, u32[]{:S(2)}, u32[]{:S(2)}) %collective-permute-start.6) | collective-permute-done | bytes 262176 | tf_op jit(solution)/shard_map/ppermute | solution.py:600
  37.1 1.7 %terms.1 = (f32[1,32,1024]{2,1,0:T(8,128)S(1)}, bf16[1,32,1024]{2,1,0:T(8,128)(2,1)S(1)}, bf16[1,32,1024]{2,1,0:T(8,128)(2,1)S(1)}, bf16[1,32,1024]{2,1,0:T(8,128)(2,1)S(1)}) custom-call(s32[1]{0:T(128)} %bitcast.where_ref, bf16[1,256,128]{2,1,0:T(8,128)(2,1)S(1)} %get-tuple-element.39.refs_0_, bf16[4,1,256,128]{3,2,1,0:T(8,128)(2,1)S(1)} %collective-permute-done.6.refs_1_, ...), custom_call_target="tpu_custom_call" | custom-call | tf_op jit(solution)/shard_map/terms/pallas_call | solution.py:602
  38.8 0.7 %collective-permute-start.7 = (bf16[1,32,1024]{2,1,0:T(8,128)(2,1)S(1)}, bf16[1,32,1024]{2,1,0:T(8,128)(2,1)S(1)}, u32[]{:S(2)}, u32[]{:S(2)}) collective-permute-start(bf16[1,32,1024]{2,1,0:T(8,128)(2,1)S(1)} %get-tuple-element.50), channel_id=1, source_target_pairs={{0,1},{1,2},{2,3},{3,0},{4,5},{5,6},{6,7},{7,4},{8,9},{9,10},{10,1... | collective-permute-start | bytes 196616 | tf_op jit(solution)/shard_map/ppermute | solution.py:629
  39.6 2.9 %collective-permute-start.8 = (bf16[1,32,1024]{2,1,0:T(8,128)(2,1)S(1)}, bf16[1,32,1024]{2,1,0:T(8,128)(2,1)S(1)}, u32[]{:S(2)}, u32[]{:S(2)}) collective-permute-start(bf16[1,32,1024]{2,1,0:T(8,128)(2,1)S(1)} %get-tuple-element.51), channel_id=1, source_target_pairs={{0,2},{1,3},{2,0},{3,1},{4,6},{5,7},{6,4},{7,5},{8,10},{9,11},{10,... | collective-permute-start | bytes 196616 | tf_op jit(solution)/shard_map/ppermute | solution.py:629
  42.5 1.0 %collective-permute-start.9 = (bf16[1,32,1024]{2,1,0:T(8,128)(2,1)S(1)}, bf16[1,32,1024]{2,1,0:T(8,128)(2,1)S(1)}, u32[]{:S(2)}, u32[]{:S(2)}) collective-permute-start(bf16[1,32,1024]{2,1,0:T(8,128)(2,1)S(1)} %get-tuple-element.52), channel_id=1, source_target_pairs={{0,3},{1,0},{2,1},{3,2},{4,7},{5,4},{6,5},{7,6},{8,11},{9,8},{10,9... | collective-permute-start | bytes 196616 | tf_op jit(solution)/shard_map/ppermute | solution.py:629
  43.5 2.3 %collective-permute-done.7.refs_1_ = bf16[1,32,1024]{2,1,0:T(8,128)(2,1)S(1)} collective-permute-done((bf16[1,32,1024]{2,1,0:T(8,128)(2,1)S(1)}, bf16[1,32,1024]{2,1,0:T(8,128)(2,1)S(1)}, u32[]{:S(2)}, u32[]{:S(2)}) %collective-permute-start.7) | collective-permute-done | bytes 65568 | tf_op jit(solution)/shard_map/ppermute | solution.py:629
  45.8 1.9 %collective-permute-done.8.refs_2_ = bf16[1,32,1024]{2,1,0:T(8,128)(2,1)S(1)} collective-permute-done((bf16[1,32,1024]{2,1,0:T(8,128)(2,1)S(1)}, bf16[1,32,1024]{2,1,0:T(8,128)(2,1)S(1)}, u32[]{:S(2)}, u32[]{:S(2)}) %collective-permute-start.8) | collective-permute-done | bytes 65568 | tf_op jit(solution)/shard_map/ppermute | solution.py:629
  47.7 0.7 %sum.1 = bf16[1,4,8192]{2,1,0:T(4,128)(2,1)} custom-call(f32[1,32,1024]{2,1,0:T(8,128)S(1)} %get-tuple-element.49.refs_0_, bf16[1,32,1024]{2,1,0:T(8,128)(2,1)S(1)} %collective-permute-done.7.refs_1_, bf16[1,32,1024]{2,1,0:T(8,128)(2,1)S(1)} %collective-permute-done.8.refs_2_, bf16[1,32,1024]{2,1,0:T(8,128)(2,1)S(1)} %collective-permute-done.9.refs_3_), custom_call_target="tpu_custom_call" | custom-call | tf_op jit(solution)/shard_map/sum/pallas_call | solution.py:631
  (10 shorter events, 0.0 us)
Async XLA Ops:
  5.0 32.1 %copy-start = (f32[1,32,32,128]{3,2,1,0:T(8,128)S(1)}, f32[1,32,32,128]{3,2,1,0:T(8,128)}, u32[]{:S(2)}) copy-start(f32[1,32,32,128]{3,2,1,0:T(8,128)} %get-tuple-element.44.refs_5_) | copy-start | bytes 1572868
  5.0 32.1 %copy-start.2 = (f32[1,64,128]{2,1,0:T(8,128)S(1)}, f32[1,64,128]{2,1,0:T(8,128)}, u32[]{:S(2)}) copy-start(f32[1,64,128]{2,1,0:T(8,128)} %get-tuple-element.45.refs_6_) | copy-start | bytes 98308
  5.0 15.4 %all-to-all-start = ((bf16[8,1,272,128]{3,2,1,0:T(8,128)(2,1)}), bf16[8,1,272,128]{3,2,1,0:T(8,128)(2,1)S(1)}, u32[]{:S(2)}, u32[]{:S(2)}) async-start(bf16[8,1,272,128]{3,2,1,0:T(8,128)(2,1)} %get-tuple-element.29), calls=%async_computation | async-start | bytes 1114112 | tf_op jit(solution)/shard_map/all_to_all | solution.py:547
  10.3 9.7 %collective-permute-start = (f32[64,8,128]{2,1,0:T(8,128)}, f32[64,8,128]{2,1,0:T(8,128)S(1)}, u32[]{:S(2)}, u32[]{:S(2)}) collective-permute-start(f32[64,8,128]{2,1,0:T(8,128)} %get-tuple-element.32), channel_id=1, source_target_pairs={{0,1},{1,0},{2,3},{3,2},{4,5},{5,4},{6,7},{7,6},{8,9},{9,8},{10,11... | collective-permute-start | bytes 786440 | tf_op jit(solution)/shard_map/ppermute | solution.py:551
  11.9 8.1 %collective-permute-start.1 = (f32[1,8,128]{2,1,0:T(8,128)}, f32[1,8,128]{2,1,0:T(8,128)S(1)}, u32[]{:S(2)}, u32[]{:S(2)}) collective-permute-start(f32[1,8,128]{2,1,0:T(8,128)} %get-tuple-element.33), channel_id=1, source_target_pairs={{0,2},{2,0},{4,6},{6,4},{8,10},{10,8},{12,14},{14,12},{16,18},{18,... | collective-permute-start | bytes 12296 | tf_op jit(solution)/shard_map/ppermute | solution.py:553
  16.4 3.7 %collective-permute-start.2 = (f32[1,8,128]{2,1,0:T(8,128)}, f32[1,8,128]{2,1,0:T(8,128)S(1)}, u32[]{:S(2)}, u32[]{:S(2)}) collective-permute-start(f32[1,8,128]{2,1,0:T(8,128)} %get-tuple-element.34), channel_id=1, source_target_pairs={{0,3},{2,1},{4,7},{6,5},{8,11},{10,9},{12,15},{14,13},{16,19},{18,... | collective-permute-start | bytes 12296 | tf_op jit(solution)/shard_map/ppermute | solution.py:553
  17.7 1.0 %copy-start.1 = (f32[64,8,128]{2,1,0:T(8,128)S(1)}, f32[64,8,128]{2,1,0:T(8,128)}, u32[]{:S(2)}) copy-start(f32[64,8,128]{2,1,0:T(8,128)} %get-tuple-element.30) | copy-start | bytes 786436
  26.0 5.7 %collective-permute-start.3 = (bf16[2,1,256,128]{3,2,1,0:T(8,128)(2,1)S(1)}, bf16[2,1,256,128]{3,2,1,0:T(8,128)(2,1)S(1)}, u32[]{:S(2)}, u32[]{:S(2)}) collective-permute-start(bf16[2,1,256,128]{3,2,1,0:T(8,128)(2,1)S(1)} %get-tuple-element.41), channel_id=1, source_target_pairs={{0,8},{4,12},{8,0},{12,4},{16,24},{20,28},{24,16},{28,20},{1,9},{5... | collective-permute-start | bytes 393224 | tf_op jit(solution)/shard_map/ppermute | solution.py:591
  27.7 7.8 %collective-permute-start.4 = (bf16[2,1,256,128]{3,2,1,0:T(8,128)(2,1)S(1)}, bf16[2,1,256,128]{3,2,1,0:T(8,128)(2,1)S(1)}, u32[]{:S(2)}, u32[]{:S(2)}) collective-permute-start(bf16[2,1,256,128]{3,2,1,0:T(8,128)(2,1)S(1)} %get-tuple-element.42), channel_id=1, source_target_pairs={{0,16},{4,20},{8,24},{12,28},{16,0},{20,4},{24,8},{28,12},{1,17},{... | collective-permute-start | bytes 393224 | tf_op jit(solution)/shard_map/ppermute | solution.py:591
  29.2 6.3 %collective-permute-start.5 = (bf16[2,1,256,128]{3,2,1,0:T(8,128)(2,1)S(1)}, bf16[2,1,256,128]{3,2,1,0:T(8,128)(2,1)S(1)}, u32[]{:S(2)}, u32[]{:S(2)}) collective-permute-start(bf16[2,1,256,128]{3,2,1,0:T(8,128)(2,1)S(1)} %get-tuple-element.43), channel_id=1, source_target_pairs={{0,24},{4,28},{8,16},{12,20},{16,8},{20,12},{24,0},{28,4},{1,25},{... | collective-permute-start | bytes 393224 | tf_op jit(solution)/shard_map/ppermute | solution.py:591
  35.5 1.6 %collective-permute-start.6 = (bf16[4,1,256,128]{3,2,1,0:T(8,128)(2,1)S(1)}, bf16[4,1,256,128]{3,2,1,0:T(8,128)(2,1)S(1)}, u32[]{:S(2)}, u32[]{:S(2)}) collective-permute-start(bf16[4,1,256,128]{3,2,1,0:T(8,128)(2,1)S(1)} %gather.1), channel_id=1, source_target_pairs={{0,4},{4,0},{8,12},{12,8},{16,20},{20,16},{24,28},{28,24},{1,5},{5... | collective-permute-start | bytes 786440 | tf_op jit(solution)/shard_map/ppermute | solution.py:600
  38.8 6.9 %collective-permute-start.7 = (bf16[1,32,1024]{2,1,0:T(8,128)(2,1)S(1)}, bf16[1,32,1024]{2,1,0:T(8,128)(2,1)S(1)}, u32[]{:S(2)}, u32[]{:S(2)}) collective-permute-start(bf16[1,32,1024]{2,1,0:T(8,128)(2,1)S(1)} %get-tuple-element.50), channel_id=1, source_target_pairs={{0,1},{1,2},{2,3},{3,0},{4,5},{5,6},{6,7},{7,4},{8,9},{9,10},{10,1... | collective-permute-start | bytes 196616 | tf_op jit(solution)/shard_map/ppermute | solution.py:629
  39.6 8.2 %collective-permute-start.8 = (bf16[1,32,1024]{2,1,0:T(8,128)(2,1)S(1)}, bf16[1,32,1024]{2,1,0:T(8,128)(2,1)S(1)}, u32[]{:S(2)}, u32[]{:S(2)}) collective-permute-start(bf16[1,32,1024]{2,1,0:T(8,128)(2,1)S(1)} %get-tuple-element.51), channel_id=1, source_target_pairs={{0,2},{1,3},{2,0},{3,1},{4,6},{5,7},{6,4},{7,5},{8,10},{9,11},{10,... | collective-permute-start | bytes 196616 | tf_op jit(solution)/shard_map/ppermute | solution.py:629
  42.5 5.2 %collective-permute-start.9 = (bf16[1,32,1024]{2,1,0:T(8,128)(2,1)S(1)}, bf16[1,32,1024]{2,1,0:T(8,128)(2,1)S(1)}, u32[]{:S(2)}, u32[]{:S(2)}) collective-permute-start(bf16[1,32,1024]{2,1,0:T(8,128)(2,1)S(1)} %get-tuple-element.52), channel_id=1, source_target_pairs={{0,3},{1,0},{2,1},{3,2},{4,7},{5,4},{6,5},{7,6},{8,11},{9,8},{10,9... | collective-permute-start | bytes 196616 | tf_op jit(solution)/shard_map/ppermute | solution.py:629

commit v8 on v7

--- a/solution.py
+++ b/solution.py
@@ -246,13 +246,16 @@
     for copy in spectrum:
         copy.start()
     owner = lane_owner((1, grid), box)
+    owner_pair = jnp.concatenate([owner, owner], axis=1)
     coef_copy.wait()
-    wait_copies(fetched)
+    wait_copies(fetched[:1])
     for group in range(plan.groups):
         for p in range(box):
             stage_ref[count * p : count * (p + 1), :] = coef_ref[group, :, section * p : section * (p + 1)].astype(F32)
         coef = stage_ref[...].astype(BF16)
         first = dot(jnp.concatenate([coef, coef], axis=0), depth_ref[...], ((0,), (0,)))
+        if group == 0:
+            wait_copies(fetched[1:])
         inner, outer = inner_ref[...], outer_ref[...]
         second = side_by_side(inner, [first[span * t : span * (t + 1)] for t in range(box // SUB)])
         second = jnp.concatenate(second, axis=0).reshape(box, box // SUB, SUB, grid)
@@ -263,12 +266,18 @@
         whole_wave = wave_ref[...]
         wave = jnp.zeros_like(whole_wave)
         weight = jnp.zeros((1, grid), F32)
+        wave_terms = []
         kind = iota((2 * SUB, 1), 0)
         corner = jnp.zeros((2 * SUB, grid), F32)
         for n in range(count):
             number = group * count + n
-            shift = lax.rem(box * n - corner_ref[number, 2] + grid, grid)
-            wave = jnp.where(owner == n, pltpu.roll(whole_wave, shift, 1), wave)
+            every = jnp.zeros_like(whole_wave)
+            for block in range(count):
+                shift = lax.rem(box * block - corner_ref[number, 2] + grid, grid)
+                every = jnp.where(owner == block, pltpu.roll(whole_wave, shift, 1), every)
+            high, low = split(every)
+            wave_terms.append(jnp.where((owner & 1) == 0, high.astype(F32), low.astype(F32)).astype(BF16))
+            wave = jnp.where(owner == n, every, wave)
             weight = jnp.where(owner == n, weight_ref[number], weight)
             place = jnp.where(kind == 0, corner_ref[number, 0], corner_ref[number, 1])
             corner = jnp.where(owner == n, place.astype(F32), corner)
@@ -276,8 +285,7 @@
         sent += start_copies(sems, 6, (own_wave_ref, wave_out_any.at[group]))
         for o in range(plan.orb):
             send_ref[o, plan.area :, :] = corner.astype(send_ref.dtype)
-        high, low = split(wave)
-        wave_terms = jnp.concatenate([high, low, high], axis=1)
+        wave_terms = jnp.concatenate(wave_terms, axis=0)
         if group == 0:
             wait_copies(spectrum)
             folded = fold_spectrum(plan, piece_anys, block_ref, edge_ref, block_out_ref, edge_out_ref, out_sems)
@@ -285,15 +293,15 @@
         sent += start_copies(sems, 7, (send_ref.at[:, rows, :], send_any.at[:, group, rows, :]))
         per_part = plan.quarter // 2
         for pair in range(box // 2):
-            columns = []
-            for b in (2 * pair, 2 * pair + 1):
-                psi = psi_ref[b]
-                density = psi * psi * weight
-                columns.append(jnp.concatenate([jnp.where(owner == n, density, 0.0) for n in range(count)], axis=0))
-            out = dot(wave_terms, terms_of(jnp.concatenate(columns, axis=1), 0))
+            columns = [psi_ref[b] * psi_ref[b] * weight for b in (2 * pair, 2 * pair + 1)]
+            up, down = split(jnp.concatenate(columns, axis=1))
+            out = dot(wave_terms, jnp.concatenate([up, up, down, down], axis=0))
+            mine = out[: plan.rows]
+            for n in range(1, count):
+                mine = jnp.where(owner_pair == n, out[plan.rows * n : plan.rows * (n + 1)], mine)
             for o in range(plan.orb):
-                mine = out[slots * o : slots * (o + 1)]
-                tile = jnp.concatenate([mine[:, :grid], mine[:, grid:]], axis=0)
+                part = mine[slots * o : slots * (o + 1)]
+                tile = jnp.concatenate([part[:, :grid], part[:, grid:]], axis=0)
                 send_ref[o, 2 * slots * pair : 2 * slots * (pair + 1), :] = tile.astype(send_ref.dtype)
             if pair % per_part == per_part - 1:
                 part = pair // per_part
@@ -379,11 +387,11 @@
         return pl.multiple_of(corner_ref[2 * group + 1, box * n] * slots, SUB)
 
     def place(group, carry):
-        values = recv_ref[group, :depth, :].astype(F32)
+        values = recv_ref[group, :depth, :]
         for n in range(count):
             shift = lax.rem(corner_ref[2 * group, box * n] - box * n + grid, grid)
-            moved = pltpu.roll(jnp.where(owner == n, values, 0.0), shift, 1)
-            field_ref[pl.ds(start(group, n), depth), :] += moved
+            moved = pltpu.roll(jnp.where(owner == n, values, jnp.zeros_like(values)), shift, 1)
+            field_ref[pl.ds(start(group, n), depth), :] += moved.astype(F32)
         return carry
 
     lax.fori_loop(0, all_groups, place, 0)
@@ -412,15 +420,15 @@
 
     def cut(d, group, carry):
         number = (own ^ d) * plan.groups + group
-        values = jnp.zeros((depth, grid), F32)
+        values = jnp.zeros((depth, grid), BF16)
         for n in range(count):
             shift = lax.rem(box * n - corner_ref[2 * number, box * n] + grid, grid)
-            rows = result_ref[pl.ds(start(number, n), depth), :]
+            rows = result_ref[pl.ds(start(number, n), depth), :].astype(BF16)
             values = jnp.where(owner == n, pltpu.roll(rows, shift, 1), values)
         if d < 2:
-            (own_ref, swap_ref)[d][group] = values.astype(BF16)
+            (own_ref, swap_ref)[d][group] = values
         else:
-            send_refs[d // 2 - 1][d % 2, group] = values.astype(BF16)
+            send_refs[d // 2 - 1][d % 2, group] = values
         return carry
 
     for d in range(plan.orb):

time: 48.7 us -> 48.4 us (level)
  no operation moved by 1% of the time
where the time goes in v8:
time: 48.4 us; the launch traced here: 48 us
  starting transfers between devices  21 us (43%)
  Pallas kernels  13.9 us (29%)
  waiting for transfers between devices  12.1 us (25%)
  local copies, waits for them, and re-layouts  0.95 us (2%)
    ppermute x3, waiting for transfers between devices, per_device(): lax.ppermute(send[e - 1], 'orb', [(o, o ^ 2 * e) for o in range(orb)])  5.97 us
    ppermute x2, starting transfers between devices, per_device(): lax.ppermute(pieces[half + step], 'pln', [(0, half + step), (half, step)])  5.78 us
    pallas_call x1, Pallas kernels, per_device(): pl.pallas_call(functools.partial(solve_kernel, plan), in_specs=[smem] + [...  5.42 us
    all_to_all x1, starting transfers between devices, per_device(): lax.all_to_all(send, 'orb', split_axis=0, concat_axis=0, tiled=True)  5.31 us
    pallas_call x1, Pallas kernels, per_device(): pl.pallas_call(functools.partial(density_kernel, plan), in_specs=[smem, s...  4.76 us
    ppermute x3, starting transfers between devices, per_device(): lax.ppermute(finished[step], 'pln', [(p, (p + step) % pln) for p in range...  4.67 us
    ppermute x3, waiting for transfers between devices, per_device(): lax.ppermute(finished[step], 'pln', [(p, (p + step) % pln) for p in range...  4.21 us
    ppermute x3, starting transfers between devices, per_device(): lax.ppermute(send[e - 1], 'orb', [(o, o ^ 2 * e) for o in range(orb)])  3.55 us
  transfers between devices with their start and end apart: 11, of which 6 were waited for; matrix products, arithmetic and copies ran while one was open for 0% of the time, Pallas kernels for 3%

profile of v8, /device:TPU:0, one launch (start us, length us, event | category | flops | bytes accessed | tf_op | source)
XLA Modules:
  0.0 48.0 jit_solution(2096153958247078987)
XLA Ops:
  0.0 4.8 %density.1 = (bf16[8,1,272,128]{3,2,1,0:T(8,128)(2,1)}, f32[1,32,32,128]{3,2,1,0:T(8,128)}, f32[1,64,128]{2,1,0:T(8,128)}, f32[64,8,128]{2,1,0:T(8,128)}, f32[64...) custom-call(s32[1]{0:T(128)} %bitcast.where_ref, s32[4,3]{1,0:T(4,128)} %corner_ref.1, f32[4]{0:T(128)} %weight_ref.1, ...), custom_call_target="tpu_custom_call" | custom-call | tf_op jit(solution)/shard_map/density/pallas_call | solution.py:525
  4.8 0.0 copy-start.2
  4.8 5.3 %all-to-all-start = ((bf16[8,1,272,128]{3,2,1,0:T(8,128)(2,1)}), bf16[8,1,272,128]{3,2,1,0:T(8,128)(2,1)S(1)}, u32[]{:S(2)}, u32[]{:S(2)}) async-start(bf16[8,1,272,128]{3,2,1,0:T(8,128)(2,1)} %get-tuple-element.29), calls=%async_computation | async-start | bytes 1114112 | tf_op jit(solution)/shard_map/all_to_all | solution.py:555
  10.1 1.6 %collective-permute-start = (f32[64,8,128]{2,1,0:T(8,128)}, f32[64,8,128]{2,1,0:T(8,128)S(1)}, u32[]{:S(2)}, u32[]{:S(2)}) collective-permute-start(f32[64,8,128]{2,1,0:T(8,128)} %get-tuple-element.32), channel_id=1, source_target_pairs={{0,1},{1,0},{2,3},{3,2},{4,5},{5,4},{6,7},{7,6},{8,9},{9,8},{10,11... | collective-permute-start | bytes 786440 | tf_op jit(solution)/shard_map/ppermute | solution.py:559
  11.7 4.5 %collective-permute-start.1 = (f32[1,8,128]{2,1,0:T(8,128)}, f32[1,8,128]{2,1,0:T(8,128)S(1)}, u32[]{:S(2)}, u32[]{:S(2)}) collective-permute-start(f32[1,8,128]{2,1,0:T(8,128)} %get-tuple-element.33), channel_id=1, source_target_pairs={{0,2},{2,0},{4,6},{6,4},{8,10},{10,8},{12,14},{14,12},{16,18},{18,... | collective-permute-start | bytes 12296 | tf_op jit(solution)/shard_map/ppermute | solution.py:561
  16.2 1.3 %collective-permute-start.2 = (f32[1,8,128]{2,1,0:T(8,128)}, f32[1,8,128]{2,1,0:T(8,128)S(1)}, u32[]{:S(2)}, u32[]{:S(2)}) collective-permute-start(f32[1,8,128]{2,1,0:T(8,128)} %get-tuple-element.34), channel_id=1, source_target_pairs={{0,3},{2,1},{4,7},{6,5},{8,11},{10,9},{12,15},{14,13},{16,19},{18,... | collective-permute-start | bytes 12296 | tf_op jit(solution)/shard_map/ppermute | solution.py:561
  17.5 0.9 %copy-done.1 = f32[64,8,128]{2,1,0:T(8,128)S(1)} copy-done((f32[64,8,128]{2,1,0:T(8,128)S(1)}, f32[64,8,128]{2,1,0:T(8,128)}, u32[]{:S(2)}) %copy-start.1) | copy-done | bytes 262168
  18.4 1.4 %tables.1 = (bf16[256,256]{1,0:T(8,128)(2,1)S(1)}, bf16[256,256]{1,0:T(8,128)(2,1)S(1)}, bf16[128,768]{1,0:T(8,128)(2,1)S(1)}, bf16[768,128]{1,0:T(8,128)(2,1)S(...) custom-call(s32[1]{0:T(128)} %bitcast.where_ref, ...), custom_call_target="tpu_custom_call" | custom-call | tf_op jit(solution)/shard_map/tables/pallas_call | solution.py:568
  19.9 0.4 all-to-all-done
  20.2 5.4 %solve.1 = (bf16[1,256,128]{2,1,0:T(8,128)(2,1)S(1)}, bf16[1,256,128]{2,1,0:T(8,128)(2,1)S(1)}, bf16[2,1,256,128]{3,2,1,0:T(8,128)(2,1)S(1)}, bf16[2,1,256,128]{...) custom-call(s32[1]{0:T(128)} %bitcast.where_ref, bf16[8,272,128]{2,1,0:T(8,128)(2,1)S(1)} %bitcast.7, ...), custom_call_target="tpu_custom_call" | custom-call | tf_op jit(solution)/shard_map/solve/pallas_call | solution.py:580
  25.6 1.7 %collective-permute-start.3 = (bf16[2,1,256,128]{3,2,1,0:T(8,128)(2,1)S(1)}, bf16[2,1,256,128]{3,2,1,0:T(8,128)(2,1)S(1)}, u32[]{:S(2)}, u32[]{:S(2)}) collective-permute-start(bf16[2,1,256,128]{3,2,1,0:T(8,128)(2,1)S(1)} %get-tuple-element.41), channel_id=1, source_target_pairs={{0,8},{4,12},{8,0},{12,4},{16,24},{20,28},{24,16},{28,20},{1,9},{5... | collective-permute-start | bytes 393224 | tf_op jit(solution)/shard_map/ppermute | solution.py:599
  27.4 1.5 %collective-permute-start.4 = (bf16[2,1,256,128]{3,2,1,0:T(8,128)(2,1)S(1)}, bf16[2,1,256,128]{3,2,1,0:T(8,128)(2,1)S(1)}, u32[]{:S(2)}, u32[]{:S(2)}) collective-permute-start(bf16[2,1,256,128]{3,2,1,0:T(8,128)(2,1)S(1)} %get-tuple-element.42), channel_id=1, source_target_pairs={{0,16},{4,20},{8,24},{12,28},{16,0},{20,4},{24,8},{28,12},{1,17},{... | collective-permute-start | bytes 393224 | tf_op jit(solution)/shard_map/ppermute | solution.py:599
  28.8 0.3 collective-permute-start.5
  29.2 2.1 %collective-permute-done.3.refs_0_.refs_2_ = bf16[2,1,256,128]{3,2,1,0:T(8,128)(2,1)S(1)} collective-permute-done((bf16[2,1,256,128]{3,2,1,0:T(8,128)(2,1)S(1)}, bf16[2,1,256,128]{3,2,1,0:T(8,128)(2,1)S(1)}, u32[]{:S(2)}, u32[]{:S(2)}) %collective-permute-start.3) | collective-permute-done | bytes 131104 | tf_op jit(solution)/shard_map/ppermute | solution.py:599
  31.3 3.8 %collective-permute-done.4.refs_1_.refs_3_ = bf16[2,1,256,128]{3,2,1,0:T(8,128)(2,1)S(1)} collective-permute-done((bf16[2,1,256,128]{3,2,1,0:T(8,128)(2,1)S(1)}, bf16[2,1,256,128]{3,2,1,0:T(8,128)(2,1)S(1)}, u32[]{:S(2)}, u32[]{:S(2)}) %collective-permute-start.4) | collective-permute-done | bytes 131104 | tf_op jit(solution)/shard_map/ppermute | solution.py:599
  35.2 0.1 collective-permute-start.6
  35.3 1.5 %collective-permute-done.6.refs_1_ = bf16[4,1,256,128]{3,2,1,0:T(8,128)(2,1)S(1)} collective-permute-done((bf16[4,1,256,128]{3,2,1,0:T(8,128)(2,1)S(1)}, bf16[4,1,256,128]{3,2,1,0:T(8,128)(2,1)S(1)}, u32[]{:S(2)}, u32[]{:S(2)}) %collective-permute-start.6) | collective-permute-done | bytes 262176 | tf_op jit(solution)/shard_map/ppermute | solution.py:608
  36.8 1.7 %terms.1 = (f32[1,32,1024]{2,1,0:T(8,128)S(1)}, bf16[1,32,1024]{2,1,0:T(8,128)(2,1)S(1)}, bf16[1,32,1024]{2,1,0:T(8,128)(2,1)S(1)}, bf16[1,32,1024]{2,1,0:T(8,128)(2,1)S(1)}) custom-call(s32[1]{0:T(128)} %bitcast.where_ref, bf16[1,256,128]{2,1,0:T(8,128)(2,1)S(1)} %get-tuple-element.39.refs_0_, bf16[4,1,256,128]{3,2,1,0:T(8,128)(2,1)S(1)} %collective-permute-done.6.refs_1_, ...), custom_call_target="tpu_custom_call" | custom-call | tf_op jit(solution)/shard_map/terms/pallas_call | solution.py:610
  38.5 0.7 %collective-permute-start.7 = (bf16[1,32,1024]{2,1,0:T(8,128)(2,1)S(1)}, bf16[1,32,1024]{2,1,0:T(8,128)(2,1)S(1)}, u32[]{:S(2)}, u32[]{:S(2)}) collective-permute-start(bf16[1,32,1024]{2,1,0:T(8,128)(2,1)S(1)} %get-tuple-element.50), channel_id=1, source_target_pairs={{0,1},{1,2},{2,3},{3,0},{4,5},{5,6},{6,7},{7,4},{8,9},{9,10},{10,1... | collective-permute-start | bytes 196616 | tf_op jit(solution)/shard_map/ppermute | solution.py:637
  39.2 2.9 %collective-permute-start.8 = (bf16[1,32,1024]{2,1,0:T(8,128)(2,1)S(1)}, bf16[1,32,1024]{2,1,0:T(8,128)(2,1)S(1)}, u32[]{:S(2)}, u32[]{:S(2)}) collective-permute-start(bf16[1,32,1024]{2,1,0:T(8,128)(2,1)S(1)} %get-tuple-element.51), channel_id=1, source_target_pairs={{0,2},{1,3},{2,0},{3,1},{4,6},{5,7},{6,4},{7,5},{8,10},{9,11},{10,... | collective-permute-start | bytes 196616 | tf_op jit(solution)/shard_map/ppermute | solution.py:637
  42.1 1.0 %collective-permute-start.9 = (bf16[1,32,1024]{2,1,0:T(8,128)(2,1)S(1)}, bf16[1,32,1024]{2,1,0:T(8,128)(2,1)S(1)}, u32[]{:S(2)}, u32[]{:S(2)}) collective-permute-start(bf16[1,32,1024]{2,1,0:T(8,128)(2,1)S(1)} %get-tuple-element.52), channel_id=1, source_target_pairs={{0,3},{1,0},{2,1},{3,2},{4,7},{5,4},{6,5},{7,6},{8,11},{9,8},{10,9... | collective-permute-start | bytes 196616 | tf_op jit(solution)/shard_map/ppermute | solution.py:637
  43.1 2.3 %collective-permute-done.7.refs_1_ = bf16[1,32,1024]{2,1,0:T(8,128)(2,1)S(1)} collective-permute-done((bf16[1,32,1024]{2,1,0:T(8,128)(2,1)S(1)}, bf16[1,32,1024]{2,1,0:T(8,128)(2,1)S(1)}, u32[]{:S(2)}, u32[]{:S(2)}) %collective-permute-start.7) | collective-permute-done | bytes 65568 | tf_op jit(solution)/shard_map/ppermute | solution.py:637
  45.4 1.9 %collective-permute-done.8.refs_2_ = bf16[1,32,1024]{2,1,0:T(8,128)(2,1)S(1)} collective-permute-done((bf16[1,32,1024]{2,1,0:T(8,128)(2,1)S(1)}, bf16[1,32,1024]{2,1,0:T(8,128)(2,1)S(1)}, u32[]{:S(2)}, u32[]{:S(2)}) %collective-permute-start.8) | collective-permute-done | bytes 65568 | tf_op jit(solution)/shard_map/ppermute | solution.py:637
  47.4 0.7 %sum.1 = bf16[1,4,8192]{2,1,0:T(4,128)(2,1)} custom-call(f32[1,32,1024]{2,1,0:T(8,128)S(1)} %get-tuple-element.49.refs_0_, bf16[1,32,1024]{2,1,0:T(8,128)(2,1)S(1)} %collective-permute-done.7.refs_1_, bf16[1,32,1024]{2,1,0:T(8,128)(2,1)S(1)} %collective-permute-done.8.refs_2_, bf16[1,32,1024]{2,1,0:T(8,128)(2,1)S(1)} %collective-permute-done.9.refs_3_), custom_call_target="tpu_custom_call" | custom-call | tf_op jit(solution)/shard_map/sum/pallas_call | solution.py:639
  (10 shorter events, 0.0 us)
Async XLA Ops:
  4.8 32.0 %copy-start = (f32[1,32,32,128]{3,2,1,0:T(8,128)S(1)}, f32[1,32,32,128]{3,2,1,0:T(8,128)}, u32[]{:S(2)}) copy-start(f32[1,32,32,128]{3,2,1,0:T(8,128)} %get-tuple-element.44.refs_5_) | copy-start | bytes 1572868
  4.8 32.0 %copy-start.2 = (f32[1,64,128]{2,1,0:T(8,128)S(1)}, f32[1,64,128]{2,1,0:T(8,128)}, u32[]{:S(2)}) copy-start(f32[1,64,128]{2,1,0:T(8,128)} %get-tuple-element.45.refs_6_) | copy-start | bytes 98308
  4.8 15.4 %all-to-all-start = ((bf16[8,1,272,128]{3,2,1,0:T(8,128)(2,1)}), bf16[8,1,272,128]{3,2,1,0:T(8,128)(2,1)S(1)}, u32[]{:S(2)}, u32[]{:S(2)}) async-start(bf16[8,1,272,128]{3,2,1,0:T(8,128)(2,1)} %get-tuple-element.29), calls=%async_computation | async-start | bytes 1114112 | tf_op jit(solution)/shard_map/all_to_all | solution.py:555
  10.1 9.7 %collective-permute-start = (f32[64,8,128]{2,1,0:T(8,128)}, f32[64,8,128]{2,1,0:T(8,128)S(1)}, u32[]{:S(2)}, u32[]{:S(2)}) collective-permute-start(f32[64,8,128]{2,1,0:T(8,128)} %get-tuple-element.32), channel_id=1, source_target_pairs={{0,1},{1,0},{2,3},{3,2},{4,5},{5,4},{6,7},{7,6},{8,9},{9,8},{10,11... | collective-permute-start | bytes 786440 | tf_op jit(solution)/shard_map/ppermute | solution.py:559
  11.7 8.1 %collective-permute-start.1 = (f32[1,8,128]{2,1,0:T(8,128)}, f32[1,8,128]{2,1,0:T(8,128)S(1)}, u32[]{:S(2)}, u32[]{:S(2)}) collective-permute-start(f32[1,8,128]{2,1,0:T(8,128)} %get-tuple-element.33), channel_id=1, source_target_pairs={{0,2},{2,0},{4,6},{6,4},{8,10},{10,8},{12,14},{14,12},{16,18},{18,... | collective-permute-start | bytes 12296 | tf_op jit(solution)/shard_map/ppermute | solution.py:561
  16.2 3.7 %collective-permute-start.2 = (f32[1,8,128]{2,1,0:T(8,128)}, f32[1,8,128]{2,1,0:T(8,128)S(1)}, u32[]{:S(2)}, u32[]{:S(2)}) collective-permute-start(f32[1,8,128]{2,1,0:T(8,128)} %get-tuple-element.34), channel_id=1, source_target_pairs={{0,3},{2,1},{4,7},{6,5},{8,11},{10,9},{12,15},{14,13},{16,19},{18,... | collective-permute-start | bytes 12296 | tf_op jit(solution)/shard_map/ppermute | solution.py:561
  17.5 1.0 %copy-start.1 = (f32[64,8,128]{2,1,0:T(8,128)S(1)}, f32[64,8,128]{2,1,0:T(8,128)}, u32[]{:S(2)}) copy-start(f32[64,8,128]{2,1,0:T(8,128)} %get-tuple-element.30) | copy-start | bytes 786436
  25.6 5.7 %collective-permute-start.3 = (bf16[2,1,256,128]{3,2,1,0:T(8,128)(2,1)S(1)}, bf16[2,1,256,128]{3,2,1,0:T(8,128)(2,1)S(1)}, u32[]{:S(2)}, u32[]{:S(2)}) collective-permute-start(bf16[2,1,256,128]{3,2,1,0:T(8,128)(2,1)S(1)} %get-tuple-element.41), channel_id=1, source_target_pairs={{0,8},{4,12},{8,0},{12,4},{16,24},{20,28},{24,16},{28,20},{1,9},{5... | collective-permute-start | bytes 393224 | tf_op jit(solution)/shard_map/ppermute | solution.py:599
  27.4 7.8 %collective-permute-start.4 = (bf16[2,1,256,128]{3,2,1,0:T(8,128)(2,1)S(1)}, bf16[2,1,256,128]{3,2,1,0:T(8,128)(2,1)S(1)}, u32[]{:S(2)}, u32[]{:S(2)}) collective-permute-start(bf16[2,1,256,128]{3,2,1,0:T(8,128)(2,1)S(1)} %get-tuple-element.42), channel_id=1, source_target_pairs={{0,16},{4,20},{8,24},{12,28},{16,0},{20,4},{24,8},{28,12},{1,17},{... | collective-permute-start | bytes 393224 | tf_op jit(solution)/shard_map/ppermute | solution.py:599
  28.8 6.3 %collective-permute-start.5 = (bf16[2,1,256,128]{3,2,1,0:T(8,128)(2,1)S(1)}, bf16[2,1,256,128]{3,2,1,0:T(8,128)(2,1)S(1)}, u32[]{:S(2)}, u32[]{:S(2)}) collective-permute-start(bf16[2,1,256,128]{3,2,1,0:T(8,128)(2,1)S(1)} %get-tuple-element.43), channel_id=1, source_target_pairs={{0,24},{4,28},{8,16},{12,20},{16,8},{20,12},{24,0},{28,4},{1,25},{... | collective-permute-start | bytes 393224 | tf_op jit(solution)/shard_map/ppermute | solution.py:599
  35.2 1.6 %collective-permute-start.6 = (bf16[4,1,256,128]{3,2,1,0:T(8,128)(2,1)S(1)}, bf16[4,1,256,128]{3,2,1,0:T(8,128)(2,1)S(1)}, u32[]{:S(2)}, u32[]{:S(2)}) collective-permute-start(bf16[4,1,256,128]{3,2,1,0:T(8,128)(2,1)S(1)} %gather.1), channel_id=1, source_target_pairs={{0,4},{4,0},{8,12},{12,8},{16,20},{20,16},{24,28},{28,24},{1,5},{5... | collective-permute-start | bytes 786440 | tf_op jit(solution)/shard_map/ppermute | solution.py:608
  38.5 6.9 %collective-permute-start.7 = (bf16[1,32,1024]{2,1,0:T(8,128)(2,1)S(1)}, bf16[1,32,1024]{2,1,0:T(8,128)(2,1)S(1)}, u32[]{:S(2)}, u32[]{:S(2)}) collective-permute-start(bf16[1,32,1024]{2,1,0:T(8,128)(2,1)S(1)} %get-tuple-element.50), channel_id=1, source_target_pairs={{0,1},{1,2},{2,3},{3,0},{4,5},{5,6},{6,7},{7,4},{8,9},{9,10},{10,1... | collective-permute-start | bytes 196616 | tf_op jit(solution)/shard_map/ppermute | solution.py:637
  39.2 8.2 %collective-permute-start.8 = (bf16[1,32,1024]{2,1,0:T(8,128)(2,1)S(1)}, bf16[1,32,1024]{2,1,0:T(8,128)(2,1)S(1)}, u32[]{:S(2)}, u32[]{:S(2)}) collective-permute-start(bf16[1,32,1024]{2,1,0:T(8,128)(2,1)S(1)} %get-tuple-element.51), channel_id=1, source_target_pairs={{0,2},{1,3},{2,0},{3,1},{4,6},{5,7},{6,4},{7,5},{8,10},{9,11},{10,... | collective-permute-start | bytes 196616 | tf_op jit(solution)/shard_map/ppermute | solution.py:637
  42.1 5.2 %collective-permute-start.9 = (bf16[1,32,1024]{2,1,0:T(8,128)(2,1)S(1)}, bf16[1,32,1024]{2,1,0:T(8,128)(2,1)S(1)}, u32[]{:S(2)}, u32[]{:S(2)}) collective-permute-start(bf16[1,32,1024]{2,1,0:T(8,128)(2,1)S(1)} %get-tuple-element.52), channel_id=1, source_target_pairs={{0,3},{1,0},{2,1},{3,2},{4,7},{5,4},{6,5},{7,6},{8,11},{9,8},{10,9... | collective-permute-start | bytes 196616 | tf_op jit(solution)/shard_map/ppermute | solution.py:637

commit v9 on v8

--- a/solution.py
+++ b/solution.py
@@ -394,29 +394,36 @@
             field_ref[pl.ds(start(group, n), depth), :] += moved.astype(F32)
         return carry
 
-    lax.fori_loop(0, all_groups, place, 0)
+    if plan.groups == 1:
+        for group in range(all_groups):
+            place(group, 0)
+    else:
+        lax.fori_loop(0, all_groups, place, 0)
     row = iota((grid, 1), 0)
     edge_row = lax.rem(me, half) * plan.ky_block
     edges = edge_refs[0][0]
     for ref in edge_refs[1:]:
         edges = edges + ref[0]
-    for pair in range(slots // 2):
-        both = (2 * pair, 2 * pair + 1)
-        planes = jnp.concatenate([field_ref[pl.ds(s, grid, stride=slots), :] for s in both], axis=1)
-        planes = planes.astype(BF16)
-        modes = dot(forward_y, jnp.concatenate([planes, planes], axis=0)).astype(BF16)
-        back = []
-        for side, s in enumerate(both):
+    batch = slots // 2
+    for first in range(0, slots, batch):
+        rows, spectra = [], []
+        for s in range(first, first + batch, 2):
+            planes = [field_ref[pl.ds(t, grid, stride=slots), :] for t in (s, s + 1)]
+            planes = jnp.concatenate(planes, axis=1).astype(BF16)
+            modes = dot(forward_y, jnp.concatenate([planes, planes], axis=0)).astype(BF16)
+            rows += [modes[:, :grid], modes[:, grid:]]
+        for s in range(first, first + batch):
             spectrum = jnp.concatenate([ref[pl.ds(s, plan.ky_block, stride=slots), :] for ref in piece_refs], axis=0)
-            other = jnp.where(row == edge_row, edges[s : s + 1], spectrum)
-            spectrum = jnp.concatenate([spectrum, other], axis=0)
-            mine = modes[:, grid * side : grid * (side + 1)]
-            mine = dot(jnp.concatenate([mine, mine], axis=1), forward_z)
-            mine = mine * jnp.concatenate([spectrum, spectrum], axis=1)
-            back.append(dot(terms_of(mine, 1), inverse_z))
-        planes = dot(inverse_y, terms_of(jnp.concatenate(back, axis=1), 0))
-        for side, s in enumerate(both):
-            result_ref[pl.ds(s, grid, stride=slots), :] = planes[:, grid * side : grid * (side + 1)]
+            spectra += [spectrum, jnp.where(row == edge_row, edges[s : s + 1], spectrum)]
+        rows, spectra = jnp.concatenate(rows, axis=0), jnp.concatenate(spectra, axis=0)
+        modes = dot(jnp.concatenate([rows, rows], axis=1), forward_z) * jnp.concatenate([spectra, spectra], axis=1)
+        back = dot(terms_of(modes, 1), inverse_z)
+        for t in range(0, batch, 2):
+            size = 2 * grid
+            both = [back[size * u : size * (u + 1)] for u in (t, t + 1)]
+            planes = dot(inverse_y, terms_of(jnp.concatenate(both, axis=1), 0))
+            for side in range(2):
+                result_ref[pl.ds(first + t + side, grid, stride=slots), :] = planes[:, grid * side : grid * (side + 1)]
 
     def cut(d, group, carry):
         number = (own ^ d) * plan.groups + group

time: 48.4 us -> 47.4 us (0.979)
  Pallas kernels: 13.9 us -> 13 us
    pallas_call x1, Pallas kernels: 5.42 us -> 4.47 us  [per_device(): pl.pallas_call(functools.partial(solve_kernel, plan), in_specs=[smem] + [...]
where the time goes in v9:
time: 47.4 us; the launch traced here: 47.1 us
  starting transfers between devices  21 us (44%)
  Pallas kernels  13 us (27%)
  waiting for transfers between devices  12.1 us (26%)
  local copies, waits for them, and re-layouts  0.95 us (2%)
    ppermute x3, waiting for transfers between devices, per_device(): lax.ppermute(send[e - 1], 'orb', [(o, o ^ 2 * e) for o in range(orb)])  5.98 us
    ppermute x2, starting transfers between devices, per_device(): lax.ppermute(pieces[half + step], 'pln', [(0, half + step), (half, step)])  5.78 us
    all_to_all x1, starting transfers between devices, per_device(): lax.all_to_all(send, 'orb', split_axis=0, concat_axis=0, tiled=True)  5.31 us
    pallas_call x1, Pallas kernels, per_device(): pl.pallas_call(functools.partial(density_kernel, plan), in_specs=[smem, s...  4.76 us
    ppermute x3, starting transfers between devices, per_device(): lax.ppermute(finished[step], 'pln', [(p, (p + step) % pln) for p in range...  4.67 us
    pallas_call x1, Pallas kernels, per_device(): pl.pallas_call(functools.partial(solve_kernel, plan), in_specs=[smem] + [...  4.47 us
    ppermute x3, waiting for transfers between devices, per_device(): lax.ppermute(finished[step], 'pln', [(p, (p + step) % pln) for p in range...  4.22 us
    ppermute x3, starting transfers between devices, per_device(): lax.ppermute(send[e - 1], 'orb', [(o, o ^ 2 * e) for o in range(orb)])  3.55 us
  transfers between devices with their start and end apart: 11, of which 6 were waited for; matrix products, arithmetic and copies ran while one was open for 0% of the time, Pallas kernels for 3%

profile of v9, /device:TPU:0, one launch (start us, length us, event | category | flops | bytes accessed | tf_op | source)
XLA Modules:
  0.0 47.1 jit_solution(16330054705239340394)
XLA Ops:
  0.0 4.8 %density.1 = (bf16[8,1,272,128]{3,2,1,0:T(8,128)(2,1)}, f32[1,32,32,128]{3,2,1,0:T(8,128)}, f32[1,64,128]{2,1,0:T(8,128)}, f32[64,8,128]{2,1,0:T(8,128)}, f32[64...) custom-call(s32[1]{0:T(128)} %bitcast.where_ref, s32[4,3]{1,0:T(4,128)} %corner_ref.1, f32[4]{0:T(128)} %weight_ref.1, ...), custom_call_target="tpu_custom_call" | custom-call | tf_op jit(solution)/shard_map/density/pallas_call | solution.py:532
  4.8 0.0 copy-start.2
  4.8 5.3 %all-to-all-start = ((bf16[8,1,272,128]{3,2,1,0:T(8,128)(2,1)}), bf16[8,1,272,128]{3,2,1,0:T(8,128)(2,1)S(1)}, u32[]{:S(2)}, u32[]{:S(2)}) async-start(bf16[8,1,272,128]{3,2,1,0:T(8,128)(2,1)} %get-tuple-element.29), calls=%async_computation | async-start | bytes 1114112 | tf_op jit(solution)/shard_map/all_to_all | solution.py:562
  10.1 1.6 %collective-permute-start = (f32[64,8,128]{2,1,0:T(8,128)}, f32[64,8,128]{2,1,0:T(8,128)S(1)}, u32[]{:S(2)}, u32[]{:S(2)}) collective-permute-start(f32[64,8,128]{2,1,0:T(8,128)} %get-tuple-element.32), channel_id=1, source_target_pairs={{0,1},{1,0},{2,3},{3,2},{4,5},{5,4},{6,7},{7,6},{8,9},{9,8},{10,11... | collective-permute-start | bytes 786440 | tf_op jit(solution)/shard_map/ppermute | solution.py:566
  11.7 4.5 %collective-permute-start.1 = (f32[1,8,128]{2,1,0:T(8,128)}, f32[1,8,128]{2,1,0:T(8,128)S(1)}, u32[]{:S(2)}, u32[]{:S(2)}) collective-permute-start(f32[1,8,128]{2,1,0:T(8,128)} %get-tuple-element.33), channel_id=1, source_target_pairs={{0,2},{2,0},{4,6},{6,4},{8,10},{10,8},{12,14},{14,12},{16,18},{18,... | collective-permute-start | bytes 12296 | tf_op jit(solution)/shard_map/ppermute | solution.py:568
  16.2 1.3 %collective-permute-start.2 = (f32[1,8,128]{2,1,0:T(8,128)}, f32[1,8,128]{2,1,0:T(8,128)S(1)}, u32[]{:S(2)}, u32[]{:S(2)}) collective-permute-start(f32[1,8,128]{2,1,0:T(8,128)} %get-tuple-element.34), channel_id=1, source_target_pairs={{0,3},{2,1},{4,7},{6,5},{8,11},{10,9},{12,15},{14,13},{16,19},{18,... | collective-permute-start | bytes 12296 | tf_op jit(solution)/shard_map/ppermute | solution.py:568
  17.5 0.9 %copy-done.1 = f32[64,8,128]{2,1,0:T(8,128)S(1)} copy-done((f32[64,8,128]{2,1,0:T(8,128)S(1)}, f32[64,8,128]{2,1,0:T(8,128)}, u32[]{:S(2)}) %copy-start.1) | copy-done | bytes 262168
  18.4 1.4 %tables.1 = (bf16[256,256]{1,0:T(8,128)(2,1)S(1)}, bf16[256,256]{1,0:T(8,128)(2,1)S(1)}, bf16[128,768]{1,0:T(8,128)(2,1)S(1)}, bf16[768,128]{1,0:T(8,128)(2,1)S(...) custom-call(s32[1]{0:T(128)} %bitcast.where_ref, ...), custom_call_target="tpu_custom_call" | custom-call | tf_op jit(solution)/shard_map/tables/pallas_call | solution.py:575
  19.9 0.4 all-to-all-done
  20.2 4.5 %solve.1 = (bf16[1,256,128]{2,1,0:T(8,128)(2,1)S(1)}, bf16[1,256,128]{2,1,0:T(8,128)(2,1)S(1)}, bf16[2,1,256,128]{3,2,1,0:T(8,128)(2,1)S(1)}, bf16[2,1,256,128]{...) custom-call(s32[1]{0:T(128)} %bitcast.where_ref, bf16[8,272,128]{2,1,0:T(8,128)(2,1)S(1)} %bitcast.7, ...), custom_call_target="tpu_custom_call" | custom-call | tf_op jit(solution)/shard_map/solve/pallas_call | solution.py:587
  24.7 1.8 %collective-permute-start.3 = (bf16[2,1,256,128]{3,2,1,0:T(8,128)(2,1)S(1)}, bf16[2,1,256,128]{3,2,1,0:T(8,128)(2,1)S(1)}, u32[]{:S(2)}, u32[]{:S(2)}) collective-permute-start(bf16[2,1,256,128]{3,2,1,0:T(8,128)(2,1)S(1)} %get-tuple-element.41), channel_id=1, source_target_pairs={{0,8},{4,12},{8,0},{12,4},{16,24},{20,28},{24,16},{28,20},{1,9},{5... | collective-permute-start | bytes 393224 | tf_op jit(solution)/shard_map/ppermute | solution.py:606
  26.4 1.5 %collective-permute-start.4 = (bf16[2,1,256,128]{3,2,1,0:T(8,128)(2,1)S(1)}, bf16[2,1,256,128]{3,2,1,0:T(8,128)(2,1)S(1)}, u32[]{:S(2)}, u32[]{:S(2)}) collective-permute-start(bf16[2,1,256,128]{3,2,1,0:T(8,128)(2,1)S(1)} %get-tuple-element.42), channel_id=1, source_target_pairs={{0,16},{4,20},{8,24},{12,28},{16,0},{20,4},{24,8},{28,12},{1,17},{... | collective-permute-start | bytes 393224 | tf_op jit(solution)/shard_map/ppermute | solution.py:606
  27.9 0.3 collective-permute-start.5
  28.2 2.1 %collective-permute-done.3.refs_0_.refs_2_ = bf16[2,1,256,128]{3,2,1,0:T(8,128)(2,1)S(1)} collective-permute-done((bf16[2,1,256,128]{3,2,1,0:T(8,128)(2,1)S(1)}, bf16[2,1,256,128]{3,2,1,0:T(8,128)(2,1)S(1)}, u32[]{:S(2)}, u32[]{:S(2)}) %collective-permute-start.3) | collective-permute-done | bytes 131104 | tf_op jit(solution)/shard_map/ppermute | solution.py:606
  30.4 3.8 %collective-permute-done.4.refs_1_.refs_3_ = bf16[2,1,256,128]{3,2,1,0:T(8,128)(2,1)S(1)} collective-permute-done((bf16[2,1,256,128]{3,2,1,0:T(8,128)(2,1)S(1)}, bf16[2,1,256,128]{3,2,1,0:T(8,128)(2,1)S(1)}, u32[]{:S(2)}, u32[]{:S(2)}) %collective-permute-start.4) | collective-permute-done | bytes 131104 | tf_op jit(solution)/shard_map/ppermute | solution.py:606
  34.2 0.1 collective-permute-start.6
  34.3 1.5 %collective-permute-done.6.refs_1_ = bf16[4,1,256,128]{3,2,1,0:T(8,128)(2,1)S(1)} collective-permute-done((bf16[4,1,256,128]{3,2,1,0:T(8,128)(2,1)S(1)}, bf16[4,1,256,128]{3,2,1,0:T(8,128)(2,1)S(1)}, u32[]{:S(2)}, u32[]{:S(2)}) %collective-permute-start.6) | collective-permute-done | bytes 262176 | tf_op jit(solution)/shard_map/ppermute | solution.py:615
  35.8 1.7 %terms.1 = (f32[1,32,1024]{2,1,0:T(8,128)S(1)}, bf16[1,32,1024]{2,1,0:T(8,128)(2,1)S(1)}, bf16[1,32,1024]{2,1,0:T(8,128)(2,1)S(1)}, bf16[1,32,1024]{2,1,0:T(8,128)(2,1)S(1)}) custom-call(s32[1]{0:T(128)} %bitcast.where_ref, bf16[1,256,128]{2,1,0:T(8,128)(2,1)S(1)} %get-tuple-element.39.refs_0_, bf16[4,1,256,128]{3,2,1,0:T(8,128)(2,1)S(1)} %collective-permute-done.6.refs_1_, ...), custom_call_target="tpu_custom_call" | custom-call | tf_op jit(solution)/shard_map/terms/pallas_call | solution.py:617
  37.5 0.7 %collective-permute-start.7 = (bf16[1,32,1024]{2,1,0:T(8,128)(2,1)S(1)}, bf16[1,32,1024]{2,1,0:T(8,128)(2,1)S(1)}, u32[]{:S(2)}, u32[]{:S(2)}) collective-permute-start(bf16[1,32,1024]{2,1,0:T(8,128)(2,1)S(1)} %get-tuple-element.50), channel_id=1, source_target_pairs={{0,1},{1,2},{2,3},{3,0},{4,5},{5,6},{6,7},{7,4},{8,9},{9,10},{10,1... | collective-permute-start | bytes 196616 | tf_op jit(solution)/shard_map/ppermute | solution.py:644
  38.3 2.9 %collective-permute-start.8 = (bf16[1,32,1024]{2,1,0:T(8,128)(2,1)S(1)}, bf16[1,32,1024]{2,1,0:T(8,128)(2,1)S(1)}, u32[]{:S(2)}, u32[]{:S(2)}) collective-permute-start(bf16[1,32,1024]{2,1,0:T(8,128)(2,1)S(1)} %get-tuple-element.51), channel_id=1, source_target_pairs={{0,2},{1,3},{2,0},{3,1},{4,6},{5,7},{6,4},{7,5},{8,10},{9,11},{10,... | collective-permute-start | bytes 196616 | tf_op jit(solution)/shard_map/ppermute | solution.py:644
  41.2 1.0 %collective-permute-start.9 = (bf16[1,32,1024]{2,1,0:T(8,128)(2,1)S(1)}, bf16[1,32,1024]{2,1,0:T(8,128)(2,1)S(1)}, u32[]{:S(2)}, u32[]{:S(2)}) collective-permute-start(bf16[1,32,1024]{2,1,0:T(8,128)(2,1)S(1)} %get-tuple-element.52), channel_id=1, source_target_pairs={{0,3},{1,0},{2,1},{3,2},{4,7},{5,4},{6,5},{7,6},{8,11},{9,8},{10,9... | collective-permute-start | bytes 196616 | tf_op jit(solution)/shard_map/ppermute | solution.py:644
  42.2 2.3 %collective-permute-done.7.refs_1_ = bf16[1,32,1024]{2,1,0:T(8,128)(2,1)S(1)} collective-permute-done((bf16[1,32,1024]{2,1,0:T(8,128)(2,1)S(1)}, bf16[1,32,1024]{2,1,0:T(8,128)(2,1)S(1)}, u32[]{:S(2)}, u32[]{:S(2)}) %collective-permute-start.7) | collective-permute-done | bytes 65568 | tf_op jit(solution)/shard_map/ppermute | solution.py:644
  44.5 2.0 %collective-permute-done.8.refs_2_ = bf16[1,32,1024]{2,1,0:T(8,128)(2,1)S(1)} collective-permute-done((bf16[1,32,1024]{2,1,0:T(8,128)(2,1)S(1)}, bf16[1,32,1024]{2,1,0:T(8,128)(2,1)S(1)}, u32[]{:S(2)}, u32[]{:S(2)}) %collective-permute-start.8) | collective-permute-done | bytes 65568 | tf_op jit(solution)/shard_map/ppermute | solution.py:644
  46.4 0.7 %sum.1 = bf16[1,4,8192]{2,1,0:T(4,128)(2,1)} custom-call(f32[1,32,1024]{2,1,0:T(8,128)S(1)} %get-tuple-element.49.refs_0_, bf16[1,32,1024]{2,1,0:T(8,128)(2,1)S(1)} %collective-permute-done.7.refs_1_, bf16[1,32,1024]{2,1,0:T(8,128)(2,1)S(1)} %collective-permute-done.8.refs_2_, bf16[1,32,1024]{2,1,0:T(8,128)(2,1)S(1)} %collective-permute-done.9.refs_3_), custom_call_target="tpu_custom_call" | custom-call | tf_op jit(solution)/shard_map/sum/pallas_call | solution.py:646
  (10 shorter events, 0.0 us)
Async XLA Ops:
  4.8 31.1 %copy-start = (f32[1,32,32,128]{3,2,1,0:T(8,128)S(1)}, f32[1,32,32,128]{3,2,1,0:T(8,128)}, u32[]{:S(2)}) copy-start(f32[1,32,32,128]{3,2,1,0:T(8,128)} %get-tuple-element.44.refs_5_) | copy-start | bytes 1572868
  4.8 31.1 %copy-start.2 = (f32[1,64,128]{2,1,0:T(8,128)S(1)}, f32[1,64,128]{2,1,0:T(8,128)}, u32[]{:S(2)}) copy-start(f32[1,64,128]{2,1,0:T(8,128)} %get-tuple-element.45.refs_6_) | copy-start | bytes 98308
  4.8 15.4 %all-to-all-start = ((bf16[8,1,272,128]{3,2,1,0:T(8,128)(2,1)}), bf16[8,1,272,128]{3,2,1,0:T(8,128)(2,1)S(1)}, u32[]{:S(2)}, u32[]{:S(2)}) async-start(bf16[8,1,272,128]{3,2,1,0:T(8,128)(2,1)} %get-tuple-element.29), calls=%async_computation | async-start | bytes 1114112 | tf_op jit(solution)/shard_map/all_to_all | solution.py:562
  10.1 9.7 %collective-permute-start = (f32[64,8,128]{2,1,0:T(8,128)}, f32[64,8,128]{2,1,0:T(8,128)S(1)}, u32[]{:S(2)}, u32[]{:S(2)}) collective-permute-start(f32[64,8,128]{2,1,0:T(8,128)} %get-tuple-element.32), channel_id=1, source_target_pairs={{0,1},{1,0},{2,3},{3,2},{4,5},{5,4},{6,7},{7,6},{8,9},{9,8},{10,11... | collective-permute-start | bytes 786440 | tf_op jit(solution)/shard_map/ppermute | solution.py:566
  11.7 8.1 %collective-permute-start.1 = (f32[1,8,128]{2,1,0:T(8,128)}, f32[1,8,128]{2,1,0:T(8,128)S(1)}, u32[]{:S(2)}, u32[]{:S(2)}) collective-permute-start(f32[1,8,128]{2,1,0:T(8,128)} %get-tuple-element.33), channel_id=1, source_target_pairs={{0,2},{2,0},{4,6},{6,4},{8,10},{10,8},{12,14},{14,12},{16,18},{18,... | collective-permute-start | bytes 12296 | tf_op jit(solution)/shard_map/ppermute | solution.py:568
  16.2 3.7 %collective-permute-start.2 = (f32[1,8,128]{2,1,0:T(8,128)}, f32[1,8,128]{2,1,0:T(8,128)S(1)}, u32[]{:S(2)}, u32[]{:S(2)}) collective-permute-start(f32[1,8,128]{2,1,0:T(8,128)} %get-tuple-element.34), channel_id=1, source_target_pairs={{0,3},{2,1},{4,7},{6,5},{8,11},{10,9},{12,15},{14,13},{16,19},{18,... | collective-permute-start | bytes 12296 | tf_op jit(solution)/shard_map/ppermute | solution.py:568
  17.5 1.0 %copy-start.1 = (f32[64,8,128]{2,1,0:T(8,128)S(1)}, f32[64,8,128]{2,1,0:T(8,128)}, u32[]{:S(2)}) copy-start(f32[64,8,128]{2,1,0:T(8,128)} %get-tuple-element.30) | copy-start | bytes 786436
  24.7 5.7 %collective-permute-start.3 = (bf16[2,1,256,128]{3,2,1,0:T(8,128)(2,1)S(1)}, bf16[2,1,256,128]{3,2,1,0:T(8,128)(2,1)S(1)}, u32[]{:S(2)}, u32[]{:S(2)}) collective-permute-start(bf16[2,1,256,128]{3,2,1,0:T(8,128)(2,1)S(1)} %get-tuple-element.41), channel_id=1, source_target_pairs={{0,8},{4,12},{8,0},{12,4},{16,24},{20,28},{24,16},{28,20},{1,9},{5... | collective-permute-start | bytes 393224 | tf_op jit(solution)/shard_map/ppermute | solution.py:606
  26.4 7.8 %collective-permute-start.4 = (bf16[2,1,256,128]{3,2,1,0:T(8,128)(2,1)S(1)}, bf16[2,1,256,128]{3,2,1,0:T(8,128)(2,1)S(1)}, u32[]{:S(2)}, u32[]{:S(2)}) collective-permute-start(bf16[2,1,256,128]{3,2,1,0:T(8,128)(2,1)S(1)} %get-tuple-element.42), channel_id=1, source_target_pairs={{0,16},{4,20},{8,24},{12,28},{16,0},{20,4},{24,8},{28,12},{1,17},{... | collective-permute-start | bytes 393224 | tf_op jit(solution)/shard_map/ppermute | solution.py:606
  27.9 6.3 %collective-permute-start.5 = (bf16[2,1,256,128]{3,2,1,0:T(8,128)(2,1)S(1)}, bf16[2,1,256,128]{3,2,1,0:T(8,128)(2,1)S(1)}, u32[]{:S(2)}, u32[]{:S(2)}) collective-permute-start(bf16[2,1,256,128]{3,2,1,0:T(8,128)(2,1)S(1)} %get-tuple-element.43), channel_id=1, source_target_pairs={{0,24},{4,28},{8,16},{12,20},{16,8},{20,12},{24,0},{28,4},{1,25},{... | collective-permute-start | bytes 393224 | tf_op jit(solution)/shard_map/ppermute | solution.py:606
  34.2 1.6 %collective-permute-start.6 = (bf16[4,1,256,128]{3,2,1,0:T(8,128)(2,1)S(1)}, bf16[4,1,256,128]{3,2,1,0:T(8,128)(2,1)S(1)}, u32[]{:S(2)}, u32[]{:S(2)}) collective-permute-start(bf16[4,1,256,128]{3,2,1,0:T(8,128)(2,1)S(1)} %gather.1), channel_id=1, source_target_pairs={{0,4},{4,0},{8,12},{12,8},{16,20},{20,16},{24,28},{28,24},{1,5},{5... | collective-permute-start | bytes 786440 | tf_op jit(solution)/shard_map/ppermute | solution.py:615
  37.5 6.9 %collective-permute-start.7 = (bf16[1,32,1024]{2,1,0:T(8,128)(2,1)S(1)}, bf16[1,32,1024]{2,1,0:T(8,128)(2,1)S(1)}, u32[]{:S(2)}, u32[]{:S(2)}) collective-permute-start(bf16[1,32,1024]{2,1,0:T(8,128)(2,1)S(1)} %get-tuple-element.50), channel_id=1, source_target_pairs={{0,1},{1,2},{2,3},{3,0},{4,5},{5,6},{6,7},{7,4},{8,9},{9,10},{10,1... | collective-permute-start | bytes 196616 | tf_op jit(solution)/shard_map/ppermute | solution.py:644
  38.3 8.2 %collective-permute-start.8 = (bf16[1,32,1024]{2,1,0:T(8,128)(2,1)S(1)}, bf16[1,32,1024]{2,1,0:T(8,128)(2,1)S(1)}, u32[]{:S(2)}, u32[]{:S(2)}) collective-permute-start(bf16[1,32,1024]{2,1,0:T(8,128)(2,1)S(1)} %get-tuple-element.51), channel_id=1, source_target_pairs={{0,2},{1,3},{2,0},{3,1},{4,6},{5,7},{6,4},{7,5},{8,10},{9,11},{10,... | collective-permute-start | bytes 196616 | tf_op jit(solution)/shard_map/ppermute | solution.py:644
  41.2 5.2 %collective-permute-start.9 = (bf16[1,32,1024]{2,1,0:T(8,128)(2,1)S(1)}, bf16[1,32,1024]{2,1,0:T(8,128)(2,1)S(1)}, u32[]{:S(2)}, u32[]{:S(2)}) collective-permute-start(bf16[1,32,1024]{2,1,0:T(8,128)(2,1)S(1)} %get-tuple-element.52), channel_id=1, source_target_pairs={{0,3},{1,0},{2,1},{3,2},{4,7},{5,4},{6,5},{7,6},{8,11},{9,8},{10,9... | collective-permute-start | bytes 196616 | tf_op jit(solution)/shard_map/ppermute | solution.py:644

commit v10 on v9

--- a/solution.py
+++ b/solution.py
@@ -404,7 +404,7 @@
     edges = edge_refs[0][0]
     for ref in edge_refs[1:]:
         edges = edges + ref[0]
-    batch = slots // 2
+    batch = slots
     for first in range(0, slots, batch):
         rows, spectra = [], []
         for s in range(first, first + batch, 2):
@@ -564,7 +564,7 @@
     for step in range(1, half):
         pairs = [(g * half + i, g * half + (i + step) % half) for g in range(2) for i in range(half)]
         pieces[step] = lax.ppermute(pieces[step], "pln", pairs)
-    for step in range(half):
+    for step in reversed(range(half)):
         pieces[half + step] = lax.ppermute(pieces[half + step], "pln", [(0, half + step), (half, step)])
     pieces[:half] = [p.reshape(plan.ky_block * slots, grid) for p in pieces[:half]]
 

time: 47.4 us -> 47.2 us (level)
  no operation moved by 1% of the time
where the time goes in v10:
time: 47.2 us; the launch traced here: 46.9 us
  starting transfers between devices  20.9 us (44%)
  Pallas kernels  12.8 us (27%)
  waiting for transfers between devices  12.1 us (26%)
  local copies, waits for them, and re-layouts  0.95 us (2%)
    ppermute x3, waiting for transfers between devices, per_device(): lax.ppermute(send[e - 1], 'orb', [(o, o ^ 2 * e) for o in range(orb)])  5.98 us
    ppermute x2, starting transfers between devices, per_device(): lax.ppermute(pieces[half + step], 'pln', [(0, half + step), (half, step)])  5.78 us
    all_to_all x1, starting transfers between devices, per_device(): lax.all_to_all(send, 'orb', split_axis=0, concat_axis=0, tiled=True)  5.31 us
    pallas_call x1, Pallas kernels, per_device(): pl.pallas_call(functools.partial(density_kernel, plan), in_specs=[smem, s...  4.76 us
    ppermute x3, starting transfers between devices, per_device(): lax.ppermute(finished[step], 'pln', [(p, (p + step) % pln) for p in range...  4.65 us
    pallas_call x1, Pallas kernels, per_device(): pl.pallas_call(functools.partial(solve_kernel, plan), in_specs=[smem] + [...  4.29 us
    ppermute x3, waiting for transfers between devices, per_device(): lax.ppermute(finished[step], 'pln', [(p, (p + step) % pln) for p in range...  4.23 us
    ppermute x3, starting transfers between devices, per_device(): lax.ppermute(send[e - 1], 'orb', [(o, o ^ 2 * e) for o in range(orb)])  3.55 us
  transfers between devices with their start and end apart: 11, of which 6 were waited for; matrix products, arithmetic and copies ran while one was open for 0% of the time, Pallas kernels for 3%

profile of v10, /device:TPU:0, one launch (start us, length us, event | category | flops | bytes accessed | tf_op | source)
XLA Modules:
  0.0 46.9 jit_solution(16162476815413162471)
XLA Ops:
  0.0 4.8 %density.1 = (bf16[8,1,272,128]{3,2,1,0:T(8,128)(2,1)}, f32[1,32,32,128]{3,2,1,0:T(8,128)}, f32[1,64,128]{2,1,0:T(8,128)}, f32[64,8,128]{2,1,0:T(8,128)}, f32[64...) custom-call(s32[1]{0:T(128)} %bitcast.where_ref, s32[4,3]{1,0:T(4,128)} %corner_ref.1, f32[4]{0:T(128)} %weight_ref.1, ...), custom_call_target="tpu_custom_call" | custom-call | tf_op jit(solution)/shard_map/density/pallas_call | solution.py:532
  4.8 0.0 copy-start.2
  4.8 5.3 %all-to-all-start = ((bf16[8,1,272,128]{3,2,1,0:T(8,128)(2,1)}), bf16[8,1,272,128]{3,2,1,0:T(8,128)(2,1)S(1)}, u32[]{:S(2)}, u32[]{:S(2)}) async-start(bf16[8,1,272,128]{3,2,1,0:T(8,128)(2,1)} %get-tuple-element.29), calls=%async_computation | async-start | bytes 1114112 | tf_op jit(solution)/shard_map/all_to_all | solution.py:562
  10.1 1.6 %collective-permute-start = (f32[64,8,128]{2,1,0:T(8,128)}, f32[64,8,128]{2,1,0:T(8,128)S(1)}, u32[]{:S(2)}, u32[]{:S(2)}) collective-permute-start(f32[64,8,128]{2,1,0:T(8,128)} %get-tuple-element.32), channel_id=1, source_target_pairs={{0,1},{1,0},{2,3},{3,2},{4,5},{5,4},{6,7},{7,6},{8,9},{9,8},{10,11... | collective-permute-start | bytes 786440 | tf_op jit(solution)/shard_map/ppermute | solution.py:566
  11.7 4.5 %collective-permute-start.1 = (f32[1,8,128]{2,1,0:T(8,128)}, f32[1,8,128]{2,1,0:T(8,128)S(1)}, u32[]{:S(2)}, u32[]{:S(2)}) collective-permute-start(f32[1,8,128]{2,1,0:T(8,128)} %get-tuple-element.33), channel_id=1, source_target_pairs={{0,2},{2,0},{4,6},{6,4},{8,10},{10,8},{12,14},{14,12},{16,18},{18,... | collective-permute-start | bytes 12296 | tf_op jit(solution)/shard_map/ppermute | solution.py:568
  16.2 1.3 %collective-permute-start.2 = (f32[1,8,128]{2,1,0:T(8,128)}, f32[1,8,128]{2,1,0:T(8,128)S(1)}, u32[]{:S(2)}, u32[]{:S(2)}) collective-permute-start(f32[1,8,128]{2,1,0:T(8,128)} %get-tuple-element.34), channel_id=1, source_target_pairs={{0,3},{2,1},{4,7},{6,5},{8,11},{10,9},{12,15},{14,13},{16,19},{18,... | collective-permute-start | bytes 12296 | tf_op jit(solution)/shard_map/ppermute | solution.py:568
  17.5 0.9 %copy-done.1 = f32[64,8,128]{2,1,0:T(8,128)S(1)} copy-done((f32[64,8,128]{2,1,0:T(8,128)S(1)}, f32[64,8,128]{2,1,0:T(8,128)}, u32[]{:S(2)}) %copy-start.1) | copy-done | bytes 262168
  18.4 1.4 %tables.1 = (bf16[256,256]{1,0:T(8,128)(2,1)S(1)}, bf16[256,256]{1,0:T(8,128)(2,1)S(1)}, bf16[128,768]{1,0:T(8,128)(2,1)S(1)}, bf16[768,128]{1,0:T(8,128)(2,1)S(...) custom-call(s32[1]{0:T(128)} %bitcast.where_ref, ...), custom_call_target="tpu_custom_call" | custom-call | tf_op jit(solution)/shard_map/tables/pallas_call | solution.py:575
  19.9 0.4 all-to-all-done
  20.2 4.3 %solve.1 = (bf16[1,256,128]{2,1,0:T(8,128)(2,1)S(1)}, bf16[1,256,128]{2,1,0:T(8,128)(2,1)S(1)}, bf16[2,1,256,128]{3,2,1,0:T(8,128)(2,1)S(1)}, bf16[2,1,256,128]{...) custom-call(s32[1]{0:T(128)} %bitcast.where_ref, bf16[8,272,128]{2,1,0:T(8,128)(2,1)S(1)} %bitcast.7, ...), custom_call_target="tpu_custom_call" | custom-call | tf_op jit(solution)/shard_map/solve/pallas_call | solution.py:587
  24.5 1.8 %collective-permute-start.3 = (bf16[2,1,256,128]{3,2,1,0:T(8,128)(2,1)S(1)}, bf16[2,1,256,128]{3,2,1,0:T(8,128)(2,1)S(1)}, u32[]{:S(2)}, u32[]{:S(2)}) collective-permute-start(bf16[2,1,256,128]{3,2,1,0:T(8,128)(2,1)S(1)} %get-tuple-element.41), channel_id=1, source_target_pairs={{0,8},{4,12},{8,0},{12,4},{16,24},{20,28},{24,16},{28,20},{1,9},{5... | collective-permute-start | bytes 393224 | tf_op jit(solution)/shard_map/ppermute | solution.py:606
  26.3 1.5 %collective-permute-start.4 = (bf16[2,1,256,128]{3,2,1,0:T(8,128)(2,1)S(1)}, bf16[2,1,256,128]{3,2,1,0:T(8,128)(2,1)S(1)}, u32[]{:S(2)}, u32[]{:S(2)}) collective-permute-start(bf16[2,1,256,128]{3,2,1,0:T(8,128)(2,1)S(1)} %get-tuple-element.42), channel_id=1, source_target_pairs={{0,16},{4,20},{8,24},{12,28},{16,0},{20,4},{24,8},{28,12},{1,17},{... | collective-permute-start | bytes 393224 | tf_op jit(solution)/shard_map/ppermute | solution.py:606
  27.7 0.3 collective-permute-start.5
  28.1 2.1 %collective-permute-done.3.refs_0_.refs_2_ = bf16[2,1,256,128]{3,2,1,0:T(8,128)(2,1)S(1)} collective-permute-done((bf16[2,1,256,128]{3,2,1,0:T(8,128)(2,1)S(1)}, bf16[2,1,256,128]{3,2,1,0:T(8,128)(2,1)S(1)}, u32[]{:S(2)}, u32[]{:S(2)}) %collective-permute-start.3) | collective-permute-done | bytes 131104 | tf_op jit(solution)/shard_map/ppermute | solution.py:606
  30.2 3.8 %collective-permute-done.4.refs_1_.refs_3_ = bf16[2,1,256,128]{3,2,1,0:T(8,128)(2,1)S(1)} collective-permute-done((bf16[2,1,256,128]{3,2,1,0:T(8,128)(2,1)S(1)}, bf16[2,1,256,128]{3,2,1,0:T(8,128)(2,1)S(1)}, u32[]{:S(2)}, u32[]{:S(2)}) %collective-permute-start.4) | collective-permute-done | bytes 131104 | tf_op jit(solution)/shard_map/ppermute | solution.py:606
  34.1 0.1 collective-permute-start.6
  34.1 1.5 %collective-permute-done.6.refs_1_ = bf16[4,1,256,128]{3,2,1,0:T(8,128)(2,1)S(1)} collective-permute-done((bf16[4,1,256,128]{3,2,1,0:T(8,128)(2,1)S(1)}, bf16[4,1,256,128]{3,2,1,0:T(8,128)(2,1)S(1)}, u32[]{:S(2)}, u32[]{:S(2)}) %collective-permute-start.6) | collective-permute-done | bytes 262176 | tf_op jit(solution)/shard_map/ppermute | solution.py:615
  35.7 1.7 %terms.1 = (f32[1,32,1024]{2,1,0:T(8,128)S(1)}, bf16[1,32,1024]{2,1,0:T(8,128)(2,1)S(1)}, bf16[1,32,1024]{2,1,0:T(8,128)(2,1)S(1)}, bf16[1,32,1024]{2,1,0:T(8,128)(2,1)S(1)}) custom-call(s32[1]{0:T(128)} %bitcast.where_ref, bf16[1,256,128]{2,1,0:T(8,128)(2,1)S(1)} %get-tuple-element.39.refs_0_, bf16[4,1,256,128]{3,2,1,0:T(8,128)(2,1)S(1)} %collective-permute-done.6.refs_1_, ...), custom_call_target="tpu_custom_call" | custom-call | tf_op jit(solution)/shard_map/terms/pallas_call | solution.py:617
  37.4 0.7 %collective-permute-start.7 = (bf16[1,32,1024]{2,1,0:T(8,128)(2,1)S(1)}, bf16[1,32,1024]{2,1,0:T(8,128)(2,1)S(1)}, u32[]{:S(2)}, u32[]{:S(2)}) collective-permute-start(bf16[1,32,1024]{2,1,0:T(8,128)(2,1)S(1)} %get-tuple-element.50), channel_id=1, source_target_pairs={{0,1},{1,2},{2,3},{3,0},{4,5},{5,6},{6,7},{7,4},{8,9},{9,10},{10,1... | collective-permute-start | bytes 196616 | tf_op jit(solution)/shard_map/ppermute | solution.py:644
  38.1 2.9 %collective-permute-start.8 = (bf16[1,32,1024]{2,1,0:T(8,128)(2,1)S(1)}, bf16[1,32,1024]{2,1,0:T(8,128)(2,1)S(1)}, u32[]{:S(2)}, u32[]{:S(2)}) collective-permute-start(bf16[1,32,1024]{2,1,0:T(8,128)(2,1)S(1)} %get-tuple-element.51), channel_id=1, source_target_pairs={{0,2},{1,3},{2,0},{3,1},{4,6},{5,7},{6,4},{7,5},{8,10},{9,11},{10,... | collective-permute-start | bytes 196616 | tf_op jit(solution)/shard_map/ppermute | solution.py:644
  41.0 1.0 %collective-permute-start.9 = (bf16[1,32,1024]{2,1,0:T(8,128)(2,1)S(1)}, bf16[1,32,1024]{2,1,0:T(8,128)(2,1)S(1)}, u32[]{:S(2)}, u32[]{:S(2)}) collective-permute-start(bf16[1,32,1024]{2,1,0:T(8,128)(2,1)S(1)} %get-tuple-element.52), channel_id=1, source_target_pairs={{0,3},{1,0},{2,1},{3,2},{4,7},{5,4},{6,5},{7,6},{8,11},{9,8},{10,9... | collective-permute-start | bytes 196616 | tf_op jit(solution)/shard_map/ppermute | solution.py:644
  42.0 2.3 %collective-permute-done.7.refs_1_ = bf16[1,32,1024]{2,1,0:T(8,128)(2,1)S(1)} collective-permute-done((bf16[1,32,1024]{2,1,0:T(8,128)(2,1)S(1)}, bf16[1,32,1024]{2,1,0:T(8,128)(2,1)S(1)}, u32[]{:S(2)}, u32[]{:S(2)}) %collective-permute-start.7) | collective-permute-done | bytes 65568 | tf_op jit(solution)/shard_map/ppermute | solution.py:644
  44.3 1.9 %collective-permute-done.8.refs_2_ = bf16[1,32,1024]{2,1,0:T(8,128)(2,1)S(1)} collective-permute-done((bf16[1,32,1024]{2,1,0:T(8,128)(2,1)S(1)}, bf16[1,32,1024]{2,1,0:T(8,128)(2,1)S(1)}, u32[]{:S(2)}, u32[]{:S(2)}) %collective-permute-start.8) | collective-permute-done | bytes 65568 | tf_op jit(solution)/shard_map/ppermute | solution.py:644
  46.2 0.7 %sum.1 = bf16[1,4,8192]{2,1,0:T(4,128)(2,1)} custom-call(f32[1,32,1024]{2,1,0:T(8,128)S(1)} %get-tuple-element.49.refs_0_, bf16[1,32,1024]{2,1,0:T(8,128)(2,1)S(1)} %collective-permute-done.7.refs_1_, bf16[1,32,1024]{2,1,0:T(8,128)(2,1)S(1)} %collective-permute-done.8.refs_2_, bf16[1,32,1024]{2,1,0:T(8,128)(2,1)S(1)} %collective-permute-done.9.refs_3_), custom_call_target="tpu_custom_call" | custom-call | tf_op jit(solution)/shard_map/sum/pallas_call | solution.py:646
  (10 shorter events, 0.0 us)
Async XLA Ops:
  4.8 30.9 %copy-start = (f32[1,32,32,128]{3,2,1,0:T(8,128)S(1)}, f32[1,32,32,128]{3,2,1,0:T(8,128)}, u32[]{:S(2)}) copy-start(f32[1,32,32,128]{3,2,1,0:T(8,128)} %get-tuple-element.44.refs_5_) | copy-start | bytes 1572868
  4.8 30.9 %copy-start.2 = (f32[1,64,128]{2,1,0:T(8,128)S(1)}, f32[1,64,128]{2,1,0:T(8,128)}, u32[]{:S(2)}) copy-start(f32[1,64,128]{2,1,0:T(8,128)} %get-tuple-element.45.refs_6_) | copy-start | bytes 98308
  4.8 15.4 %all-to-all-start = ((bf16[8,1,272,128]{3,2,1,0:T(8,128)(2,1)}), bf16[8,1,272,128]{3,2,1,0:T(8,128)(2,1)S(1)}, u32[]{:S(2)}, u32[]{:S(2)}) async-start(bf16[8,1,272,128]{3,2,1,0:T(8,128)(2,1)} %get-tuple-element.29), calls=%async_computation | async-start | bytes 1114112 | tf_op jit(solution)/shard_map/all_to_all | solution.py:562
  10.1 9.7 %collective-permute-start = (f32[64,8,128]{2,1,0:T(8,128)}, f32[64,8,128]{2,1,0:T(8,128)S(1)}, u32[]{:S(2)}, u32[]{:S(2)}) collective-permute-start(f32[64,8,128]{2,1,0:T(8,128)} %get-tuple-element.32), channel_id=1, source_target_pairs={{0,1},{1,0},{2,3},{3,2},{4,5},{5,4},{6,7},{7,6},{8,9},{9,8},{10,11... | collective-permute-start | bytes 786440 | tf_op jit(solution)/shard_map/ppermute | solution.py:566
  11.7 8.1 %collective-permute-start.1 = (f32[1,8,128]{2,1,0:T(8,128)}, f32[1,8,128]{2,1,0:T(8,128)S(1)}, u32[]{:S(2)}, u32[]{:S(2)}) collective-permute-start(f32[1,8,128]{2,1,0:T(8,128)} %get-tuple-element.33), channel_id=1, source_target_pairs={{0,2},{2,0},{4,6},{6,4},{8,10},{10,8},{12,14},{14,12},{16,18},{18,... | collective-permute-start | bytes 12296 | tf_op jit(solution)/shard_map/ppermute | solution.py:568
  16.2 3.7 %collective-permute-start.2 = (f32[1,8,128]{2,1,0:T(8,128)}, f32[1,8,128]{2,1,0:T(8,128)S(1)}, u32[]{:S(2)}, u32[]{:S(2)}) collective-permute-start(f32[1,8,128]{2,1,0:T(8,128)} %get-tuple-element.34), channel_id=1, source_target_pairs={{0,3},{2,1},{4,7},{6,5},{8,11},{10,9},{12,15},{14,13},{16,19},{18,... | collective-permute-start | bytes 12296 | tf_op jit(solution)/shard_map/ppermute | solution.py:568
  17.5 1.0 %copy-start.1 = (f32[64,8,128]{2,1,0:T(8,128)S(1)}, f32[64,8,128]{2,1,0:T(8,128)}, u32[]{:S(2)}) copy-start(f32[64,8,128]{2,1,0:T(8,128)} %get-tuple-element.30) | copy-start | bytes 786436
  24.5 5.7 %collective-permute-start.3 = (bf16[2,1,256,128]{3,2,1,0:T(8,128)(2,1)S(1)}, bf16[2,1,256,128]{3,2,1,0:T(8,128)(2,1)S(1)}, u32[]{:S(2)}, u32[]{:S(2)}) collective-permute-start(bf16[2,1,256,128]{3,2,1,0:T(8,128)(2,1)S(1)} %get-tuple-element.41), channel_id=1, source_target_pairs={{0,8},{4,12},{8,0},{12,4},{16,24},{20,28},{24,16},{28,20},{1,9},{5... | collective-permute-start | bytes 393224 | tf_op jit(solution)/shard_map/ppermute | solution.py:606
  26.3 7.8 %collective-permute-start.4 = (bf16[2,1,256,128]{3,2,1,0:T(8,128)(2,1)S(1)}, bf16[2,1,256,128]{3,2,1,0:T(8,128)(2,1)S(1)}, u32[]{:S(2)}, u32[]{:S(2)}) collective-permute-start(bf16[2,1,256,128]{3,2,1,0:T(8,128)(2,1)S(1)} %get-tuple-element.42), channel_id=1, source_target_pairs={{0,16},{4,20},{8,24},{12,28},{16,0},{20,4},{24,8},{28,12},{1,17},{... | collective-permute-start | bytes 393224 | tf_op jit(solution)/shard_map/ppermute | solution.py:606
  27.7 6.3 %collective-permute-start.5 = (bf16[2,1,256,128]{3,2,1,0:T(8,128)(2,1)S(1)}, bf16[2,1,256,128]{3,2,1,0:T(8,128)(2,1)S(1)}, u32[]{:S(2)}, u32[]{:S(2)}) collective-permute-start(bf16[2,1,256,128]{3,2,1,0:T(8,128)(2,1)S(1)} %get-tuple-element.43), channel_id=1, source_target_pairs={{0,24},{4,28},{8,16},{12,20},{16,8},{20,12},{24,0},{28,4},{1,25},{... | collective-permute-start | bytes 393224 | tf_op jit(solution)/shard_map/ppermute | solution.py:606
  34.1 1.6 %collective-permute-start.6 = (bf16[4,1,256,128]{3,2,1,0:T(8,128)(2,1)S(1)}, bf16[4,1,256,128]{3,2,1,0:T(8,128)(2,1)S(1)}, u32[]{:S(2)}, u32[]{:S(2)}) collective-permute-start(bf16[4,1,256,128]{3,2,1,0:T(8,128)(2,1)S(1)} %gather.1), channel_id=1, source_target_pairs={{0,4},{4,0},{8,12},{12,8},{16,20},{20,16},{24,28},{28,24},{1,5},{5... | collective-permute-start | bytes 786440 | tf_op jit(solution)/shard_map/ppermute | solution.py:615
  37.4 6.9 %collective-permute-start.7 = (bf16[1,32,1024]{2,1,0:T(8,128)(2,1)S(1)}, bf16[1,32,1024]{2,1,0:T(8,128)(2,1)S(1)}, u32[]{:S(2)}, u32[]{:S(2)}) collective-permute-start(bf16[1,32,1024]{2,1,0:T(8,128)(2,1)S(1)} %get-tuple-element.50), channel_id=1, source_target_pairs={{0,1},{1,2},{2,3},{3,0},{4,5},{5,6},{6,7},{7,4},{8,9},{9,10},{10,1... | collective-permute-start | bytes 196616 | tf_op jit(solution)/shard_map/ppermute | solution.py:644
  38.1 8.2 %collective-permute-start.8 = (bf16[1,32,1024]{2,1,0:T(8,128)(2,1)S(1)}, bf16[1,32,1024]{2,1,0:T(8,128)(2,1)S(1)}, u32[]{:S(2)}, u32[]{:S(2)}) collective-permute-start(bf16[1,32,1024]{2,1,0:T(8,128)(2,1)S(1)} %get-tuple-element.51), channel_id=1, source_target_pairs={{0,2},{1,3},{2,0},{3,1},{4,6},{5,7},{6,4},{7,5},{8,10},{9,11},{10,... | collective-permute-start | bytes 196616 | tf_op jit(solution)/shard_map/ppermute | solution.py:644
  41.0 5.2 %collective-permute-start.9 = (bf16[1,32,1024]{2,1,0:T(8,128)(2,1)S(1)}, bf16[1,32,1024]{2,1,0:T(8,128)(2,1)S(1)}, u32[]{:S(2)}, u32[]{:S(2)}) collective-permute-start(bf16[1,32,1024]{2,1,0:T(8,128)(2,1)S(1)} %get-tuple-element.52), channel_id=1, source_target_pairs={{0,3},{1,0},{2,1},{3,2},{4,7},{5,4},{6,5},{7,6},{8,11},{9,8},{10,9... | collective-permute-start | bytes 196616 | tf_op jit(solution)/shard_map/ppermute | solution.py:644

commit v11 on v10

--- a/solution.py
+++ b/solution.py
@@ -341,7 +341,7 @@
         block_out_ref[step] = fold(block_ref[step])
     edge_out_ref[...] = fold(edge_ref[...])
     pairs = [(block_out_ref.at[step], piece_anys[step]) for step in range(half)]
-    pairs += [(edge_out_ref.at[pl.ds(step, 1)], piece_anys[half + step]) for step in range(half)]
+    pairs += [(edge_out_ref.at[pl.ds(step, 1)], piece_anys[plan.pln - 1 - step]) for step in range(half)]
     return start_copies(sems, 0, *pairs)
 
 
@@ -565,7 +565,8 @@
         pairs = [(g * half + i, g * half + (i + step) % half) for g in range(2) for i in range(half)]
         pieces[step] = lax.ppermute(pieces[step], "pln", pairs)
     for step in reversed(range(half)):
-        pieces[half + step] = lax.ppermute(pieces[half + step], "pln", [(0, half + step), (half, step)])
+        place = pln - 1 - step
+        pieces[place] = lax.ppermute(pieces[place], "pln", [(0, half + step), (half, step)])
     pieces[:half] = [p.reshape(plan.ky_block * slots, grid) for p in pieces[:half]]
 
     small = pltpu.CompilerParams(vmem_limit_bytes=SMALL)

time: 47.2 us -> 49.4 us (1.047)
  waiting for transfers between devices: 12.1 us -> 14.3 us
    ppermute x2, waiting for transfers between devices: 0.01 us -> 2.33 us  [per_device(): lax.ppermute(pieces[place], 'pln', [(0, half + step), (half, step)])]
    ppermute x3, starting transfers between devices: 4.65 us -> 4.02 us  [per_device(): lax.ppermute(finished[step], 'pln', [(p, (p + step) % pln) for p in range...]
    ppermute x2, starting transfers between devices: 5.78 us -> 6.29 us  [per_device(): lax.ppermute(pieces[place], 'pln', [(0, half + step), (half, step)])]
  transfers between devices with their start and end apart: 11 -> 11, of which waited for: 6 -> 7; matrix products, arithmetic and copies ran while one was open for 0% -> 0% of each run, Pallas kernels for 3% -> 3%
where the time goes in v11:
time: 49.4 us; the launch traced here: 49.1 us
  starting transfers between devices  20.9 us (42%)
  waiting for transfers between devices  14.3 us (29%)
  Pallas kernels  12.8 us (26%)
  local copies, waits for them, and re-layouts  0.95 us (2%)
    ppermute x2, starting transfers between devices, per_device(): lax.ppermute(pieces[place], 'pln', [(0, half + step), (half, step)])  6.29 us
    ppermute x3, waiting for transfers between devices, per_device(): lax.ppermute(send[e - 1], 'orb', [(o, o ^ 2 * e) for o in range(orb)])  5.79 us
    all_to_all x1, starting transfers between devices, per_device(): lax.all_to_all(send, 'orb', split_axis=0, concat_axis=0, tiled=True)  5.31 us
    pallas_call x1, Pallas kernels, per_device(): pl.pallas_call(functools.partial(density_kernel, plan), in_specs=[smem, s...  4.76 us
    ppermute x3, waiting for transfers between devices, per_device(): lax.ppermute(finished[step], 'pln', [(p, (p + step) % pln) for p in range...  4.65 us
    pallas_call x1, Pallas kernels, per_device(): pl.pallas_call(functools.partial(solve_kernel, plan), in_specs=[smem] + [...  4.28 us
    ppermute x3, starting transfers between devices, per_device(): lax.ppermute(finished[step], 'pln', [(p, (p + step) % pln) for p in range...  4.02 us
    ppermute x3, starting transfers between devices, per_device(): lax.ppermute(send[e - 1], 'orb', [(o, o ^ 2 * e) for o in range(orb)])  3.63 us
  transfers between devices with their start and end apart: 11, of which 7 were waited for; matrix products, arithmetic and copies ran while one was open for 0% of the time, Pallas kernels for 3%

profile of v11, /device:TPU:0, one launch (start us, length us, event | category | flops | bytes accessed | tf_op | source)
XLA Modules:
  0.0 49.1 jit_solution(9192834832815200800)
XLA Ops:
  0.0 4.8 %density.1 = (bf16[8,1,272,128]{3,2,1,0:T(8,128)(2,1)}, f32[1,32,32,128]{3,2,1,0:T(8,128)}, f32[1,64,128]{2,1,0:T(8,128)}, f32[64,8,128]{2,1,0:T(8,128)}, f32[64...) custom-call(s32[1]{0:T(128)} %bitcast.where_ref, s32[4,3]{1,0:T(4,128)} %corner_ref.1, f32[4]{0:T(128)} %weight_ref.1, ...), custom_call_target="tpu_custom_call" | custom-call | tf_op jit(solution)/shard_map/density/pallas_call | solution.py:532
  4.8 5.3 %all-to-all-start = ((bf16[8,1,272,128]{3,2,1,0:T(8,128)(2,1)}), bf16[8,1,272,128]{3,2,1,0:T(8,128)(2,1)S(1)}, u32[]{:S(2)}, u32[]{:S(2)}) async-start(bf16[8,1,272,128]{3,2,1,0:T(8,128)(2,1)} %get-tuple-element.29), calls=%async_computation | async-start | bytes 1114112 | tf_op jit(solution)/shard_map/all_to_all | solution.py:562
  10.1 1.6 %collective-permute-start = (f32[64,8,128]{2,1,0:T(8,128)}, f32[64,8,128]{2,1,0:T(8,128)S(1)}, u32[]{:S(2)}, u32[]{:S(2)}) collective-permute-start(f32[64,8,128]{2,1,0:T(8,128)} %get-tuple-element.32), channel_id=1, source_target_pairs={{0,1},{1,0},{2,3},{3,2},{4,5},{5,4},{6,7},{7,6},{8,9},{9,8},{10,11... | collective-permute-start | bytes 786440 | tf_op jit(solution)/shard_map/ppermute | solution.py:566
  11.7 4.4 %collective-permute-start.1 = (f32[1,8,128]{2,1,0:T(8,128)}, f32[1,8,128]{2,1,0:T(8,128)S(1)}, u32[]{:S(2)}, u32[]{:S(2)}) collective-permute-start(f32[1,8,128]{2,1,0:T(8,128)} %get-tuple-element.33), channel_id=1, source_target_pairs={{0,3},{2,1},{4,7},{6,5},{8,11},{10,9},{12,15},{14,13},{16,19},{18,... | collective-permute-start | bytes 12296 | tf_op jit(solution)/shard_map/ppermute | solution.py:569
  16.1 1.9 %collective-permute-start.2 = (f32[1,8,128]{2,1,0:T(8,128)}, f32[1,8,128]{2,1,0:T(8,128)S(1)}, u32[]{:S(2)}, u32[]{:S(2)}) collective-permute-start(f32[1,8,128]{2,1,0:T(8,128)} %get-tuple-element.34), channel_id=1, source_target_pairs={{0,2},{2,0},{4,6},{6,4},{8,10},{10,8},{12,14},{14,12},{16,18},{18,... | collective-permute-start | bytes 12296 | tf_op jit(solution)/shard_map/ppermute | solution.py:569
  18.0 0.9 %copy-done.1 = f32[64,8,128]{2,1,0:T(8,128)S(1)} copy-done((f32[64,8,128]{2,1,0:T(8,128)S(1)}, f32[64,8,128]{2,1,0:T(8,128)}, u32[]{:S(2)}) %copy-start.1) | copy-done | bytes 262168
  18.9 1.4 %tables.1 = (bf16[256,256]{1,0:T(8,128)(2,1)S(1)}, bf16[256,256]{1,0:T(8,128)(2,1)S(1)}, bf16[128,768]{1,0:T(8,128)(2,1)S(1)}, bf16[768,128]{1,0:T(8,128)(2,1)S(...) custom-call(s32[1]{0:T(128)} %bitcast.where_ref, ...), custom_call_target="tpu_custom_call" | custom-call | tf_op jit(solution)/shard_map/tables/pallas_call | solution.py:576
  20.3 2.3 %collective-permute-done.2.refs_3_ = f32[1,8,128]{2,1,0:T(8,128)S(1)} collective-permute-done((f32[1,8,128]{2,1,0:T(8,128)}, f32[1,8,128]{2,1,0:T(8,128)S(1)}, u32[]{:S(2)}, u32[]{:S(2)}) %collective-permute-start.2) | collective-permute-done | bytes 4128 | tf_op jit(solution)/shard_map/ppermute | solution.py:569
  22.7 4.3 %solve.1 = (bf16[1,256,128]{2,1,0:T(8,128)(2,1)S(1)}, bf16[1,256,128]{2,1,0:T(8,128)(2,1)S(1)}, bf16[2,1,256,128]{3,2,1,0:T(8,128)(2,1)S(1)}, bf16[2,1,256,128]{...) custom-call(s32[1]{0:T(128)} %bitcast.where_ref, bf16[8,272,128]{2,1,0:T(8,128)(2,1)S(1)} %bitcast.7, ...), custom_call_target="tpu_custom_call" | custom-call | tf_op jit(solution)/shard_map/solve/pallas_call | solution.py:588
  27.0 2.1 %collective-permute-start.3 = (bf16[2,1,256,128]{3,2,1,0:T(8,128)(2,1)S(1)}, bf16[2,1,256,128]{3,2,1,0:T(8,128)(2,1)S(1)}, u32[]{:S(2)}, u32[]{:S(2)}) collective-permute-start(bf16[2,1,256,128]{3,2,1,0:T(8,128)(2,1)S(1)} %get-tuple-element.41), channel_id=1, source_target_pairs={{0,8},{4,12},{8,0},{12,4},{16,24},{20,28},{24,16},{28,20},{1,9},{5... | collective-permute-start | bytes 393224 | tf_op jit(solution)/shard_map/ppermute | solution.py:607
  29.1 1.5 %collective-permute-start.4 = (bf16[2,1,256,128]{3,2,1,0:T(8,128)(2,1)S(1)}, bf16[2,1,256,128]{3,2,1,0:T(8,128)(2,1)S(1)}, u32[]{:S(2)}, u32[]{:S(2)}) collective-permute-start(bf16[2,1,256,128]{3,2,1,0:T(8,128)(2,1)S(1)} %get-tuple-element.42), channel_id=1, source_target_pairs={{0,16},{4,20},{8,24},{12,28},{16,0},{20,4},{24,8},{28,12},{1,17},{... | collective-permute-start | bytes 393224 | tf_op jit(solution)/shard_map/ppermute | solution.py:607
  30.5 0.1 collective-permute-start.5
  30.6 2.5 %collective-permute-done.3.refs_0_.refs_2_ = bf16[2,1,256,128]{3,2,1,0:T(8,128)(2,1)S(1)} collective-permute-done((bf16[2,1,256,128]{3,2,1,0:T(8,128)(2,1)S(1)}, bf16[2,1,256,128]{3,2,1,0:T(8,128)(2,1)S(1)}, u32[]{:S(2)}, u32[]{:S(2)}) %collective-permute-start.3) | collective-permute-done | bytes 131104 | tf_op jit(solution)/shard_map/ppermute | solution.py:607
  33.1 1.9 %collective-permute-done.4.refs_1_.refs_3_ = bf16[2,1,256,128]{3,2,1,0:T(8,128)(2,1)S(1)} collective-permute-done((bf16[2,1,256,128]{3,2,1,0:T(8,128)(2,1)S(1)}, bf16[2,1,256,128]{3,2,1,0:T(8,128)(2,1)S(1)}, u32[]{:S(2)}, u32[]{:S(2)}) %collective-permute-start.4) | collective-permute-done | bytes 131104 | tf_op jit(solution)/shard_map/ppermute | solution.py:607
  35.0 1.4 %collective-permute-done.5.refs_2_.refs_4_ = bf16[2,1,256,128]{3,2,1,0:T(8,128)(2,1)S(1)} collective-permute-done((bf16[2,1,256,128]{3,2,1,0:T(8,128)(2,1)S(1)}, bf16[2,1,256,128]{3,2,1,0:T(8,128)(2,1)S(1)}, u32[]{:S(2)}, u32[]{:S(2)}) %collective-permute-start.5) | collective-permute-done | bytes 131104 | tf_op jit(solution)/shard_map/ppermute | solution.py:607
  36.4 0.1 collective-permute-start.6
  36.5 1.5 %collective-permute-done.6.refs_1_ = bf16[4,1,256,128]{3,2,1,0:T(8,128)(2,1)S(1)} collective-permute-done((bf16[4,1,256,128]{3,2,1,0:T(8,128)(2,1)S(1)}, bf16[4,1,256,128]{3,2,1,0:T(8,128)(2,1)S(1)}, u32[]{:S(2)}, u32[]{:S(2)}) %collective-permute-start.6) | collective-permute-done | bytes 262176 | tf_op jit(solution)/shard_map/ppermute | solution.py:616
  38.0 1.7 %terms.1 = (f32[1,32,1024]{2,1,0:T(8,128)S(1)}, bf16[1,32,1024]{2,1,0:T(8,128)(2,1)S(1)}, bf16[1,32,1024]{2,1,0:T(8,128)(2,1)S(1)}, bf16[1,32,1024]{2,1,0:T(8,128)(2,1)S(1)}) custom-call(s32[1]{0:T(128)} %bitcast.where_ref, bf16[1,256,128]{2,1,0:T(8,128)(2,1)S(1)} %get-tuple-element.39.refs_0_, bf16[4,1,256,128]{3,2,1,0:T(8,128)(2,1)S(1)} %collective-permute-done.6.refs_1_, ...), custom_call_target="tpu_custom_call" | custom-call | tf_op jit(solution)/shard_map/terms/pallas_call | solution.py:618
  39.7 0.1 collective-permute-start.7
  39.8 1.1 %collective-permute-start.8 = (bf16[1,32,1024]{2,1,0:T(8,128)(2,1)S(1)}, bf16[1,32,1024]{2,1,0:T(8,128)(2,1)S(1)}, u32[]{:S(2)}, u32[]{:S(2)}) collective-permute-start(bf16[1,32,1024]{2,1,0:T(8,128)(2,1)S(1)} %get-tuple-element.51), channel_id=1, source_target_pairs={{0,2},{1,3},{2,0},{3,1},{4,6},{5,7},{6,4},{7,5},{8,10},{9,11},{10,... | collective-permute-start | bytes 196616 | tf_op jit(solution)/shard_map/ppermute | solution.py:645
  40.9 2.8 %collective-permute-start.9 = (bf16[1,32,1024]{2,1,0:T(8,128)(2,1)S(1)}, bf16[1,32,1024]{2,1,0:T(8,128)(2,1)S(1)}, u32[]{:S(2)}, u32[]{:S(2)}) collective-permute-start(bf16[1,32,1024]{2,1,0:T(8,128)(2,1)S(1)} %get-tuple-element.52), channel_id=1, source_target_pairs={{0,3},{1,0},{2,1},{3,2},{4,7},{5,4},{6,5},{7,6},{8,11},{9,8},{10,9... | collective-permute-start | bytes 196616 | tf_op jit(solution)/shard_map/ppermute | solution.py:645
  43.7 2.8 %collective-permute-done.7.refs_1_ = bf16[1,32,1024]{2,1,0:T(8,128)(2,1)S(1)} collective-permute-done((bf16[1,32,1024]{2,1,0:T(8,128)(2,1)S(1)}, bf16[1,32,1024]{2,1,0:T(8,128)(2,1)S(1)}, u32[]{:S(2)}, u32[]{:S(2)}) %collective-permute-start.7) | collective-permute-done | bytes 65568 | tf_op jit(solution)/shard_map/ppermute | solution.py:645
  46.5 1.8 %collective-permute-done.8.refs_2_ = bf16[1,32,1024]{2,1,0:T(8,128)(2,1)S(1)} collective-permute-done((bf16[1,32,1024]{2,1,0:T(8,128)(2,1)S(1)}, bf16[1,32,1024]{2,1,0:T(8,128)(2,1)S(1)}, u32[]{:S(2)}, u32[]{:S(2)}) %collective-permute-start.8) | collective-permute-done | bytes 65568 | tf_op jit(solution)/shard_map/ppermute | solution.py:645
  48.4 0.7 %sum.1 = bf16[1,4,8192]{2,1,0:T(4,128)(2,1)} custom-call(f32[1,32,1024]{2,1,0:T(8,128)S(1)} %get-tuple-element.49.refs_0_, bf16[1,32,1024]{2,1,0:T(8,128)(2,1)S(1)} %collective-permute-done.7.refs_1_, bf16[1,32,1024]{2,1,0:T(8,128)(2,1)S(1)} %collective-permute-done.8.refs_2_, bf16[1,32,1024]{2,1,0:T(8,128)(2,1)S(1)} %collective-permute-done.9.refs_3_), custom_call_target="tpu_custom_call" | custom-call | tf_op jit(solution)/shard_map/sum/pallas_call | solution.py:647
  (10 shorter events, 0.0 us)
Async XLA Ops:
  4.8 33.2 %copy-start = (f32[1,32,32,128]{3,2,1,0:T(8,128)S(1)}, f32[1,32,32,128]{3,2,1,0:T(8,128)}, u32[]{:S(2)}) copy-start(f32[1,32,32,128]{3,2,1,0:T(8,128)} %get-tuple-element.44.refs_5_) | copy-start | bytes 1572868
  4.8 33.2 %copy-start.2 = (f32[1,64,128]{2,1,0:T(8,128)S(1)}, f32[1,64,128]{2,1,0:T(8,128)}, u32[]{:S(2)}) copy-start(f32[1,64,128]{2,1,0:T(8,128)} %get-tuple-element.45.refs_6_) | copy-start | bytes 98308
  4.8 17.9 %all-to-all-start = ((bf16[8,1,272,128]{3,2,1,0:T(8,128)(2,1)}), bf16[8,1,272,128]{3,2,1,0:T(8,128)(2,1)S(1)}, u32[]{:S(2)}, u32[]{:S(2)}) async-start(bf16[8,1,272,128]{3,2,1,0:T(8,128)(2,1)} %get-tuple-element.29), calls=%async_computation | async-start | bytes 1114112 | tf_op jit(solution)/shard_map/all_to_all | solution.py:562
  10.1 12.6 %collective-permute-start = (f32[64,8,128]{2,1,0:T(8,128)}, f32[64,8,128]{2,1,0:T(8,128)S(1)}, u32[]{:S(2)}, u32[]{:S(2)}) collective-permute-start(f32[64,8,128]{2,1,0:T(8,128)} %get-tuple-element.32), channel_id=1, source_target_pairs={{0,1},{1,0},{2,3},{3,2},{4,5},{5,4},{6,7},{7,6},{8,9},{9,8},{10,11... | collective-permute-start | bytes 786440 | tf_op jit(solution)/shard_map/ppermute | solution.py:566
  11.7 8.6 %collective-permute-start.1 = (f32[1,8,128]{2,1,0:T(8,128)}, f32[1,8,128]{2,1,0:T(8,128)S(1)}, u32[]{:S(2)}, u32[]{:S(2)}) collective-permute-start(f32[1,8,128]{2,1,0:T(8,128)} %get-tuple-element.33), channel_id=1, source_target_pairs={{0,3},{2,1},{4,7},{6,5},{8,11},{10,9},{12,15},{14,13},{16,19},{18,... | collective-permute-start | bytes 12296 | tf_op jit(solution)/shard_map/ppermute | solution.py:569
  16.1 6.6 %collective-permute-start.2 = (f32[1,8,128]{2,1,0:T(8,128)}, f32[1,8,128]{2,1,0:T(8,128)S(1)}, u32[]{:S(2)}, u32[]{:S(2)}) collective-permute-start(f32[1,8,128]{2,1,0:T(8,128)} %get-tuple-element.34), channel_id=1, source_target_pairs={{0,2},{2,0},{4,6},{6,4},{8,10},{10,8},{12,14},{14,12},{16,18},{18,... | collective-permute-start | bytes 12296 | tf_op jit(solution)/shard_map/ppermute | solution.py:569
  18.0 1.0 %copy-start.1 = (f32[64,8,128]{2,1,0:T(8,128)S(1)}, f32[64,8,128]{2,1,0:T(8,128)}, u32[]{:S(2)}) copy-start(f32[64,8,128]{2,1,0:T(8,128)} %get-tuple-element.30) | copy-start | bytes 786436
  27.0 6.1 %collective-permute-start.3 = (bf16[2,1,256,128]{3,2,1,0:T(8,128)(2,1)S(1)}, bf16[2,1,256,128]{3,2,1,0:T(8,128)(2,1)S(1)}, u32[]{:S(2)}, u32[]{:S(2)}) collective-permute-start(bf16[2,1,256,128]{3,2,1,0:T(8,128)(2,1)S(1)} %get-tuple-element.41), channel_id=1, source_target_pairs={{0,8},{4,12},{8,0},{12,4},{16,24},{20,28},{24,16},{28,20},{1,9},{5... | collective-permute-start | bytes 393224 | tf_op jit(solution)/shard_map/ppermute | solution.py:607
  29.1 5.9 %collective-permute-start.4 = (bf16[2,1,256,128]{3,2,1,0:T(8,128)(2,1)S(1)}, bf16[2,1,256,128]{3,2,1,0:T(8,128)(2,1)S(1)}, u32[]{:S(2)}, u32[]{:S(2)}) collective-permute-start(bf16[2,1,256,128]{3,2,1,0:T(8,128)(2,1)S(1)} %get-tuple-element.42), channel_id=1, source_target_pairs={{0,16},{4,20},{8,24},{12,28},{16,0},{20,4},{24,8},{28,12},{1,17},{... | collective-permute-start | bytes 393224 | tf_op jit(solution)/shard_map/ppermute | solution.py:607
  30.5 5.9 %collective-permute-start.5 = (bf16[2,1,256,128]{3,2,1,0:T(8,128)(2,1)S(1)}, bf16[2,1,256,128]{3,2,1,0:T(8,128)(2,1)S(1)}, u32[]{:S(2)}, u32[]{:S(2)}) collective-permute-start(bf16[2,1,256,128]{3,2,1,0:T(8,128)(2,1)S(1)} %get-tuple-element.43), channel_id=1, source_target_pairs={{0,24},{4,28},{8,16},{12,20},{16,8},{20,12},{24,0},{28,4},{1,25},{... | collective-permute-start | bytes 393224 | tf_op jit(solution)/shard_map/ppermute | solution.py:607
  36.4 1.6 %collective-permute-start.6 = (bf16[4,1,256,128]{3,2,1,0:T(8,128)(2,1)S(1)}, bf16[4,1,256,128]{3,2,1,0:T(8,128)(2,1)S(1)}, u32[]{:S(2)}, u32[]{:S(2)}) collective-permute-start(bf16[4,1,256,128]{3,2,1,0:T(8,128)(2,1)S(1)} %gather.1), channel_id=1, source_target_pairs={{0,4},{4,0},{8,12},{12,8},{16,20},{20,16},{24,28},{28,24},{1,5},{5... | collective-permute-start | bytes 786440 | tf_op jit(solution)/shard_map/ppermute | solution.py:616
  39.7 6.8 %collective-permute-start.7 = (bf16[1,32,1024]{2,1,0:T(8,128)(2,1)S(1)}, bf16[1,32,1024]{2,1,0:T(8,128)(2,1)S(1)}, u32[]{:S(2)}, u32[]{:S(2)}) collective-permute-start(bf16[1,32,1024]{2,1,0:T(8,128)(2,1)S(1)} %get-tuple-element.50), channel_id=1, source_target_pairs={{0,1},{1,2},{2,3},{3,0},{4,5},{5,6},{6,7},{7,4},{8,9},{9,10},{10,1... | collective-permute-start | bytes 196616 | tf_op jit(solution)/shard_map/ppermute | solution.py:645
  39.8 8.6 %collective-permute-start.8 = (bf16[1,32,1024]{2,1,0:T(8,128)(2,1)S(1)}, bf16[1,32,1024]{2,1,0:T(8,128)(2,1)S(1)}, u32[]{:S(2)}, u32[]{:S(2)}) collective-permute-start(bf16[1,32,1024]{2,1,0:T(8,128)(2,1)S(1)} %get-tuple-element.51), channel_id=1, source_target_pairs={{0,2},{1,3},{2,0},{3,1},{4,6},{5,7},{6,4},{7,5},{8,10},{9,11},{10,... | collective-permute-start | bytes 196616 | tf_op jit(solution)/shard_map/ppermute | solution.py:645
  40.9 7.5 %collective-permute-start.9 = (bf16[1,32,1024]{2,1,0:T(8,128)(2,1)S(1)}, bf16[1,32,1024]{2,1,0:T(8,128)(2,1)S(1)}, u32[]{:S(2)}, u32[]{:S(2)}) collective-permute-start(bf16[1,32,1024]{2,1,0:T(8,128)(2,1)S(1)} %get-tuple-element.52), channel_id=1, source_target_pairs={{0,3},{1,0},{2,1},{3,2},{4,7},{5,4},{6,5},{7,6},{8,11},{9,8},{10,9... | collective-permute-start | bytes 196616 | tf_op jit(solution)/shard_map/ppermute | solution.py:645
